TPU v7x, 32 devices: a whole 2x2x4 slice. The times are simulated.
32 devices in a mesh: row: 4 (over z), col: 8 (over y, x, core).
Axes of the slice: x: 2, y: 2, z: 4, core: 2. Of those that a mesh axis runs over, the one named last changes fastest.
Arguments:
- tiles: bfloat16 [4, 8, 16, 576, 576], P('row', 'col'), may hold values from -0.0625 to 0.0625
- diag_tiles: bfloat16 [32, 576, 576], P(('row', 'col')), as said below
- probes: float32 [32, 64, 576], P(('row', 'col'))
- rows_list: int32 [4, 8, 16], P('row', 'col'), may hold values from 0 to 7, as said below
- cols_list: int32 [4, 8, 16], P('row', 'col'), may hold values from 0 to 3, as said below
- counts: int32 [4, 8], P('row', 'col'), may hold values from 0 to 16, as said below
Outputs:
- solution: float32 [32, 64, 576], P(('row', 'col'))
- residual: float32 [32, 64, 576], P(('row', 'col'))
Inputs may be any that keep to these rules, and one draw needn't show every extreme that they name: `rows_list`: slots past a device's count hold 0; a held slot lies strictly below the diagonal. `cols_list`: slots past a device's count hold 0. `counts`: the busiest device holds 16 tiles. `diag_tiles`: each diagonal tile is symmetric positive definite: its diagonal entries are at least 4.4 and its off-diagonal part has spectral radius below about 1.
All inputs are finite; a program needn't handle non-finite values.
Results may differ from a plain program's by a relative error of at most 0.039.
Values may be sent and summed in bfloat16 or wider, within the bound.
No kernel may reach another device: no remote copies, remote signals or barrier semaphores. Data moves between devices by JAX's collectives and lax.ppermute only.
A program may use at most 128 MiB of HBM per device.

v0:
```python
import jax
import jax.numpy as jnp
from jax import lax
from jax.sharding import PartitionSpec as P

ITERS = 2


def gram_local(left, right):
    return jnp.einsum("tpb,tqb->pq", left, right, precision=lax.Precision.HIGHEST)


def combine(coef, block):
    return jnp.einsum("pq,tpb->tqb", coef, block, precision=lax.Precision.HIGHEST)


def solve_with(matrix, rhs):
    factor = jnp.linalg.cholesky(matrix)
    middle = lax.linalg.triangular_solve(factor, rhs, left_side=True, lower=True, transpose_a=False)
    return lax.linalg.triangular_solve(factor, middle, left_side=True, lower=True, transpose_a=True)


def curvature_sum(direction, image):
    return lax.psum(gram_local(direction, image), ("row", "col"))


def apply_operator(rounded, tiles, diag_tiles, rows_list, cols_list, counts):
    row_probe = lax.all_gather(rounded, "col", axis=0, tiled=True)
    col_probe = lax.all_gather(rounded, "row", axis=0, tiled=True)
    width_p = rounded.shape[1]
    width_b = rounded.shape[2]
    own = lax.dot_general(
        rounded[0], diag_tiles[0], (((1,), (1,)), ((), ())), preferred_element_type=jnp.float32
    )

    def turn(slot, carry):
        acc_row, acc_col = carry
        local = rows_list[0, 0, slot]
        source = cols_list[0, 0, slot]
        block = tiles[0, 0, slot]
        far = col_probe[source]
        near = row_probe[local]
        fwd = lax.dot_general(
            far, block, (((1,), (1,)), ((), ())), preferred_element_type=jnp.float32
        )
        bwd = jnp.dot(near, block, preferred_element_type=jnp.float32)
        return (acc_row.at[local].add(fwd), acc_col.at[source].add(bwd))

    start = (
        jnp.zeros((row_probe.shape[0], width_p, width_b), jnp.float32),
        jnp.zeros((col_probe.shape[0], width_p, width_b), jnp.float32),
    )
    acc_row, acc_col = lax.fori_loop(0, counts[0, 0], turn, start)
    forward = lax.psum_scatter(
        acc_row.astype(jnp.bfloat16), "col", scatter_dimension=0, tiled=True
    ).astype(jnp.float32)
    mirrored = lax.psum_scatter(
        acc_col.astype(jnp.bfloat16), "row", scatter_dimension=0, tiled=True
    ).astype(jnp.float32)
    return forward + mirrored + own[None]


def body(tiles, diag_tiles, probes, rows_list, cols_list, counts):
    solution = jnp.zeros(probes.shape, jnp.float32)
    residual = probes
    direction = probes
    norm_now = lax.psum(gram_local(residual, residual), ("row", "col"))
    for step in range(ITERS):
        image = apply_operator(
            direction.astype(jnp.bfloat16), tiles, diag_tiles, rows_list, cols_list, counts
        )
        final = step + 1 == ITERS
        curv = curvature_sum(direction, image)
        alpha = solve_with(curv, norm_now)
        solution = solution + combine(alpha, direction)
        residual = residual - combine(alpha, image)
        if not final:
            norm_next = lax.psum(gram_local(residual, residual), ("row", "col"))
            beta = solve_with(norm_now, norm_next)
            direction = residual + combine(beta, direction)
            norm_now = norm_next
    return (solution, residual)


def solution(mesh):
    placed = (
        P("row", "col", None, None, None),
        P(("row", "col"), None, None),
        P(("row", "col"), None, None),
        P("row", "col", None),
        P("row", "col", None),
        P("row", "col"),
    )
    return jax.shard_map(
        body,
        mesh=mesh,
        in_specs=placed,
        out_specs=(P(("row", "col"), None, None), P(("row", "col"), None, None)),
        check_vma=False,
    )
```

profile of v0, /device:TPU:0, one launch (start us, length us, event | category | flops | bytes accessed | tf_op | source)
XLA Modules:
  0.0 718.9 jit_solution(10008179581525326745)
XLA Ops:
  7.2 1.0 convert_element_type.30
  8.2 11.6 %all_gather.13 = bf16[8,64,576]{2,1,0:T(8,128)(2,1)S(1)} all-gather(bf16[1,64,576]{2,1,0:T(8,128)(2,1)S(1)} %convert_element_type.30), channel_id=1, replica_groups=mesh['row'=4,'col'=8] {'col'}, dimensions={0}, use_global_device_ids=true | all-gather | bytes 663552 | tf_op jit(solution)/shard_map/all_gather | solution.py:28
  19.8 15.5 %all_gather.12 = bf16[4,64,576]{2,1,0:T(8,128)(2,1)} all-gather(bf16[1,64,576]{2,1,0:T(8,128)(2,1)S(1)} %convert_element_type.30), channel_id=1, replica_groups=mesh['row'=4,'col'=8] {'row'}, dimensions={0}, use_global_device_ids=true | all-gather | bytes 368640 | tf_op jit(solution)/shard_map/all_gather | solution.py:29
  35.5 32.0 %while.28 = (s32[]{:T(128)}, f32[8,64,576]{2,1,0:T(8,128)S(1)}, f32[4,64,576]{2,1,0:T(8,128)S(1)}, s32[]{:T(128)}, s32[1,1,16]{2,1,0:T(1,128)S(1)}, /*index=5*/s...) while((s32[]{:T(128)}, f32[8,64,576]{2,1,0:T(8,128)S(1)}, ...), condition=%wide.region_3.4_spmd, body=%wide.region_0.3_spmd.sunk | while | flops 85082160 | bytes 2297161 | solution.py:53
  36.2 0.6 constant_dynamic-slice_fusion.6
  40.3 0.7 and_reduce_fusion.8
  41.1 2.1 fusion.104
  43.2 0.7 and_reduce_fusion.9
  43.9 2.0 fusion.105
  46.6 0.6 constant_dynamic-slice_fusion.6
  50.8 0.7 and_reduce_fusion.8
  51.5 2.1 fusion.104
  53.6 0.7 and_reduce_fusion.9
  54.4 2.0 fusion.105
  57.0 0.6 constant_dynamic-slice_fusion.6
  61.2 0.7 and_reduce_fusion.8
  61.9 2.1 fusion.104
  64.1 0.7 and_reduce_fusion.9
  64.8 2.0 fusion.105
  67.5 0.8 convert_element_type.33
  68.3 0.9 convert_element_type.31
  69.6 155.1 %reduce-scatter.7.cloned.1.call-done = bf16[1,64,576]{2,1,0:T(8,128)(2,1)} async-done(((bf16[4,64,576]{2,1,0:T(8,128)(2,1)}), bf16[1,64,576]{2,1,0:T(8,128)(2,1)}) %reduce-scatter.7.cloned.1.call-update) | async-done | bytes 73744 | tf_op jit(solution)/shard_map/reduce_scatter | solution.py:57
  224.7 35.9 %reduce-scatter.5.cloned.1.call-done = bf16[1,64,576]{2,1,0:T(8,128)(2,1)} async-done(((bf16[8,64,576]{2,1,0:T(8,128)(2,1)}), bf16[1,64,576]{2,1,0:T(8,128)(2,1)}) %reduce-scatter.5.cloned.1.call-update) | async-done | bytes 73744 | tf_op jit(solution)/shard_map/reduce_scatter | solution.py:54
  260.7 1.3 fusion.37
  262.2 39.8 %all-reduce = (f32[64,64]{0,1:T(8,128)S(1)}, f32[64,64]{0,1:T(8,128)S(1)}) all-reduce(f32[64,64]{0,1:T(8,128)S(1)} %fusion.49, f32[64,64]{0,1:T(8,128)S(1)} %convolution_bitcast_fusion.10), channel_id=1, replica_groups=mesh['row'=4,'col'=8] {'row','col'}, use_global_device_ids=true, to_apply=%region_9.11 | all-reduce | flops 8192 | bytes 65536 | tf_op jit(solution)/shard_map/psum | solution.py:67
  302.3 5.8 cholesky.70
  308.2 0.6 compare_reduce_fusion.1
  308.8 0.7 fusion.55
  309.5 4.9 custom-call.15
  314.4 5.9 cholesky.59
  320.3 0.6 compare_reduce_fusion.2
  320.9 0.7 fusion.54
  321.6 4.9 custom-call.13
  327.8 41.1 %psum.30 = f32[64,64]{1,0:T(8,128)S(1)} all-reduce(f32[64,64]{1,0:T(8,128)S(1)} %fusion.45), channel_id=1, replica_groups=mesh['row'=4,'col'=8] {'row','col'}, use_global_device_ids=true, to_apply=%region_10.14 | all-reduce | flops 4096 | bytes 32768 | tf_op jit(solution)/shard_map/psum | solution.py:78
  369.7 11.9 %all_gather.15 = bf16[8,64,576]{2,1,0:T(8,128)(2,1)} all-gather(bf16[1,64,576]{2,1,0:T(8,128)(2,1)S(1)} %get-tuple-element.197), channel_id=1, replica_groups=mesh['row'=4,'col'=8] {'col'}, dimensions={0}, use_global_device_ids=true | all-gather | bytes 663552 | tf_op jit(solution)/shard_map/all_gather | solution.py:28
  381.6 14.3 %all_gather.14 = bf16[4,64,576]{2,1,0:T(8,128)(2,1)S(1)} all-gather(bf16[1,64,576]{2,1,0:T(8,128)(2,1)S(1)} %get-tuple-element.197), channel_id=1, replica_groups=mesh['row'=4,'col'=8] {'row'}, dimensions={0}, use_global_device_ids=true | all-gather | bytes 368640 | tf_op jit(solution)/shard_map/all_gather | solution.py:29
  396.0 38.8 %while.29 = (s32[]{:T(128)}, f32[8,64,576]{2,1,0:T(8,128)S(1)}, f32[4,64,576]{2,1,0:T(8,128)S(1)}, s32[]{:T(128)}, s32[1,1,16]{2,1,0:T(1,128)}, /*index=5*/s32[1...) while((s32[]{:T(128)}, f32[8,64,576]{2,1,0:T(8,128)S(1)}, ...), condition=%wide.region_14.18_spmd, body=%wide.region_11.17_spmd.sunk | while | flops 85082160 | bytes 2297161 | solution.py:53
  396.7 1.3 constant_dynamic-slice_fusion.7
  401.8 1.4 and_reduce_fusion.10
  403.2 2.1 fusion.110
  405.3 1.4 and_reduce_fusion.11
  406.7 2.1 fusion.111
  409.4 1.3 constant_dynamic-slice_fusion.7
  414.5 1.4 and_reduce_fusion.10
  415.9 2.1 fusion.110
  418.0 1.4 and_reduce_fusion.11
  419.4 2.1 fusion.111
  422.1 1.3 constant_dynamic-slice_fusion.7
  427.2 1.4 and_reduce_fusion.10
  428.6 2.1 fusion.110
  430.7 1.4 and_reduce_fusion.11
  432.1 2.1 fusion.111
  434.9 0.8 convert_element_type.38
  435.7 0.9 convert_element_type.36
  437.0 183.6 %reduce-scatter.11.cloned.1.call-done = bf16[1,64,576]{2,1,0:T(8,128)(2,1)} async-done(((bf16[4,64,576]{2,1,0:T(8,128)(2,1)}), bf16[1,64,576]{2,1,0:T(8,128)(2,1)}) %reduce-scatter.11.cloned.1.call-update) | async-done | bytes 73744 | tf_op jit(solution)/shard_map/reduce_scatter | solution.py:57
  620.6 35.9 %reduce-scatter.9.cloned.1.call-done = bf16[1,64,576]{2,1,0:T(8,128)(2,1)} async-done(((bf16[8,64,576]{2,1,0:T(8,128)(2,1)}), bf16[1,64,576]{2,1,0:T(8,128)(2,1)}) %reduce-scatter.9.cloned.1.call-update) | async-done | bytes 73744 | tf_op jit(solution)/shard_map/reduce_scatter | solution.py:54
  656.5 1.3 fusion.39
  658.1 39.7 %psum.31 = f32[64,64]{0,1:T(8,128)S(1)} all-reduce(f32[64,64]{0,1:T(8,128)S(1)} %fusion.43), channel_id=1, replica_groups=mesh['row'=4,'col'=8] {'row','col'}, use_global_device_ids=true, to_apply=%region_17.21 | all-reduce | flops 4096 | bytes 32768 | tf_op jit(solution)/shard_map/psum | solution.py:24
  697.8 5.8 cholesky.81
  703.7 0.6 compare_reduce_fusion
  704.4 0.7 fusion.56
  705.0 4.9 custom-call.17
  710.4 1.0 fusion.34
  711.4 1.0 fusion.32
  (57 shorter events, 4.6 us)
Async XLA Ops:
  7.2 253.5 %copy-start = (bf16[1,576,576]{2,1,0:T(8,128)(2,1)S(1)}, bf16[1,576,576]{2,1,0:T(8,128)(2,1)}, u32[]{:S(2)}) copy-start(bf16[1,576,576]{2,1,0:T(8,128)(2,1)} %param.24) | copy-start | bytes 1990660
  7.2 217.5 %reduce-scatter.7.cloned.1.call-start = ((), (), s32[]{:S(2)}) async-start(), calls=%async_computation.5 | async-start | bytes 409600 | tf_op jit(solution)/shard_map/reduce_scatter | solution.py:57
  8.2 27.2 %copy-start.4 = (bf16[1,64,576]{2,1,0:T(8,128)(2,1)}, bf16[1,64,576]{2,1,0:T(8,128)(2,1)S(1)}, u32[]{:S(2)}) copy-start(bf16[1,64,576]{2,1,0:T(8,128)(2,1)S(1)} %convert_element_type.30) | copy-start | bytes 221188
  19.8 15.6 %copy-start.8 = (s32[1,1,16]{2,1,0:T(1,128)S(1)}, s32[1,1,16]{2,1,0:T(1,128)}, u32[]{:S(2)}) copy-start(s32[1,1,16]{2,1,0:T(1,128)} %param.26) | copy-start | bytes 196
  19.8 15.7 %copy-start.9 = (s32[1,1,16]{2,1,0:T(1,128)S(1)}, s32[1,1,16]{2,1,0:T(1,128)}, u32[]{:S(2)}) copy-start(s32[1,1,16]{2,1,0:T(1,128)} %param.27) | copy-start | bytes 196
  19.8 15.7 %copy-start.10 = (s32[3]{0:T(128)S(1)}, s32[3]{0:T(128)}, u32[]{:S(2)}) copy-start(s32[3]{0:T(128)} %constant.124.clone.1) | copy-start | bytes 40
  19.8 15.7 %copy-start.11 = (s32[3]{0:T(128)S(1)}, s32[3]{0:T(128)}, u32[]{:S(2)}) copy-start(s32[3]{0:T(128)} %constant.127.clone.1) | copy-start | bytes 40
  68.3 192.4 %reduce-scatter.5.cloned.1.call-start = ((), (), s32[]{:S(2)}) async-start(), calls=%async_computation.4 | async-start | bytes 737280 | tf_op jit(solution)/shard_map/reduce_scatter | solution.py:54
  68.3 1.0 copy-start.1
  68.3 192.3 %copy-start.5 = (bf16[1,64,576]{2,1,0:T(8,128)(2,1)S(1)}, bf16[1,64,576]{2,1,0:T(8,128)(2,1)}, u32[]{:S(2)}) copy-start(bf16[1,64,576]{2,1,0:T(8,128)(2,1)} %copy-done.4) | copy-start | bytes 221188
  69.3 551.3 %reduce-scatter.11.cloned.1.call-start = ((), (), s32[]{:S(2)}) async-start(), calls=%async_computation.7 | async-start | bytes 409600 | tf_op jit(solution)/shard_map/reduce_scatter | solution.py:57
  326.9 0.6 copy-start.6
  369.7 11.9 %copy-start.2 = (bf16[1,64,576]{2,1,0:T(8,128)(2,1)}, bf16[1,64,576]{2,1,0:T(8,128)(2,1)S(1)}, u32[]{:S(2)}) copy-start(bf16[1,64,576]{2,1,0:T(8,128)(2,1)S(1)} %get-tuple-element.197) | copy-start | bytes 221188
  435.7 220.8 %reduce-scatter.9.cloned.1.call-start = ((), (), s32[]{:S(2)}) async-start(), calls=%async_computation.6 | async-start | bytes 737280 | tf_op jit(solution)/shard_map/reduce_scatter | solution.py:54
  435.7 1.0 copy-start.7
  435.7 220.8 %copy-start.3 = (bf16[1,64,576]{2,1,0:T(8,128)(2,1)S(1)}, bf16[1,64,576]{2,1,0:T(8,128)(2,1)}, u32[]{:S(2)}) copy-start(bf16[1,64,576]{2,1,0:T(8,128)(2,1)} %copy-done.2) | copy-start | bytes 221188
Sparse Core Ops, SparseCore 0:
  68.4 156.2 reduce-scatter.6
  227.8 32.7 reduce-scatter.4
  435.8 184.7 reduce-scatter.10
  623.6 32.8 reduce-scatter.8
where the time goes:
time: 724 us; the launch traced here: 719 us
  waiting for transfers between devices  411 us (57%)
  blocking collectives  174 us (24%)
  other arithmetic  53.3 us (7%)
  matrix products  33 us (5%)
  loops' own time  27.4 us (4%)
  between operations  14.1 us (2%)
    reduce_scatter x2, waiting for transfers between devices, apply_operator(): lax.psum_scatter(acc_col.astype(jnp.bfloat16), 'row', scatter_dimension=0...  339 us
    reduce_scatter x2, waiting for transfers between devices, apply_operator(): lax.psum_scatter(acc_row.astype(jnp.bfloat16), 'col', scatter_dimension=0...  71.8 us
    psum x1, blocking collectives, body(): norm_next = lax.psum(gram_local(residual, residual), ('row', 'col'))  41.1 us
    psum x1, blocking collectives, body(): norm_now = lax.psum(gram_local(residual, residual), ('row', 'col'))  39.8 us
    psum x1, blocking collectives, curvature_sum(): return lax.psum(gram_local(direction, image), ('row', 'col'))  39.7 us
    all_gather x2, blocking collectives, apply_operator(): col_probe = lax.all_gather(rounded, 'row', axis=0, tiled=True)  29.8 us
    another operation x2, loops' own time, apply_operator(): acc_row, acc_col = lax.fori_loop(0, counts[0, 0], turn, start)  27.4 us
    all_gather x2, blocking collectives, apply_operator(): row_probe = lax.all_gather(rounded, 'col', axis=0, tiled=True)  23.5 us
  transfers between devices with their start and end apart: 4, of which 4 were waited for; matrix products, arithmetic and copies ran while one was open for 0% of the time, Pallas kernels for 0%

commit v1 on v0

v1 whole, which is shorter than its diff:
```python
import functools

import jax
import jax.numpy as jnp
from jax import lax
from jax.experimental import pallas as pl
from jax.experimental.pallas import tpu as pltpu
from jax.sharding import PartitionSpec as P

ITERS = 2
F32 = jnp.float32
BF16 = jnp.bfloat16
HI = lax.Precision.HIGHEST
NT = (((1,), (1,)), ((), ()))
NN = (((1,), (0,)), ((), ()))
TN = (((0,), (0,)), ((), ()))
VMEM = pl.BlockSpec(memory_space=pltpu.VMEM)
SMEM = pl.BlockSpec(memory_space=pltpu.SMEM)
ANY = pl.BlockSpec(memory_space=pl.ANY)


def dot32(left, right, dims):
    return lax.dot_general(left, right, dims, precision=HI, preferred_element_type=F32)


def dot16(left, right, dims):
    return lax.dot_general(left, right, dims, preferred_element_type=F32)


def dot_exact16(left, right, dims):
    first = right.astype(BF16)
    rest = right - first.astype(F32)
    second = rest.astype(BF16)
    third = (rest - second.astype(F32)).astype(BF16)
    return dot16(left, first, dims) + (dot16(left, second, dims) + dot16(left, third, dims))


def eliminate(systems):
    size = systems[0].shape[0]
    rows = lax.broadcasted_iota(jnp.int32, (size, 1), 0)
    for k in range(size):
        after = []
        for system in systems:
            row = system[k : k + 1, :]
            pivot = row[:, k : k + 1]
            scaled = row * (1.0 / pivot)
            after.append(jnp.where(rows == k, scaled, system - system[:, k : k + 1] * scaled))
        systems = after
    return [system[:, size:] for system in systems]


def operator_kernel(
    counts, rows_at, cols_at, near_own, near_far, *rest, n_row, n_chip, slots
):
    far_in = rest[:n_row]
    tiles, diag, extra = rest[n_row : n_row + 3]
    out = rest[n_row + 3 :]
    give_core, keep = out[0], out[1]
    give_row = out[2 : 2 + n_row - 1]
    grams = out[2 + n_row - 1]
    near, far, acc_row, acc_col, held, arrived = out[2 + n_row :]
    count = counts[0]

    def fetch(slot):
        return pltpu.make_async_copy(tiles.at[slot], held.at[slot], arrived.at[slot])

    def begin(slot, carry):
        fetch(slot).start()
        return carry

    lax.fori_loop(0, count, begin, 0)
    for d in range(n_chip):
        near[d] = near_own[d]
        near[n_chip + d] = near_far[d]
    for d in range(n_row):
        far[d] = far_in[d][...]
    acc_row[...] = jnp.zeros_like(acc_row)
    acc_col[...] = jnp.zeros_like(acc_col)
    mine = near_own[0]
    own = dot16(mine, diag[...], NT)
    p_size = own.shape[0]

    def turn(slot, carry):
        fetch(slot).wait()
        tile = held[slot]
        i = rows_at[slot]
        j = cols_at[slot]
        acc_row[i] += dot16(far[j], tile, NT)
        acc_col[j] += dot16(near[i], tile, NN)
        return carry

    lax.fori_loop(0, count, turn, 0)
    half = dot_exact16(far[0], acc_col[0], NT)
    for d in range(1, n_row):
        half += dot_exact16(far[d], acc_col[d], NT)
        give_row[d - 1][...] = acc_col[d].astype(BF16)
    grams[:, :p_size] = half + half.T + dot_exact16(mine, own, NT)
    grams[:, p_size:] = extra[...]
    for d in range(n_chip):
        give_core[d] = acc_row[n_chip + d].astype(BF16)
        keep[d] = acc_row[d]
    keep[0] += own + acc_col[0]


def join_kernel(keep, came, grams, grams_came, mine, *give):
    mine[...] = keep[0] + came[0].astype(F32)
    for d in range(1, keep.shape[0]):
        give[d - 1][...] = (keep[d] + came[d].astype(F32)).astype(BF16)
    give[-1][...] = grams[...] + grams_came[...]


def sum_kernel(*refs):
    total = refs[0][...]
    for ref in refs[1:-1]:
        total += ref[...]
    refs[-1][...] = total


def first_kernel(mine, probes, *rest, n_in, n_gram):
    image = mine[...]
    for ref in rest[:n_in]:
        image += ref[...].astype(F32)
    total = rest[n_in][...]
    for ref in rest[n_in + 1 : n_in + n_gram]:
        total += ref[...]
    image_out, residual_out, rounded, extra, small = rest[n_in + n_gram :]
    size = image.shape[0]
    curv = total[:, :size]
    norm = total[:, size : 2 * size]
    eye = (
        lax.broadcasted_iota(jnp.int32, (size, size), 0)
        == lax.broadcasted_iota(jnp.int32, (size, size), 1)
    ).astype(F32)
    alpha, inverse = eliminate(
        [jnp.concatenate([curv, norm], 1), jnp.concatenate([norm, eye], 1)]
    )
    residual = probes[...] - dot32(alpha, image, TN)
    image_out[...] = image
    residual_out[...] = residual
    rounded[...] = residual.astype(BF16)
    extra[:, :size] = dot32(residual, residual, NT)
    extra[:, size:] = dot32(image, residual, NT)
    small[0] = curv
    small[1] = alpha
    small[2] = inverse


def last_kernel(mine, probes, image_in, residual_in, small, *rest, n_in, n_gram):
    forward = mine[...]
    for ref in rest[:n_in]:
        forward += ref[...].astype(F32)
    total = rest[n_in][...]
    for ref in rest[n_in + 1 : n_in + n_gram]:
        total += ref[...]
    solution_out, residual_out = rest[n_in + n_gram :]
    size = forward.shape[0]
    curv, alpha, inverse = small[0], small[1], small[2]
    norm = total[:, size : 2 * size]
    cross = total[:, 2 * size :]
    beta = dot32(inverse, norm, NN)
    mixed = dot32(cross, beta, TN)
    curv_next = total[:, :size] + mixed + mixed.T + dot32(beta, dot32(curv, beta, NN), TN)
    (step,) = eliminate([jnp.concatenate([curv_next, norm], 1)])
    both = dot32(beta, step, NN)
    residual = residual_in[...]
    solution_out[...] = dot32(alpha + both, probes[...], TN) + dot32(step, residual, TN)
    residual_out[...] = residual - dot32(step, forward, TN) - dot32(both, image_in[...], TN)


def call(kernel, outs, args, specs=None, scratch=(), limit=48, name=None):
    return pl.pallas_call(
        kernel,
        out_shape=outs,
        in_specs=[VMEM] * len(args) if specs is None else specs,
        out_specs=[VMEM] * len(outs),
        scratch_shapes=list(scratch),
        compiler_params=pltpu.CompilerParams(vmem_limit_bytes=limit << 20),
        name=name,
    )(*args)


def body(n_row, n_col, tiles, diag_tiles, probes, rows_list, cols_list, counts):
    n_chip = n_col // 2
    p_size, width = probes.shape[1:]
    slots = tiles.shape[2]
    shape = jax.ShapeDtypeStruct
    block32 = shape((p_size, width), F32)
    block16 = shape((p_size, width), BF16)

    def over(value, axis, delta):
        size = n_row if axis == "row" else n_col
        return lax.ppermute(value, axis, [(i, i ^ delta) for i in range(size)])

    def over_chips(value):
        return [over(value, "col", 2 * d) for d in range(1, n_chip)]

    def over_rows(value):
        return [over(value, "row", d) for d in range(1, n_row)]

    apart = rows_list[0, 0] ^ lax.axis_index("col")
    rows_at = (apart % 2) * n_chip + apart // 2
    cols_at = cols_list[0, 0] ^ lax.axis_index("row")
    probes = probes[0]

    def apply_operator(rounded, extra):
        far = [rounded] + over_rows(rounded)
        near_own = jnp.stack([rounded] + over_chips(rounded))
        near_far = over(near_own, "col", 1)
        args = [counts[0], rows_at, cols_at, near_own, near_far, *far, tiles[0, 0], diag_tiles[0], extra]
        specs = [SMEM] * 3 + [VMEM] * (2 + n_row) + [ANY, VMEM, VMEM]
        outs = [shape((n_chip, p_size, width), BF16), shape((n_chip, p_size, width), F32)]
        outs += [block16] * (n_row - 1) + [shape((p_size, 3 * p_size), F32)]
        scratch = [
            pltpu.VMEM((n_col, p_size, width), BF16),
            pltpu.VMEM((n_row, p_size, width), BF16),
            pltpu.VMEM((n_col, p_size, width), F32),
            pltpu.VMEM((n_row, p_size, width), F32),
            pltpu.VMEM((slots, width, width), BF16),
            pltpu.SemaphoreType.DMA((slots,)),
        ]
        kernel = functools.partial(operator_kernel, n_row=n_row, n_chip=n_chip, slots=slots)
        got = call(kernel, outs, args, specs, scratch, name="operator")
        give_core, keep, give_row, grams = got[0], got[1], got[2:-1], got[-1]
        came = over(give_core, "col", 1)
        grams_came = over(grams, "col", 1)
        from_rows = [over(block, "row", d + 1) for d, block in enumerate(give_row)]
        outs = [block32] + [block16] * (n_chip - 1) + [shape(grams.shape, F32)]
        got = call(join_kernel, outs, [keep, came, grams, grams_came], name="join")
        from_chips = [over(block, "col", 2 * d + 2) for d, block in enumerate(got[1:-1])]
        grams = got[-1]
        chip_grams = [grams] + over_chips(grams)
        (grams,) = call(sum_kernel, [shape(grams.shape, F32)], chip_grams, name="gram_sum")
        return got[0], from_chips + from_rows, [grams] + over_rows(grams)

    norm = dot32(probes, probes, NT)
    extra = jnp.concatenate([norm, jnp.zeros_like(norm)], 1)
    mine, parts, grams = apply_operator(probes.astype(BF16), extra)
    outs = [block32, block32, block16, shape((p_size, 2 * p_size), F32), shape((3, p_size, p_size), F32)]
    counted = {"n_in": len(parts), "n_gram": len(grams)}
    image, residual, rounded, extra, small = call(
        functools.partial(first_kernel, **counted), outs, [mine, probes, *parts, *grams], name="first_step"
    )
    mine, parts, grams = apply_operator(rounded, extra)
    solved, residual = call(
        functools.partial(last_kernel, **counted),
        [block32, block32],
        [mine, probes, image, residual, small, *parts, *grams],
        name="last_step",
    )
    return solved[None], residual[None]


def solution(mesh):
    placed = (
        P("row", "col", None, None, None),
        P(("row", "col"), None, None),
        P(("row", "col"), None, None),
        P("row", "col", None),
        P("row", "col", None),
        P("row", "col"),
    )
    return jax.shard_map(
        functools.partial(body, mesh.shape["row"], mesh.shape["col"]),
        mesh=mesh,
        in_specs=placed,
        out_specs=(P(("row", "col"), None, None), P(("row", "col"), None, None)),
        check_vma=False,
    )
```

time: 724 us -> 112 us (0.15)
  waiting for transfers between devices: 411 us -> 21.6 us
  blocking collectives: 174 us -> 0 us
  starting transfers between devices: 0.16 us -> 61.4 us
  other arithmetic: 53.3 us -> 2.56 us
  matrix products: 33 us -> 1.29 us
  loops' own time: 27.4 us -> 0 us
  Pallas kernels: 0 us -> 22.4 us
  between operations: 14.1 us -> 1.46 us
    reduce_scatter x4 -> x0, waiting for transfers between devices: 410 us -> none  [the longest x2 339 us: apply_operator(): lax.psum_scatter(acc_col.astype(jnp.bfloat16), 'row', scatter_dimension=0...]
    psum x3 -> x0, blocking collectives: 121 us -> none  [the longest x1 41.1 us: body(): norm_next = lax.psum(gram_local(residual, residual), ('row', 'col'))]
    ppermute x0 -> x42, starting transfers between devices: none -> 61.4 us  [over(): return lax.ppermute(value, axis, [(i, i ^ delta) for i in range(size)])]
    all_gather x4 -> x0, blocking collectives: 53.2 us -> none  [the longest x2 29.8 us: apply_operator(): col_probe = lax.all_gather(rounded, 'row', axis=0, tiled=True)]
    another operation x27 -> x2, other arithmetic: 49 us -> 0.14 us  [apply_operator(): near_own = jnp.stack([rounded] + over_chips(rounded))]
    dot_general x23 -> x1, matrix products: 31.8 us -> 1.29 us  [dot32(): lax.dot_general(left, right, dims, precision=HI, preferred_element_type=F32)]
    another operation x2 -> x0, loops' own time: 27.4 us -> none  [apply_operator(): acc_row, acc_col = lax.fori_loop(0, counts[0, 0], turn, start)]
    pallas_call x0 -> x8, Pallas kernels: none -> 22.4 us  [call(): pl.pallas_call(kernel, out_shape=outs, in_specs=[VMEM] * len(args) if spe...]
  transfers between devices with their start and end apart: 4 -> 42, of which waited for: 4 -> 19; matrix products, arithmetic and copies ran while one was open for 0% -> 2% of each run, Pallas kernels for 0% -> 0%
where the time goes in v1:
time: 112 us
  starting transfers between devices  61.4 us (55%)
  Pallas kernels  22.4 us (20%)
  waiting for transfers between devices  21.6 us (19%)
  other arithmetic  2.56 us (2%)
  between operations  1.46 us (1%)
  matrix products  1.29 us (1%)
  local copies, waits for them, and re-layouts  1.14 us (1%)
    ppermute x42, starting transfers between devices, over(): return lax.ppermute(value, axis, [(i, i ^ delta) for i in range(size)])  61.4 us
    pallas_call x8, Pallas kernels, call(): pl.pallas_call(kernel, out_shape=outs, in_specs=[VMEM] * len(args) if spe...  22.4 us
    ppermute x42, waiting for transfers between devices, over(): return lax.ppermute(value, axis, [(i, i ^ delta) for i in range(size)])  21.6 us
  transfers between devices with their start and end apart: 42, of which 19 were waited for; matrix products, arithmetic and copies ran while one was open for 2% of the time, Pallas kernels for 0%

profile of v1, /device:TPU:0, one launch (start us, length us, event | category | flops | bytes accessed | tf_op | source)
XLA Modules:
  0.0 111.8 jit_solution(1956040301479597451)
XLA Ops:
  0.7 1.1 fusion.4
  1.8 5.1 %collective-permute-start.6 = (bf16[64,576]{1,0:T(8,128)(2,1)S(1)}, bf16[64,576]{1,0:T(8,128)(2,1)S(1)}, u32[]{:S(2)}, u32[]{:S(2)}) collective-permute-start(bf16[64,576]{1,0:T(8,128)(2,1)S(1)} %get-tuple-element.61.rest_0_), channel_id=1, source_target_pairs={{0,24},{8,16},{16,8},{24,0},{1,25},{9,17},{17,9},{25,1},{2,26},{10... | collective-permute-start | bytes 221192 | tf_op jit(solution)/shard_map/ppermute | solution.py:192
  6.9 2.4 %collective-permute-start.2 = (bf16[64,576]{1,0:T(8,128)(2,1)S(1)}, bf16[64,576]{1,0:T(8,128)(2,1)S(1)}, u32[]{:S(2)}, u32[]{:S(2)}) collective-permute-start(bf16[64,576]{1,0:T(8,128)(2,1)S(1)} %get-tuple-element.61.rest_0_), channel_id=1, source_target_pairs={{0,6},{1,7},{2,4},{3,5},{4,2},{5,3},{6,0},{7,1},{8,14},{9,15},{10,... | collective-permute-start | bytes 221192 | tf_op jit(solution)/shard_map/ppermute | solution.py:192
  9.3 0.5 collective-permute-start.1
  9.8 0.5 collective-permute-start
  10.4 1.3 %fusion.2 = f32[64,64]{1,0:T(8,128)S(1)} fusion(f32[1,64,576]{2,1,0:T(8,128)} %param.8), kind=kOutput, calls=%fused_computation.11 | convolution fusion | flops 28311552 | bytes 163840 | tf_op jit(solution)/shard_map/dot_general | solution.py:23
  11.7 0.7 collective-permute-done.2
  12.3 0.6 collective-permute-start.4
  13.0 0.9 collective-permute-done.1
  13.8 0.4 collective-permute-done
  14.4 0.7 xor_bitcast_fusion.cols_at
  15.1 0.7 fusion.1.rows_at
  16.4 0.3 collective-permute-done.4.rest_1_
  16.8 1.1 copy-done
  17.9 3.9 %operator.2 = (bf16[4,64,576]{2,1,0:T(8,128)(2,1)S(1)}, f32[4,64,576]{2,1,0:T(8,128)S(1)}, bf16[64,576]{1,0:T(8,128)(2,1)S(1)}, bf16[64,576]{1,0:T(8,128)(2,1)S(...) custom-call(s32[1]{0:T(128)} %bitcast.31.counts, s32[16]{0:T(128)S(1)} %fusion.1.rows_at, ...), custom_call_target="tpu_custom_call" | custom-call | tf_op jit(solution)/shard_map/operator/pallas_call | solution.py:171
  21.8 0.2 collective-permute-start.7
  22.0 0.3 collective-permute-start.8
  22.4 2.9 %collective-permute-start.12 = (bf16[64,576]{1,0:T(8,128)(2,1)S(1)}, bf16[64,576]{1,0:T(8,128)(2,1)S(1)}, u32[]{:S(2)}, u32[]{:S(2)}) collective-permute-start(bf16[64,576]{1,0:T(8,128)(2,1)S(1)} %get-tuple-element.38), channel_id=1, source_target_pairs={{0,8},{8,0},{16,24},{24,16},{1,9},{9,1},{17,25},{25,17},{2,10},{10... | collective-permute-start | bytes 221192 | tf_op jit(solution)/shard_map/ppermute | solution.py:192
  25.4 2.5 %collective-permute-start.17 = (f32[64,192]{1,0:T(8,128)S(1)}, f32[64,192]{1,0:T(8,128)S(1)}, u32[]{:S(2)}, u32[]{:S(2)}) collective-permute-start(f32[64,192]{1,0:T(8,128)S(1)} %get-tuple-element.41.refs_0_), channel_id=1, source_target_pairs={{0,6},{1,7},{2,4},{3,5},{4,2},{5,3},{6,0},{7,1},{8,14},{9,15},{10,... | collective-permute-start | bytes 147464 | tf_op jit(solution)/shard_map/ppermute | solution.py:192
  27.9 6.3 %collective-permute-start.13 = (bf16[64,576]{1,0:T(8,128)(2,1)S(1)}, bf16[64,576]{1,0:T(8,128)(2,1)S(1)}, u32[]{:S(2)}, u32[]{:S(2)}) collective-permute-start(bf16[64,576]{1,0:T(8,128)(2,1)S(1)} %get-tuple-element.39), channel_id=1, source_target_pairs={{0,16},{8,24},{16,0},{24,8},{1,17},{9,25},{17,1},{25,9},{2,18},{10... | collective-permute-start | bytes 221192 | tf_op jit(solution)/shard_map/ppermute | solution.py:192
  34.1 1.1 %collective-permute-start.16 = (f32[64,192]{1,0:T(8,128)S(1)}, f32[64,192]{1,0:T(8,128)S(1)}, u32[]{:S(2)}, u32[]{:S(2)}) collective-permute-start(f32[64,192]{1,0:T(8,128)S(1)} %get-tuple-element.41.refs_0_), channel_id=1, source_target_pairs={{0,4},{1,5},{2,6},{3,7},{4,0},{5,1},{6,2},{7,3},{8,12},{9,13},{10,... | collective-permute-start | bytes 147464 | tf_op jit(solution)/shard_map/ppermute | solution.py:192
  35.2 0.6 collective-permute-start.14
  35.9 2.0 %collective-permute-start.9 = (bf16[64,576]{1,0:T(8,128)(2,1)S(1)}, bf16[64,576]{1,0:T(8,128)(2,1)S(1)}, u32[]{:S(2)}, u32[]{:S(2)}) collective-permute-start(bf16[64,576]{1,0:T(8,128)(2,1)S(1)} %get-tuple-element.35), channel_id=1, source_target_pairs={{0,2},{1,3},{2,0},{3,1},{4,6},{5,7},{6,4},{7,5},{8,10},{9,11},{10,... | collective-permute-start | bytes 221192 | tf_op jit(solution)/shard_map/ppermute | solution.py:192
  37.9 0.5 collective-permute-done.16.refs_2_
  38.4 1.1 %collective-permute-start.10 = (bf16[64,576]{1,0:T(8,128)(2,1)S(1)}, bf16[64,576]{1,0:T(8,128)(2,1)S(1)}, u32[]{:S(2)}, u32[]{:S(2)}) collective-permute-start(bf16[64,576]{1,0:T(8,128)(2,1)S(1)} %get-tuple-element.36), channel_id=1, source_target_pairs={{0,4},{1,5},{2,6},{3,7},{4,0},{5,1},{6,2},{7,3},{8,12},{9,13},{10,... | collective-permute-start | bytes 221192 | tf_op jit(solution)/shard_map/ppermute | solution.py:192
  39.5 1.6 %collective-permute-start.11 = (bf16[64,576]{1,0:T(8,128)(2,1)S(1)}, bf16[64,576]{1,0:T(8,128)(2,1)S(1)}, u32[]{:S(2)}, u32[]{:S(2)}) collective-permute-start(bf16[64,576]{1,0:T(8,128)(2,1)S(1)} %get-tuple-element.37), channel_id=1, source_target_pairs={{0,6},{1,7},{2,4},{3,5},{4,2},{5,3},{6,0},{7,1},{8,14},{9,15},{10,... | collective-permute-start | bytes 221192 | tf_op jit(solution)/shard_map/ppermute | solution.py:192
  41.1 2.5 %collective-permute-start.20 = (f32[64,192]{1,0:T(8,128)S(1)}, f32[64,192]{1,0:T(8,128)S(1)}, u32[]{:S(2)}, u32[]{:S(2)}) collective-permute-start(f32[64,192]{1,0:T(8,128)S(1)} %gram_sum.2.rest_6_), channel_id=1, source_target_pairs={{0,24},{8,16},{16,8},{24,0},{1,25},{9,17},{17,9},{25,1},{2,26},{10... | collective-permute-start | bytes 147464 | tf_op jit(solution)/shard_map/ppermute | solution.py:192
  43.6 0.9 collective-permute-start.19
  44.5 1.1 collective-permute-start.18
  45.6 1.9 %collective-permute-done.20.rest_9_ = f32[64,192]{1,0:T(8,128)S(1)} collective-permute-done((f32[64,192]{1,0:T(8,128)S(1)}, f32[64,192]{1,0:T(8,128)S(1)}, u32[]{:S(2)}, u32[]{:S(2)}) %collective-permute-start.20) | collective-permute-done | bytes 49184 | tf_op jit(solution)/shard_map/ppermute | solution.py:192
  47.4 1.8 %collective-permute-done.19.rest_8_ = f32[64,192]{1,0:T(8,128)S(1)} collective-permute-done((f32[64,192]{1,0:T(8,128)S(1)}, f32[64,192]{1,0:T(8,128)S(1)}, u32[]{:S(2)}, u32[]{:S(2)}) %collective-permute-start.19) | collective-permute-done | bytes 49184 | tf_op jit(solution)/shard_map/ppermute | solution.py:192
  49.2 0.5 collective-permute-done.18.rest_7_
  49.8 6.9 %first_step.1 = (f32[64,576]{1,0:T(8,128)S(1)}, f32[64,576]{1,0:T(8,128)S(1)}, bf16[64,576]{1,0:T(8,128)(2,1)S(1)}, f32[64,128]{1,0:T(8,128)S(1)}, f32[3,64,64]{2,1,0:T(8,128)S(1)}) custom-call(f32[64,576]{1,0:T(8,128)S(1)} %get-tuple-element.34.mine, f32[64,576]{1,0:T(8,128)S(1)} %bitcast.35, bf16[64,576]{1,0:T(8,128)(2,1)S(1)} %collective-permute-done.9.rest_0_, ...), custom_call_target="tpu_custom_call" | custom-call | tf_op jit(solution)/shard_map/first_step/pallas_call | solution.py:171
  56.7 0.6 collective-permute-start.23
  57.3 1.7 %collective-permute-start.22 = (bf16[64,576]{1,0:T(8,128)(2,1)S(1)}, bf16[64,576]{1,0:T(8,128)(2,1)S(1)}, u32[]{:S(2)}, u32[]{:S(2)}) collective-permute-start(bf16[64,576]{1,0:T(8,128)(2,1)S(1)} %get-tuple-element.42.rest_0_), channel_id=1, source_target_pairs={{0,4},{1,5},{2,6},{3,7},{4,0},{5,1},{6,2},{7,3},{8,12},{9,13},{10,... | collective-permute-start | bytes 221192 | tf_op jit(solution)/shard_map/ppermute | solution.py:192
  58.9 1.3 %collective-permute-start.21 = (bf16[64,576]{1,0:T(8,128)(2,1)S(1)}, bf16[64,576]{1,0:T(8,128)(2,1)S(1)}, u32[]{:S(2)}, u32[]{:S(2)}) collective-permute-start(bf16[64,576]{1,0:T(8,128)(2,1)S(1)} %get-tuple-element.42.rest_0_), channel_id=1, source_target_pairs={{0,2},{1,3},{2,0},{3,1},{4,6},{5,7},{6,4},{7,5},{8,10},{9,11},{10,... | collective-permute-start | bytes 221192 | tf_op jit(solution)/shard_map/ppermute | solution.py:192
  60.3 2.0 %collective-permute-done.23 = bf16[64,576]{1,0:T(8,128)(2,1)S(1)} collective-permute-done((bf16[64,576]{1,0:T(8,128)(2,1)S(1)}, bf16[64,576]{1,0:T(8,128)(2,1)S(1)}, u32[]{:S(2)}, u32[]{:S(2)}) %collective-permute-start.23) | collective-permute-done | bytes 73760 | tf_op jit(solution)/shard_map/ppermute | solution.py:192
  62.2 0.4 collective-permute-done.22
  62.6 0.8 collective-permute-done.21
  63.5 2.0 %collective-permute-start.27 = (bf16[64,576]{1,0:T(8,128)(2,1)S(1)}, bf16[64,576]{1,0:T(8,128)(2,1)S(1)}, u32[]{:S(2)}, u32[]{:S(2)}) collective-permute-start(bf16[64,576]{1,0:T(8,128)(2,1)S(1)} %get-tuple-element.42.rest_0_), channel_id=1, source_target_pairs={{0,24},{8,16},{16,8},{24,0},{1,25},{9,17},{17,9},{25,1},{2,26},{10... | collective-permute-start | bytes 221192 | tf_op jit(solution)/shard_map/ppermute | solution.py:192
  65.6 2.4 %collective-permute-start.25 = (bf16[64,576]{1,0:T(8,128)(2,1)S(1)}, bf16[64,576]{1,0:T(8,128)(2,1)S(1)}, u32[]{:S(2)}, u32[]{:S(2)}) collective-permute-start(bf16[64,576]{1,0:T(8,128)(2,1)S(1)} %get-tuple-element.42.rest_0_), channel_id=1, source_target_pairs={{0,8},{8,0},{16,24},{24,16},{1,9},{9,1},{17,25},{25,17},{2,10},{10... | collective-permute-start | bytes 221192 | tf_op jit(solution)/shard_map/ppermute | solution.py:192
  68.0 2.8 %collective-permute-done.27.rest_3_ = bf16[64,576]{1,0:T(8,128)(2,1)S(1)} collective-permute-done((bf16[64,576]{1,0:T(8,128)(2,1)S(1)}, bf16[64,576]{1,0:T(8,128)(2,1)S(1)}, u32[]{:S(2)}, u32[]{:S(2)}) %collective-permute-start.27) | collective-permute-done | bytes 73760 | tf_op jit(solution)/shard_map/ppermute | solution.py:192
  70.7 3.0 %collective-permute-done.26.rest_2_ = bf16[64,576]{1,0:T(8,128)(2,1)S(1)} collective-permute-done((bf16[64,576]{1,0:T(8,128)(2,1)S(1)}, bf16[64,576]{1,0:T(8,128)(2,1)S(1)}, u32[]{:S(2)}, u32[]{:S(2)}) %collective-permute-start.26) | collective-permute-done | bytes 73760 | tf_op jit(solution)/shard_map/ppermute | solution.py:192
  73.7 3.9 %operator.3 = (bf16[4,64,576]{2,1,0:T(8,128)(2,1)S(1)}, f32[4,64,576]{2,1,0:T(8,128)S(1)}, bf16[64,576]{1,0:T(8,128)(2,1)S(1)}, bf16[64,576]{1,0:T(8,128)(2,1)S(...) custom-call(s32[1]{0:T(128)} %bitcast.32.counts, s32[16]{0:T(128)S(1)} %fusion.1.rows_at, ...), custom_call_target="tpu_custom_call" | custom-call | tf_op jit(solution)/shard_map/operator/pallas_call | solution.py:171
  77.7 0.5 collective-permute-start.29
  78.2 2.1 %collective-permute-start.33 = (bf16[64,576]{1,0:T(8,128)(2,1)S(1)}, bf16[64,576]{1,0:T(8,128)(2,1)S(1)}, u32[]{:S(2)}, u32[]{:S(2)}) collective-permute-start(bf16[64,576]{1,0:T(8,128)(2,1)S(1)} %get-tuple-element.54), channel_id=1, source_target_pairs={{0,8},{8,0},{16,24},{24,16},{1,9},{9,1},{17,25},{25,17},{2,10},{10... | collective-permute-start | bytes 221192 | tf_op jit(solution)/shard_map/ppermute | solution.py:192
  80.4 1.7 %collective-permute-start.38 = (f32[64,192]{1,0:T(8,128)S(1)}, f32[64,192]{1,0:T(8,128)S(1)}, u32[]{:S(2)}, u32[]{:S(2)}) collective-permute-start(f32[64,192]{1,0:T(8,128)S(1)} %get-tuple-element.57.refs_0_), channel_id=1, source_target_pairs={{0,6},{1,7},{2,4},{3,5},{4,2},{5,3},{6,0},{7,1},{8,14},{9,15},{10,... | collective-permute-start | bytes 147464 | tf_op jit(solution)/shard_map/ppermute | solution.py:192
  82.0 6.9 %collective-permute-start.34 = (bf16[64,576]{1,0:T(8,128)(2,1)S(1)}, bf16[64,576]{1,0:T(8,128)(2,1)S(1)}, u32[]{:S(2)}, u32[]{:S(2)}) collective-permute-start(bf16[64,576]{1,0:T(8,128)(2,1)S(1)} %get-tuple-element.55), channel_id=1, source_target_pairs={{0,16},{8,24},{16,0},{24,8},{1,17},{9,25},{17,1},{25,9},{2,18},{10... | collective-permute-start | bytes 221192 | tf_op jit(solution)/shard_map/ppermute | solution.py:192
  88.9 0.9 collective-permute-start.37
  89.8 1.1 collective-permute-start.36
  90.9 0.6 collective-permute-start.35
  91.5 1.0 collective-permute-start.30
  92.5 0.7 collective-permute-done.37.refs_2_
  93.1 0.9 collective-permute-start.31
  94.0 0.7 collective-permute-done.36.refs_1_
  94.7 0.7 collective-permute-start.32
  95.5 2.9 %collective-permute-start.41 = (f32[64,192]{1,0:T(8,128)S(1)}, f32[64,192]{1,0:T(8,128)S(1)}, u32[]{:S(2)}, u32[]{:S(2)}) collective-permute-start(f32[64,192]{1,0:T(8,128)S(1)} %gram_sum.3.rest_6_), channel_id=1, source_target_pairs={{0,24},{8,16},{16,8},{24,0},{1,25},{9,17},{17,9},{25,1},{2,26},{10... | collective-permute-start | bytes 147464 | tf_op jit(solution)/shard_map/ppermute | solution.py:192
  98.4 0.9 collective-permute-start.40
  99.2 0.7 collective-permute-start.39
  99.9 0.1 collective-permute-done.32.rest_2_
  100.0 1.8 %collective-permute-done.41.rest_9_ = f32[64,192]{1,0:T(8,128)S(1)} collective-permute-done((f32[64,192]{1,0:T(8,128)S(1)}, f32[64,192]{1,0:T(8,128)S(1)}, u32[]{:S(2)}, u32[]{:S(2)}) %collective-permute-start.41) | collective-permute-done | bytes 49184 | tf_op jit(solution)/shard_map/ppermute | solution.py:192
  101.9 2.1 %collective-permute-done.40.rest_8_ = f32[64,192]{1,0:T(8,128)S(1)} collective-permute-done((f32[64,192]{1,0:T(8,128)S(1)}, f32[64,192]{1,0:T(8,128)S(1)}, u32[]{:S(2)}, u32[]{:S(2)}) %collective-permute-start.40) | collective-permute-done | bytes 49184 | tf_op jit(solution)/shard_map/ppermute | solution.py:192
  104.0 0.3 collective-permute-done.39.rest_7_
  104.3 7.5 %last_step.1 = (f32[64,576]{1,0:T(8,128)}, f32[64,576]{1,0:T(8,128)}) custom-call(f32[64,576]{1,0:T(8,128)S(1)} %get-tuple-element.47.mine, f32[64,576]{1,0:T(8,128)S(1)} %bitcast.36, f32[64,576]{1,0:T(8,128)S(1)} %get-tuple-element.48.image_in, f32[64,576]{1,0:T(8,128)S(1)} %get-tuple-element.49.residual_in, f32[3,64,64]{2,1,0:T(8,128)S(1)} %get-tuple-element.50.small, ...), custom_call_target="tpu_custom_call" | custom-call | tf_op jit(solution)/shard_map/last_step/pallas_call | solution.py:171
  (41 shorter events, 0.8 us)
Async XLA Ops:
  0.6 49.1 %copy-start.2 = (f32[1,64,576]{2,1,0:T(8,128)S(1)}, f32[1,64,576]{2,1,0:T(8,128)}, u32[]{:S(2)}) copy-start(f32[1,64,576]{2,1,0:T(8,128)} %param.8) | copy-start | bytes 442372
  0.6 73.1 %copy-start.1 = (bf16[1,576,576]{2,1,0:T(8,128)(2,1)S(1)}, bf16[1,576,576]{2,1,0:T(8,128)(2,1)}, u32[]{:S(2)}) copy-start(bf16[1,576,576]{2,1,0:T(8,128)(2,1)} %param.7) | copy-start | bytes 1990660
  1.8 14.7 %collective-permute-start.6 = (bf16[64,576]{1,0:T(8,128)(2,1)S(1)}, bf16[64,576]{1,0:T(8,128)(2,1)S(1)}, u32[]{:S(2)}, u32[]{:S(2)}) collective-permute-start(bf16[64,576]{1,0:T(8,128)(2,1)S(1)} %get-tuple-element.61.rest_0_), channel_id=1, source_target_pairs={{0,24},{8,16},{16,8},{24,0},{1,25},{9,17},{17,9},{25,1},{2,26},{10... | collective-permute-start | bytes 221192 | tf_op jit(solution)/shard_map/ppermute | solution.py:192
  6.9 9.6 %collective-permute-start.5 = (bf16[64,576]{1,0:T(8,128)(2,1)S(1)}, bf16[64,576]{1,0:T(8,128)(2,1)S(1)}, u32[]{:S(2)}, u32[]{:S(2)}) collective-permute-start(bf16[64,576]{1,0:T(8,128)(2,1)S(1)} %get-tuple-element.61.rest_0_), channel_id=1, source_target_pairs={{0,16},{8,24},{16,0},{24,8},{1,17},{9,25},{17,1},{25,9},{2,18},{10... | collective-permute-start | bytes 221192 | tf_op jit(solution)/shard_map/ppermute | solution.py:192
  6.9 5.4 %collective-permute-start.2 = (bf16[64,576]{1,0:T(8,128)(2,1)S(1)}, bf16[64,576]{1,0:T(8,128)(2,1)S(1)}, u32[]{:S(2)}, u32[]{:S(2)}) collective-permute-start(bf16[64,576]{1,0:T(8,128)(2,1)S(1)} %get-tuple-element.61.rest_0_), channel_id=1, source_target_pairs={{0,6},{1,7},{2,4},{3,5},{4,2},{5,3},{6,0},{7,1},{8,14},{9,15},{10,... | collective-permute-start | bytes 221192 | tf_op jit(solution)/shard_map/ppermute | solution.py:192
  9.3 4.5 %collective-permute-start.1 = (bf16[64,576]{1,0:T(8,128)(2,1)S(1)}, bf16[64,576]{1,0:T(8,128)(2,1)S(1)}, u32[]{:S(2)}, u32[]{:S(2)}) collective-permute-start(bf16[64,576]{1,0:T(8,128)(2,1)S(1)} %get-tuple-element.61.rest_0_), channel_id=1, source_target_pairs={{0,4},{1,5},{2,6},{3,7},{4,0},{5,1},{6,2},{7,3},{8,12},{9,13},{10,... | collective-permute-start | bytes 221192 | tf_op jit(solution)/shard_map/ppermute | solution.py:192
  9.8 4.4 %collective-permute-start = (bf16[64,576]{1,0:T(8,128)(2,1)S(1)}, bf16[64,576]{1,0:T(8,128)(2,1)S(1)}, u32[]{:S(2)}, u32[]{:S(2)}) collective-permute-start(bf16[64,576]{1,0:T(8,128)(2,1)S(1)} %get-tuple-element.61.rest_0_), channel_id=1, source_target_pairs={{0,2},{1,3},{2,0},{3,1},{4,6},{5,7},{6,4},{7,5},{8,10},{9,11},{10,... | collective-permute-start | bytes 221192 | tf_op jit(solution)/shard_map/ppermute | solution.py:192
  12.3 4.4 %collective-permute-start.4 = (bf16[64,576]{1,0:T(8,128)(2,1)S(1)}, bf16[64,576]{1,0:T(8,128)(2,1)S(1)}, u32[]{:S(2)}, u32[]{:S(2)}) collective-permute-start(bf16[64,576]{1,0:T(8,128)(2,1)S(1)} %get-tuple-element.61.rest_0_), channel_id=1, source_target_pairs={{0,8},{8,0},{16,24},{24,16},{1,9},{9,1},{17,25},{25,17},{2,10},{10... | collective-permute-start | bytes 221192 | tf_op jit(solution)/shard_map/ppermute | solution.py:192
  14.3 2.4 %collective-permute-start.3 = (bf16[4,64,576]{2,1,0:T(8,128)(2,1)S(1)}, bf16[4,64,576]{2,1,0:T(8,128)(2,1)S(1)}, u32[]{:S(2)}, u32[]{:S(2)}) collective-permute-start(bf16[4,64,576]{2,1,0:T(8,128)(2,1)S(1)} %pad_maximum_fusion.near_own), channel_id=1, source_target_pairs={{0,1},{1,0},{2,3},{3,2},{4,5},{5,4},{6,7},{7,6},{8,9},{9,8},{10,11... | collective-permute-start | bytes 884744 | tf_op jit(solution)/shard_map/ppermute | solution.py:192
  16.8 1.1 copy-start
  21.8 3.5 %collective-permute-start.7 = (bf16[4,64,576]{2,1,0:T(8,128)(2,1)S(1)}, bf16[4,64,576]{2,1,0:T(8,128)(2,1)S(1)}, u32[]{:S(2)}, u32[]{:S(2)}) collective-permute-start(bf16[4,64,576]{2,1,0:T(8,128)(2,1)S(1)} %get-tuple-element.32), channel_id=1, source_target_pairs={{0,1},{1,0},{2,3},{3,2},{4,5},{5,4},{6,7},{7,6},{8,9},{9,8},{10,11... | collective-permute-start | bytes 884744 | tf_op jit(solution)/shard_map/ppermute | solution.py:192
  22.0 3.2 %collective-permute-start.8 = (f32[64,192]{1,0:T(8,128)S(1)}, f32[64,192]{1,0:T(8,128)S(1)}, u32[]{:S(2)}, u32[]{:S(2)}) collective-permute-start(f32[64,192]{1,0:T(8,128)S(1)} %get-tuple-element.33.grams), channel_id=1, source_target_pairs={{0,1},{1,0},{2,3},{3,2},{4,5},{5,4},{6,7},{7,6},{8,9},{9,8},{10,11... | collective-permute-start | bytes 147464 | tf_op jit(solution)/shard_map/ppermute | solution.py:192
  22.4 12.9 %collective-permute-start.12 = (bf16[64,576]{1,0:T(8,128)(2,1)S(1)}, bf16[64,576]{1,0:T(8,128)(2,1)S(1)}, u32[]{:S(2)}, u32[]{:S(2)}) collective-permute-start(bf16[64,576]{1,0:T(8,128)(2,1)S(1)} %get-tuple-element.38), channel_id=1, source_target_pairs={{0,8},{8,0},{16,24},{24,16},{1,9},{9,1},{17,25},{25,17},{2,10},{10... | collective-permute-start | bytes 221192 | tf_op jit(solution)/shard_map/ppermute | solution.py:192
  25.4 10.5 %collective-permute-start.17 = (f32[64,192]{1,0:T(8,128)S(1)}, f32[64,192]{1,0:T(8,128)S(1)}, u32[]{:S(2)}, u32[]{:S(2)}) collective-permute-start(f32[64,192]{1,0:T(8,128)S(1)} %get-tuple-element.41.refs_0_), channel_id=1, source_target_pairs={{0,6},{1,7},{2,4},{3,5},{4,2},{5,3},{6,0},{7,1},{8,14},{9,15},{10,... | collective-permute-start | bytes 147464 | tf_op jit(solution)/shard_map/ppermute | solution.py:192
  27.9 13.2 %collective-permute-start.13 = (bf16[64,576]{1,0:T(8,128)(2,1)S(1)}, bf16[64,576]{1,0:T(8,128)(2,1)S(1)}, u32[]{:S(2)}, u32[]{:S(2)}) collective-permute-start(bf16[64,576]{1,0:T(8,128)(2,1)S(1)} %get-tuple-element.39), channel_id=1, source_target_pairs={{0,16},{8,24},{16,0},{24,8},{1,17},{9,25},{17,1},{25,9},{2,18},{10... | collective-permute-start | bytes 221192 | tf_op jit(solution)/shard_map/ppermute | solution.py:192
  34.1 4.3 %collective-permute-start.16 = (f32[64,192]{1,0:T(8,128)S(1)}, f32[64,192]{1,0:T(8,128)S(1)}, u32[]{:S(2)}, u32[]{:S(2)}) collective-permute-start(f32[64,192]{1,0:T(8,128)S(1)} %get-tuple-element.41.refs_0_), channel_id=1, source_target_pairs={{0,4},{1,5},{2,6},{3,7},{4,0},{5,1},{6,2},{7,3},{8,12},{9,13},{10,... | collective-permute-start | bytes 147464 | tf_op jit(solution)/shard_map/ppermute | solution.py:192
  35.2 4.3 %collective-permute-start.15 = (f32[64,192]{1,0:T(8,128)S(1)}, f32[64,192]{1,0:T(8,128)S(1)}, u32[]{:S(2)}, u32[]{:S(2)}) collective-permute-start(f32[64,192]{1,0:T(8,128)S(1)} %get-tuple-element.41.refs_0_), channel_id=1, source_target_pairs={{0,2},{1,3},{2,0},{3,1},{4,6},{5,7},{6,4},{7,5},{8,10},{9,11},{10,... | collective-permute-start | bytes 147464 | tf_op jit(solution)/shard_map/ppermute | solution.py:192
  35.2 8.4 %collective-permute-start.14 = (bf16[64,576]{1,0:T(8,128)(2,1)S(1)}, bf16[64,576]{1,0:T(8,128)(2,1)S(1)}, u32[]{:S(2)}, u32[]{:S(2)}) collective-permute-start(bf16[64,576]{1,0:T(8,128)(2,1)S(1)} %get-tuple-element.40), channel_id=1, source_target_pairs={{0,24},{8,16},{16,8},{24,0},{1,25},{9,17},{17,9},{25,1},{2,26},{10... | collective-permute-start | bytes 221192 | tf_op jit(solution)/shard_map/ppermute | solution.py:192
  35.9 8.6 %collective-permute-start.9 = (bf16[64,576]{1,0:T(8,128)(2,1)S(1)}, bf16[64,576]{1,0:T(8,128)(2,1)S(1)}, u32[]{:S(2)}, u32[]{:S(2)}) collective-permute-start(bf16[64,576]{1,0:T(8,128)(2,1)S(1)} %get-tuple-element.35), channel_id=1, source_target_pairs={{0,2},{1,3},{2,0},{3,1},{4,6},{5,7},{6,4},{7,5},{8,10},{9,11},{10,... | collective-permute-start | bytes 221192 | tf_op jit(solution)/shard_map/ppermute | solution.py:192
  38.4 7.2 %collective-permute-start.10 = (bf16[64,576]{1,0:T(8,128)(2,1)S(1)}, bf16[64,576]{1,0:T(8,128)(2,1)S(1)}, u32[]{:S(2)}, u32[]{:S(2)}) collective-permute-start(bf16[64,576]{1,0:T(8,128)(2,1)S(1)} %get-tuple-element.36), channel_id=1, source_target_pairs={{0,4},{1,5},{2,6},{3,7},{4,0},{5,1},{6,2},{7,3},{8,12},{9,13},{10,... | collective-permute-start | bytes 221192 | tf_op jit(solution)/shard_map/ppermute | solution.py:192
  39.5 6.1 %collective-permute-start.11 = (bf16[64,576]{1,0:T(8,128)(2,1)S(1)}, bf16[64,576]{1,0:T(8,128)(2,1)S(1)}, u32[]{:S(2)}, u32[]{:S(2)}) collective-permute-start(bf16[64,576]{1,0:T(8,128)(2,1)S(1)} %get-tuple-element.37), channel_id=1, source_target_pairs={{0,6},{1,7},{2,4},{3,5},{4,2},{5,3},{6,0},{7,1},{8,14},{9,15},{10,... | collective-permute-start | bytes 221192 | tf_op jit(solution)/shard_map/ppermute | solution.py:192
  41.1 6.3 %collective-permute-start.20 = (f32[64,192]{1,0:T(8,128)S(1)}, f32[64,192]{1,0:T(8,128)S(1)}, u32[]{:S(2)}, u32[]{:S(2)}) collective-permute-start(f32[64,192]{1,0:T(8,128)S(1)} %gram_sum.2.rest_6_), channel_id=1, source_target_pairs={{0,24},{8,16},{16,8},{24,0},{1,25},{9,17},{17,9},{25,1},{2,26},{10... | collective-permute-start | bytes 147464 | tf_op jit(solution)/shard_map/ppermute | solution.py:192
  43.6 5.6 %collective-permute-start.19 = (f32[64,192]{1,0:T(8,128)S(1)}, f32[64,192]{1,0:T(8,128)S(1)}, u32[]{:S(2)}, u32[]{:S(2)}) collective-permute-start(f32[64,192]{1,0:T(8,128)S(1)} %gram_sum.2.rest_6_), channel_id=1, source_target_pairs={{0,16},{8,24},{16,0},{24,8},{1,17},{9,25},{17,1},{25,9},{2,18},{10... | collective-permute-start | bytes 147464 | tf_op jit(solution)/shard_map/ppermute | solution.py:192
  44.5 5.3 %collective-permute-start.18 = (f32[64,192]{1,0:T(8,128)S(1)}, f32[64,192]{1,0:T(8,128)S(1)}, u32[]{:S(2)}, u32[]{:S(2)}) collective-permute-start(f32[64,192]{1,0:T(8,128)S(1)} %gram_sum.2.rest_6_), channel_id=1, source_target_pairs={{0,8},{8,0},{16,24},{24,16},{1,9},{9,1},{17,25},{25,17},{2,10},{10... | collective-permute-start | bytes 147464 | tf_op jit(solution)/shard_map/ppermute | solution.py:192
  56.7 5.5 %collective-permute-start.23 = (bf16[64,576]{1,0:T(8,128)(2,1)S(1)}, bf16[64,576]{1,0:T(8,128)(2,1)S(1)}, u32[]{:S(2)}, u32[]{:S(2)}) collective-permute-start(bf16[64,576]{1,0:T(8,128)(2,1)S(1)} %get-tuple-element.42.rest_0_), channel_id=1, source_target_pairs={{0,6},{1,7},{2,4},{3,5},{4,2},{5,3},{6,0},{7,1},{8,14},{9,15},{10,... | collective-permute-start | bytes 221192 | tf_op jit(solution)/shard_map/ppermute | solution.py:192
  57.3 5.3 %collective-permute-start.22 = (bf16[64,576]{1,0:T(8,128)(2,1)S(1)}, bf16[64,576]{1,0:T(8,128)(2,1)S(1)}, u32[]{:S(2)}, u32[]{:S(2)}) collective-permute-start(bf16[64,576]{1,0:T(8,128)(2,1)S(1)} %get-tuple-element.42.rest_0_), channel_id=1, source_target_pairs={{0,4},{1,5},{2,6},{3,7},{4,0},{5,1},{6,2},{7,3},{8,12},{9,13},{10,... | collective-permute-start | bytes 221192 | tf_op jit(solution)/shard_map/ppermute | solution.py:192
  58.9 4.4 %collective-permute-start.21 = (bf16[64,576]{1,0:T(8,128)(2,1)S(1)}, bf16[64,576]{1,0:T(8,128)(2,1)S(1)}, u32[]{:S(2)}, u32[]{:S(2)}) collective-permute-start(bf16[64,576]{1,0:T(8,128)(2,1)S(1)} %get-tuple-element.42.rest_0_), channel_id=1, source_target_pairs={{0,2},{1,3},{2,0},{3,1},{4,6},{5,7},{6,4},{7,5},{8,10},{9,11},{10,... | collective-permute-start | bytes 221192 | tf_op jit(solution)/shard_map/ppermute | solution.py:192
  63.4 10.3 %collective-permute-start.24 = (bf16[4,64,576]{2,1,0:T(8,128)(2,1)S(1)}, bf16[4,64,576]{2,1,0:T(8,128)(2,1)S(1)}, u32[]{:S(2)}, u32[]{:S(2)}) collective-permute-start(bf16[4,64,576]{2,1,0:T(8,128)(2,1)S(1)} %pad_maximum_fusion.1.near_own), channel_id=1, source_target_pairs={{0,1},{1,0},{2,3},{3,2},{4,5},{5,4},{6,7},{7,6},{8,9},{9,8},{10,11... | collective-permute-start | bytes 884744 | tf_op jit(solution)/shard_map/ppermute | solution.py:192
  63.5 7.2 %collective-permute-start.27 = (bf16[64,576]{1,0:T(8,128)(2,1)S(1)}, bf16[64,576]{1,0:T(8,128)(2,1)S(1)}, u32[]{:S(2)}, u32[]{:S(2)}) collective-permute-start(bf16[64,576]{1,0:T(8,128)(2,1)S(1)} %get-tuple-element.42.rest_0_), channel_id=1, source_target_pairs={{0,24},{8,16},{16,8},{24,0},{1,25},{9,17},{17,9},{25,1},{2,26},{10... | collective-permute-start | bytes 221192 | tf_op jit(solution)/shard_map/ppermute | solution.py:192
  65.5 8.2 %collective-permute-start.26 = (bf16[64,576]{1,0:T(8,128)(2,1)S(1)}, bf16[64,576]{1,0:T(8,128)(2,1)S(1)}, u32[]{:S(2)}, u32[]{:S(2)}) collective-permute-start(bf16[64,576]{1,0:T(8,128)(2,1)S(1)} %get-tuple-element.42.rest_0_), channel_id=1, source_target_pairs={{0,16},{8,24},{16,0},{24,8},{1,17},{9,25},{17,1},{25,9},{2,18},{10... | collective-permute-start | bytes 221192 | tf_op jit(solution)/shard_map/ppermute | solution.py:192
  65.6 8.1 %collective-permute-start.25 = (bf16[64,576]{1,0:T(8,128)(2,1)S(1)}, bf16[64,576]{1,0:T(8,128)(2,1)S(1)}, u32[]{:S(2)}, u32[]{:S(2)}) collective-permute-start(bf16[64,576]{1,0:T(8,128)(2,1)S(1)} %get-tuple-element.42.rest_0_), channel_id=1, source_target_pairs={{0,8},{8,0},{16,24},{24,16},{1,9},{9,1},{17,25},{25,17},{2,10},{10... | collective-permute-start | bytes 221192 | tf_op jit(solution)/shard_map/ppermute | solution.py:192
  77.6 2.6 %collective-permute-start.28 = (bf16[4,64,576]{2,1,0:T(8,128)(2,1)S(1)}, bf16[4,64,576]{2,1,0:T(8,128)(2,1)S(1)}, u32[]{:S(2)}, u32[]{:S(2)}) collective-permute-start(bf16[4,64,576]{2,1,0:T(8,128)(2,1)S(1)} %get-tuple-element.45), channel_id=1, source_target_pairs={{0,1},{1,0},{2,3},{3,2},{4,5},{5,4},{6,7},{7,6},{8,9},{9,8},{10,11... | collective-permute-start | bytes 884744 | tf_op jit(solution)/shard_map/ppermute | solution.py:192
  77.7 2.5 %collective-permute-start.29 = (f32[64,192]{1,0:T(8,128)S(1)}, f32[64,192]{1,0:T(8,128)S(1)}, u32[]{:S(2)}, u32[]{:S(2)}) collective-permute-start(f32[64,192]{1,0:T(8,128)S(1)} %get-tuple-element.46.grams), channel_id=1, source_target_pairs={{0,1},{1,0},{2,3},{3,2},{4,5},{5,4},{6,7},{7,6},{8,9},{9,8},{10,11... | collective-permute-start | bytes 147464 | tf_op jit(solution)/shard_map/ppermute | solution.py:192
  78.2 12.7 %collective-permute-start.33 = (bf16[64,576]{1,0:T(8,128)(2,1)S(1)}, bf16[64,576]{1,0:T(8,128)(2,1)S(1)}, u32[]{:S(2)}, u32[]{:S(2)}) collective-permute-start(bf16[64,576]{1,0:T(8,128)(2,1)S(1)} %get-tuple-element.54), channel_id=1, source_target_pairs={{0,8},{8,0},{16,24},{24,16},{1,9},{9,1},{17,25},{25,17},{2,10},{10... | collective-permute-start | bytes 221192 | tf_op jit(solution)/shard_map/ppermute | solution.py:192
  80.4 11.1 %collective-permute-start.38 = (f32[64,192]{1,0:T(8,128)S(1)}, f32[64,192]{1,0:T(8,128)S(1)}, u32[]{:S(2)}, u32[]{:S(2)}) collective-permute-start(f32[64,192]{1,0:T(8,128)S(1)} %get-tuple-element.57.refs_0_), channel_id=1, source_target_pairs={{0,6},{1,7},{2,4},{3,5},{4,2},{5,3},{6,0},{7,1},{8,14},{9,15},{10,... | collective-permute-start | bytes 147464 | tf_op jit(solution)/shard_map/ppermute | solution.py:192
  82.0 13.4 %collective-permute-start.34 = (bf16[64,576]{1,0:T(8,128)(2,1)S(1)}, bf16[64,576]{1,0:T(8,128)(2,1)S(1)}, u32[]{:S(2)}, u32[]{:S(2)}) collective-permute-start(bf16[64,576]{1,0:T(8,128)(2,1)S(1)} %get-tuple-element.55), channel_id=1, source_target_pairs={{0,16},{8,24},{16,0},{24,8},{1,17},{9,25},{17,1},{25,9},{2,18},{10... | collective-permute-start | bytes 221192 | tf_op jit(solution)/shard_map/ppermute | solution.py:192
  88.9 4.3 %collective-permute-start.37 = (f32[64,192]{1,0:T(8,128)S(1)}, f32[64,192]{1,0:T(8,128)S(1)}, u32[]{:S(2)}, u32[]{:S(2)}) collective-permute-start(f32[64,192]{1,0:T(8,128)S(1)} %get-tuple-element.57.refs_0_), channel_id=1, source_target_pairs={{0,4},{1,5},{2,6},{3,7},{4,0},{5,1},{6,2},{7,3},{8,12},{9,13},{10,... | collective-permute-start | bytes 147464 | tf_op jit(solution)/shard_map/ppermute | solution.py:192
  89.8 4.9 %collective-permute-start.36 = (f32[64,192]{1,0:T(8,128)S(1)}, f32[64,192]{1,0:T(8,128)S(1)}, u32[]{:S(2)}, u32[]{:S(2)}) collective-permute-start(f32[64,192]{1,0:T(8,128)S(1)} %get-tuple-element.57.refs_0_), channel_id=1, source_target_pairs={{0,2},{1,3},{2,0},{3,1},{4,6},{5,7},{6,4},{7,5},{8,10},{9,11},{10,... | collective-permute-start | bytes 147464 | tf_op jit(solution)/shard_map/ppermute | solution.py:192
  90.9 7.5 %collective-permute-start.35 = (bf16[64,576]{1,0:T(8,128)(2,1)S(1)}, bf16[64,576]{1,0:T(8,128)(2,1)S(1)}, u32[]{:S(2)}, u32[]{:S(2)}) collective-permute-start(bf16[64,576]{1,0:T(8,128)(2,1)S(1)} %get-tuple-element.56), channel_id=1, source_target_pairs={{0,24},{8,16},{16,8},{24,0},{1,25},{9,17},{17,9},{25,1},{2,26},{10... | collective-permute-start | bytes 221192 | tf_op jit(solution)/shard_map/ppermute | solution.py:192
  91.5 7.7 %collective-permute-start.30 = (bf16[64,576]{1,0:T(8,128)(2,1)S(1)}, bf16[64,576]{1,0:T(8,128)(2,1)S(1)}, u32[]{:S(2)}, u32[]{:S(2)}) collective-permute-start(bf16[64,576]{1,0:T(8,128)(2,1)S(1)} %get-tuple-element.51), channel_id=1, source_target_pairs={{0,2},{1,3},{2,0},{3,1},{4,6},{5,7},{6,4},{7,5},{8,10},{9,11},{10,... | collective-permute-start | bytes 221192 | tf_op jit(solution)/shard_map/ppermute | solution.py:192
  93.1 6.8 %collective-permute-start.31 = (bf16[64,576]{1,0:T(8,128)(2,1)S(1)}, bf16[64,576]{1,0:T(8,128)(2,1)S(1)}, u32[]{:S(2)}, u32[]{:S(2)}) collective-permute-start(bf16[64,576]{1,0:T(8,128)(2,1)S(1)} %get-tuple-element.52), channel_id=1, source_target_pairs={{0,4},{1,5},{2,6},{3,7},{4,0},{5,1},{6,2},{7,3},{8,12},{9,13},{10,... | collective-permute-start | bytes 221192 | tf_op jit(solution)/shard_map/ppermute | solution.py:192
  94.7 5.3 %collective-permute-start.32 = (bf16[64,576]{1,0:T(8,128)(2,1)S(1)}, bf16[64,576]{1,0:T(8,128)(2,1)S(1)}, u32[]{:S(2)}, u32[]{:S(2)}) collective-permute-start(bf16[64,576]{1,0:T(8,128)(2,1)S(1)} %get-tuple-element.53), channel_id=1, source_target_pairs={{0,6},{1,7},{2,4},{3,5},{4,2},{5,3},{6,0},{7,1},{8,14},{9,15},{10,... | collective-permute-start | bytes 221192 | tf_op jit(solution)/shard_map/ppermute | solution.py:192
  95.5 6.4 %collective-permute-start.41 = (f32[64,192]{1,0:T(8,128)S(1)}, f32[64,192]{1,0:T(8,128)S(1)}, u32[]{:S(2)}, u32[]{:S(2)}) collective-permute-start(f32[64,192]{1,0:T(8,128)S(1)} %gram_sum.3.rest_6_), channel_id=1, source_target_pairs={{0,24},{8,16},{16,8},{24,0},{1,25},{9,17},{17,9},{25,1},{2,26},{10... | collective-permute-start | bytes 147464 | tf_op jit(solution)/shard_map/ppermute | solution.py:192
  98.4 5.6 %collective-permute-start.40 = (f32[64,192]{1,0:T(8,128)S(1)}, f32[64,192]{1,0:T(8,128)S(1)}, u32[]{:S(2)}, u32[]{:S(2)}) collective-permute-start(f32[64,192]{1,0:T(8,128)S(1)} %gram_sum.3.rest_6_), channel_id=1, source_target_pairs={{0,16},{8,24},{16,0},{24,8},{1,17},{9,25},{17,1},{25,9},{2,18},{10... | collective-permute-start | bytes 147464 | tf_op jit(solution)/shard_map/ppermute | solution.py:192
  99.2 5.1 %collective-permute-start.39 = (f32[64,192]{1,0:T(8,128)S(1)}, f32[64,192]{1,0:T(8,128)S(1)}, u32[]{:S(2)}, u32[]{:S(2)}) collective-permute-start(f32[64,192]{1,0:T(8,128)S(1)} %gram_sum.3.rest_6_), channel_id=1, source_target_pairs={{0,8},{8,0},{16,24},{24,16},{1,9},{9,1},{17,25},{25,17},{2,10},{10... | collective-permute-start | bytes 147464 | tf_op jit(solution)/shard_map/ppermute | solution.py:192

commit v2 on v1

v2 whole, which is shorter than its diff:
```python
import functools

import jax
import jax.numpy as jnp
from jax import lax
from jax.experimental import pallas as pl
from jax.experimental.pallas import tpu as pltpu
from jax.sharding import PartitionSpec as P

ITERS = 2
F32 = jnp.float32
BF16 = jnp.bfloat16
HI = lax.Precision.HIGHEST
NT = (((1,), (1,)), ((), ()))
NN = (((1,), (0,)), ((), ()))
TN = (((0,), (0,)), ((), ()))
ANY = pl.BlockSpec(memory_space=pl.ANY)
VMEM = pl.BlockSpec(memory_space=pltpu.VMEM)
SMEM = pl.BlockSpec(memory_space=pltpu.SMEM)


def dot32(left, right, dims):
    return lax.dot_general(left, right, dims, precision=HI, preferred_element_type=F32)


def dot16(left, right, dims):
    return lax.dot_general(left, right, dims, preferred_element_type=F32)


def dot_exact16(left, right, dims):
    first = right.astype(BF16)
    rest = right - first.astype(F32)
    second = rest.astype(BF16)
    third = (rest - second.astype(F32)).astype(BF16)
    return dot16(left, first, dims) + (dot16(left, second, dims) + dot16(left, third, dims))


def eliminate(systems, group=8):
    size, width = systems[0].shape
    rows = lax.broadcasted_iota(jnp.int32, (size, width), 0)
    for start in range(0, size, group):
        after = []
        for system in systems:
            columns = [
                jnp.broadcast_to(system[:, k : k + 1], (size, width)) for k in range(start, start + group)
            ]
            for place, k in enumerate(range(start, start + group)):
                inverse = 1.0 / columns[place][k : k + 1, :]
                here = rows == k
                scaled = system[k : k + 1, :] * inverse
                for later in range(place + 1, group):
                    factor = columns[later][k : k + 1, :] * inverse
                    columns[later] = jnp.where(here, factor, columns[later] - columns[place] * factor)
                system = jnp.where(here, scaled, system - columns[place] * scaled)
            after.append(system)
        systems = after
    return [system[:, size:] for system in systems]


def split16(value):
    first = value.astype(BF16)
    return first, (value - first.astype(F32)).astype(BF16)


def pack(block, grams):
    size = grams.shape[0]
    rows = lax.broadcasted_iota(jnp.int32, (size, size), 0)
    columns = lax.broadcasted_iota(jnp.int32, (size, size), 1)
    both = jnp.where(rows >= columns, grams[:, :size], grams[:, size:])
    diagonal = jnp.sum(jnp.where(rows == columns, grams[:, size:], 0.0), axis=1, keepdims=True)
    first, second = split16(both)
    top, rest = split16(jnp.broadcast_to(diagonal, (size, size)))
    return jnp.concatenate([block, first, second, jnp.where(columns == 0, top, rest)], 1)


def unpack(message, width):
    size = message.shape[0]
    parts = message[:, width:].astype(F32)
    both = parts[:, :size] + parts[:, size : 2 * size]
    diagonal = parts[:, 2 * size : 2 * size + 1] + parts[:, 2 * size + 1 : 2 * size + 2]
    rows = lax.broadcasted_iota(jnp.int32, (size, size), 0)
    columns = lax.broadcasted_iota(jnp.int32, (size, size), 1)
    turned = both.T
    first = jnp.where(rows >= columns, both, turned)
    second = jnp.where(rows < columns, both, turned)
    return jnp.concatenate([first, jnp.where(rows == columns, diagonal, second)], 1)


def held_slots(count, slots, work):
    group = 4 if slots % 4 == 0 else 1

    def turn(g, carry):
        for u in range(group):
            slot = g * group + u
            work(slot, slot < count)
        return carry

    lax.fori_loop(0, (count + group - 1) // group, turn, 0)


def load_kernel(index, tiles, out, arrived):
    def fetch(slot):
        return pltpu.make_async_copy(tiles.at[slot], out.at[slot], arrived.at[slot])

    def begin(slot, carry):
        fetch(slot).start()
        return carry

    def end(slot, carry):
        fetch(slot).wait()
        return carry

    lax.fori_loop(0, index[0], begin, 0)
    lax.fori_loop(0, index[0], end, 0)


def mirrored_kernel(index, near_own, near_far, tiles, diag, acc, own, near):
    n_chip = near_own.shape[0]
    slots = tiles.shape[0]
    for d in range(n_chip):
        near[d] = near_own[d]
        near[n_chip + d] = near_far[d]
    acc[...] = jnp.zeros_like(acc)

    def work(slot, held):
        i = index[1 + slot]
        j = index[1 + slots + slot]
        acc[j] += jnp.where(held, dot16(near[i], tiles[slot], NN), 0.0)

    held_slots(index[0], slots, work)
    own[...] = dot16(near_own[0], diag[...], NT)


def gram_kernel(acc, own, residual, *rest):
    n_row, size = acc.shape[0], own.shape[0]
    far, grams, give = rest[:n_row], rest[n_row], rest[n_row + 1 :]
    half = dot_exact16(far[0][...], acc[0] + 0.5 * own[...], NT)
    for d in range(1, n_row):
        half += dot_exact16(far[d][...], acc[d], NT)
    total = jnp.concatenate([half + half.T, dot32(residual[...], residual[...], NT)], 1)
    grams[...] = total
    for d in range(1, n_row):
        give[d - 1][...] = pack(acc[d].astype(BF16), total)


def forward_kernel(index, tiles, after, *rest, n_row):
    far_in = rest[:n_row]
    give_core, keep, far, acc = rest[n_row:]
    n_chip = keep.shape[0]
    slots = tiles.shape[0]
    for d in range(n_row):
        far[d] = far_in[d][...]
    acc[...] = jnp.zeros_like(acc)

    def work(slot, held):
        i = index[1 + slot]
        j = index[1 + slots + slot]
        acc[i] += jnp.where(held, dot16(far[j], tiles[slot], NT), 0.0)

    held_slots(index[0], slots, work)
    for d in range(n_chip):
        give_core[d] = acc[n_chip + d].astype(BF16)
        keep[d] = acc[d]


def rows_kernel(grams, *rest):
    *came, out = rest
    total = grams[...]
    for message in came:
        total += unpack(message[...], message.shape[1] - 3 * grams.shape[0])
    out[...] = total


def join_kernel(keep, came, grams, grams_came, acc, own, *rest, n_in):
    mine, grams_out, *give = rest[n_in:]
    width = own.shape[1]
    total = keep[0] + came[0].astype(F32) + own[...] + acc[0]
    for message in rest[:n_in]:
        total += message[:, :width].astype(F32)
    mine[...] = total
    total = grams[...] + grams_came[...]
    grams_out[...] = total
    for d in range(1, keep.shape[0]):
        give[d - 1][...] = pack((keep[d] + came[d].astype(F32)).astype(BF16), total)


def gather_sums(mine, grams, rest, n_in):
    image, total = mine[...], grams[...]
    width = image.shape[1]
    for message in rest[:n_in]:
        image += message[:, :width].astype(F32)
        total += unpack(message[...], width)
    return image, total, rest[n_in:]


def first_kernel(mine, grams, probes, *rest, n_in):
    image, total, (image_out, residual_out, rounded, totals, alpha_out) = gather_sums(
        mine, grams, rest, n_in
    )
    (alpha,) = eliminate([total])
    residual = probes[...] - dot32(alpha, image, TN)
    rounded[...] = residual.astype(BF16)
    residual_out[...] = residual
    image_out[...] = image
    totals[...] = total
    alpha_out[...] = alpha


def between_kernel(totals, alpha, probes, inverse_out, middle_out, solved_out):
    size = alpha.shape[0]
    eye = (
        lax.broadcasted_iota(jnp.int32, (size, size), 0)
        == lax.broadcasted_iota(jnp.int32, (size, size), 1)
    ).astype(F32)
    (inverse,) = eliminate([jnp.concatenate([totals[:, size:], eye], 1)])
    inverse_out[...] = inverse
    middle_out[...] = dot32(inverse, dot32(totals[:, :size], inverse, NN), TN)
    solved_out[...] = dot32(alpha[...], probes[...], TN)


def last_kernel(mine, grams, probes, image_in, residual_in, inverse, middle, solved, *rest, n_in):
    forward, total, (solution_out, residual_out) = gather_sums(mine, grams, rest, n_in)
    size = forward.shape[0]
    norm = total[:, size:]
    curv = total[:, :size] - dot32(norm, dot32(middle[...], norm, NN), TN)
    beta = dot32(inverse[...], norm, NN)
    residual = residual_in[...]
    direction = residual + dot32(beta, probes[...], TN)
    image = forward + dot32(beta, image_in[...], TN)
    (step,) = eliminate([jnp.concatenate([curv, norm], 1)])
    solution_out[...] = solved[...] + dot32(step, direction, TN)
    residual_out[...] = residual - dot32(step, image, TN)


def call(kernel, outs, args, specs=None, scratch=(), limit=32, name=None, work=None):
    return pl.pallas_call(
        kernel,
        out_shape=outs,
        in_specs=[VMEM] * len(args) if specs is None else specs,
        out_specs=[VMEM] * len(outs),
        scratch_shapes=list(scratch),
        compiler_params=pltpu.CompilerParams(vmem_limit_bytes=limit << 20),
        cost_estimate=None if work is None else pl.CostEstimate(flops=work, bytes_accessed=0, transcendentals=0),
        name=name,
    )(*args)


def body(n_row, n_col, tiles, diag_tiles, probes, rows_list, cols_list, counts):
    n_chip = n_col // 2
    p_size, width = probes.shape[1:]
    shape = jax.ShapeDtypeStruct
    block32 = shape((p_size, width), F32)
    block16 = shape((p_size, width), BF16)

    def over(value, axis, delta):
        size = n_row if axis == "row" else n_col
        return lax.ppermute(value, axis, [(i, i ^ delta) for i in range(size)])

    def over_chips(value):
        return [over(value, "col", 2 * d) for d in range(1, n_chip)]

    def over_rows(value):
        return [over(value, "row", d) for d in range(1, n_row)]

    apart = rows_list[0, 0] ^ lax.axis_index("col")
    index = jnp.concatenate(
        [counts[0], (apart % 2) * n_chip + apart // 2, cols_list[0, 0] ^ lax.axis_index("row")]
    )
    probes = probes[0]
    diag = diag_tiles[0]
    square = shape((p_size, 2 * p_size), F32)
    slots = tiles.shape[2]
    (held,) = call(
        load_kernel,
        [shape(tiles.shape[2:], BF16)],
        [index, tiles[0, 0]],
        [SMEM, ANY],
        [pltpu.SemaphoreType.DMA((slots,))],
        name="load",
    )
    passes = 2 * slots * p_size * width * width

    message = shape((p_size, width + 3 * p_size), BF16)

    def apply_operator(rounded, residual, held):
        *gathered, held = lax.optimization_barrier((*over_chips(rounded), *over_rows(rounded), held))
        far = [rounded, *gathered[n_chip - 1 :]]
        near_own = jnp.stack([rounded, *gathered[: n_chip - 1]])
        near_far = over(near_own, "col", 1)
        acc, own = call(
            mirrored_kernel,
            [shape((n_row, p_size, width), F32), block32],
            [index, near_own, near_far, held, diag],
            [SMEM] + [VMEM] * 4,
            [pltpu.VMEM((n_col, p_size, width), BF16)],
            name="mirrored",
            work=passes,
        )
        grams, *give_row = call(
            gram_kernel, [square] + [message] * (n_row - 1), [acc, own, residual, *far], name="gram"
        )
        from_rows = [over(block, "row", d + 1) for d, block in enumerate(give_row)]
        outs = [shape((n_chip, p_size, width), BF16), shape((n_chip, p_size, width), F32)]
        scratch = [pltpu.VMEM((n_row, p_size, width), BF16), pltpu.VMEM((n_col, p_size, width), F32)]
        give_core, keep = call(
            functools.partial(forward_kernel, n_row=n_row),
            outs,
            [index, held, grams, *far],
            [SMEM, VMEM, ANY] + [VMEM] * n_row,
            scratch,
            name="forward",
            work=passes,
        )
        give_core, *from_rows = lax.optimization_barrier((give_core, *from_rows))
        came = over(give_core, "col", 1)
        (grams,) = call(rows_kernel, [square], [grams, *from_rows], name="gram_rows")
        grams_came = over(grams, "col", 1)
        mine, grams, *give_chip = call(
            functools.partial(join_kernel, n_in=n_row - 1),
            [block32, square] + [message] * (n_chip - 1),
            [keep, came, grams, grams_came, acc, own, *from_rows],
            name="join",
        )
        return mine, grams, [over(block, "col", 2 * d + 2) for d, block in enumerate(give_chip)]

    small = shape((p_size, p_size), F32)
    mine, grams, parts = apply_operator(probes.astype(BF16), probes, held)
    image, residual, rounded, totals, alpha = call(
        functools.partial(first_kernel, n_in=n_chip - 1),
        [block32, block32, block16, square, small],
        [mine, grams, probes, *parts],
        name="first_step",
    )
    inverse, middle, solved = call(
        between_kernel, [small, small, block32], [totals, alpha, probes], name="between"
    )
    mine, grams, parts = apply_operator(rounded, residual, held)
    solved, residual = call(
        functools.partial(last_kernel, n_in=n_chip - 1),
        [block32, block32],
        [mine, grams, probes, image, residual, inverse, middle, solved, *parts],
        name="last_step",
    )
    return solved[None], residual[None]


def solution(mesh):
    placed = (
        P("row", "col", None, None, None),
        P(("row", "col"), None, None),
        P(("row", "col"), None, None),
        P("row", "col", None),
        P("row", "col", None),
        P("row", "col"),
    )
    return jax.shard_map(
        functools.partial(body, mesh.shape["row"], mesh.shape["col"]),
        mesh=mesh,
        in_specs=placed,
        out_specs=(P(("row", "col"), None, None), P(("row", "col"), None, None)),
        check_vma=False,
    )
```

time: 112 us -> 95 us (0.85)
  starting transfers between devices: 61.4 us -> 36 us
  waiting for transfers between devices: 21.6 us -> 33 us
  matrix products: 1.29 us -> 0 us
  local copies, waits for them, and re-layouts: 1.14 us -> 0.01 us
    ppermute x42 -> x30, starting transfers between devices: 61.4 us -> 36 us  [over(): return lax.ppermute(value, axis, [(i, i ^ delta) for i in range(size)])]
    ppermute x42 -> x30, waiting for transfers between devices: 21.6 us -> 33 us  [over(): return lax.ppermute(value, axis, [(i, i ^ delta) for i in range(size)])]
    dot_general x1 -> x0, matrix products: 1.29 us -> none  [dot32(): lax.dot_general(left, right, dims, precision=HI, preferred_element_type=F32)]
    pallas_call x8 -> x14, Pallas kernels: 22.4 us -> 21.7 us  [call(): pl.pallas_call(kernel, out_shape=outs, in_specs=[VMEM] * len(args) if spe...]
  transfers between devices with their start and end apart: 42 -> 30, of which waited for: 19 -> 14; matrix products, arithmetic and copies ran while one was open for 2% -> 1% of each run, Pallas kernels for 0% -> 10%
where the time goes in v2:
time: 95 us; the launch traced here: 94.8 us
  starting transfers between devices  36 us (38%)
  waiting for transfers between devices  33 us (35%)
  Pallas kernels  21.7 us (23%)
  other arithmetic  2.55 us (3%)
  between operations  1.52 us (2%)
    ppermute x30, starting transfers between devices, over(): return lax.ppermute(value, axis, [(i, i ^ delta) for i in range(size)])  36 us
    ppermute x30, waiting for transfers between devices, over(): return lax.ppermute(value, axis, [(i, i ^ delta) for i in range(size)])  33 us
    pallas_call x14, Pallas kernels, call(): pl.pallas_call(kernel, out_shape=outs, in_specs=[VMEM] * len(args) if spe...  21.7 us
  transfers between devices with their start and end apart: 30, of which 14 were waited for; matrix products, arithmetic and copies ran while one was open for 1% of the time, Pallas kernels for 10%

profile of v2, /device:TPU:0, one launch (start us, length us, event | category | flops | bytes accessed | tf_op | source)
XLA Modules:
  0.0 94.8 jit_solution(6550421294936886273)
XLA Ops:
  0.6 1.0 %fusion.2 = (bf16[1,64,576]{2,1,0:T(8,128)(2,1)S(1)}, bf16[64,576]{1,0:T(8,128)(2,1)S(1)}) fusion(f32[1,64,576]{2,1,0:T(8,128)} %param.8), kind=kLoop, calls=%fused_computation.13 | loop fusion | flops 73728 | bytes 294912 | tf_op jit(solution)/shard_map/convert_element_type | solution.py:327
  1.6 3.0 %collective-permute-start = (bf16[64,576]{1,0:T(8,128)(2,1)S(1)}, bf16[64,576]{1,0:T(8,128)(2,1)S(1)}, u32[]{:S(2)}, u32[]{:S(2)}) collective-permute-start(bf16[64,576]{1,0:T(8,128)(2,1)S(1)} %get-tuple-element.119.rest_0_), channel_id=1, source_target_pairs={{0,2},{1,3},{2,0},{3,1},{4,6},{5,7},{6,4},{7,5},{8,10},{9,11},{10,... | collective-permute-start | bytes 221192 | tf_op jit(solution)/shard_map/ppermute | solution.py:257
  4.7 1.5 %collective-permute-start.1 = (bf16[64,576]{1,0:T(8,128)(2,1)S(1)}, bf16[64,576]{1,0:T(8,128)(2,1)S(1)}, u32[]{:S(2)}, u32[]{:S(2)}) collective-permute-start(bf16[64,576]{1,0:T(8,128)(2,1)S(1)} %get-tuple-element.119.rest_0_), channel_id=1, source_target_pairs={{0,4},{1,5},{2,6},{3,7},{4,0},{5,1},{6,2},{7,3},{8,12},{9,13},{10,... | collective-permute-start | bytes 221192 | tf_op jit(solution)/shard_map/ppermute | solution.py:257
  6.2 0.0 collective-permute-start.2
  6.2 2.0 %collective-permute-start.3 = (bf16[64,576]{1,0:T(8,128)(2,1)S(1)}, bf16[64,576]{1,0:T(8,128)(2,1)S(1)}, u32[]{:S(2)}, u32[]{:S(2)}) collective-permute-start(bf16[64,576]{1,0:T(8,128)(2,1)S(1)} %get-tuple-element.119.rest_0_), channel_id=1, source_target_pairs={{0,8},{8,0},{16,24},{24,16},{1,9},{9,1},{17,25},{25,17},{2,10},{10... | collective-permute-start | bytes 221192 | tf_op jit(solution)/shard_map/ppermute | solution.py:257
  8.2 2.6 %collective-permute-start.4 = (bf16[64,576]{1,0:T(8,128)(2,1)S(1)}, bf16[64,576]{1,0:T(8,128)(2,1)S(1)}, u32[]{:S(2)}, u32[]{:S(2)}) collective-permute-start(bf16[64,576]{1,0:T(8,128)(2,1)S(1)} %get-tuple-element.119.rest_0_), channel_id=1, source_target_pairs={{0,16},{8,24},{16,0},{24,8},{1,17},{9,25},{17,1},{25,9},{2,18},{10... | collective-permute-start | bytes 221192 | tf_op jit(solution)/shard_map/ppermute | solution.py:257
  10.8 0.7 xor_bitcast_fusion
  11.5 0.7 fusion.1
  12.8 0.1 collective-permute-start.5
  12.9 0.1 pad_add_fusion.index
  13.0 2.3 %load.1.tiles = bf16[16,576,576]{2,1,0:T(8,128)(2,1)S(1)} custom-call(s32[33]{0:T(128)S(1)} %pad_add_fusion.index, bf16[16,576,576]{2,1,0:T(8,128)(2,1)} %bitcast.37), custom_call_target="tpu_custom_call" | custom-call | tf_op jit(solution)/shard_map/load/pallas_call | solution.py:236
  15.2 0.0 copy-start
  15.2 0.0 collective-permute-done.2
  15.3 0.0 collective-permute-done.3.rest_1_
  15.3 3.8 %collective-permute-done.5.rest_3_ = bf16[64,576]{1,0:T(8,128)(2,1)S(1)} collective-permute-done((bf16[64,576]{1,0:T(8,128)(2,1)S(1)}, bf16[64,576]{1,0:T(8,128)(2,1)S(1)}, u32[]{:S(2)}, u32[]{:S(2)}) %collective-permute-start.5) | collective-permute-done | bytes 73760 | tf_op jit(solution)/shard_map/ppermute | solution.py:257
  19.1 0.1 pad_maximum_fusion.near_own
  19.2 0.1 collective-permute-start.6
  19.3 1.6 %collective-permute-done.6.near_far = bf16[4,64,576]{2,1,0:T(8,128)(2,1)S(1)} collective-permute-done((bf16[4,64,576]{2,1,0:T(8,128)(2,1)S(1)}, bf16[4,64,576]{2,1,0:T(8,128)(2,1)S(1)}, u32[]{:S(2)}, u32[]{:S(2)}) %collective-permute-start.6) | collective-permute-done | bytes 294944 | tf_op jit(solution)/shard_map/ppermute | solution.py:257
  20.9 1.6 %mirrored.2 = (f32[4,64,576]{2,1,0:T(8,128)S(1)}, f32[64,576]{1,0:T(8,128)S(1)}) custom-call(s32[33]{0:T(128)S(1)} %pad_add_fusion.index, bf16[4,64,576]{2,1,0:T(8,128)(2,1)S(1)} %pad_maximum_fusion.near_own, bf16[4,64,576]{2,1,0:T(8,128)(2,1)S(1)} %collective-permute-done.6.near_far, bf16[16,576,576]{2,1,0:T(8,128)(2,1)S(1)} %load.1.tiles, ...), custom_call_target="tpu_custom_call" | custom-call | flops 679477248 | tf_op jit(solution)/shard_map/mirrored/pallas_call | solution.py:236
  22.5 0.9 gram.2
  23.5 0.1 collective-permute-start.7
  23.6 5.3 %collective-permute-start.8 = (bf16[64,768]{1,0:T(8,128)(2,1)S(1)}, bf16[64,768]{1,0:T(8,128)(2,1)S(1)}, u32[]{:S(2)}, u32[]{:S(2)}) collective-permute-start(bf16[64,768]{1,0:T(8,128)(2,1)S(1)} %get-tuple-element.73), channel_id=1, source_target_pairs={{0,16},{8,24},{16,0},{24,8},{1,17},{9,25},{17,1},{25,9},{2,18},{10... | collective-permute-start | bytes 294920 | tf_op jit(solution)/shard_map/ppermute | solution.py:257
  28.9 1.7 %forward.2 = (bf16[4,64,576]{2,1,0:T(8,128)(2,1)S(1)}, f32[4,64,576]{2,1,0:T(8,128)S(1)}) custom-call(s32[33]{0:T(128)S(1)} %pad_add_fusion.index, bf16[16,576,576]{2,1,0:T(8,128)(2,1)S(1)} %load.1.tiles, f32[64,128]{1,0:T(8,128)S(1)} %get-tuple-element.69.after.grams, bf16[64,576]{1,0:T(8,128)(2,1)S(1)} %get-tuple-element.119.rest_0_, ...), custom_call_target="tpu_custom_call" | custom-call | flops 679477248 | tf_op jit(solution)/shard_map/forward/pallas_call | solution.py:236
  30.6 6.1 %collective-permute-done.8.rest_1_ = bf16[64,768]{1,0:T(8,128)(2,1)S(1)} collective-permute-done((bf16[64,768]{1,0:T(8,128)(2,1)S(1)}, bf16[64,768]{1,0:T(8,128)(2,1)S(1)}, u32[]{:S(2)}, u32[]{:S(2)}) %collective-permute-start.8) | collective-permute-done | bytes 98336 | tf_op jit(solution)/shard_map/ppermute | solution.py:257
  36.7 0.4 gram_rows.2.grams
  37.1 0.6 collective-permute-start.11
  37.7 0.9 collective-permute-done.11.grams_came
  38.6 0.2 join.2
  38.8 1.6 %collective-permute-start.12 = (bf16[64,768]{1,0:T(8,128)(2,1)S(1)}, bf16[64,768]{1,0:T(8,128)(2,1)S(1)}, u32[]{:S(2)}, u32[]{:S(2)}) collective-permute-start(bf16[64,768]{1,0:T(8,128)(2,1)S(1)} %get-tuple-element.81), channel_id=1, source_target_pairs={{0,2},{1,3},{2,0},{3,1},{4,6},{5,7},{6,4},{7,5},{8,10},{9,11},{10,... | collective-permute-start | bytes 294920 | tf_op jit(solution)/shard_map/ppermute | solution.py:257
  40.4 1.5 %collective-permute-start.13 = (bf16[64,768]{1,0:T(8,128)(2,1)S(1)}, bf16[64,768]{1,0:T(8,128)(2,1)S(1)}, u32[]{:S(2)}, u32[]{:S(2)}) collective-permute-start(bf16[64,768]{1,0:T(8,128)(2,1)S(1)} %get-tuple-element.82), channel_id=1, source_target_pairs={{0,4},{1,5},{2,6},{3,7},{4,0},{5,1},{6,2},{7,3},{8,12},{9,13},{10,... | collective-permute-start | bytes 294920 | tf_op jit(solution)/shard_map/ppermute | solution.py:257
  41.9 0.5 collective-permute-start.14
  42.4 1.6 %collective-permute-done.12.rest_0_ = bf16[64,768]{1,0:T(8,128)(2,1)S(1)} collective-permute-done((bf16[64,768]{1,0:T(8,128)(2,1)S(1)}, bf16[64,768]{1,0:T(8,128)(2,1)S(1)}, u32[]{:S(2)}, u32[]{:S(2)}) %collective-permute-start.12) | collective-permute-done | bytes 98336 | tf_op jit(solution)/shard_map/ppermute | solution.py:257
  43.9 2.4 %collective-permute-done.13.rest_1_ = bf16[64,768]{1,0:T(8,128)(2,1)S(1)} collective-permute-done((bf16[64,768]{1,0:T(8,128)(2,1)S(1)}, bf16[64,768]{1,0:T(8,128)(2,1)S(1)}, u32[]{:S(2)}, u32[]{:S(2)}) %collective-permute-start.13) | collective-permute-done | bytes 98336 | tf_op jit(solution)/shard_map/ppermute | solution.py:257
  46.3 1.1 %collective-permute-done.14.rest_2_ = bf16[64,768]{1,0:T(8,128)(2,1)S(1)} collective-permute-done((bf16[64,768]{1,0:T(8,128)(2,1)S(1)}, bf16[64,768]{1,0:T(8,128)(2,1)S(1)}, u32[]{:S(2)}, u32[]{:S(2)}) %collective-permute-start.14) | collective-permute-done | bytes 98336 | tf_op jit(solution)/shard_map/ppermute | solution.py:257
  47.4 2.9 %first_step.1 = (f32[64,576]{1,0:T(8,128)S(1)}, f32[64,576]{1,0:T(8,128)S(1)}, bf16[64,576]{1,0:T(8,128)(2,1)S(1)}, f32[64,128]{1,0:T(8,128)S(1)}, f32[64,64]{1,0:T(8,128)S(1)}) custom-call(f32[64,576]{1,0:T(8,128)S(1)} %get-tuple-element.79.mine, f32[64,128]{1,0:T(8,128)S(1)} %get-tuple-element.80.grams, f32[64,576]{1,0:T(8,128)S(1)} %bitcast.31, ...), custom_call_target="tpu_custom_call" | custom-call | tf_op jit(solution)/shard_map/first_step/pallas_call | solution.py:236
  50.3 1.1 %collective-permute-start.15 = (bf16[64,576]{1,0:T(8,128)(2,1)S(1)}, bf16[64,576]{1,0:T(8,128)(2,1)S(1)}, u32[]{:S(2)}, u32[]{:S(2)}) collective-permute-start(bf16[64,576]{1,0:T(8,128)(2,1)S(1)} %get-tuple-element.84.rest_0_), channel_id=1, source_target_pairs={{0,2},{1,3},{2,0},{3,1},{4,6},{5,7},{6,4},{7,5},{8,10},{9,11},{10,... | collective-permute-start | bytes 221192 | tf_op jit(solution)/shard_map/ppermute | solution.py:257
  51.4 0.8 collective-permute-start.16
  52.3 1.6 %collective-permute-start.17 = (bf16[64,576]{1,0:T(8,128)(2,1)S(1)}, bf16[64,576]{1,0:T(8,128)(2,1)S(1)}, u32[]{:S(2)}, u32[]{:S(2)}) collective-permute-start(bf16[64,576]{1,0:T(8,128)(2,1)S(1)} %get-tuple-element.84.rest_0_), channel_id=1, source_target_pairs={{0,6},{1,7},{2,4},{3,5},{4,2},{5,3},{6,0},{7,1},{8,14},{9,15},{10,... | collective-permute-start | bytes 221192 | tf_op jit(solution)/shard_map/ppermute | solution.py:257
  53.9 1.9 %collective-permute-start.18 = (bf16[64,576]{1,0:T(8,128)(2,1)S(1)}, bf16[64,576]{1,0:T(8,128)(2,1)S(1)}, u32[]{:S(2)}, u32[]{:S(2)}) collective-permute-start(bf16[64,576]{1,0:T(8,128)(2,1)S(1)} %get-tuple-element.84.rest_0_), channel_id=1, source_target_pairs={{0,8},{8,0},{16,24},{24,16},{1,9},{9,1},{17,25},{25,17},{2,10},{10... | collective-permute-start | bytes 221192 | tf_op jit(solution)/shard_map/ppermute | solution.py:257
  55.7 1.2 %collective-permute-start.19 = (bf16[64,576]{1,0:T(8,128)(2,1)S(1)}, bf16[64,576]{1,0:T(8,128)(2,1)S(1)}, u32[]{:S(2)}, u32[]{:S(2)}) collective-permute-start(bf16[64,576]{1,0:T(8,128)(2,1)S(1)} %get-tuple-element.84.rest_0_), channel_id=1, source_target_pairs={{0,16},{8,24},{16,0},{24,8},{1,17},{9,25},{17,1},{25,9},{2,18},{10... | collective-permute-start | bytes 221192 | tf_op jit(solution)/shard_map/ppermute | solution.py:257
  56.9 1.3 %collective-permute-start.20 = (bf16[64,576]{1,0:T(8,128)(2,1)S(1)}, bf16[64,576]{1,0:T(8,128)(2,1)S(1)}, u32[]{:S(2)}, u32[]{:S(2)}) collective-permute-start(bf16[64,576]{1,0:T(8,128)(2,1)S(1)} %get-tuple-element.84.rest_0_), channel_id=1, source_target_pairs={{0,24},{8,16},{16,8},{24,0},{1,25},{9,17},{17,9},{25,1},{2,26},{10... | collective-permute-start | bytes 221192 | tf_op jit(solution)/shard_map/ppermute | solution.py:257
  58.3 0.5 collective-permute-done.18.rest_1_
  58.8 3.6 %collective-permute-done.19.rest_2_ = bf16[64,576]{1,0:T(8,128)(2,1)S(1)} collective-permute-done((bf16[64,576]{1,0:T(8,128)(2,1)S(1)}, bf16[64,576]{1,0:T(8,128)(2,1)S(1)}, u32[]{:S(2)}, u32[]{:S(2)}) %collective-permute-start.19) | collective-permute-done | bytes 73760 | tf_op jit(solution)/shard_map/ppermute | solution.py:257
  62.3 0.9 collective-permute-done.20.rest_3_
  63.3 0.1 pad_maximum_fusion.1.near_own
  63.3 0.1 collective-permute-start.21
  63.4 1.6 %collective-permute-done.21.near_far = bf16[4,64,576]{2,1,0:T(8,128)(2,1)S(1)} collective-permute-done((bf16[4,64,576]{2,1,0:T(8,128)(2,1)S(1)}, bf16[4,64,576]{2,1,0:T(8,128)(2,1)S(1)}, u32[]{:S(2)}, u32[]{:S(2)}) %collective-permute-start.21) | collective-permute-done | bytes 294944 | tf_op jit(solution)/shard_map/ppermute | solution.py:257
  65.0 1.6 %mirrored.3 = (f32[4,64,576]{2,1,0:T(8,128)S(1)}, f32[64,576]{1,0:T(8,128)S(1)}) custom-call(s32[33]{0:T(128)S(1)} %pad_add_fusion.index, bf16[4,64,576]{2,1,0:T(8,128)(2,1)S(1)} %pad_maximum_fusion.1.near_own, bf16[4,64,576]{2,1,0:T(8,128)(2,1)S(1)} %collective-permute-done.21.near_far, bf16[16,576,576]{2,1,0:T(8,128)(2,1)S(1)} %load.1.tiles, ...), custom_call_target="tpu_custom_call" | custom-call | flops 679477248 | tf_op jit(solution)/shard_map/mirrored/pallas_call | solution.py:236
  66.7 1.0 %gram.3 = (f32[64,128]{1,0:T(8,128)S(1)}, bf16[64,768]{1,0:T(8,128)(2,1)S(1)}, bf16[64,768]{1,0:T(8,128)(2,1)S(1)}, bf16[64,768]{1,0:T(8,128)(2,1)S(1)}) custom-call(f32[4,64,576]{2,1,0:T(8,128)S(1)} %get-tuple-element.89.acc, f32[64,576]{1,0:T(8,128)S(1)} %get-tuple-element.90.own, f32[64,576]{1,0:T(8,128)S(1)} %get-tuple-element.91.residual.residual_in, ...), custom_call_target="tpu_custom_call" | custom-call | tf_op jit(solution)/shard_map/gram/pallas_call | solution.py:236
  67.6 2.1 %collective-permute-start.22 = (bf16[64,768]{1,0:T(8,128)(2,1)S(1)}, bf16[64,768]{1,0:T(8,128)(2,1)S(1)}, u32[]{:S(2)}, u32[]{:S(2)}) collective-permute-start(bf16[64,768]{1,0:T(8,128)(2,1)S(1)} %get-tuple-element.98), channel_id=1, source_target_pairs={{0,8},{8,0},{16,24},{24,16},{1,9},{9,1},{17,25},{25,17},{2,10},{10... | collective-permute-start | bytes 294920 | tf_op jit(solution)/shard_map/ppermute | solution.py:257
  69.7 2.7 %collective-permute-start.23 = (bf16[64,768]{1,0:T(8,128)(2,1)S(1)}, bf16[64,768]{1,0:T(8,128)(2,1)S(1)}, u32[]{:S(2)}, u32[]{:S(2)}) collective-permute-start(bf16[64,768]{1,0:T(8,128)(2,1)S(1)} %get-tuple-element.99), channel_id=1, source_target_pairs={{0,16},{8,24},{16,0},{24,8},{1,17},{9,25},{17,1},{25,9},{2,18},{10... | collective-permute-start | bytes 294920 | tf_op jit(solution)/shard_map/ppermute | solution.py:257
  72.4 0.2 collective-permute-start.24
  72.6 1.9 %forward.3 = (bf16[4,64,576]{2,1,0:T(8,128)(2,1)S(1)}, f32[4,64,576]{2,1,0:T(8,128)S(1)}) custom-call(s32[33]{0:T(128)S(1)} %pad_add_fusion.index, bf16[16,576,576]{2,1,0:T(8,128)(2,1)S(1)} %load.1.tiles, f32[64,128]{1,0:T(8,128)S(1)} %get-tuple-element.95.after.grams, bf16[64,576]{1,0:T(8,128)(2,1)S(1)} %get-tuple-element.84.rest_0_, ...), custom_call_target="tpu_custom_call" | custom-call | flops 679477248 | tf_op jit(solution)/shard_map/forward/pallas_call | solution.py:236
  74.6 5.4 %collective-permute-done.23.rest_1_ = bf16[64,768]{1,0:T(8,128)(2,1)S(1)} collective-permute-done((bf16[64,768]{1,0:T(8,128)(2,1)S(1)}, bf16[64,768]{1,0:T(8,128)(2,1)S(1)}, u32[]{:S(2)}, u32[]{:S(2)}) %collective-permute-start.23) | collective-permute-done | bytes 98336 | tf_op jit(solution)/shard_map/ppermute | solution.py:257
  80.0 0.4 gram_rows.3.grams
  80.4 0.6 collective-permute-start.26
  81.0 0.9 collective-permute-done.26.grams_came
  81.9 0.2 join.3
  82.1 1.8 %collective-permute-start.27 = (bf16[64,768]{1,0:T(8,128)(2,1)S(1)}, bf16[64,768]{1,0:T(8,128)(2,1)S(1)}, u32[]{:S(2)}, u32[]{:S(2)}) collective-permute-start(bf16[64,768]{1,0:T(8,128)(2,1)S(1)} %get-tuple-element.113), channel_id=1, source_target_pairs={{0,2},{1,3},{2,0},{3,1},{4,6},{5,7},{6,4},{7,5},{8,10},{9,11},{10,... | collective-permute-start | bytes 294920 | tf_op jit(solution)/shard_map/ppermute | solution.py:257
  83.9 0.5 collective-permute-start.28
  84.4 1.2 %collective-permute-start.29 = (bf16[64,768]{1,0:T(8,128)(2,1)S(1)}, bf16[64,768]{1,0:T(8,128)(2,1)S(1)}, u32[]{:S(2)}, u32[]{:S(2)}) collective-permute-start(bf16[64,768]{1,0:T(8,128)(2,1)S(1)} %get-tuple-element.115), channel_id=1, source_target_pairs={{0,6},{1,7},{2,4},{3,5},{4,2},{5,3},{6,0},{7,1},{8,14},{9,15},{10,... | collective-permute-start | bytes 294920 | tf_op jit(solution)/shard_map/ppermute | solution.py:257
  85.7 2.5 %between.1 = (f32[64,64]{1,0:T(8,128)S(1)}, f32[64,64]{1,0:T(8,128)S(1)}, f32[64,576]{1,0:T(8,128)S(1)}) custom-call(f32[64,128]{1,0:T(8,128)S(1)} %get-tuple-element.108.totals, f32[64,64]{1,0:T(8,128)S(1)} %get-tuple-element.109.alpha, f32[64,576]{1,0:T(8,128)S(1)} %bitcast.32), custom_call_target="tpu_custom_call" | custom-call | tf_op jit(solution)/shard_map/between/pallas_call | solution.py:236
  88.2 2.6 %collective-permute-done.28.rest_1_ = bf16[64,768]{1,0:T(8,128)(2,1)S(1)} collective-permute-done((bf16[64,768]{1,0:T(8,128)(2,1)S(1)}, bf16[64,768]{1,0:T(8,128)(2,1)S(1)}, u32[]{:S(2)}, u32[]{:S(2)}) %collective-permute-start.28) | collective-permute-done | bytes 98336 | tf_op jit(solution)/shard_map/ppermute | solution.py:257
  90.8 4.0 %last_step.1 = (f32[64,576]{1,0:T(8,128)}, f32[64,576]{1,0:T(8,128)}) custom-call(f32[64,576]{1,0:T(8,128)S(1)} %get-tuple-element.105.mine, f32[64,128]{1,0:T(8,128)S(1)} %get-tuple-element.106.grams, f32[64,576]{1,0:T(8,128)S(1)} %bitcast.33, f32[64,576]{1,0:T(8,128)S(1)} %get-tuple-element.107.image_in, ...), custom_call_target="tpu_custom_call" | custom-call | tf_op jit(solution)/shard_map/last_step/pallas_call | solution.py:236
  (20 shorter events, 0.1 us)
Async XLA Ops:
  1.6 11.1 %collective-permute-start = (bf16[64,576]{1,0:T(8,128)(2,1)S(1)}, bf16[64,576]{1,0:T(8,128)(2,1)S(1)}, u32[]{:S(2)}, u32[]{:S(2)}) collective-permute-start(bf16[64,576]{1,0:T(8,128)(2,1)S(1)} %get-tuple-element.119.rest_0_), channel_id=1, source_target_pairs={{0,2},{1,3},{2,0},{3,1},{4,6},{5,7},{6,4},{7,5},{8,10},{9,11},{10,... | collective-permute-start | bytes 221192 | tf_op jit(solution)/shard_map/ppermute | solution.py:257
  4.7 10.6 %collective-permute-start.1 = (bf16[64,576]{1,0:T(8,128)(2,1)S(1)}, bf16[64,576]{1,0:T(8,128)(2,1)S(1)}, u32[]{:S(2)}, u32[]{:S(2)}) collective-permute-start(bf16[64,576]{1,0:T(8,128)(2,1)S(1)} %get-tuple-element.119.rest_0_), channel_id=1, source_target_pairs={{0,4},{1,5},{2,6},{3,7},{4,0},{5,1},{6,2},{7,3},{8,12},{9,13},{10,... | collective-permute-start | bytes 221192 | tf_op jit(solution)/shard_map/ppermute | solution.py:257
  6.2 9.1 %collective-permute-start.2 = (bf16[64,576]{1,0:T(8,128)(2,1)S(1)}, bf16[64,576]{1,0:T(8,128)(2,1)S(1)}, u32[]{:S(2)}, u32[]{:S(2)}) collective-permute-start(bf16[64,576]{1,0:T(8,128)(2,1)S(1)} %get-tuple-element.119.rest_0_), channel_id=1, source_target_pairs={{0,6},{1,7},{2,4},{3,5},{4,2},{5,3},{6,0},{7,1},{8,14},{9,15},{10,... | collective-permute-start | bytes 221192 | tf_op jit(solution)/shard_map/ppermute | solution.py:257
  6.2 9.1 %collective-permute-start.3 = (bf16[64,576]{1,0:T(8,128)(2,1)S(1)}, bf16[64,576]{1,0:T(8,128)(2,1)S(1)}, u32[]{:S(2)}, u32[]{:S(2)}) collective-permute-start(bf16[64,576]{1,0:T(8,128)(2,1)S(1)} %get-tuple-element.119.rest_0_), channel_id=1, source_target_pairs={{0,8},{8,0},{16,24},{24,16},{1,9},{9,1},{17,25},{25,17},{2,10},{10... | collective-permute-start | bytes 221192 | tf_op jit(solution)/shard_map/ppermute | solution.py:257
  8.2 7.0 %collective-permute-start.4 = (bf16[64,576]{1,0:T(8,128)(2,1)S(1)}, bf16[64,576]{1,0:T(8,128)(2,1)S(1)}, u32[]{:S(2)}, u32[]{:S(2)}) collective-permute-start(bf16[64,576]{1,0:T(8,128)(2,1)S(1)} %get-tuple-element.119.rest_0_), channel_id=1, source_target_pairs={{0,16},{8,24},{16,0},{24,8},{1,17},{9,25},{17,1},{25,9},{2,18},{10... | collective-permute-start | bytes 221192 | tf_op jit(solution)/shard_map/ppermute | solution.py:257
  12.8 6.3 %collective-permute-start.5 = (bf16[64,576]{1,0:T(8,128)(2,1)S(1)}, bf16[64,576]{1,0:T(8,128)(2,1)S(1)}, u32[]{:S(2)}, u32[]{:S(2)}) collective-permute-start(bf16[64,576]{1,0:T(8,128)(2,1)S(1)} %get-tuple-element.119.rest_0_), channel_id=1, source_target_pairs={{0,24},{8,16},{16,8},{24,0},{1,25},{9,17},{17,9},{25,1},{2,26},{10... | collective-permute-start | bytes 221192 | tf_op jit(solution)/shard_map/ppermute | solution.py:257
  13.0 7.9 %copy-start.1 = (bf16[1,576,576]{2,1,0:T(8,128)(2,1)S(1)}, bf16[1,576,576]{2,1,0:T(8,128)(2,1)}, u32[]{:S(2)}) copy-start(bf16[1,576,576]{2,1,0:T(8,128)(2,1)} %param.7) | copy-start | bytes 1990660
  15.2 7.3 %copy-start = (f32[1,64,576]{2,1,0:T(8,128)S(1)}, f32[1,64,576]{2,1,0:T(8,128)}, u32[]{:S(2)}) copy-start(f32[1,64,576]{2,1,0:T(8,128)} %param.8) | copy-start | bytes 442372
  19.2 1.7 %collective-permute-start.6 = (bf16[4,64,576]{2,1,0:T(8,128)(2,1)S(1)}, bf16[4,64,576]{2,1,0:T(8,128)(2,1)S(1)}, u32[]{:S(2)}, u32[]{:S(2)}) collective-permute-start(bf16[4,64,576]{2,1,0:T(8,128)(2,1)S(1)} %pad_maximum_fusion.near_own), channel_id=1, source_target_pairs={{0,1},{1,0},{2,3},{3,2},{4,5},{5,4},{6,7},{7,6},{8,9},{9,8},{10,11... | collective-permute-start | bytes 884744 | tf_op jit(solution)/shard_map/ppermute | solution.py:257
  23.5 7.1 %collective-permute-start.7 = (bf16[64,768]{1,0:T(8,128)(2,1)S(1)}, bf16[64,768]{1,0:T(8,128)(2,1)S(1)}, u32[]{:S(2)}, u32[]{:S(2)}) collective-permute-start(bf16[64,768]{1,0:T(8,128)(2,1)S(1)} %get-tuple-element.72), channel_id=1, source_target_pairs={{0,8},{8,0},{16,24},{24,16},{1,9},{9,1},{17,25},{25,17},{2,10},{10... | collective-permute-start | bytes 294920 | tf_op jit(solution)/shard_map/ppermute | solution.py:257
  23.6 13.1 %collective-permute-start.8 = (bf16[64,768]{1,0:T(8,128)(2,1)S(1)}, bf16[64,768]{1,0:T(8,128)(2,1)S(1)}, u32[]{:S(2)}, u32[]{:S(2)}) collective-permute-start(bf16[64,768]{1,0:T(8,128)(2,1)S(1)} %get-tuple-element.73), channel_id=1, source_target_pairs={{0,16},{8,24},{16,0},{24,8},{1,17},{9,25},{17,1},{25,9},{2,18},{10... | collective-permute-start | bytes 294920 | tf_op jit(solution)/shard_map/ppermute | solution.py:257
  28.9 7.8 %collective-permute-start.9 = (bf16[64,768]{1,0:T(8,128)(2,1)S(1)}, bf16[64,768]{1,0:T(8,128)(2,1)S(1)}, u32[]{:S(2)}, u32[]{:S(2)}) collective-permute-start(bf16[64,768]{1,0:T(8,128)(2,1)S(1)} %get-tuple-element.74), channel_id=1, source_target_pairs={{0,24},{8,16},{16,8},{24,0},{1,25},{9,17},{17,9},{25,1},{2,26},{10... | collective-permute-start | bytes 294920 | tf_op jit(solution)/shard_map/ppermute | solution.py:257
  36.7 1.8 %collective-permute-start.10 = (bf16[4,64,576]{2,1,0:T(8,128)(2,1)S(1)}, bf16[4,64,576]{2,1,0:T(8,128)(2,1)S(1)}, u32[]{:S(2)}, u32[]{:S(2)}) collective-permute-start(bf16[4,64,576]{2,1,0:T(8,128)(2,1)S(1)} %get-tuple-element.75), channel_id=1, source_target_pairs={{0,1},{1,0},{2,3},{3,2},{4,5},{5,4},{6,7},{7,6},{8,9},{9,8},{10,11... | collective-permute-start | bytes 884744 | tf_op jit(solution)/shard_map/ppermute | solution.py:257
  37.1 1.4 %collective-permute-start.11 = (f32[64,128]{1,0:T(8,128)S(1)}, f32[64,128]{1,0:T(8,128)S(1)}, u32[]{:S(2)}, u32[]{:S(2)}) collective-permute-start(f32[64,128]{1,0:T(8,128)S(1)} %gram_rows.2.grams), channel_id=1, source_target_pairs={{0,1},{1,0},{2,3},{3,2},{4,5},{5,4},{6,7},{7,6},{8,9},{9,8},{10,11... | collective-permute-start | bytes 98312 | tf_op jit(solution)/shard_map/ppermute | solution.py:257
  38.8 5.1 %collective-permute-start.12 = (bf16[64,768]{1,0:T(8,128)(2,1)S(1)}, bf16[64,768]{1,0:T(8,128)(2,1)S(1)}, u32[]{:S(2)}, u32[]{:S(2)}) collective-permute-start(bf16[64,768]{1,0:T(8,128)(2,1)S(1)} %get-tuple-element.81), channel_id=1, source_target_pairs={{0,2},{1,3},{2,0},{3,1},{4,6},{5,7},{6,4},{7,5},{8,10},{9,11},{10,... | collective-permute-start | bytes 294920 | tf_op jit(solution)/shard_map/ppermute | solution.py:257
  40.4 5.9 %collective-permute-start.13 = (bf16[64,768]{1,0:T(8,128)(2,1)S(1)}, bf16[64,768]{1,0:T(8,128)(2,1)S(1)}, u32[]{:S(2)}, u32[]{:S(2)}) collective-permute-start(bf16[64,768]{1,0:T(8,128)(2,1)S(1)} %get-tuple-element.82), channel_id=1, source_target_pairs={{0,4},{1,5},{2,6},{3,7},{4,0},{5,1},{6,2},{7,3},{8,12},{9,13},{10,... | collective-permute-start | bytes 294920 | tf_op jit(solution)/shard_map/ppermute | solution.py:257
  41.9 5.5 %collective-permute-start.14 = (bf16[64,768]{1,0:T(8,128)(2,1)S(1)}, bf16[64,768]{1,0:T(8,128)(2,1)S(1)}, u32[]{:S(2)}, u32[]{:S(2)}) collective-permute-start(bf16[64,768]{1,0:T(8,128)(2,1)S(1)} %get-tuple-element.83), channel_id=1, source_target_pairs={{0,6},{1,7},{2,4},{3,5},{4,2},{5,3},{6,0},{7,1},{8,14},{9,15},{10,... | collective-permute-start | bytes 294920 | tf_op jit(solution)/shard_map/ppermute | solution.py:257
  50.3 6.6 %collective-permute-start.15 = (bf16[64,576]{1,0:T(8,128)(2,1)S(1)}, bf16[64,576]{1,0:T(8,128)(2,1)S(1)}, u32[]{:S(2)}, u32[]{:S(2)}) collective-permute-start(bf16[64,576]{1,0:T(8,128)(2,1)S(1)} %get-tuple-element.84.rest_0_), channel_id=1, source_target_pairs={{0,2},{1,3},{2,0},{3,1},{4,6},{5,7},{6,4},{7,5},{8,10},{9,11},{10,... | collective-permute-start | bytes 221192 | tf_op jit(solution)/shard_map/ppermute | solution.py:257
  51.4 6.8 %collective-permute-start.16 = (bf16[64,576]{1,0:T(8,128)(2,1)S(1)}, bf16[64,576]{1,0:T(8,128)(2,1)S(1)}, u32[]{:S(2)}, u32[]{:S(2)}) collective-permute-start(bf16[64,576]{1,0:T(8,128)(2,1)S(1)} %get-tuple-element.84.rest_0_), channel_id=1, source_target_pairs={{0,4},{1,5},{2,6},{3,7},{4,0},{5,1},{6,2},{7,3},{8,12},{9,13},{10,... | collective-permute-start | bytes 221192 | tf_op jit(solution)/shard_map/ppermute | solution.py:257
  52.3 6.0 %collective-permute-start.17 = (bf16[64,576]{1,0:T(8,128)(2,1)S(1)}, bf16[64,576]{1,0:T(8,128)(2,1)S(1)}, u32[]{:S(2)}, u32[]{:S(2)}) collective-permute-start(bf16[64,576]{1,0:T(8,128)(2,1)S(1)} %get-tuple-element.84.rest_0_), channel_id=1, source_target_pairs={{0,6},{1,7},{2,4},{3,5},{4,2},{5,3},{6,0},{7,1},{8,14},{9,15},{10,... | collective-permute-start | bytes 221192 | tf_op jit(solution)/shard_map/ppermute | solution.py:257
  53.9 4.9 %collective-permute-start.18 = (bf16[64,576]{1,0:T(8,128)(2,1)S(1)}, bf16[64,576]{1,0:T(8,128)(2,1)S(1)}, u32[]{:S(2)}, u32[]{:S(2)}) collective-permute-start(bf16[64,576]{1,0:T(8,128)(2,1)S(1)} %get-tuple-element.84.rest_0_), channel_id=1, source_target_pairs={{0,8},{8,0},{16,24},{24,16},{1,9},{9,1},{17,25},{25,17},{2,10},{10... | collective-permute-start | bytes 221192 | tf_op jit(solution)/shard_map/ppermute | solution.py:257
  55.7 6.6 %collective-permute-start.19 = (bf16[64,576]{1,0:T(8,128)(2,1)S(1)}, bf16[64,576]{1,0:T(8,128)(2,1)S(1)}, u32[]{:S(2)}, u32[]{:S(2)}) collective-permute-start(bf16[64,576]{1,0:T(8,128)(2,1)S(1)} %get-tuple-element.84.rest_0_), channel_id=1, source_target_pairs={{0,16},{8,24},{16,0},{24,8},{1,17},{9,25},{17,1},{25,9},{2,18},{10... | collective-permute-start | bytes 221192 | tf_op jit(solution)/shard_map/ppermute | solution.py:257
  56.9 6.3 %collective-permute-start.20 = (bf16[64,576]{1,0:T(8,128)(2,1)S(1)}, bf16[64,576]{1,0:T(8,128)(2,1)S(1)}, u32[]{:S(2)}, u32[]{:S(2)}) collective-permute-start(bf16[64,576]{1,0:T(8,128)(2,1)S(1)} %get-tuple-element.84.rest_0_), channel_id=1, source_target_pairs={{0,24},{8,16},{16,8},{24,0},{1,25},{9,17},{17,9},{25,1},{2,26},{10... | collective-permute-start | bytes 221192 | tf_op jit(solution)/shard_map/ppermute | solution.py:257
  63.3 1.7 %collective-permute-start.21 = (bf16[4,64,576]{2,1,0:T(8,128)(2,1)S(1)}, bf16[4,64,576]{2,1,0:T(8,128)(2,1)S(1)}, u32[]{:S(2)}, u32[]{:S(2)}) collective-permute-start(bf16[4,64,576]{2,1,0:T(8,128)(2,1)S(1)} %pad_maximum_fusion.1.near_own), channel_id=1, source_target_pairs={{0,1},{1,0},{2,3},{3,2},{4,5},{5,4},{6,7},{7,6},{8,9},{9,8},{10,11... | collective-permute-start | bytes 884744 | tf_op jit(solution)/shard_map/ppermute | solution.py:257
  67.6 6.9 %collective-permute-start.22 = (bf16[64,768]{1,0:T(8,128)(2,1)S(1)}, bf16[64,768]{1,0:T(8,128)(2,1)S(1)}, u32[]{:S(2)}, u32[]{:S(2)}) collective-permute-start(bf16[64,768]{1,0:T(8,128)(2,1)S(1)} %get-tuple-element.98), channel_id=1, source_target_pairs={{0,8},{8,0},{16,24},{24,16},{1,9},{9,1},{17,25},{25,17},{2,10},{10... | collective-permute-start | bytes 294920 | tf_op jit(solution)/shard_map/ppermute | solution.py:257
  69.7 10.3 %collective-permute-start.23 = (bf16[64,768]{1,0:T(8,128)(2,1)S(1)}, bf16[64,768]{1,0:T(8,128)(2,1)S(1)}, u32[]{:S(2)}, u32[]{:S(2)}) collective-permute-start(bf16[64,768]{1,0:T(8,128)(2,1)S(1)} %get-tuple-element.99), channel_id=1, source_target_pairs={{0,16},{8,24},{16,0},{24,8},{1,17},{9,25},{17,1},{25,9},{2,18},{10... | collective-permute-start | bytes 294920 | tf_op jit(solution)/shard_map/ppermute | solution.py:257
  72.4 7.6 %collective-permute-start.24 = (bf16[64,768]{1,0:T(8,128)(2,1)S(1)}, bf16[64,768]{1,0:T(8,128)(2,1)S(1)}, u32[]{:S(2)}, u32[]{:S(2)}) collective-permute-start(bf16[64,768]{1,0:T(8,128)(2,1)S(1)} %get-tuple-element.100), channel_id=1, source_target_pairs={{0,24},{8,16},{16,8},{24,0},{1,25},{9,17},{17,9},{25,1},{2,26},{10... | collective-permute-start | bytes 294920 | tf_op jit(solution)/shard_map/ppermute | solution.py:257
  80.0 1.8 %collective-permute-start.25 = (bf16[4,64,576]{2,1,0:T(8,128)(2,1)S(1)}, bf16[4,64,576]{2,1,0:T(8,128)(2,1)S(1)}, u32[]{:S(2)}, u32[]{:S(2)}) collective-permute-start(bf16[4,64,576]{2,1,0:T(8,128)(2,1)S(1)} %get-tuple-element.101), channel_id=1, source_target_pairs={{0,1},{1,0},{2,3},{3,2},{4,5},{5,4},{6,7},{7,6},{8,9},{9,8},{10,11... | collective-permute-start | bytes 884744 | tf_op jit(solution)/shard_map/ppermute | solution.py:257
  80.4 1.4 %collective-permute-start.26 = (f32[64,128]{1,0:T(8,128)S(1)}, f32[64,128]{1,0:T(8,128)S(1)}, u32[]{:S(2)}, u32[]{:S(2)}) collective-permute-start(f32[64,128]{1,0:T(8,128)S(1)} %gram_rows.3.grams), channel_id=1, source_target_pairs={{0,1},{1,0},{2,3},{3,2},{4,5},{5,4},{6,7},{7,6},{8,9},{9,8},{10,11... | collective-permute-start | bytes 98312 | tf_op jit(solution)/shard_map/ppermute | solution.py:257
  82.1 6.0 %collective-permute-start.27 = (bf16[64,768]{1,0:T(8,128)(2,1)S(1)}, bf16[64,768]{1,0:T(8,128)(2,1)S(1)}, u32[]{:S(2)}, u32[]{:S(2)}) collective-permute-start(bf16[64,768]{1,0:T(8,128)(2,1)S(1)} %get-tuple-element.113), channel_id=1, source_target_pairs={{0,2},{1,3},{2,0},{3,1},{4,6},{5,7},{6,4},{7,5},{8,10},{9,11},{10,... | collective-permute-start | bytes 294920 | tf_op jit(solution)/shard_map/ppermute | solution.py:257
  83.9 6.9 %collective-permute-start.28 = (bf16[64,768]{1,0:T(8,128)(2,1)S(1)}, bf16[64,768]{1,0:T(8,128)(2,1)S(1)}, u32[]{:S(2)}, u32[]{:S(2)}) collective-permute-start(bf16[64,768]{1,0:T(8,128)(2,1)S(1)} %get-tuple-element.114), channel_id=1, source_target_pairs={{0,4},{1,5},{2,6},{3,7},{4,0},{5,1},{6,2},{7,3},{8,12},{9,13},{10,... | collective-permute-start | bytes 294920 | tf_op jit(solution)/shard_map/ppermute | solution.py:257
  84.4 6.4 %collective-permute-start.29 = (bf16[64,768]{1,0:T(8,128)(2,1)S(1)}, bf16[64,768]{1,0:T(8,128)(2,1)S(1)}, u32[]{:S(2)}, u32[]{:S(2)}) collective-permute-start(bf16[64,768]{1,0:T(8,128)(2,1)S(1)} %get-tuple-element.115), channel_id=1, source_target_pairs={{0,6},{1,7},{2,4},{3,5},{4,2},{5,3},{6,0},{7,1},{8,14},{9,15},{10,... | collective-permute-start | bytes 294920 | tf_op jit(solution)/shard_map/ppermute | solution.py:257

commit v3 on v2

--- a/solution.py
+++ b/solution.py
@@ -86,37 +86,84 @@
     return jnp.concatenate([first, jnp.where(rows == columns, diagonal, second)], 1)
 
 
-def held_slots(count, slots, work):
+def held_slots(count, slots, work, ready=None):
     group = 4 if slots % 4 == 0 else 1
 
     def turn(g, carry):
+        if ready is not None:
+            for u in range(group):
+                pl.when(g * group + u < count)(functools.partial(ready, g * group + u))
         for u in range(group):
-            slot = g * group + u
-            work(slot, slot < count)
+            work(g * group + u, g * group + u < count)
         return carry
 
     lax.fori_loop(0, (count + group - 1) // group, turn, 0)
 
 
-def load_kernel(index, tiles, out, arrived):
+def forward_products(index, tiles, far_in, give_core, acc, own, far, ready=None):
+    n_chip = give_core.shape[0]
+    slots = tiles.shape[0] - 1
+    for d, block in enumerate(far_in):
+        far[d] = block[...]
+    acc[...] = jnp.zeros_like(acc)
+
+    def work(slot, held):
+        i = index[1 + slot]
+        j = index[1 + slots + slot]
+        acc[i] += jnp.where(held, dot16(far[j], tiles[slot], NT), 0.0)
+
+    held_slots(index[0], slots, work, ready)
+    if ready is not None:
+        ready(slots)
+    own[...] = dot16(far[0], tiles[slots], NT)
+    for d in range(n_chip):
+        give_core[d] = acc[n_chip + d].astype(BF16)
+
+
+def forward_kernel(index, tiles, *rest, n_row):
+    give_core, acc, own, far = rest[n_row:]
+    forward_products(index, tiles, rest[:n_row], give_core, acc, own, far)
+
+
+def forward_load_kernel(index, diag, stored, *rest, n_row):
+    give_core, acc, own, tiles, far, arrived = rest[n_row:]
+    slots = stored.shape[0]
+
     def fetch(slot):
-        return pltpu.make_async_copy(tiles.at[slot], out.at[slot], arrived.at[slot])
+        return pltpu.make_async_copy(stored.at[slot], tiles.at[slot], arrived.at[slot])
+
+    last = pltpu.make_async_copy(diag, tiles.at[slots], arrived.at[slots])
+
+    def ready(slot):
+        if isinstance(slot, int):
+            last.wait()
+        else:
+            fetch(slot).wait()
 
     def begin(slot, carry):
         fetch(slot).start()
         return carry
 
-    def end(slot, carry):
-        fetch(slot).wait()
-        return carry
-
     lax.fori_loop(0, index[0], begin, 0)
-    lax.fori_loop(0, index[0], end, 0)
-
-
-def mirrored_kernel(index, near_own, near_far, tiles, diag, acc, own, near):
+    last.start()
+    forward_products(index, tiles, rest[:n_row], give_core, acc, own, far, ready)
+
+
+def gram_kernel(acc, came, own, residual, *rest):
+    *near, keep, grams = rest
+    size = own.shape[0]
+    half = 0.5 * dot_exact16(near[0][...], own[...], NT)
+    for d, block in enumerate(near):
+        both = acc[d] + came[d].astype(F32)
+        keep[d] = both
+        half += dot_exact16(block[...], both, NT)
+    grams[:, :size] = half + half.T
+    grams[:, size:] = dot32(residual[...], residual[...], NT)
+
+
+def mirrored_kernel(index, near_own, near_far, tiles, acc, near):
     n_chip = near_own.shape[0]
-    slots = tiles.shape[0]
+    slots = tiles.shape[0] - 1
     for d in range(n_chip):
         near[d] = near_own[d]
         near[n_chip + d] = near_far[d]
@@ -128,64 +175,25 @@
         acc[j] += jnp.where(held, dot16(near[i], tiles[slot], NN), 0.0)
 
     held_slots(index[0], slots, work)
-    own[...] = dot16(near_own[0], diag[...], NT)
-
-
-def gram_kernel(acc, own, residual, *rest):
-    n_row, size = acc.shape[0], own.shape[0]
-    far, grams, give = rest[:n_row], rest[n_row], rest[n_row + 1 :]
-    half = dot_exact16(far[0][...], acc[0] + 0.5 * own[...], NT)
-    for d in range(1, n_row):
-        half += dot_exact16(far[d][...], acc[d], NT)
-    total = jnp.concatenate([half + half.T, dot32(residual[...], residual[...], NT)], 1)
-    grams[...] = total
-    for d in range(1, n_row):
-        give[d - 1][...] = pack(acc[d].astype(BF16), total)
-
-
-def forward_kernel(index, tiles, after, *rest, n_row):
-    far_in = rest[:n_row]
-    give_core, keep, far, acc = rest[n_row:]
-    n_chip = keep.shape[0]
-    slots = tiles.shape[0]
-    for d in range(n_row):
-        far[d] = far_in[d][...]
-    acc[...] = jnp.zeros_like(acc)
-
-    def work(slot, held):
-        i = index[1 + slot]
-        j = index[1 + slots + slot]
-        acc[i] += jnp.where(held, dot16(far[j], tiles[slot], NT), 0.0)
-
-    held_slots(index[0], slots, work)
-    for d in range(n_chip):
-        give_core[d] = acc[n_chip + d].astype(BF16)
-        keep[d] = acc[d]
-
-
-def rows_kernel(grams, *rest):
-    *came, out = rest
-    total = grams[...]
-    for message in came:
-        total += unpack(message[...], message.shape[1] - 3 * grams.shape[0])
-    out[...] = total
-
-
-def join_kernel(keep, came, grams, grams_came, acc, own, *rest, n_in):
-    mine, grams_out, *give = rest[n_in:]
-    width = own.shape[1]
-    total = keep[0] + came[0].astype(F32) + own[...] + acc[0]
-    for message in rest[:n_in]:
-        total += message[:, :width].astype(F32)
-    mine[...] = total
+
+
+def join_kernel(keep, grams, grams_came, grams_out, *give):
     total = grams[...] + grams_came[...]
     grams_out[...] = total
     for d in range(1, keep.shape[0]):
-        give[d - 1][...] = pack((keep[d] + came[d].astype(F32)).astype(BF16), total)
+        give[d - 1][...] = pack(keep[d].astype(BF16), total)
+
+
+def rows_kernel(keep, grams, own, acc, *rest, n_in):
+    image, total, (mine_out, grams_out, *give) = gather_sums(keep[0], grams[...], rest, n_in)
+    mine_out[...] = image + own[...] + acc[0]
+    grams_out[...] = total
+    for d in range(1, acc.shape[0]):
+        give[d - 1][...] = pack(acc[d].astype(BF16), total)
 
 
 def gather_sums(mine, grams, rest, n_in):
-    image, total = mine[...], grams[...]
+    image, total = mine, grams
     width = image.shape[1]
     for message in rest[:n_in]:
         image += message[:, :width].astype(F32)
@@ -195,7 +203,7 @@
 
 def first_kernel(mine, grams, probes, *rest, n_in):
     image, total, (image_out, residual_out, rounded, totals, alpha_out) = gather_sums(
-        mine, grams, rest, n_in
+        mine[...], grams[...], rest, n_in
     )
     (alpha,) = eliminate([total])
     residual = probes[...] - dot32(alpha, image, TN)
@@ -219,7 +227,7 @@
 
 
 def last_kernel(mine, grams, probes, image_in, residual_in, inverse, middle, solved, *rest, n_in):
-    forward, total, (solution_out, residual_out) = gather_sums(mine, grams, rest, n_in)
+    forward, total, (solution_out, residual_out) = gather_sums(mine[...], grams[...], rest, n_in)
     size = forward.shape[0]
     norm = total[:, size:]
     curv = total[:, :size] - dot32(norm, dot32(middle[...], norm, NN), TN)
@@ -270,63 +278,71 @@
     diag = diag_tiles[0]
     square = shape((p_size, 2 * p_size), F32)
     slots = tiles.shape[2]
-    (held,) = call(
-        load_kernel,
-        [shape(tiles.shape[2:], BF16)],
-        [index, tiles[0, 0]],
-        [SMEM, ANY],
-        [pltpu.SemaphoreType.DMA((slots,))],
-        name="load",
-    )
     passes = 2 * slots * p_size * width * width
 
     message = shape((p_size, width + 3 * p_size), BF16)
 
-    def apply_operator(rounded, residual, held):
-        *gathered, held = lax.optimization_barrier((*over_chips(rounded), *over_rows(rounded), held))
-        far = [rounded, *gathered[n_chip - 1 :]]
-        near_own = jnp.stack([rounded, *gathered[: n_chip - 1]])
+    def apply_operator(rounded, residual, held=None):
+        from_rows = over_rows(rounded)
+        near = over_chips(rounded)
+        outs = [shape((n_chip, p_size, width), BF16), shape((n_col, p_size, width), F32), block32]
+        scratch = [pltpu.VMEM((n_row, p_size, width), BF16)]
+        if held is None:
+            give_core, acc_row, own, held = call(
+                functools.partial(forward_load_kernel, n_row=n_row),
+                outs + [shape((slots + 1, width, width), BF16)],
+                [index, diag, tiles[0, 0], rounded, *from_rows],
+                [SMEM, ANY, ANY] + [VMEM] * n_row,
+                scratch + [pltpu.SemaphoreType.DMA((slots + 1,))],
+                name="forward_load",
+                work=1,
+            )
+        else:
+            give_core, acc_row, own = call(
+                functools.partial(forward_kernel, n_row=n_row),
+                outs,
+                [index, held, rounded, *from_rows],
+                [SMEM] + [VMEM] * (1 + n_row),
+                scratch,
+                name="forward",
+                work=1,
+            )
+        give_core, *near = lax.optimization_barrier((give_core, *near))
+        came = over(give_core, "col", 1)
+        near_own = jnp.stack([rounded, *near])
         near_far = over(near_own, "col", 1)
-        acc, own = call(
+        keep, grams = call(
+            gram_kernel,
+            [shape((n_chip, p_size, width), F32), square],
+            [acc_row, came, own, residual, rounded, *near],
+            name="gram",
+        )
+        grams_came = over(grams, "col", 1)
+        grams, *give = call(
+            join_kernel, [square] + [message] * (n_chip - 1), [keep, grams, grams_came], name="join"
+        )
+        parts = [over(block, "col", 2 * d + 2) for d, block in enumerate(give)]
+        (acc_col,) = call(
             mirrored_kernel,
-            [shape((n_row, p_size, width), F32), block32],
-            [index, near_own, near_far, held, diag],
-            [SMEM] + [VMEM] * 4,
+            [shape((n_row, p_size, width), F32)],
+            [index, near_own, near_far, held],
+            [SMEM] + [VMEM] * 3,
             [pltpu.VMEM((n_col, p_size, width), BF16)],
             name="mirrored",
             work=passes,
         )
-        grams, *give_row = call(
-            gram_kernel, [square] + [message] * (n_row - 1), [acc, own, residual, *far], name="gram"
+        mine, grams, *give = call(
+            functools.partial(rows_kernel, n_in=n_chip - 1),
+            [block32, square] + [message] * (n_row - 1),
+            [keep, grams, own, acc_col, *parts],
+            name="rows",
         )
-        from_rows = [over(block, "row", d + 1) for d, block in enumerate(give_row)]
-        outs = [shape((n_chip, p_size, width), BF16), shape((n_chip, p_size, width), F32)]
-        scratch = [pltpu.VMEM((n_row, p_size, width), BF16), pltpu.VMEM((n_col, p_size, width), F32)]
-        give_core, keep = call(
-            functools.partial(forward_kernel, n_row=n_row),
-            outs,
-            [index, held, grams, *far],
-            [SMEM, VMEM, ANY] + [VMEM] * n_row,
-            scratch,
-            name="forward",
-            work=passes,
-        )
-        give_core, *from_rows = lax.optimization_barrier((give_core, *from_rows))
-        came = over(give_core, "col", 1)
-        (grams,) = call(rows_kernel, [square], [grams, *from_rows], name="gram_rows")
-        grams_came = over(grams, "col", 1)
-        mine, grams, *give_chip = call(
-            functools.partial(join_kernel, n_in=n_row - 1),
-            [block32, square] + [message] * (n_chip - 1),
-            [keep, came, grams, grams_came, acc, own, *from_rows],
-            name="join",
-        )
-        return mine, grams, [over(block, "col", 2 * d + 2) for d, block in enumerate(give_chip)]
+        return mine, grams, [over(block, "row", d + 1) for d, block in enumerate(give)], held
 
     small = shape((p_size, p_size), F32)
-    mine, grams, parts = apply_operator(probes.astype(BF16), probes, held)
+    mine, grams, parts, held = apply_operator(probes.astype(BF16), probes)
     image, residual, rounded, totals, alpha = call(
-        functools.partial(first_kernel, n_in=n_chip - 1),
+        functools.partial(first_kernel, n_in=n_row - 1),
         [block32, block32, block16, square, small],
         [mine, grams, probes, *parts],
         name="first_step",
@@ -334,9 +350,9 @@
     inverse, middle, solved = call(
         between_kernel, [small, small, block32], [totals, alpha, probes], name="between"
     )
-    mine, grams, parts = apply_operator(rounded, residual, held)
+    mine, grams, parts, held = apply_operator(rounded, residual, held)
     solved, residual = call(
-        functools.partial(last_kernel, n_in=n_chip - 1),
+        functools.partial(last_kernel, n_in=n_row - 1),
         [block32, block32],
         [mine, grams, probes, image, residual, inverse, middle, solved, *parts],
         name="last_step",

time: 95 us -> 106 us (1.12)
  waiting for transfers between devices: 33 us -> 21.8 us
  local copies, waits for them, and re-layouts: 0.01 us -> 10 us
  starting transfers between devices: 36 us -> 44 us
  Pallas kernels: 21.7 us -> 25.4 us
    ppermute x30, waiting for transfers between devices: 33 us -> 21.8 us  [over(): return lax.ppermute(value, axis, [(i, i ^ delta) for i in range(size)])]
    unnamed x4 -> x10, local copies, waits for them, and re-layouts: 0.01 us -> 10 us
    ppermute x30, starting transfers between devices: 36 us -> 44 us  [over(): return lax.ppermute(value, axis, [(i, i ^ delta) for i in range(size)])]
    pallas_call x14 -> x13, Pallas kernels: 21.7 us -> 25.4 us  [call(): pl.pallas_call(kernel, out_shape=outs, in_specs=[VMEM] * len(args) if spe...]
  transfers between devices with their start and end apart: 30 -> 30, of which waited for: 14 -> 13; matrix products, arithmetic and copies ran while one was open for 1% -> 1% of each run, Pallas kernels for 10% -> 16%
where the time goes in v3:
time: 106 us; the launch traced here: 105 us
  starting transfers between devices  44 us (42%)
  Pallas kernels  25.4 us (24%)
  waiting for transfers between devices  21.8 us (21%)
  local copies, waits for them, and re-layouts  10 us (9%)
  other arithmetic  2.61 us (2%)
  between operations  1.5 us (1%)
    ppermute x30, starting transfers between devices, over(): return lax.ppermute(value, axis, [(i, i ^ delta) for i in range(size)])  44 us
    pallas_call x13, Pallas kernels, call(): pl.pallas_call(kernel, out_shape=outs, in_specs=[VMEM] * len(args) if spe...  25.4 us
    ppermute x30, waiting for transfers between devices, over(): return lax.ppermute(value, axis, [(i, i ^ delta) for i in range(size)])  21.8 us
    unnamed x10, local copies, waits for them, and re-layouts  10 us
  transfers between devices with their start and end apart: 30, of which 13 were waited for; matrix products, arithmetic and copies ran while one was open for 1% of the time, Pallas kernels for 16%

profile of v3, /device:TPU:0, one launch (start us, length us, event | category | flops | bytes accessed | tf_op | source)
XLA Modules:
  0.0 105.3 jit_solution(16066736389110101254)
XLA Ops:
  0.6 1.1 %fusion.2 = (bf16[1,64,576]{2,1,0:T(8,128)(2,1)S(1)}, bf16[64,576]{1,0:T(8,128)(2,1)S(1)}) fusion(f32[1,64,576]{2,1,0:T(8,128)} %param.8), kind=kLoop, calls=%fused_computation.13 | loop fusion | flops 73728 | bytes 294912 | tf_op jit(solution)/shard_map/convert_element_type | solution.py:343
  1.7 3.1 %collective-permute-start = (bf16[64,576]{1,0:T(8,128)(2,1)S(1)}, bf16[64,576]{1,0:T(8,128)(2,1)S(1)}, u32[]{:S(2)}, u32[]{:S(2)}) collective-permute-start(bf16[64,576]{1,0:T(8,128)(2,1)S(1)} %get-tuple-element.97.rest_0_), channel_id=1, source_target_pairs={{0,8},{8,0},{16,24},{24,16},{1,9},{9,1},{17,25},{25,17},{2,10},{10... | collective-permute-start | bytes 221192 | tf_op jit(solution)/shard_map/ppermute | solution.py:265
  4.8 2.6 %collective-permute-start.1 = (bf16[64,576]{1,0:T(8,128)(2,1)S(1)}, bf16[64,576]{1,0:T(8,128)(2,1)S(1)}, u32[]{:S(2)}, u32[]{:S(2)}) collective-permute-start(bf16[64,576]{1,0:T(8,128)(2,1)S(1)} %get-tuple-element.97.rest_0_), channel_id=1, source_target_pairs={{0,16},{8,24},{16,0},{24,8},{1,17},{9,25},{17,1},{25,9},{2,18},{10... | collective-permute-start | bytes 221192 | tf_op jit(solution)/shard_map/ppermute | solution.py:265
  7.4 1.7 %collective-permute-start.3 = (bf16[64,576]{1,0:T(8,128)(2,1)S(1)}, bf16[64,576]{1,0:T(8,128)(2,1)S(1)}, u32[]{:S(2)}, u32[]{:S(2)}) collective-permute-start(bf16[64,576]{1,0:T(8,128)(2,1)S(1)} %get-tuple-element.97.rest_0_), channel_id=1, source_target_pairs={{0,2},{1,3},{2,0},{3,1},{4,6},{5,7},{6,4},{7,5},{8,10},{9,11},{10,... | collective-permute-start | bytes 221192 | tf_op jit(solution)/shard_map/ppermute | solution.py:265
  9.1 1.5 %collective-permute-start.4 = (bf16[64,576]{1,0:T(8,128)(2,1)S(1)}, bf16[64,576]{1,0:T(8,128)(2,1)S(1)}, u32[]{:S(2)}, u32[]{:S(2)}) collective-permute-start(bf16[64,576]{1,0:T(8,128)(2,1)S(1)} %get-tuple-element.97.rest_0_), channel_id=1, source_target_pairs={{0,4},{1,5},{2,6},{3,7},{4,0},{5,1},{6,2},{7,3},{8,12},{9,13},{10,... | collective-permute-start | bytes 221192 | tf_op jit(solution)/shard_map/ppermute | solution.py:265
  10.6 0.7 xor_bitcast_fusion
  11.3 0.7 fusion.1
  12.6 0.0 collective-permute-done.rest_1_
  12.6 0.3 collective-permute-start.5
  12.9 0.1 pad_add_fusion.index
  13.0 1.0 collective-permute-done.1.rest_2_
  14.0 0.0 collective-permute-done.2.rest_3_
  14.0 4.4 %copy-done.2 = bf16[1,1,16,576,576]{4,3,2,1,0:T(8,128)(2,1)S(1)} copy-done((bf16[1,1,16,576,576]{4,3,2,1,0:T(8,128)(2,1)S(1)}, bf16[1,1,16,576,576]{4,3,2,1,0:T(8,128)(2,1)}, u32[]{:S(2)}) %copy-start.2) | copy-done | bytes 10616856
  18.4 1.1 %copy-done.4 = bf16[1,576,576]{2,1,0:T(8,128)(2,1)S(1)} copy-done((bf16[1,576,576]{2,1,0:T(8,128)(2,1)S(1)}, bf16[1,576,576]{2,1,0:T(8,128)(2,1)}, u32[]{:S(2)}) %copy-start.4) | copy-done | bytes 663576
  19.5 7.9 %forward_load.1 = (bf16[4,64,576]{2,1,0:T(8,128)(2,1)S(1)}, f32[8,64,576]{2,1,0:T(8,128)S(1)}, f32[64,576]{1,0:T(8,128)S(1)}, bf16[17,576,576]{2,1,0:T(8,128)(2,1)}) custom-call(s32[33]{0:T(128)S(1)} %pad_add_fusion.index, bf16[576,576]{1,0:T(8,128)(2,1)S(1)} %bitcast.36, bf16[16,576,576]{2,1,0:T(8,128)(2,1)S(1)} %bitcast.30, ...), custom_call_target="tpu_custom_call" | custom-call | flops 1 | tf_op jit(solution)/shard_map/forward_load/pallas_call | solution.py:244
  27.4 0.0 collective-permute-done.3.rest_1_
  27.5 0.1 collective-permute-start.6
  27.5 0.1 pad_maximum_fusion.near_own
  27.6 0.6 collective-permute-start.8
  28.2 1.0 collective-permute-done.6.came
  29.2 0.8 gram.2
  30.0 0.2 collective-permute-start.7
  30.2 1.1 %collective-permute-done.7.grams_came = f32[64,128]{1,0:T(8,128)S(1)} collective-permute-done((f32[64,128]{1,0:T(8,128)S(1)}, f32[64,128]{1,0:T(8,128)S(1)}, u32[]{:S(2)}, u32[]{:S(2)}) %collective-permute-start.7) | collective-permute-done | bytes 32800 | tf_op jit(solution)/shard_map/ppermute | solution.py:265
  31.3 0.2 join.2
  31.5 1.2 %collective-permute-start.9 = (bf16[64,768]{1,0:T(8,128)(2,1)S(1)}, bf16[64,768]{1,0:T(8,128)(2,1)S(1)}, u32[]{:S(2)}, u32[]{:S(2)}) collective-permute-start(bf16[64,768]{1,0:T(8,128)(2,1)S(1)} %get-tuple-element.60), channel_id=1, source_target_pairs={{0,2},{1,3},{2,0},{3,1},{4,6},{5,7},{6,4},{7,5},{8,10},{9,11},{10,... | collective-permute-start | bytes 294920 | tf_op jit(solution)/shard_map/ppermute | solution.py:265
  32.7 1.8 %collective-permute-start.10 = (bf16[64,768]{1,0:T(8,128)(2,1)S(1)}, bf16[64,768]{1,0:T(8,128)(2,1)S(1)}, u32[]{:S(2)}, u32[]{:S(2)}) collective-permute-start(bf16[64,768]{1,0:T(8,128)(2,1)S(1)} %get-tuple-element.61), channel_id=1, source_target_pairs={{0,4},{1,5},{2,6},{3,7},{4,0},{5,1},{6,2},{7,3},{8,12},{9,13},{10,... | collective-permute-start | bytes 294920 | tf_op jit(solution)/shard_map/ppermute | solution.py:265
  34.6 0.5 collective-permute-start.11
  35.1 4.6 %copy-done = bf16[17,576,576]{2,1,0:T(8,128)(2,1)S(1)} copy-done((bf16[17,576,576]{2,1,0:T(8,128)(2,1)S(1)}, bf16[17,576,576]{2,1,0:T(8,128)(2,1)}, u32[]{:S(2)}) %copy-start) | copy-done | bytes 11280408
  39.6 1.3 %mirrored.2.acc = f32[4,64,576]{2,1,0:T(8,128)S(1)} custom-call(s32[33]{0:T(128)S(1)} %pad_add_fusion.index, bf16[4,64,576]{2,1,0:T(8,128)(2,1)S(1)} %pad_maximum_fusion.near_own, bf16[4,64,576]{2,1,0:T(8,128)(2,1)S(1)} %collective-permute-done.8.near_far, bf16[17,576,576]{2,1,0:T(8,128)(2,1)S(1)} %copy-done), custom_call_target="tpu_custom_call" | custom-call | flops 679477248 | tf_op jit(solution)/shard_map/mirrored/pallas_call | solution.py:244
  40.9 0.6 rows.2
  41.5 4.4 %collective-permute-start.12 = (bf16[64,768]{1,0:T(8,128)(2,1)S(1)}, bf16[64,768]{1,0:T(8,128)(2,1)S(1)}, u32[]{:S(2)}, u32[]{:S(2)}) collective-permute-start(bf16[64,768]{1,0:T(8,128)(2,1)S(1)} %get-tuple-element.65), channel_id=1, source_target_pairs={{0,8},{8,0},{16,24},{24,16},{1,9},{9,1},{17,25},{25,17},{2,10},{10... | collective-permute-start | bytes 294920 | tf_op jit(solution)/shard_map/ppermute | solution.py:265
  46.0 7.8 %collective-permute-start.13 = (bf16[64,768]{1,0:T(8,128)(2,1)S(1)}, bf16[64,768]{1,0:T(8,128)(2,1)S(1)}, u32[]{:S(2)}, u32[]{:S(2)}) collective-permute-start(bf16[64,768]{1,0:T(8,128)(2,1)S(1)} %get-tuple-element.66), channel_id=1, source_target_pairs={{0,16},{8,24},{16,0},{24,8},{1,17},{9,25},{17,1},{25,9},{2,18},{10... | collective-permute-start | bytes 294920 | tf_op jit(solution)/shard_map/ppermute | solution.py:265
  53.8 7.3 %collective-permute-done.13.rest_1_ = bf16[64,768]{1,0:T(8,128)(2,1)S(1)} collective-permute-done((bf16[64,768]{1,0:T(8,128)(2,1)S(1)}, bf16[64,768]{1,0:T(8,128)(2,1)S(1)}, u32[]{:S(2)}, u32[]{:S(2)}) %collective-permute-start.13) | collective-permute-done | bytes 98336 | tf_op jit(solution)/shard_map/ppermute | solution.py:265
  61.1 2.9 %first_step.1 = (f32[64,576]{1,0:T(8,128)S(1)}, f32[64,576]{1,0:T(8,128)S(1)}, bf16[64,576]{1,0:T(8,128)(2,1)S(1)}, f32[64,128]{1,0:T(8,128)S(1)}, f32[64,64]{1,0:T(8,128)S(1)}) custom-call(f32[64,576]{1,0:T(8,128)S(1)} %get-tuple-element.63.mine, f32[64,128]{1,0:T(8,128)S(1)} %get-tuple-element.64.grams, f32[64,576]{1,0:T(8,128)S(1)} %bitcast.32, ...), custom_call_target="tpu_custom_call" | custom-call | tf_op jit(solution)/shard_map/first_step/pallas_call | solution.py:244
  64.0 1.7 %collective-permute-start.15 = (bf16[64,576]{1,0:T(8,128)(2,1)S(1)}, bf16[64,576]{1,0:T(8,128)(2,1)S(1)}, u32[]{:S(2)}, u32[]{:S(2)}) collective-permute-start(bf16[64,576]{1,0:T(8,128)(2,1)S(1)} %get-tuple-element.68.rest_0_), channel_id=1, source_target_pairs={{0,8},{8,0},{16,24},{24,16},{1,9},{9,1},{17,25},{25,17},{2,10},{10... | collective-permute-start | bytes 221192 | tf_op jit(solution)/shard_map/ppermute | solution.py:265
  65.6 1.4 %collective-permute-start.16 = (bf16[64,576]{1,0:T(8,128)(2,1)S(1)}, bf16[64,576]{1,0:T(8,128)(2,1)S(1)}, u32[]{:S(2)}, u32[]{:S(2)}) collective-permute-start(bf16[64,576]{1,0:T(8,128)(2,1)S(1)} %get-tuple-element.68.rest_0_), channel_id=1, source_target_pairs={{0,16},{8,24},{16,0},{24,8},{1,17},{9,25},{17,1},{25,9},{2,18},{10... | collective-permute-start | bytes 221192 | tf_op jit(solution)/shard_map/ppermute | solution.py:265
  67.1 1.4 %collective-permute-start.17 = (bf16[64,576]{1,0:T(8,128)(2,1)S(1)}, bf16[64,576]{1,0:T(8,128)(2,1)S(1)}, u32[]{:S(2)}, u32[]{:S(2)}) collective-permute-start(bf16[64,576]{1,0:T(8,128)(2,1)S(1)} %get-tuple-element.68.rest_0_), channel_id=1, source_target_pairs={{0,24},{8,16},{16,8},{24,0},{1,25},{9,17},{17,9},{25,1},{2,26},{10... | collective-permute-start | bytes 221192 | tf_op jit(solution)/shard_map/ppermute | solution.py:265
  68.4 1.5 %collective-permute-start.18 = (bf16[64,576]{1,0:T(8,128)(2,1)S(1)}, bf16[64,576]{1,0:T(8,128)(2,1)S(1)}, u32[]{:S(2)}, u32[]{:S(2)}) collective-permute-start(bf16[64,576]{1,0:T(8,128)(2,1)S(1)} %get-tuple-element.68.rest_0_), channel_id=1, source_target_pairs={{0,2},{1,3},{2,0},{3,1},{4,6},{5,7},{6,4},{7,5},{8,10},{9,11},{10,... | collective-permute-start | bytes 221192 | tf_op jit(solution)/shard_map/ppermute | solution.py:265
  69.9 1.5 %collective-permute-start.19 = (bf16[64,576]{1,0:T(8,128)(2,1)S(1)}, bf16[64,576]{1,0:T(8,128)(2,1)S(1)}, u32[]{:S(2)}, u32[]{:S(2)}) collective-permute-start(bf16[64,576]{1,0:T(8,128)(2,1)S(1)} %get-tuple-element.68.rest_0_), channel_id=1, source_target_pairs={{0,4},{1,5},{2,6},{3,7},{4,0},{5,1},{6,2},{7,3},{8,12},{9,13},{10,... | collective-permute-start | bytes 221192 | tf_op jit(solution)/shard_map/ppermute | solution.py:265
  71.4 0.5 collective-permute-start.20
  71.9 1.8 %collective-permute-done.16.rest_2_ = bf16[64,576]{1,0:T(8,128)(2,1)S(1)} collective-permute-done((bf16[64,576]{1,0:T(8,128)(2,1)S(1)}, bf16[64,576]{1,0:T(8,128)(2,1)S(1)}, u32[]{:S(2)}, u32[]{:S(2)}) %collective-permute-start.16) | collective-permute-done | bytes 73760 | tf_op jit(solution)/shard_map/ppermute | solution.py:265
  73.7 2.0 %forward.1 = (bf16[4,64,576]{2,1,0:T(8,128)(2,1)S(1)}, f32[8,64,576]{2,1,0:T(8,128)S(1)}, f32[64,576]{1,0:T(8,128)S(1)}) custom-call(s32[33]{0:T(128)S(1)} %pad_add_fusion.index, bf16[17,576,576]{2,1,0:T(8,128)(2,1)S(1)} %copy-done.1, bf16[64,576]{1,0:T(8,128)(2,1)S(1)} %get-tuple-element.68.rest_0_, bf16[64,576]{1,0:T(8,128)(2,1)S(1)} %collective-permute-done.15.rest_1_, ...), custom_call_target="tpu_custom_call" | custom-call | flops 1 | tf_op jit(solution)/shard_map/forward/pallas_call | solution.py:244
  75.8 1.0 collective-permute-done.20.rest_3_
  76.8 0.1 pad_maximum_fusion.1.near_own
  76.8 0.6 collective-permute-start.23
  77.4 1.0 collective-permute-done.21.came
  78.4 0.8 gram.3
  79.2 0.2 collective-permute-start.22
  79.4 1.1 %collective-permute-done.22.grams_came = f32[64,128]{1,0:T(8,128)S(1)} collective-permute-done((f32[64,128]{1,0:T(8,128)S(1)}, f32[64,128]{1,0:T(8,128)S(1)}, u32[]{:S(2)}, u32[]{:S(2)}) %collective-permute-start.22) | collective-permute-done | bytes 32800 | tf_op jit(solution)/shard_map/ppermute | solution.py:265
  80.5 0.2 join.3
  80.7 0.6 collective-permute-start.24
  81.4 1.5 %collective-permute-start.25 = (bf16[64,768]{1,0:T(8,128)(2,1)S(1)}, bf16[64,768]{1,0:T(8,128)(2,1)S(1)}, u32[]{:S(2)}, u32[]{:S(2)}) collective-permute-start(bf16[64,768]{1,0:T(8,128)(2,1)S(1)} %get-tuple-element.81), channel_id=1, source_target_pairs={{0,4},{1,5},{2,6},{3,7},{4,0},{5,1},{6,2},{7,3},{8,12},{9,13},{10,... | collective-permute-start | bytes 294920 | tf_op jit(solution)/shard_map/ppermute | solution.py:265
  82.9 1.4 %collective-permute-start.26 = (bf16[64,768]{1,0:T(8,128)(2,1)S(1)}, bf16[64,768]{1,0:T(8,128)(2,1)S(1)}, u32[]{:S(2)}, u32[]{:S(2)}) collective-permute-start(bf16[64,768]{1,0:T(8,128)(2,1)S(1)} %get-tuple-element.82), channel_id=1, source_target_pairs={{0,6},{1,7},{2,4},{3,5},{4,2},{5,3},{6,0},{7,1},{8,14},{9,15},{10,... | collective-permute-start | bytes 294920 | tf_op jit(solution)/shard_map/ppermute | solution.py:265
  84.3 1.5 %mirrored.3.acc = f32[4,64,576]{2,1,0:T(8,128)S(1)} custom-call(s32[33]{0:T(128)S(1)} %pad_add_fusion.index, bf16[4,64,576]{2,1,0:T(8,128)(2,1)S(1)} %pad_maximum_fusion.1.near_own, bf16[4,64,576]{2,1,0:T(8,128)(2,1)S(1)} %collective-permute-done.23.near_far, bf16[17,576,576]{2,1,0:T(8,128)(2,1)S(1)} %copy-done.1), custom_call_target="tpu_custom_call" | custom-call | flops 679477248 | tf_op jit(solution)/shard_map/mirrored/pallas_call | solution.py:244
  85.8 0.6 collective-permute-done.24.rest_0_
  86.3 0.8 collective-permute-done.25.rest_1_
  87.1 1.2 %collective-permute-done.26.rest_2_ = bf16[64,768]{1,0:T(8,128)(2,1)S(1)} collective-permute-done((bf16[64,768]{1,0:T(8,128)(2,1)S(1)}, bf16[64,768]{1,0:T(8,128)(2,1)S(1)}, u32[]{:S(2)}, u32[]{:S(2)}) %collective-permute-start.26) | collective-permute-done | bytes 98336 | tf_op jit(solution)/shard_map/ppermute | solution.py:265
  88.4 0.6 rows.3
  89.0 2.5 %collective-permute-start.27 = (bf16[64,768]{1,0:T(8,128)(2,1)S(1)}, bf16[64,768]{1,0:T(8,128)(2,1)S(1)}, u32[]{:S(2)}, u32[]{:S(2)}) collective-permute-start(bf16[64,768]{1,0:T(8,128)(2,1)S(1)} %get-tuple-element.91), channel_id=1, source_target_pairs={{0,8},{8,0},{16,24},{24,16},{1,9},{9,1},{17,25},{25,17},{2,10},{10... | collective-permute-start | bytes 294920 | tf_op jit(solution)/shard_map/ppermute | solution.py:265
  91.5 3.3 %collective-permute-start.28 = (bf16[64,768]{1,0:T(8,128)(2,1)S(1)}, bf16[64,768]{1,0:T(8,128)(2,1)S(1)}, u32[]{:S(2)}, u32[]{:S(2)}) collective-permute-start(bf16[64,768]{1,0:T(8,128)(2,1)S(1)} %get-tuple-element.92), channel_id=1, source_target_pairs={{0,16},{8,24},{16,0},{24,8},{1,17},{9,25},{17,1},{25,9},{2,18},{10... | collective-permute-start | bytes 294920 | tf_op jit(solution)/shard_map/ppermute | solution.py:265
  94.8 2.5 %between.1 = (f32[64,64]{1,0:T(8,128)S(1)}, f32[64,64]{1,0:T(8,128)S(1)}, f32[64,576]{1,0:T(8,128)S(1)}) custom-call(f32[64,128]{1,0:T(8,128)S(1)} %get-tuple-element.86.totals, f32[64,64]{1,0:T(8,128)S(1)} %get-tuple-element.87.alpha, f32[64,576]{1,0:T(8,128)S(1)} %bitcast.33), custom_call_target="tpu_custom_call" | custom-call | tf_op jit(solution)/shard_map/between/pallas_call | solution.py:244
  97.3 2.8 %collective-permute-done.28.rest_1_ = bf16[64,768]{1,0:T(8,128)(2,1)S(1)} collective-permute-done((bf16[64,768]{1,0:T(8,128)(2,1)S(1)}, bf16[64,768]{1,0:T(8,128)(2,1)S(1)}, u32[]{:S(2)}, u32[]{:S(2)}) %collective-permute-start.28) | collective-permute-done | bytes 98336 | tf_op jit(solution)/shard_map/ppermute | solution.py:265
  100.1 1.2 %collective-permute-done.29.rest_2_ = bf16[64,768]{1,0:T(8,128)(2,1)S(1)} collective-permute-done((bf16[64,768]{1,0:T(8,128)(2,1)S(1)}, bf16[64,768]{1,0:T(8,128)(2,1)S(1)}, u32[]{:S(2)}, u32[]{:S(2)}) %collective-permute-start.29) | collective-permute-done | bytes 98336 | tf_op jit(solution)/shard_map/ppermute | solution.py:265
  101.3 4.0 %last_step.1 = (f32[64,576]{1,0:T(8,128)}, f32[64,576]{1,0:T(8,128)}) custom-call(f32[64,576]{1,0:T(8,128)S(1)} %get-tuple-element.83.mine, f32[64,128]{1,0:T(8,128)S(1)} %get-tuple-element.84.grams, f32[64,576]{1,0:T(8,128)S(1)} %bitcast.34, f32[64,576]{1,0:T(8,128)S(1)} %get-tuple-element.85.image_in, ...), custom_call_target="tpu_custom_call" | custom-call | tf_op jit(solution)/shard_map/last_step/pallas_call | solution.py:244
  (25 shorter events, 0.1 us)
Async XLA Ops:
  0.6 28.5 %copy-start.3 = (f32[1,64,576]{2,1,0:T(8,128)S(1)}, f32[1,64,576]{2,1,0:T(8,128)}, u32[]{:S(2)}) copy-start(f32[1,64,576]{2,1,0:T(8,128)} %param.8) | copy-start | bytes 442372
  1.7 10.9 %collective-permute-start = (bf16[64,576]{1,0:T(8,128)(2,1)S(1)}, bf16[64,576]{1,0:T(8,128)(2,1)S(1)}, u32[]{:S(2)}, u32[]{:S(2)}) collective-permute-start(bf16[64,576]{1,0:T(8,128)(2,1)S(1)} %get-tuple-element.97.rest_0_), channel_id=1, source_target_pairs={{0,8},{8,0},{16,24},{24,16},{1,9},{9,1},{17,25},{25,17},{2,10},{10... | collective-permute-start | bytes 221192 | tf_op jit(solution)/shard_map/ppermute | solution.py:265
  4.8 9.2 %collective-permute-start.1 = (bf16[64,576]{1,0:T(8,128)(2,1)S(1)}, bf16[64,576]{1,0:T(8,128)(2,1)S(1)}, u32[]{:S(2)}, u32[]{:S(2)}) collective-permute-start(bf16[64,576]{1,0:T(8,128)(2,1)S(1)} %get-tuple-element.97.rest_0_), channel_id=1, source_target_pairs={{0,16},{8,24},{16,0},{24,8},{1,17},{9,25},{17,1},{25,9},{2,18},{10... | collective-permute-start | bytes 221192 | tf_op jit(solution)/shard_map/ppermute | solution.py:265
  7.4 6.6 %collective-permute-start.2 = (bf16[64,576]{1,0:T(8,128)(2,1)S(1)}, bf16[64,576]{1,0:T(8,128)(2,1)S(1)}, u32[]{:S(2)}, u32[]{:S(2)}) collective-permute-start(bf16[64,576]{1,0:T(8,128)(2,1)S(1)} %get-tuple-element.97.rest_0_), channel_id=1, source_target_pairs={{0,24},{8,16},{16,8},{24,0},{1,25},{9,17},{17,9},{25,1},{2,26},{10... | collective-permute-start | bytes 221192 | tf_op jit(solution)/shard_map/ppermute | solution.py:265
  7.4 20.0 %collective-permute-start.3 = (bf16[64,576]{1,0:T(8,128)(2,1)S(1)}, bf16[64,576]{1,0:T(8,128)(2,1)S(1)}, u32[]{:S(2)}, u32[]{:S(2)}) collective-permute-start(bf16[64,576]{1,0:T(8,128)(2,1)S(1)} %get-tuple-element.97.rest_0_), channel_id=1, source_target_pairs={{0,2},{1,3},{2,0},{3,1},{4,6},{5,7},{6,4},{7,5},{8,10},{9,11},{10,... | collective-permute-start | bytes 221192 | tf_op jit(solution)/shard_map/ppermute | solution.py:265
  9.1 18.3 %collective-permute-start.4 = (bf16[64,576]{1,0:T(8,128)(2,1)S(1)}, bf16[64,576]{1,0:T(8,128)(2,1)S(1)}, u32[]{:S(2)}, u32[]{:S(2)}) collective-permute-start(bf16[64,576]{1,0:T(8,128)(2,1)S(1)} %get-tuple-element.97.rest_0_), channel_id=1, source_target_pairs={{0,4},{1,5},{2,6},{3,7},{4,0},{5,1},{6,2},{7,3},{8,12},{9,13},{10,... | collective-permute-start | bytes 221192 | tf_op jit(solution)/shard_map/ppermute | solution.py:265
  12.6 14.8 %collective-permute-start.5 = (bf16[64,576]{1,0:T(8,128)(2,1)S(1)}, bf16[64,576]{1,0:T(8,128)(2,1)S(1)}, u32[]{:S(2)}, u32[]{:S(2)}) collective-permute-start(bf16[64,576]{1,0:T(8,128)(2,1)S(1)} %get-tuple-element.97.rest_0_), channel_id=1, source_target_pairs={{0,6},{1,7},{2,4},{3,5},{4,2},{5,3},{6,0},{7,1},{8,14},{9,15},{10,... | collective-permute-start | bytes 221192 | tf_op jit(solution)/shard_map/ppermute | solution.py:265
  14.0 4.4 %copy-start.2 = (bf16[1,1,16,576,576]{4,3,2,1,0:T(8,128)(2,1)S(1)}, bf16[1,1,16,576,576]{4,3,2,1,0:T(8,128)(2,1)}, u32[]{:S(2)}) copy-start(bf16[1,1,16,576,576]{4,3,2,1,0:T(8,128)(2,1)} %param.6) | copy-start | bytes 31850500
  18.4 1.1 %copy-start.4 = (bf16[1,576,576]{2,1,0:T(8,128)(2,1)S(1)}, bf16[1,576,576]{2,1,0:T(8,128)(2,1)}, u32[]{:S(2)}) copy-start(bf16[1,576,576]{2,1,0:T(8,128)(2,1)} %param.7) | copy-start | bytes 1990660
  27.5 1.7 %collective-permute-start.6 = (bf16[4,64,576]{2,1,0:T(8,128)(2,1)S(1)}, bf16[4,64,576]{2,1,0:T(8,128)(2,1)S(1)}, u32[]{:S(2)}, u32[]{:S(2)}) collective-permute-start(bf16[4,64,576]{2,1,0:T(8,128)(2,1)S(1)} %get-tuple-element.52), channel_id=1, source_target_pairs={{0,1},{1,0},{2,3},{3,2},{4,5},{5,4},{6,7},{7,6},{8,9},{9,8},{10,11... | collective-permute-start | bytes 884744 | tf_op jit(solution)/shard_map/ppermute | solution.py:265
  27.6 7.4 %collective-permute-start.8 = (bf16[4,64,576]{2,1,0:T(8,128)(2,1)S(1)}, bf16[4,64,576]{2,1,0:T(8,128)(2,1)S(1)}, u32[]{:S(2)}, u32[]{:S(2)}) collective-permute-start(bf16[4,64,576]{2,1,0:T(8,128)(2,1)S(1)} %pad_maximum_fusion.near_own), channel_id=1, source_target_pairs={{0,1},{1,0},{2,3},{3,2},{4,5},{5,4},{6,7},{7,6},{8,9},{9,8},{10,11... | collective-permute-start | bytes 884744 | tf_op jit(solution)/shard_map/ppermute | solution.py:265
  30.0 1.3 %collective-permute-start.7 = (f32[64,128]{1,0:T(8,128)S(1)}, f32[64,128]{1,0:T(8,128)S(1)}, u32[]{:S(2)}, u32[]{:S(2)}) collective-permute-start(f32[64,128]{1,0:T(8,128)S(1)} %get-tuple-element.58.grams), channel_id=1, source_target_pairs={{0,1},{1,0},{2,3},{3,2},{4,5},{5,4},{6,7},{7,6},{8,9},{9,8},{10,11... | collective-permute-start | bytes 98312 | tf_op jit(solution)/shard_map/ppermute | solution.py:265
  31.5 9.4 %collective-permute-start.9 = (bf16[64,768]{1,0:T(8,128)(2,1)S(1)}, bf16[64,768]{1,0:T(8,128)(2,1)S(1)}, u32[]{:S(2)}, u32[]{:S(2)}) collective-permute-start(bf16[64,768]{1,0:T(8,128)(2,1)S(1)} %get-tuple-element.60), channel_id=1, source_target_pairs={{0,2},{1,3},{2,0},{3,1},{4,6},{5,7},{6,4},{7,5},{8,10},{9,11},{10,... | collective-permute-start | bytes 294920 | tf_op jit(solution)/shard_map/ppermute | solution.py:265
  32.7 8.2 %collective-permute-start.10 = (bf16[64,768]{1,0:T(8,128)(2,1)S(1)}, bf16[64,768]{1,0:T(8,128)(2,1)S(1)}, u32[]{:S(2)}, u32[]{:S(2)}) collective-permute-start(bf16[64,768]{1,0:T(8,128)(2,1)S(1)} %get-tuple-element.61), channel_id=1, source_target_pairs={{0,4},{1,5},{2,6},{3,7},{4,0},{5,1},{6,2},{7,3},{8,12},{9,13},{10,... | collective-permute-start | bytes 294920 | tf_op jit(solution)/shard_map/ppermute | solution.py:265
  34.6 6.4 %collective-permute-start.11 = (bf16[64,768]{1,0:T(8,128)(2,1)S(1)}, bf16[64,768]{1,0:T(8,128)(2,1)S(1)}, u32[]{:S(2)}, u32[]{:S(2)}) collective-permute-start(bf16[64,768]{1,0:T(8,128)(2,1)S(1)} %get-tuple-element.62), channel_id=1, source_target_pairs={{0,6},{1,7},{2,4},{3,5},{4,2},{5,3},{6,0},{7,1},{8,14},{9,15},{10,... | collective-permute-start | bytes 294920 | tf_op jit(solution)/shard_map/ppermute | solution.py:265
  35.1 4.6 %copy-start = (bf16[17,576,576]{2,1,0:T(8,128)(2,1)S(1)}, bf16[17,576,576]{2,1,0:T(8,128)(2,1)}, u32[]{:S(2)}) copy-start(bf16[17,576,576]{2,1,0:T(8,128)(2,1)} %get-tuple-element.49.tiles) | copy-start | bytes 33841156
  39.6 34.1 %copy-start.1 = (bf16[17,576,576]{2,1,0:T(8,128)(2,1)S(1)}, bf16[17,576,576]{2,1,0:T(8,128)(2,1)}, u32[]{:S(2)}) copy-start(bf16[17,576,576]{2,1,0:T(8,128)(2,1)} %get-tuple-element.49.tiles) | copy-start | bytes 33841156
  41.5 12.3 %collective-permute-start.12 = (bf16[64,768]{1,0:T(8,128)(2,1)S(1)}, bf16[64,768]{1,0:T(8,128)(2,1)S(1)}, u32[]{:S(2)}, u32[]{:S(2)}) collective-permute-start(bf16[64,768]{1,0:T(8,128)(2,1)S(1)} %get-tuple-element.65), channel_id=1, source_target_pairs={{0,8},{8,0},{16,24},{24,16},{1,9},{9,1},{17,25},{25,17},{2,10},{10... | collective-permute-start | bytes 294920 | tf_op jit(solution)/shard_map/ppermute | solution.py:265
  46.0 15.1 %collective-permute-start.13 = (bf16[64,768]{1,0:T(8,128)(2,1)S(1)}, bf16[64,768]{1,0:T(8,128)(2,1)S(1)}, u32[]{:S(2)}, u32[]{:S(2)}) collective-permute-start(bf16[64,768]{1,0:T(8,128)(2,1)S(1)} %get-tuple-element.66), channel_id=1, source_target_pairs={{0,16},{8,24},{16,0},{24,8},{1,17},{9,25},{17,1},{25,9},{2,18},{10... | collective-permute-start | bytes 294920 | tf_op jit(solution)/shard_map/ppermute | solution.py:265
  53.8 7.3 %collective-permute-start.14 = (bf16[64,768]{1,0:T(8,128)(2,1)S(1)}, bf16[64,768]{1,0:T(8,128)(2,1)S(1)}, u32[]{:S(2)}, u32[]{:S(2)}) collective-permute-start(bf16[64,768]{1,0:T(8,128)(2,1)S(1)} %get-tuple-element.67), channel_id=1, source_target_pairs={{0,24},{8,16},{16,8},{24,0},{1,25},{9,17},{17,9},{25,1},{2,26},{10... | collective-permute-start | bytes 294920 | tf_op jit(solution)/shard_map/ppermute | solution.py:265
  64.0 7.5 %collective-permute-start.15 = (bf16[64,576]{1,0:T(8,128)(2,1)S(1)}, bf16[64,576]{1,0:T(8,128)(2,1)S(1)}, u32[]{:S(2)}, u32[]{:S(2)}) collective-permute-start(bf16[64,576]{1,0:T(8,128)(2,1)S(1)} %get-tuple-element.68.rest_0_), channel_id=1, source_target_pairs={{0,8},{8,0},{16,24},{24,16},{1,9},{9,1},{17,25},{25,17},{2,10},{10... | collective-permute-start | bytes 221192 | tf_op jit(solution)/shard_map/ppermute | solution.py:265
  65.6 8.1 %collective-permute-start.16 = (bf16[64,576]{1,0:T(8,128)(2,1)S(1)}, bf16[64,576]{1,0:T(8,128)(2,1)S(1)}, u32[]{:S(2)}, u32[]{:S(2)}) collective-permute-start(bf16[64,576]{1,0:T(8,128)(2,1)S(1)} %get-tuple-element.68.rest_0_), channel_id=1, source_target_pairs={{0,16},{8,24},{16,0},{24,8},{1,17},{9,25},{17,1},{25,9},{2,18},{10... | collective-permute-start | bytes 221192 | tf_op jit(solution)/shard_map/ppermute | solution.py:265
  67.1 6.7 %collective-permute-start.17 = (bf16[64,576]{1,0:T(8,128)(2,1)S(1)}, bf16[64,576]{1,0:T(8,128)(2,1)S(1)}, u32[]{:S(2)}, u32[]{:S(2)}) collective-permute-start(bf16[64,576]{1,0:T(8,128)(2,1)S(1)} %get-tuple-element.68.rest_0_), channel_id=1, source_target_pairs={{0,24},{8,16},{16,8},{24,0},{1,25},{9,17},{17,9},{25,1},{2,26},{10... | collective-permute-start | bytes 221192 | tf_op jit(solution)/shard_map/ppermute | solution.py:265
  68.4 7.3 %collective-permute-start.18 = (bf16[64,576]{1,0:T(8,128)(2,1)S(1)}, bf16[64,576]{1,0:T(8,128)(2,1)S(1)}, u32[]{:S(2)}, u32[]{:S(2)}) collective-permute-start(bf16[64,576]{1,0:T(8,128)(2,1)S(1)} %get-tuple-element.68.rest_0_), channel_id=1, source_target_pairs={{0,2},{1,3},{2,0},{3,1},{4,6},{5,7},{6,4},{7,5},{8,10},{9,11},{10,... | collective-permute-start | bytes 221192 | tf_op jit(solution)/shard_map/ppermute | solution.py:265
  69.9 5.8 %collective-permute-start.19 = (bf16[64,576]{1,0:T(8,128)(2,1)S(1)}, bf16[64,576]{1,0:T(8,128)(2,1)S(1)}, u32[]{:S(2)}, u32[]{:S(2)}) collective-permute-start(bf16[64,576]{1,0:T(8,128)(2,1)S(1)} %get-tuple-element.68.rest_0_), channel_id=1, source_target_pairs={{0,4},{1,5},{2,6},{3,7},{4,0},{5,1},{6,2},{7,3},{8,12},{9,13},{10,... | collective-permute-start | bytes 221192 | tf_op jit(solution)/shard_map/ppermute | solution.py:265
  71.4 5.3 %collective-permute-start.20 = (bf16[64,576]{1,0:T(8,128)(2,1)S(1)}, bf16[64,576]{1,0:T(8,128)(2,1)S(1)}, u32[]{:S(2)}, u32[]{:S(2)}) collective-permute-start(bf16[64,576]{1,0:T(8,128)(2,1)S(1)} %get-tuple-element.68.rest_0_), channel_id=1, source_target_pairs={{0,6},{1,7},{2,4},{3,5},{4,2},{5,3},{6,0},{7,1},{8,14},{9,15},{10,... | collective-permute-start | bytes 221192 | tf_op jit(solution)/shard_map/ppermute | solution.py:265
  76.8 1.6 %collective-permute-start.21 = (bf16[4,64,576]{2,1,0:T(8,128)(2,1)S(1)}, bf16[4,64,576]{2,1,0:T(8,128)(2,1)S(1)}, u32[]{:S(2)}, u32[]{:S(2)}) collective-permute-start(bf16[4,64,576]{2,1,0:T(8,128)(2,1)S(1)} %get-tuple-element.71), channel_id=1, source_target_pairs={{0,1},{1,0},{2,3},{3,2},{4,5},{5,4},{6,7},{7,6},{8,9},{9,8},{10,11... | collective-permute-start | bytes 884744 | tf_op jit(solution)/shard_map/ppermute | solution.py:265
  76.8 7.4 %collective-permute-start.23 = (bf16[4,64,576]{2,1,0:T(8,128)(2,1)S(1)}, bf16[4,64,576]{2,1,0:T(8,128)(2,1)S(1)}, u32[]{:S(2)}, u32[]{:S(2)}) collective-permute-start(bf16[4,64,576]{2,1,0:T(8,128)(2,1)S(1)} %pad_maximum_fusion.1.near_own), channel_id=1, source_target_pairs={{0,1},{1,0},{2,3},{3,2},{4,5},{5,4},{6,7},{7,6},{8,9},{9,8},{10,11... | collective-permute-start | bytes 884744 | tf_op jit(solution)/shard_map/ppermute | solution.py:265
  79.2 1.3 %collective-permute-start.22 = (f32[64,128]{1,0:T(8,128)S(1)}, f32[64,128]{1,0:T(8,128)S(1)}, u32[]{:S(2)}, u32[]{:S(2)}) collective-permute-start(f32[64,128]{1,0:T(8,128)S(1)} %get-tuple-element.78.grams), channel_id=1, source_target_pairs={{0,1},{1,0},{2,3},{3,2},{4,5},{5,4},{6,7},{7,6},{8,9},{9,8},{10,11... | collective-permute-start | bytes 98312 | tf_op jit(solution)/shard_map/ppermute | solution.py:265
  80.7 5.6 %collective-permute-start.24 = (bf16[64,768]{1,0:T(8,128)(2,1)S(1)}, bf16[64,768]{1,0:T(8,128)(2,1)S(1)}, u32[]{:S(2)}, u32[]{:S(2)}) collective-permute-start(bf16[64,768]{1,0:T(8,128)(2,1)S(1)} %get-tuple-element.80), channel_id=1, source_target_pairs={{0,2},{1,3},{2,0},{3,1},{4,6},{5,7},{6,4},{7,5},{8,10},{9,11},{10,... | collective-permute-start | bytes 294920 | tf_op jit(solution)/shard_map/ppermute | solution.py:265
  81.4 5.8 %collective-permute-start.25 = (bf16[64,768]{1,0:T(8,128)(2,1)S(1)}, bf16[64,768]{1,0:T(8,128)(2,1)S(1)}, u32[]{:S(2)}, u32[]{:S(2)}) collective-permute-start(bf16[64,768]{1,0:T(8,128)(2,1)S(1)} %get-tuple-element.81), channel_id=1, source_target_pairs={{0,4},{1,5},{2,6},{3,7},{4,0},{5,1},{6,2},{7,3},{8,12},{9,13},{10,... | collective-permute-start | bytes 294920 | tf_op jit(solution)/shard_map/ppermute | solution.py:265
  82.9 5.5 %collective-permute-start.26 = (bf16[64,768]{1,0:T(8,128)(2,1)S(1)}, bf16[64,768]{1,0:T(8,128)(2,1)S(1)}, u32[]{:S(2)}, u32[]{:S(2)}) collective-permute-start(bf16[64,768]{1,0:T(8,128)(2,1)S(1)} %get-tuple-element.82), channel_id=1, source_target_pairs={{0,6},{1,7},{2,4},{3,5},{4,2},{5,3},{6,0},{7,1},{8,14},{9,15},{10,... | collective-permute-start | bytes 294920 | tf_op jit(solution)/shard_map/ppermute | solution.py:265
  89.0 8.3 %collective-permute-start.27 = (bf16[64,768]{1,0:T(8,128)(2,1)S(1)}, bf16[64,768]{1,0:T(8,128)(2,1)S(1)}, u32[]{:S(2)}, u32[]{:S(2)}) collective-permute-start(bf16[64,768]{1,0:T(8,128)(2,1)S(1)} %get-tuple-element.91), channel_id=1, source_target_pairs={{0,8},{8,0},{16,24},{24,16},{1,9},{9,1},{17,25},{25,17},{2,10},{10... | collective-permute-start | bytes 294920 | tf_op jit(solution)/shard_map/ppermute | solution.py:265
  91.5 8.6 %collective-permute-start.28 = (bf16[64,768]{1,0:T(8,128)(2,1)S(1)}, bf16[64,768]{1,0:T(8,128)(2,1)S(1)}, u32[]{:S(2)}, u32[]{:S(2)}) collective-permute-start(bf16[64,768]{1,0:T(8,128)(2,1)S(1)} %get-tuple-element.92), channel_id=1, source_target_pairs={{0,16},{8,24},{16,0},{24,8},{1,17},{9,25},{17,1},{25,9},{2,18},{10... | collective-permute-start | bytes 294920 | tf_op jit(solution)/shard_map/ppermute | solution.py:265
  94.8 6.5 %collective-permute-start.29 = (bf16[64,768]{1,0:T(8,128)(2,1)S(1)}, bf16[64,768]{1,0:T(8,128)(2,1)S(1)}, u32[]{:S(2)}, u32[]{:S(2)}) collective-permute-start(bf16[64,768]{1,0:T(8,128)(2,1)S(1)} %get-tuple-element.93), channel_id=1, source_target_pairs={{0,24},{8,16},{16,8},{24,0},{1,25},{9,17},{17,9},{25,1},{2,26},{10... | collective-permute-start | bytes 294920 | tf_op jit(solution)/shard_map/ppermute | solution.py:265

commit v4 on v3

--- a/solution.py
+++ b/solution.py
@@ -7,14 +7,13 @@
 from jax.experimental.pallas import tpu as pltpu
 from jax.sharding import PartitionSpec as P
 
-ITERS = 2
+START = 10**10
 F32 = jnp.float32
 BF16 = jnp.bfloat16
 HI = lax.Precision.HIGHEST
 NT = (((1,), (1,)), ((), ()))
 NN = (((1,), (0,)), ((), ()))
 TN = (((0,), (0,)), ((), ()))
-ANY = pl.BlockSpec(memory_space=pl.ANY)
 VMEM = pl.BlockSpec(memory_space=pltpu.VMEM)
 SMEM = pl.BlockSpec(memory_space=pltpu.SMEM)
 
@@ -86,13 +85,10 @@
     return jnp.concatenate([first, jnp.where(rows == columns, diagonal, second)], 1)
 
 
-def held_slots(count, slots, work, ready=None):
+def held_slots(count, slots, work):
     group = 4 if slots % 4 == 0 else 1
 
     def turn(g, carry):
-        if ready is not None:
-            for u in range(group):
-                pl.when(g * group + u < count)(functools.partial(ready, g * group + u))
         for u in range(group):
             work(g * group + u, g * group + u < count)
         return carry
@@ -100,59 +96,45 @@
     lax.fori_loop(0, (count + group - 1) // group, turn, 0)
 
 
-def forward_products(index, tiles, far_in, give_core, acc, own, far, ready=None):
+def places(index, slots, n_row, n_chip):
+    row, column = lax.axis_index("row"), lax.axis_index("col")
+
+    def place(slot):
+        apart = index[1 + slot] ^ column
+        return (apart % 2) * n_chip + apart // 2, index[1 + slots + slot] ^ row
+
+    return place
+
+
+def round_kernel(value, out):
+    out[...] = value[...].astype(BF16)
+
+
+def forward_kernel(index, tiles, *rest, n_row):
+    far_in = rest[:n_row]
+    give_core, acc, far = rest[n_row:]
     n_chip = give_core.shape[0]
-    slots = tiles.shape[0] - 1
+    slots = tiles.shape[0]
+    place = places(index, slots, n_row, n_chip)
     for d, block in enumerate(far_in):
         far[d] = block[...]
     acc[...] = jnp.zeros_like(acc)
 
     def work(slot, held):
-        i = index[1 + slot]
-        j = index[1 + slots + slot]
+        i, j = place(slot)
         acc[i] += jnp.where(held, dot16(far[j], tiles[slot], NT), 0.0)
 
-    held_slots(index[0], slots, work, ready)
-    if ready is not None:
-        ready(slots)
-    own[...] = dot16(far[0], tiles[slots], NT)
+    held_slots(index[0], slots, work)
     for d in range(n_chip):
         give_core[d] = acc[n_chip + d].astype(BF16)
 
 
-def forward_kernel(index, tiles, *rest, n_row):
-    give_core, acc, own, far = rest[n_row:]
-    forward_products(index, tiles, rest[:n_row], give_core, acc, own, far)
-
-
-def forward_load_kernel(index, diag, stored, *rest, n_row):
-    give_core, acc, own, tiles, far, arrived = rest[n_row:]
-    slots = stored.shape[0]
-
-    def fetch(slot):
-        return pltpu.make_async_copy(stored.at[slot], tiles.at[slot], arrived.at[slot])
-
-    last = pltpu.make_async_copy(diag, tiles.at[slots], arrived.at[slots])
-
-    def ready(slot):
-        if isinstance(slot, int):
-            last.wait()
-        else:
-            fetch(slot).wait()
-
-    def begin(slot, carry):
-        fetch(slot).start()
-        return carry
-
-    lax.fori_loop(0, index[0], begin, 0)
-    last.start()
-    forward_products(index, tiles, rest[:n_row], give_core, acc, own, far, ready)
-
-
-def gram_kernel(acc, came, own, residual, *rest):
-    *near, keep, grams = rest
-    size = own.shape[0]
-    half = 0.5 * dot_exact16(near[0][...], own[...], NT)
+def gram_kernel(acc, came, diag, residual, *rest):
+    *near, keep, own_out, grams = rest
+    size = residual.shape[0]
+    own = dot16(near[0][...], diag[...], NT)
+    own_out[...] = own
+    half = 0.5 * dot_exact16(near[0][...], own, NT)
     for d, block in enumerate(near):
         both = acc[d] + came[d].astype(F32)
         keep[d] = both
@@ -163,15 +145,15 @@
 
 def mirrored_kernel(index, near_own, near_far, tiles, acc, near):
     n_chip = near_own.shape[0]
-    slots = tiles.shape[0] - 1
+    slots = tiles.shape[0]
+    place = places(index, slots, acc.shape[0], n_chip)
     for d in range(n_chip):
         near[d] = near_own[d]
         near[n_chip + d] = near_far[d]
     acc[...] = jnp.zeros_like(acc)
 
     def work(slot, held):
-        i = index[1 + slot]
-        j = index[1 + slots + slot]
+        i, j = place(slot)
         acc[j] += jnp.where(held, dot16(near[i], tiles[slot], NN), 0.0)
 
     held_slots(index[0], slots, work)
@@ -270,51 +252,36 @@
     def over_rows(value):
         return [over(value, "row", d) for d in range(1, n_row)]
 
-    apart = rows_list[0, 0] ^ lax.axis_index("col")
-    index = jnp.concatenate(
-        [counts[0], (apart % 2) * n_chip + apart // 2, cols_list[0, 0] ^ lax.axis_index("row")]
-    )
+    index = jnp.concatenate([counts[0], rows_list[0, 0], cols_list[0, 0]])
     probes = probes[0]
     diag = diag_tiles[0]
+    held = tiles[0, 0]
     square = shape((p_size, 2 * p_size), F32)
     slots = tiles.shape[2]
     passes = 2 * slots * p_size * width * width
 
     message = shape((p_size, width + 3 * p_size), BF16)
 
-    def apply_operator(rounded, residual, held=None):
+    def apply_operator(rounded, residual):
         from_rows = over_rows(rounded)
         near = over_chips(rounded)
-        outs = [shape((n_chip, p_size, width), BF16), shape((n_col, p_size, width), F32), block32]
-        scratch = [pltpu.VMEM((n_row, p_size, width), BF16)]
-        if held is None:
-            give_core, acc_row, own, held = call(
-                functools.partial(forward_load_kernel, n_row=n_row),
-                outs + [shape((slots + 1, width, width), BF16)],
-                [index, diag, tiles[0, 0], rounded, *from_rows],
-                [SMEM, ANY, ANY] + [VMEM] * n_row,
-                scratch + [pltpu.SemaphoreType.DMA((slots + 1,))],
-                name="forward_load",
-                work=1,
-            )
-        else:
-            give_core, acc_row, own = call(
-                functools.partial(forward_kernel, n_row=n_row),
-                outs,
-                [index, held, rounded, *from_rows],
-                [SMEM] + [VMEM] * (1 + n_row),
-                scratch,
-                name="forward",
-                work=1,
-            )
+        give_core, acc_row = call(
+            functools.partial(forward_kernel, n_row=n_row),
+            [shape((n_chip, p_size, width), BF16), shape((n_col, p_size, width), F32)],
+            [index, held, rounded, *from_rows],
+            [SMEM] + [VMEM] * (1 + n_row),
+            [pltpu.VMEM((n_row, p_size, width), BF16)],
+            name="forward",
+            work=1,
+        )
         give_core, *near = lax.optimization_barrier((give_core, *near))
         came = over(give_core, "col", 1)
         near_own = jnp.stack([rounded, *near])
         near_far = over(near_own, "col", 1)
-        keep, grams = call(
+        keep, own, grams = call(
             gram_kernel,
-            [shape((n_chip, p_size, width), F32), square],
-            [acc_row, came, own, residual, rounded, *near],
+            [shape((n_chip, p_size, width), F32), block32, square],
+            [acc_row, came, diag, residual, rounded, *near],
             name="gram",
         )
         grams_came = over(grams, "col", 1)
@@ -337,10 +304,11 @@
             [keep, grams, own, acc_col, *parts],
             name="rows",
         )
-        return mine, grams, [over(block, "row", d + 1) for d, block in enumerate(give)], held
+        return mine, grams, [over(block, "row", d + 1) for d, block in enumerate(give)]
 
     small = shape((p_size, p_size), F32)
-    mine, grams, parts, held = apply_operator(probes.astype(BF16), probes)
+    (rounded,) = call(round_kernel, [block16], [probes], name="round", work=START)
+    mine, grams, parts = apply_operator(rounded, probes)
     image, residual, rounded, totals, alpha = call(
         functools.partial(first_kernel, n_in=n_row - 1),
         [block32, block32, block16, square, small],
@@ -350,7 +318,7 @@
     inverse, middle, solved = call(
         between_kernel, [small, small, block32], [totals, alpha, probes], name="between"
     )
-    mine, grams, parts, held = apply_operator(rounded, residual, held)
+    mine, grams, parts = apply_operator(rounded, residual)
     solved, residual = call(
         functools.partial(last_kernel, n_in=n_row - 1),
         [block32, block32],

time: 106 us -> 86.8 us (0.82)
  local copies, waits for them, and re-layouts: 10 us -> 1.09 us
  starting transfers between devices: 44 us -> 37.9 us
  Pallas kernels: 25.4 us -> 19.8 us
  waiting for transfers between devices: 21.8 us -> 26.1 us
  other arithmetic: 2.61 us -> 0.21 us
    unnamed x10 -> x16, local copies, waits for them, and re-layouts: 10 us -> 1.09 us
    ppermute x30, starting transfers between devices: 44 us -> 37.9 us  [over(): return lax.ppermute(value, axis, [(i, i ^ delta) for i in range(size)])]
    pallas_call x13 -> x14, Pallas kernels: 25.4 us -> 19.8 us  [call(): pl.pallas_call(kernel, out_shape=outs, in_specs=[VMEM] * len(args) if spe...]
    ppermute x30, waiting for transfers between devices: 21.8 us -> 26.1 us  [over(): return lax.ppermute(value, axis, [(i, i ^ delta) for i in range(size)])]
    convert_element_type x1 -> x0, other arithmetic: 1.08 us -> none  [body(): mine, grams, parts, held = apply_operator(probes.astype(BF16), probes)]
  transfers between devices with their start and end apart: 30 -> 30, of which waited for: 13 -> 18; matrix products, arithmetic and copies ran while one was open for 1% -> 0% of each run, Pallas kernels for 16% -> 14%
where the time goes in v4:
time: 86.8 us; the launch traced here: 86.6 us
  starting transfers between devices  37.9 us (44%)
  waiting for transfers between devices  26.1 us (30%)
  Pallas kernels  19.8 us (23%)
  between operations  1.52 us (2%)
  local copies, waits for them, and re-layouts  1.09 us (1%)
    ppermute x30, starting transfers between devices, over(): return lax.ppermute(value, axis, [(i, i ^ delta) for i in range(size)])  37.9 us
    ppermute x30, waiting for transfers between devices, over(): return lax.ppermute(value, axis, [(i, i ^ delta) for i in range(size)])  26.1 us
    pallas_call x14, Pallas kernels, call(): pl.pallas_call(kernel, out_shape=outs, in_specs=[VMEM] * len(args) if spe...  19.8 us
  transfers between devices with their start and end apart: 30, of which 18 were waited for; matrix products, arithmetic and copies ran while one was open for 0% of the time, Pallas kernels for 14%

profile of v4, /device:TPU:0, one launch (start us, length us, event | category | flops | bytes accessed | tf_op | source)
XLA Modules:
  0.0 86.6 jit_solution(6886239092134091175)
XLA Ops:
  0.6 0.0 copy-start.1
  0.7 1.1 %copy-done.1 = f32[1,64,576]{2,1,0:T(8,128)S(1)} copy-done((f32[1,64,576]{2,1,0:T(8,128)S(1)}, f32[1,64,576]{2,1,0:T(8,128)}, u32[]{:S(2)}) %copy-start.1) | copy-done | bytes 147480
  1.7 3.1 %collective-permute-start = (bf16[64,576]{1,0:T(8,128)(2,1)S(1)}, bf16[64,576]{1,0:T(8,128)(2,1)S(1)}, u32[]{:S(2)}, u32[]{:S(2)}) collective-permute-start(bf16[64,576]{1,0:T(8,128)(2,1)S(1)} %round.1.rest_0_), channel_id=1, source_target_pairs={{0,8},{8,0},{16,24},{24,16},{1,9},{9,1},{17,25},{25,17},{2,10},{10... | collective-permute-start | bytes 221192 | tf_op jit(solution)/shard_map/ppermute | solution.py:247
  4.8 2.6 %collective-permute-start.1 = (bf16[64,576]{1,0:T(8,128)(2,1)S(1)}, bf16[64,576]{1,0:T(8,128)(2,1)S(1)}, u32[]{:S(2)}, u32[]{:S(2)}) collective-permute-start(bf16[64,576]{1,0:T(8,128)(2,1)S(1)} %round.1.rest_0_), channel_id=1, source_target_pairs={{0,16},{8,24},{16,0},{24,8},{1,17},{9,25},{17,1},{25,9},{2,18},{10... | collective-permute-start | bytes 221192 | tf_op jit(solution)/shard_map/ppermute | solution.py:247
  7.4 0.0 collective-permute-start.2
  7.4 1.7 %collective-permute-start.3 = (bf16[64,576]{1,0:T(8,128)(2,1)S(1)}, bf16[64,576]{1,0:T(8,128)(2,1)S(1)}, u32[]{:S(2)}, u32[]{:S(2)}) collective-permute-start(bf16[64,576]{1,0:T(8,128)(2,1)S(1)} %round.1.rest_0_), channel_id=1, source_target_pairs={{0,2},{1,3},{2,0},{3,1},{4,6},{5,7},{6,4},{7,5},{8,10},{9,11},{10,... | collective-permute-start | bytes 221192 | tf_op jit(solution)/shard_map/ppermute | solution.py:247
  9.1 1.5 %collective-permute-start.4 = (bf16[64,576]{1,0:T(8,128)(2,1)S(1)}, bf16[64,576]{1,0:T(8,128)(2,1)S(1)}, u32[]{:S(2)}, u32[]{:S(2)}) collective-permute-start(bf16[64,576]{1,0:T(8,128)(2,1)S(1)} %round.1.rest_0_), channel_id=1, source_target_pairs={{0,4},{1,5},{2,6},{3,7},{4,0},{5,1},{6,2},{7,3},{8,12},{9,13},{10,... | collective-permute-start | bytes 221192 | tf_op jit(solution)/shard_map/ppermute | solution.py:247
  11.3 0.3 collective-permute-start.5
  11.6 0.1 pad_add_fusion.index
  11.7 2.3 %collective-permute-done.1.rest_2_ = bf16[64,576]{1,0:T(8,128)(2,1)S(1)} collective-permute-done((bf16[64,576]{1,0:T(8,128)(2,1)S(1)}, bf16[64,576]{1,0:T(8,128)(2,1)S(1)}, u32[]{:S(2)}, u32[]{:S(2)}) %collective-permute-start.1) | collective-permute-done | bytes 73760 | tf_op jit(solution)/shard_map/ppermute | solution.py:247
  14.1 0.0 copy-start
  14.1 0.0 copy-start.2
  14.1 1.7 %forward.2 = (bf16[4,64,576]{2,1,0:T(8,128)(2,1)S(1)}, f32[8,64,576]{2,1,0:T(8,128)S(1)}) custom-call(s32[33]{0:T(128)S(1)} %pad_add_fusion.index, bf16[16,576,576]{2,1,0:T(8,128)(2,1)S(1)} %bitcast.19, bf16[64,576]{1,0:T(8,128)(2,1)S(1)} %round.1.rest_0_, bf16[64,576]{1,0:T(8,128)(2,1)S(1)} %collective-permute-done.rest_1_, ...), custom_call_target="tpu_custom_call" | custom-call | flops 1 | tf_op jit(solution)/shard_map/forward/pallas_call | solution.py:226
  15.8 0.9 %collective-permute-done.5.rest_3_ = bf16[64,576]{1,0:T(8,128)(2,1)S(1)} collective-permute-done((bf16[64,576]{1,0:T(8,128)(2,1)S(1)}, bf16[64,576]{1,0:T(8,128)(2,1)S(1)}, u32[]{:S(2)}, u32[]{:S(2)}) %collective-permute-start.5) | collective-permute-done | bytes 73760 | tf_op jit(solution)/shard_map/ppermute | solution.py:247
  16.7 0.1 pad_maximum_fusion.near_own
  16.8 0.6 collective-permute-start.8
  17.4 1.0 %collective-permute-done.6.came = bf16[4,64,576]{2,1,0:T(8,128)(2,1)S(1)} collective-permute-done((bf16[4,64,576]{2,1,0:T(8,128)(2,1)S(1)}, bf16[4,64,576]{2,1,0:T(8,128)(2,1)S(1)}, u32[]{:S(2)}, u32[]{:S(2)}) %collective-permute-start.6) | collective-permute-done | bytes 294944 | tf_op jit(solution)/shard_map/ppermute | solution.py:247
  18.4 1.3 %gram.2 = (f32[4,64,576]{2,1,0:T(8,128)S(1)}, f32[64,576]{1,0:T(8,128)S(1)}, f32[64,128]{1,0:T(8,128)S(1)}) custom-call(f32[8,64,576]{2,1,0:T(8,128)S(1)} %get-tuple-element.48.acc, bf16[4,64,576]{2,1,0:T(8,128)(2,1)S(1)} %collective-permute-done.6.came, bf16[576,576]{1,0:T(8,128)(2,1)S(1)} %bitcast.23, f32[64,576]{1,0:T(8,128)S(1)} %bitcast.26, ...), custom_call_target="tpu_custom_call" | custom-call | tf_op jit(solution)/shard_map/gram/pallas_call | solution.py:226
  19.7 0.2 collective-permute-start.7
  19.9 1.1 %collective-permute-done.7.grams_came = f32[64,128]{1,0:T(8,128)S(1)} collective-permute-done((f32[64,128]{1,0:T(8,128)S(1)}, f32[64,128]{1,0:T(8,128)S(1)}, u32[]{:S(2)}, u32[]{:S(2)}) %collective-permute-start.7) | collective-permute-done | bytes 32800 | tf_op jit(solution)/shard_map/ppermute | solution.py:247
  21.0 0.2 join.2
  21.2 0.7 collective-permute-start.9
  21.9 1.5 %collective-permute-start.10 = (bf16[64,768]{1,0:T(8,128)(2,1)S(1)}, bf16[64,768]{1,0:T(8,128)(2,1)S(1)}, u32[]{:S(2)}, u32[]{:S(2)}) collective-permute-start(bf16[64,768]{1,0:T(8,128)(2,1)S(1)} %get-tuple-element.59), channel_id=1, source_target_pairs={{0,4},{1,5},{2,6},{3,7},{4,0},{5,1},{6,2},{7,3},{8,12},{9,13},{10,... | collective-permute-start | bytes 294920 | tf_op jit(solution)/shard_map/ppermute | solution.py:247
  23.4 1.3 %collective-permute-start.11 = (bf16[64,768]{1,0:T(8,128)(2,1)S(1)}, bf16[64,768]{1,0:T(8,128)(2,1)S(1)}, u32[]{:S(2)}, u32[]{:S(2)}) collective-permute-start(bf16[64,768]{1,0:T(8,128)(2,1)S(1)} %get-tuple-element.60), channel_id=1, source_target_pairs={{0,6},{1,7},{2,4},{3,5},{4,2},{5,3},{6,0},{7,1},{8,14},{9,15},{10,... | collective-permute-start | bytes 294920 | tf_op jit(solution)/shard_map/ppermute | solution.py:247
  24.7 1.3 %mirrored.2.acc = f32[4,64,576]{2,1,0:T(8,128)S(1)} custom-call(s32[33]{0:T(128)S(1)} %pad_add_fusion.index, bf16[4,64,576]{2,1,0:T(8,128)(2,1)S(1)} %pad_maximum_fusion.near_own, bf16[4,64,576]{2,1,0:T(8,128)(2,1)S(1)} %collective-permute-done.8.near_far, bf16[16,576,576]{2,1,0:T(8,128)(2,1)S(1)} %bitcast.20), custom_call_target="tpu_custom_call" | custom-call | flops 679477248 | tf_op jit(solution)/shard_map/mirrored/pallas_call | solution.py:226
  26.0 0.7 collective-permute-done.9.rest_0_
  26.7 1.0 %collective-permute-done.10.rest_1_ = bf16[64,768]{1,0:T(8,128)(2,1)S(1)} collective-permute-done((bf16[64,768]{1,0:T(8,128)(2,1)S(1)}, bf16[64,768]{1,0:T(8,128)(2,1)S(1)}, u32[]{:S(2)}, u32[]{:S(2)}) %collective-permute-start.10) | collective-permute-done | bytes 98336 | tf_op jit(solution)/shard_map/ppermute | solution.py:247
  27.7 1.2 %collective-permute-done.11.rest_2_ = bf16[64,768]{1,0:T(8,128)(2,1)S(1)} collective-permute-done((bf16[64,768]{1,0:T(8,128)(2,1)S(1)}, bf16[64,768]{1,0:T(8,128)(2,1)S(1)}, u32[]{:S(2)}, u32[]{:S(2)}) %collective-permute-start.11) | collective-permute-done | bytes 98336 | tf_op jit(solution)/shard_map/ppermute | solution.py:247
  28.9 0.6 rows.2
  29.5 2.5 %collective-permute-start.12 = (bf16[64,768]{1,0:T(8,128)(2,1)S(1)}, bf16[64,768]{1,0:T(8,128)(2,1)S(1)}, u32[]{:S(2)}, u32[]{:S(2)}) collective-permute-start(bf16[64,768]{1,0:T(8,128)(2,1)S(1)} %get-tuple-element.63), channel_id=1, source_target_pairs={{0,8},{8,0},{16,24},{24,16},{1,9},{9,1},{17,25},{25,17},{2,10},{10... | collective-permute-start | bytes 294920 | tf_op jit(solution)/shard_map/ppermute | solution.py:247
  32.0 3.6 %collective-permute-start.13 = (bf16[64,768]{1,0:T(8,128)(2,1)S(1)}, bf16[64,768]{1,0:T(8,128)(2,1)S(1)}, u32[]{:S(2)}, u32[]{:S(2)}) collective-permute-start(bf16[64,768]{1,0:T(8,128)(2,1)S(1)} %get-tuple-element.64), channel_id=1, source_target_pairs={{0,16},{8,24},{16,0},{24,8},{1,17},{9,25},{17,1},{25,9},{2,18},{10... | collective-permute-start | bytes 294920 | tf_op jit(solution)/shard_map/ppermute | solution.py:247
  35.7 5.3 %collective-permute-done.13.rest_1_ = bf16[64,768]{1,0:T(8,128)(2,1)S(1)} collective-permute-done((bf16[64,768]{1,0:T(8,128)(2,1)S(1)}, bf16[64,768]{1,0:T(8,128)(2,1)S(1)}, u32[]{:S(2)}, u32[]{:S(2)}) %collective-permute-start.13) | collective-permute-done | bytes 98336 | tf_op jit(solution)/shard_map/ppermute | solution.py:247
  41.0 1.2 %collective-permute-done.14.rest_2_ = bf16[64,768]{1,0:T(8,128)(2,1)S(1)} collective-permute-done((bf16[64,768]{1,0:T(8,128)(2,1)S(1)}, bf16[64,768]{1,0:T(8,128)(2,1)S(1)}, u32[]{:S(2)}, u32[]{:S(2)}) %collective-permute-start.14) | collective-permute-done | bytes 98336 | tf_op jit(solution)/shard_map/ppermute | solution.py:247
  42.2 2.9 %first_step.1 = (f32[64,576]{1,0:T(8,128)S(1)}, f32[64,576]{1,0:T(8,128)S(1)}, bf16[64,576]{1,0:T(8,128)(2,1)S(1)}, f32[64,128]{1,0:T(8,128)S(1)}, f32[64,64]{1,0:T(8,128)S(1)}) custom-call(f32[64,576]{1,0:T(8,128)S(1)} %get-tuple-element.61.mine, f32[64,128]{1,0:T(8,128)S(1)} %get-tuple-element.62.grams, f32[64,576]{1,0:T(8,128)S(1)} %bitcast.27, ...), custom_call_target="tpu_custom_call" | custom-call | tf_op jit(solution)/shard_map/first_step/pallas_call | solution.py:226
  45.1 1.6 %collective-permute-start.15 = (bf16[64,576]{1,0:T(8,128)(2,1)S(1)}, bf16[64,576]{1,0:T(8,128)(2,1)S(1)}, u32[]{:S(2)}, u32[]{:S(2)}) collective-permute-start(bf16[64,576]{1,0:T(8,128)(2,1)S(1)} %get-tuple-element.66.rest_0_), channel_id=1, source_target_pairs={{0,8},{8,0},{16,24},{24,16},{1,9},{9,1},{17,25},{25,17},{2,10},{10... | collective-permute-start | bytes 221192 | tf_op jit(solution)/shard_map/ppermute | solution.py:247
  46.6 1.5 %collective-permute-start.16 = (bf16[64,576]{1,0:T(8,128)(2,1)S(1)}, bf16[64,576]{1,0:T(8,128)(2,1)S(1)}, u32[]{:S(2)}, u32[]{:S(2)}) collective-permute-start(bf16[64,576]{1,0:T(8,128)(2,1)S(1)} %get-tuple-element.66.rest_0_), channel_id=1, source_target_pairs={{0,16},{8,24},{16,0},{24,8},{1,17},{9,25},{17,1},{25,9},{2,18},{10... | collective-permute-start | bytes 221192 | tf_op jit(solution)/shard_map/ppermute | solution.py:247
  48.1 1.4 %collective-permute-start.17 = (bf16[64,576]{1,0:T(8,128)(2,1)S(1)}, bf16[64,576]{1,0:T(8,128)(2,1)S(1)}, u32[]{:S(2)}, u32[]{:S(2)}) collective-permute-start(bf16[64,576]{1,0:T(8,128)(2,1)S(1)} %get-tuple-element.66.rest_0_), channel_id=1, source_target_pairs={{0,24},{8,16},{16,8},{24,0},{1,25},{9,17},{17,9},{25,1},{2,26},{10... | collective-permute-start | bytes 221192 | tf_op jit(solution)/shard_map/ppermute | solution.py:247
  49.5 1.7 %collective-permute-start.18 = (bf16[64,576]{1,0:T(8,128)(2,1)S(1)}, bf16[64,576]{1,0:T(8,128)(2,1)S(1)}, u32[]{:S(2)}, u32[]{:S(2)}) collective-permute-start(bf16[64,576]{1,0:T(8,128)(2,1)S(1)} %get-tuple-element.66.rest_0_), channel_id=1, source_target_pairs={{0,2},{1,3},{2,0},{3,1},{4,6},{5,7},{6,4},{7,5},{8,10},{9,11},{10,... | collective-permute-start | bytes 221192 | tf_op jit(solution)/shard_map/ppermute | solution.py:247
  51.2 0.5 collective-permute-start.19
  51.8 1.3 %collective-permute-start.20 = (bf16[64,576]{1,0:T(8,128)(2,1)S(1)}, bf16[64,576]{1,0:T(8,128)(2,1)S(1)}, u32[]{:S(2)}, u32[]{:S(2)}) collective-permute-start(bf16[64,576]{1,0:T(8,128)(2,1)S(1)} %get-tuple-element.66.rest_0_), channel_id=1, source_target_pairs={{0,6},{1,7},{2,4},{3,5},{4,2},{5,3},{6,0},{7,1},{8,14},{9,15},{10,... | collective-permute-start | bytes 221192 | tf_op jit(solution)/shard_map/ppermute | solution.py:247
  53.0 0.4 collective-permute-done.16.rest_2_
  53.4 1.0 %collective-permute-done.17.rest_3_ = bf16[64,576]{1,0:T(8,128)(2,1)S(1)} collective-permute-done((bf16[64,576]{1,0:T(8,128)(2,1)S(1)}, bf16[64,576]{1,0:T(8,128)(2,1)S(1)}, u32[]{:S(2)}, u32[]{:S(2)}) %collective-permute-start.17) | collective-permute-done | bytes 73760 | tf_op jit(solution)/shard_map/ppermute | solution.py:247
  54.4 1.7 %forward.3 = (bf16[4,64,576]{2,1,0:T(8,128)(2,1)S(1)}, f32[8,64,576]{2,1,0:T(8,128)S(1)}) custom-call(s32[33]{0:T(128)S(1)} %pad_add_fusion.index, bf16[16,576,576]{2,1,0:T(8,128)(2,1)S(1)} %bitcast.21, bf16[64,576]{1,0:T(8,128)(2,1)S(1)} %get-tuple-element.66.rest_0_, bf16[64,576]{1,0:T(8,128)(2,1)S(1)} %collective-permute-done.15.rest_1_, ...), custom_call_target="tpu_custom_call" | custom-call | flops 1 | tf_op jit(solution)/shard_map/forward/pallas_call | solution.py:226
  56.2 0.9 %collective-permute-done.20.rest_3_ = bf16[64,576]{1,0:T(8,128)(2,1)S(1)} collective-permute-done((bf16[64,576]{1,0:T(8,128)(2,1)S(1)}, bf16[64,576]{1,0:T(8,128)(2,1)S(1)}, u32[]{:S(2)}, u32[]{:S(2)}) %collective-permute-start.20) | collective-permute-done | bytes 73760 | tf_op jit(solution)/shard_map/ppermute | solution.py:247
  57.1 0.1 pad_maximum_fusion.1.near_own
  57.2 0.6 collective-permute-start.23
  57.7 1.0 %collective-permute-done.21.came = bf16[4,64,576]{2,1,0:T(8,128)(2,1)S(1)} collective-permute-done((bf16[4,64,576]{2,1,0:T(8,128)(2,1)S(1)}, bf16[4,64,576]{2,1,0:T(8,128)(2,1)S(1)}, u32[]{:S(2)}, u32[]{:S(2)}) %collective-permute-start.21) | collective-permute-done | bytes 294944 | tf_op jit(solution)/shard_map/ppermute | solution.py:247
  58.7 1.3 %gram.3 = (f32[4,64,576]{2,1,0:T(8,128)S(1)}, f32[64,576]{1,0:T(8,128)S(1)}, f32[64,128]{1,0:T(8,128)S(1)}) custom-call(f32[8,64,576]{2,1,0:T(8,128)S(1)} %get-tuple-element.67.acc, bf16[4,64,576]{2,1,0:T(8,128)(2,1)S(1)} %collective-permute-done.21.came, bf16[576,576]{1,0:T(8,128)(2,1)S(1)} %bitcast.24, ...), custom_call_target="tpu_custom_call" | custom-call | tf_op jit(solution)/shard_map/gram/pallas_call | solution.py:226
  60.1 0.2 collective-permute-start.22
  60.3 1.1 %collective-permute-done.22.grams_came = f32[64,128]{1,0:T(8,128)S(1)} collective-permute-done((f32[64,128]{1,0:T(8,128)S(1)}, f32[64,128]{1,0:T(8,128)S(1)}, u32[]{:S(2)}, u32[]{:S(2)}) %collective-permute-start.22) | collective-permute-done | bytes 32800 | tf_op jit(solution)/shard_map/ppermute | solution.py:247
  61.3 0.2 join.3
  61.6 1.3 %collective-permute-start.24 = (bf16[64,768]{1,0:T(8,128)(2,1)S(1)}, bf16[64,768]{1,0:T(8,128)(2,1)S(1)}, u32[]{:S(2)}, u32[]{:S(2)}) collective-permute-start(bf16[64,768]{1,0:T(8,128)(2,1)S(1)} %get-tuple-element.78), channel_id=1, source_target_pairs={{0,2},{1,3},{2,0},{3,1},{4,6},{5,7},{6,4},{7,5},{8,10},{9,11},{10,... | collective-permute-start | bytes 294920 | tf_op jit(solution)/shard_map/ppermute | solution.py:247
  62.9 0.6 collective-permute-start.25
  63.5 1.6 %collective-permute-start.26 = (bf16[64,768]{1,0:T(8,128)(2,1)S(1)}, bf16[64,768]{1,0:T(8,128)(2,1)S(1)}, u32[]{:S(2)}, u32[]{:S(2)}) collective-permute-start(bf16[64,768]{1,0:T(8,128)(2,1)S(1)} %get-tuple-element.80), channel_id=1, source_target_pairs={{0,6},{1,7},{2,4},{3,5},{4,2},{5,3},{6,0},{7,1},{8,14},{9,15},{10,... | collective-permute-start | bytes 294920 | tf_op jit(solution)/shard_map/ppermute | solution.py:247
  65.1 1.5 %mirrored.3.acc = f32[4,64,576]{2,1,0:T(8,128)S(1)} custom-call(s32[33]{0:T(128)S(1)} %pad_add_fusion.index, bf16[4,64,576]{2,1,0:T(8,128)(2,1)S(1)} %pad_maximum_fusion.1.near_own, bf16[4,64,576]{2,1,0:T(8,128)(2,1)S(1)} %collective-permute-done.23.near_far, bf16[16,576,576]{2,1,0:T(8,128)(2,1)S(1)} %bitcast.22), custom_call_target="tpu_custom_call" | custom-call | flops 679477248 | tf_op jit(solution)/shard_map/mirrored/pallas_call | solution.py:226
  66.6 1.7 %collective-permute-done.25.rest_1_ = bf16[64,768]{1,0:T(8,128)(2,1)S(1)} collective-permute-done((bf16[64,768]{1,0:T(8,128)(2,1)S(1)}, bf16[64,768]{1,0:T(8,128)(2,1)S(1)}, u32[]{:S(2)}, u32[]{:S(2)}) %collective-permute-start.25) | collective-permute-done | bytes 98336 | tf_op jit(solution)/shard_map/ppermute | solution.py:247
  68.3 1.3 %collective-permute-done.26.rest_2_ = bf16[64,768]{1,0:T(8,128)(2,1)S(1)} collective-permute-done((bf16[64,768]{1,0:T(8,128)(2,1)S(1)}, bf16[64,768]{1,0:T(8,128)(2,1)S(1)}, u32[]{:S(2)}, u32[]{:S(2)}) %collective-permute-start.26) | collective-permute-done | bytes 98336 | tf_op jit(solution)/shard_map/ppermute | solution.py:247
  69.6 0.6 rows.3
  70.2 2.5 %collective-permute-start.27 = (bf16[64,768]{1,0:T(8,128)(2,1)S(1)}, bf16[64,768]{1,0:T(8,128)(2,1)S(1)}, u32[]{:S(2)}, u32[]{:S(2)}) collective-permute-start(bf16[64,768]{1,0:T(8,128)(2,1)S(1)} %get-tuple-element.89), channel_id=1, source_target_pairs={{0,8},{8,0},{16,24},{24,16},{1,9},{9,1},{17,25},{25,17},{2,10},{10... | collective-permute-start | bytes 294920 | tf_op jit(solution)/shard_map/ppermute | solution.py:247
  72.7 3.4 %collective-permute-start.28 = (bf16[64,768]{1,0:T(8,128)(2,1)S(1)}, bf16[64,768]{1,0:T(8,128)(2,1)S(1)}, u32[]{:S(2)}, u32[]{:S(2)}) collective-permute-start(bf16[64,768]{1,0:T(8,128)(2,1)S(1)} %get-tuple-element.90), channel_id=1, source_target_pairs={{0,16},{8,24},{16,0},{24,8},{1,17},{9,25},{17,1},{25,9},{2,18},{10... | collective-permute-start | bytes 294920 | tf_op jit(solution)/shard_map/ppermute | solution.py:247
  76.1 2.5 %between.1 = (f32[64,64]{1,0:T(8,128)S(1)}, f32[64,64]{1,0:T(8,128)S(1)}, f32[64,576]{1,0:T(8,128)S(1)}) custom-call(f32[64,128]{1,0:T(8,128)S(1)} %get-tuple-element.84.totals, f32[64,64]{1,0:T(8,128)S(1)} %get-tuple-element.85.alpha, f32[64,576]{1,0:T(8,128)S(1)} %bitcast.28), custom_call_target="tpu_custom_call" | custom-call | tf_op jit(solution)/shard_map/between/pallas_call | solution.py:226
  78.6 2.3 %collective-permute-done.28.rest_1_ = bf16[64,768]{1,0:T(8,128)(2,1)S(1)} collective-permute-done((bf16[64,768]{1,0:T(8,128)(2,1)S(1)}, bf16[64,768]{1,0:T(8,128)(2,1)S(1)}, u32[]{:S(2)}, u32[]{:S(2)}) %collective-permute-start.28) | collective-permute-done | bytes 98336 | tf_op jit(solution)/shard_map/ppermute | solution.py:247
  80.9 1.7 %collective-permute-done.29.rest_2_ = bf16[64,768]{1,0:T(8,128)(2,1)S(1)} collective-permute-done((bf16[64,768]{1,0:T(8,128)(2,1)S(1)}, bf16[64,768]{1,0:T(8,128)(2,1)S(1)}, u32[]{:S(2)}, u32[]{:S(2)}) %collective-permute-start.29) | collective-permute-done | bytes 98336 | tf_op jit(solution)/shard_map/ppermute | solution.py:247
  82.6 4.0 %last_step.1 = (f32[64,576]{1,0:T(8,128)}, f32[64,576]{1,0:T(8,128)}) custom-call(f32[64,576]{1,0:T(8,128)S(1)} %get-tuple-element.81.mine, f32[64,128]{1,0:T(8,128)S(1)} %get-tuple-element.82.grams, f32[64,576]{1,0:T(8,128)S(1)} %bitcast.29, f32[64,576]{1,0:T(8,128)S(1)} %get-tuple-element.83.image_in, ...), custom_call_target="tpu_custom_call" | custom-call | tf_op jit(solution)/shard_map/last_step/pallas_call | solution.py:226
  (30 shorter events, 0.1 us)
Async XLA Ops:
  0.6 13.4 %slice-start = ((s8[11796480]{0:T(1024)(128)(4,1)}), s8[4194304]{0:T(1024)(128)(4,1)S(1)}, s32[]{:S(2)}) async-start(s8[11796480]{0:T(1024)(128)(4,1)} %bitcast.17), calls=%async_computation | async-start | bytes 8388608
  0.6 1.1 %copy-start.1 = (f32[1,64,576]{2,1,0:T(8,128)S(1)}, f32[1,64,576]{2,1,0:T(8,128)}, u32[]{:S(2)}) copy-start(f32[1,64,576]{2,1,0:T(8,128)} %param.8) | copy-start | bytes 442372
  1.7 9.9 %copy-start.3 = (s32[1,1,16]{2,1,0:T(1,128)S(1)}, s32[1,1,16]{2,1,0:T(1,128)}, u32[]{:S(2)}) copy-start(s32[1,1,16]{2,1,0:T(1,128)} %param.10) | copy-start | bytes 196
  1.7 9.9 %copy-start.4 = (s32[1,1,16]{2,1,0:T(1,128)S(1)}, s32[1,1,16]{2,1,0:T(1,128)}, u32[]{:S(2)}) copy-start(s32[1,1,16]{2,1,0:T(1,128)} %param.9) | copy-start | bytes 196
  1.7 12.3 %slice-start.1 = ((s8[11796480]{0:T(1024)(128)(4,1)}), s8[4194304]{0:T(1024)(128)(4,1)S(1)}, s32[]{:S(2)}) async-start(s8[11796480]{0:T(1024)(128)(4,1)} %bitcast.17), calls=%async_computation.1 | async-start | bytes 8388608
  1.7 12.3 %slice-start.2 = ((s8[11796480]{0:T(1024)(128)(4,1)}), s8[3407872]{0:T(1024)(128)(4,1)S(1)}, s32[]{:S(2)}) async-start(s8[11796480]{0:T(1024)(128)(4,1)} %bitcast.17), calls=%async_computation.2 | async-start | bytes 6815744
  1.7 9.6 %collective-permute-start = (bf16[64,576]{1,0:T(8,128)(2,1)S(1)}, bf16[64,576]{1,0:T(8,128)(2,1)S(1)}, u32[]{:S(2)}, u32[]{:S(2)}) collective-permute-start(bf16[64,576]{1,0:T(8,128)(2,1)S(1)} %round.1.rest_0_), channel_id=1, source_target_pairs={{0,8},{8,0},{16,24},{24,16},{1,9},{9,1},{17,25},{25,17},{2,10},{10... | collective-permute-start | bytes 221192 | tf_op jit(solution)/shard_map/ppermute | solution.py:247
  4.8 9.2 %collective-permute-start.1 = (bf16[64,576]{1,0:T(8,128)(2,1)S(1)}, bf16[64,576]{1,0:T(8,128)(2,1)S(1)}, u32[]{:S(2)}, u32[]{:S(2)}) collective-permute-start(bf16[64,576]{1,0:T(8,128)(2,1)S(1)} %round.1.rest_0_), channel_id=1, source_target_pairs={{0,16},{8,24},{16,0},{24,8},{1,17},{9,25},{17,1},{25,9},{2,18},{10... | collective-permute-start | bytes 221192 | tf_op jit(solution)/shard_map/ppermute | solution.py:247
  7.4 6.6 %collective-permute-start.2 = (bf16[64,576]{1,0:T(8,128)(2,1)S(1)}, bf16[64,576]{1,0:T(8,128)(2,1)S(1)}, u32[]{:S(2)}, u32[]{:S(2)}) collective-permute-start(bf16[64,576]{1,0:T(8,128)(2,1)S(1)} %round.1.rest_0_), channel_id=1, source_target_pairs={{0,24},{8,16},{16,8},{24,0},{1,25},{9,17},{17,9},{25,1},{2,26},{10... | collective-permute-start | bytes 221192 | tf_op jit(solution)/shard_map/ppermute | solution.py:247
  7.4 8.4 %collective-permute-start.3 = (bf16[64,576]{1,0:T(8,128)(2,1)S(1)}, bf16[64,576]{1,0:T(8,128)(2,1)S(1)}, u32[]{:S(2)}, u32[]{:S(2)}) collective-permute-start(bf16[64,576]{1,0:T(8,128)(2,1)S(1)} %round.1.rest_0_), channel_id=1, source_target_pairs={{0,2},{1,3},{2,0},{3,1},{4,6},{5,7},{6,4},{7,5},{8,10},{9,11},{10,... | collective-permute-start | bytes 221192 | tf_op jit(solution)/shard_map/ppermute | solution.py:247
  9.1 6.7 %collective-permute-start.4 = (bf16[64,576]{1,0:T(8,128)(2,1)S(1)}, bf16[64,576]{1,0:T(8,128)(2,1)S(1)}, u32[]{:S(2)}, u32[]{:S(2)}) collective-permute-start(bf16[64,576]{1,0:T(8,128)(2,1)S(1)} %round.1.rest_0_), channel_id=1, source_target_pairs={{0,4},{1,5},{2,6},{3,7},{4,0},{5,1},{6,2},{7,3},{8,12},{9,13},{10,... | collective-permute-start | bytes 221192 | tf_op jit(solution)/shard_map/ppermute | solution.py:247
  11.3 5.4 %collective-permute-start.5 = (bf16[64,576]{1,0:T(8,128)(2,1)S(1)}, bf16[64,576]{1,0:T(8,128)(2,1)S(1)}, u32[]{:S(2)}, u32[]{:S(2)}) collective-permute-start(bf16[64,576]{1,0:T(8,128)(2,1)S(1)} %round.1.rest_0_), channel_id=1, source_target_pairs={{0,6},{1,7},{2,4},{3,5},{4,2},{5,3},{6,0},{7,1},{8,14},{9,15},{10,... | collective-permute-start | bytes 221192 | tf_op jit(solution)/shard_map/ppermute | solution.py:247
  14.1 4.3 %copy-start = (bf16[1,576,576]{2,1,0:T(8,128)(2,1)S(1)}, bf16[1,576,576]{2,1,0:T(8,128)(2,1)}, u32[]{:S(2)}) copy-start(bf16[1,576,576]{2,1,0:T(8,128)(2,1)} %param.7) | copy-start | bytes 1990660
  14.1 4.3 %copy-start.2 = (f32[1,64,576]{2,1,0:T(8,128)S(1)}, f32[1,64,576]{2,1,0:T(8,128)}, u32[]{:S(2)}) copy-start(f32[1,64,576]{2,1,0:T(8,128)} %param.8) | copy-start | bytes 442372
  16.7 1.6 %collective-permute-start.6 = (bf16[4,64,576]{2,1,0:T(8,128)(2,1)S(1)}, bf16[4,64,576]{2,1,0:T(8,128)(2,1)S(1)}, u32[]{:S(2)}, u32[]{:S(2)}) collective-permute-start(bf16[4,64,576]{2,1,0:T(8,128)(2,1)S(1)} %get-tuple-element.50), channel_id=1, source_target_pairs={{0,1},{1,0},{2,3},{3,2},{4,5},{5,4},{6,7},{7,6},{8,9},{9,8},{10,11... | collective-permute-start | bytes 884744 | tf_op jit(solution)/shard_map/ppermute | solution.py:247
  16.8 8.0 %collective-permute-start.8 = (bf16[4,64,576]{2,1,0:T(8,128)(2,1)S(1)}, bf16[4,64,576]{2,1,0:T(8,128)(2,1)S(1)}, u32[]{:S(2)}, u32[]{:S(2)}) collective-permute-start(bf16[4,64,576]{2,1,0:T(8,128)(2,1)S(1)} %pad_maximum_fusion.near_own), channel_id=1, source_target_pairs={{0,1},{1,0},{2,3},{3,2},{4,5},{5,4},{6,7},{7,6},{8,9},{9,8},{10,11... | collective-permute-start | bytes 884744 | tf_op jit(solution)/shard_map/ppermute | solution.py:247
  19.7 1.3 %collective-permute-start.7 = (f32[64,128]{1,0:T(8,128)S(1)}, f32[64,128]{1,0:T(8,128)S(1)}, u32[]{:S(2)}, u32[]{:S(2)}) collective-permute-start(f32[64,128]{1,0:T(8,128)S(1)} %get-tuple-element.55.grams), channel_id=1, source_target_pairs={{0,1},{1,0},{2,3},{3,2},{4,5},{5,4},{6,7},{7,6},{8,9},{9,8},{10,11... | collective-permute-start | bytes 98312 | tf_op jit(solution)/shard_map/ppermute | solution.py:247
  21.2 5.5 %collective-permute-start.9 = (bf16[64,768]{1,0:T(8,128)(2,1)S(1)}, bf16[64,768]{1,0:T(8,128)(2,1)S(1)}, u32[]{:S(2)}, u32[]{:S(2)}) collective-permute-start(bf16[64,768]{1,0:T(8,128)(2,1)S(1)} %get-tuple-element.58), channel_id=1, source_target_pairs={{0,2},{1,3},{2,0},{3,1},{4,6},{5,7},{6,4},{7,5},{8,10},{9,11},{10,... | collective-permute-start | bytes 294920 | tf_op jit(solution)/shard_map/ppermute | solution.py:247
  21.9 5.8 %collective-permute-start.10 = (bf16[64,768]{1,0:T(8,128)(2,1)S(1)}, bf16[64,768]{1,0:T(8,128)(2,1)S(1)}, u32[]{:S(2)}, u32[]{:S(2)}) collective-permute-start(bf16[64,768]{1,0:T(8,128)(2,1)S(1)} %get-tuple-element.59), channel_id=1, source_target_pairs={{0,4},{1,5},{2,6},{3,7},{4,0},{5,1},{6,2},{7,3},{8,12},{9,13},{10,... | collective-permute-start | bytes 294920 | tf_op jit(solution)/shard_map/ppermute | solution.py:247
  23.4 5.5 %collective-permute-start.11 = (bf16[64,768]{1,0:T(8,128)(2,1)S(1)}, bf16[64,768]{1,0:T(8,128)(2,1)S(1)}, u32[]{:S(2)}, u32[]{:S(2)}) collective-permute-start(bf16[64,768]{1,0:T(8,128)(2,1)S(1)} %get-tuple-element.60), channel_id=1, source_target_pairs={{0,6},{1,7},{2,4},{3,5},{4,2},{5,3},{6,0},{7,1},{8,14},{9,15},{10,... | collective-permute-start | bytes 294920 | tf_op jit(solution)/shard_map/ppermute | solution.py:247
  29.5 6.1 %collective-permute-start.12 = (bf16[64,768]{1,0:T(8,128)(2,1)S(1)}, bf16[64,768]{1,0:T(8,128)(2,1)S(1)}, u32[]{:S(2)}, u32[]{:S(2)}) collective-permute-start(bf16[64,768]{1,0:T(8,128)(2,1)S(1)} %get-tuple-element.63), channel_id=1, source_target_pairs={{0,8},{8,0},{16,24},{24,16},{1,9},{9,1},{17,25},{25,17},{2,10},{10... | collective-permute-start | bytes 294920 | tf_op jit(solution)/shard_map/ppermute | solution.py:247
  32.0 9.0 %collective-permute-start.13 = (bf16[64,768]{1,0:T(8,128)(2,1)S(1)}, bf16[64,768]{1,0:T(8,128)(2,1)S(1)}, u32[]{:S(2)}, u32[]{:S(2)}) collective-permute-start(bf16[64,768]{1,0:T(8,128)(2,1)S(1)} %get-tuple-element.64), channel_id=1, source_target_pairs={{0,16},{8,24},{16,0},{24,8},{1,17},{9,25},{17,1},{25,9},{2,18},{10... | collective-permute-start | bytes 294920 | tf_op jit(solution)/shard_map/ppermute | solution.py:247
  35.7 6.5 %collective-permute-start.14 = (bf16[64,768]{1,0:T(8,128)(2,1)S(1)}, bf16[64,768]{1,0:T(8,128)(2,1)S(1)}, u32[]{:S(2)}, u32[]{:S(2)}) collective-permute-start(bf16[64,768]{1,0:T(8,128)(2,1)S(1)} %get-tuple-element.65), channel_id=1, source_target_pairs={{0,24},{8,16},{16,8},{24,0},{1,25},{9,17},{17,9},{25,1},{2,26},{10... | collective-permute-start | bytes 294920 | tf_op jit(solution)/shard_map/ppermute | solution.py:247
  45.1 6.7 %collective-permute-start.15 = (bf16[64,576]{1,0:T(8,128)(2,1)S(1)}, bf16[64,576]{1,0:T(8,128)(2,1)S(1)}, u32[]{:S(2)}, u32[]{:S(2)}) collective-permute-start(bf16[64,576]{1,0:T(8,128)(2,1)S(1)} %get-tuple-element.66.rest_0_), channel_id=1, source_target_pairs={{0,8},{8,0},{16,24},{24,16},{1,9},{9,1},{17,25},{25,17},{2,10},{10... | collective-permute-start | bytes 221192 | tf_op jit(solution)/shard_map/ppermute | solution.py:247
  46.6 6.8 %collective-permute-start.16 = (bf16[64,576]{1,0:T(8,128)(2,1)S(1)}, bf16[64,576]{1,0:T(8,128)(2,1)S(1)}, u32[]{:S(2)}, u32[]{:S(2)}) collective-permute-start(bf16[64,576]{1,0:T(8,128)(2,1)S(1)} %get-tuple-element.66.rest_0_), channel_id=1, source_target_pairs={{0,16},{8,24},{16,0},{24,8},{1,17},{9,25},{17,1},{25,9},{2,18},{10... | collective-permute-start | bytes 221192 | tf_op jit(solution)/shard_map/ppermute | solution.py:247
  48.1 6.3 %collective-permute-start.17 = (bf16[64,576]{1,0:T(8,128)(2,1)S(1)}, bf16[64,576]{1,0:T(8,128)(2,1)S(1)}, u32[]{:S(2)}, u32[]{:S(2)}) collective-permute-start(bf16[64,576]{1,0:T(8,128)(2,1)S(1)} %get-tuple-element.66.rest_0_), channel_id=1, source_target_pairs={{0,24},{8,16},{16,8},{24,0},{1,25},{9,17},{17,9},{25,1},{2,26},{10... | collective-permute-start | bytes 221192 | tf_op jit(solution)/shard_map/ppermute | solution.py:247
  49.5 6.6 %collective-permute-start.18 = (bf16[64,576]{1,0:T(8,128)(2,1)S(1)}, bf16[64,576]{1,0:T(8,128)(2,1)S(1)}, u32[]{:S(2)}, u32[]{:S(2)}) collective-permute-start(bf16[64,576]{1,0:T(8,128)(2,1)S(1)} %get-tuple-element.66.rest_0_), channel_id=1, source_target_pairs={{0,2},{1,3},{2,0},{3,1},{4,6},{5,7},{6,4},{7,5},{8,10},{9,11},{10,... | collective-permute-start | bytes 221192 | tf_op jit(solution)/shard_map/ppermute | solution.py:247
  51.2 4.9 %collective-permute-start.19 = (bf16[64,576]{1,0:T(8,128)(2,1)S(1)}, bf16[64,576]{1,0:T(8,128)(2,1)S(1)}, u32[]{:S(2)}, u32[]{:S(2)}) collective-permute-start(bf16[64,576]{1,0:T(8,128)(2,1)S(1)} %get-tuple-element.66.rest_0_), channel_id=1, source_target_pairs={{0,4},{1,5},{2,6},{3,7},{4,0},{5,1},{6,2},{7,3},{8,12},{9,13},{10,... | collective-permute-start | bytes 221192 | tf_op jit(solution)/shard_map/ppermute | solution.py:247
  51.8 5.3 %collective-permute-start.20 = (bf16[64,576]{1,0:T(8,128)(2,1)S(1)}, bf16[64,576]{1,0:T(8,128)(2,1)S(1)}, u32[]{:S(2)}, u32[]{:S(2)}) collective-permute-start(bf16[64,576]{1,0:T(8,128)(2,1)S(1)} %get-tuple-element.66.rest_0_), channel_id=1, source_target_pairs={{0,6},{1,7},{2,4},{3,5},{4,2},{5,3},{6,0},{7,1},{8,14},{9,15},{10,... | collective-permute-start | bytes 221192 | tf_op jit(solution)/shard_map/ppermute | solution.py:247
  57.1 1.6 %collective-permute-start.21 = (bf16[4,64,576]{2,1,0:T(8,128)(2,1)S(1)}, bf16[4,64,576]{2,1,0:T(8,128)(2,1)S(1)}, u32[]{:S(2)}, u32[]{:S(2)}) collective-permute-start(bf16[4,64,576]{2,1,0:T(8,128)(2,1)S(1)} %get-tuple-element.69), channel_id=1, source_target_pairs={{0,1},{1,0},{2,3},{3,2},{4,5},{5,4},{6,7},{7,6},{8,9},{9,8},{10,11... | collective-permute-start | bytes 884744 | tf_op jit(solution)/shard_map/ppermute | solution.py:247
  57.2 8.0 %collective-permute-start.23 = (bf16[4,64,576]{2,1,0:T(8,128)(2,1)S(1)}, bf16[4,64,576]{2,1,0:T(8,128)(2,1)S(1)}, u32[]{:S(2)}, u32[]{:S(2)}) collective-permute-start(bf16[4,64,576]{2,1,0:T(8,128)(2,1)S(1)} %pad_maximum_fusion.1.near_own), channel_id=1, source_target_pairs={{0,1},{1,0},{2,3},{3,2},{4,5},{5,4},{6,7},{7,6},{8,9},{9,8},{10,11... | collective-permute-start | bytes 884744 | tf_op jit(solution)/shard_map/ppermute | solution.py:247
  60.1 1.3 %collective-permute-start.22 = (f32[64,128]{1,0:T(8,128)S(1)}, f32[64,128]{1,0:T(8,128)S(1)}, u32[]{:S(2)}, u32[]{:S(2)}) collective-permute-start(f32[64,128]{1,0:T(8,128)S(1)} %get-tuple-element.75.grams), channel_id=1, source_target_pairs={{0,1},{1,0},{2,3},{3,2},{4,5},{5,4},{6,7},{7,6},{8,9},{9,8},{10,11... | collective-permute-start | bytes 98312 | tf_op jit(solution)/shard_map/ppermute | solution.py:247
  61.6 5.0 %collective-permute-start.24 = (bf16[64,768]{1,0:T(8,128)(2,1)S(1)}, bf16[64,768]{1,0:T(8,128)(2,1)S(1)}, u32[]{:S(2)}, u32[]{:S(2)}) collective-permute-start(bf16[64,768]{1,0:T(8,128)(2,1)S(1)} %get-tuple-element.78), channel_id=1, source_target_pairs={{0,2},{1,3},{2,0},{3,1},{4,6},{5,7},{6,4},{7,5},{8,10},{9,11},{10,... | collective-permute-start | bytes 294920 | tf_op jit(solution)/shard_map/ppermute | solution.py:247
  62.9 5.4 %collective-permute-start.25 = (bf16[64,768]{1,0:T(8,128)(2,1)S(1)}, bf16[64,768]{1,0:T(8,128)(2,1)S(1)}, u32[]{:S(2)}, u32[]{:S(2)}) collective-permute-start(bf16[64,768]{1,0:T(8,128)(2,1)S(1)} %get-tuple-element.79), channel_id=1, source_target_pairs={{0,4},{1,5},{2,6},{3,7},{4,0},{5,1},{6,2},{7,3},{8,12},{9,13},{10,... | collective-permute-start | bytes 294920 | tf_op jit(solution)/shard_map/ppermute | solution.py:247
  63.5 6.1 %collective-permute-start.26 = (bf16[64,768]{1,0:T(8,128)(2,1)S(1)}, bf16[64,768]{1,0:T(8,128)(2,1)S(1)}, u32[]{:S(2)}, u32[]{:S(2)}) collective-permute-start(bf16[64,768]{1,0:T(8,128)(2,1)S(1)} %get-tuple-element.80), channel_id=1, source_target_pairs={{0,6},{1,7},{2,4},{3,5},{4,2},{5,3},{6,0},{7,1},{8,14},{9,15},{10,... | collective-permute-start | bytes 294920 | tf_op jit(solution)/shard_map/ppermute | solution.py:247
  70.2 8.4 %collective-permute-start.27 = (bf16[64,768]{1,0:T(8,128)(2,1)S(1)}, bf16[64,768]{1,0:T(8,128)(2,1)S(1)}, u32[]{:S(2)}, u32[]{:S(2)}) collective-permute-start(bf16[64,768]{1,0:T(8,128)(2,1)S(1)} %get-tuple-element.89), channel_id=1, source_target_pairs={{0,8},{8,0},{16,24},{24,16},{1,9},{9,1},{17,25},{25,17},{2,10},{10... | collective-permute-start | bytes 294920 | tf_op jit(solution)/shard_map/ppermute | solution.py:247
  72.7 8.2 %collective-permute-start.28 = (bf16[64,768]{1,0:T(8,128)(2,1)S(1)}, bf16[64,768]{1,0:T(8,128)(2,1)S(1)}, u32[]{:S(2)}, u32[]{:S(2)}) collective-permute-start(bf16[64,768]{1,0:T(8,128)(2,1)S(1)} %get-tuple-element.90), channel_id=1, source_target_pairs={{0,16},{8,24},{16,0},{24,8},{1,17},{9,25},{17,1},{25,9},{2,18},{10... | collective-permute-start | bytes 294920 | tf_op jit(solution)/shard_map/ppermute | solution.py:247
  76.1 6.5 %collective-permute-start.29 = (bf16[64,768]{1,0:T(8,128)(2,1)S(1)}, bf16[64,768]{1,0:T(8,128)(2,1)S(1)}, u32[]{:S(2)}, u32[]{:S(2)}) collective-permute-start(bf16[64,768]{1,0:T(8,128)(2,1)S(1)} %get-tuple-element.91), channel_id=1, source_target_pairs={{0,24},{8,16},{16,8},{24,0},{1,25},{9,17},{17,9},{25,1},{2,26},{10... | collective-permute-start | bytes 294920 | tf_op jit(solution)/shard_map/ppermute | solution.py:247

commit v5 on v4

--- a/solution.py
+++ b/solution.py
@@ -14,6 +14,7 @@
 NT = (((1,), (1,)), ((), ()))
 NN = (((1,), (0,)), ((), ()))
 TN = (((0,), (0,)), ((), ()))
+ANY = pl.BlockSpec(memory_space=pl.ANY)
 VMEM = pl.BlockSpec(memory_space=pltpu.VMEM)
 SMEM = pl.BlockSpec(memory_space=pltpu.SMEM)
 
@@ -34,7 +35,7 @@
     return dot16(left, first, dims) + (dot16(left, second, dims) + dot16(left, third, dims))
 
 
-def eliminate(systems, group=8):
+def eliminate(systems, group=16):
     size, width = systems[0].shape
     rows = lax.broadcasted_iota(jnp.int32, (size, width), 0)
     for start in range(0, size, group):
@@ -61,28 +62,51 @@
     return first, (value - first.astype(F32)).astype(BF16)
 
 
+def compact(block):
+    size, width = block.shape
+    whole = width - width % 128
+    rows = [block[:, at : at + 128] for at in range(0, whole, 128)]
+    if whole < width:
+        each = size * (width - whole) // 128
+        tail = [block[at : at + each, whole:] for at in range(0, size, each)]
+        rows.append(jnp.concatenate(tail, 1))
+    return jnp.concatenate(rows, 0)
+
+
+def spread(rows, size):
+    width = rows.shape[0] * 128 // size
+    whole, rest = width // 128, width % 128
+    columns = [rows[k * size : (k + 1) * size] for k in range(whole)]
+    if rest:
+        tail = rows[whole * size :]
+        columns.append(jnp.concatenate([tail[:, at : at + rest] for at in range(0, 128, rest)], 0))
+    return jnp.concatenate(columns, 1)
+
+
 def pack(block, grams):
     size = grams.shape[0]
     rows = lax.broadcasted_iota(jnp.int32, (size, size), 0)
     columns = lax.broadcasted_iota(jnp.int32, (size, size), 1)
     both = jnp.where(rows >= columns, grams[:, :size], grams[:, size:])
-    diagonal = jnp.sum(jnp.where(rows == columns, grams[:, size:], 0.0), axis=1, keepdims=True)
-    first, second = split16(both)
-    top, rest = split16(jnp.broadcast_to(diagonal, (size, size)))
-    return jnp.concatenate([block, first, second, jnp.where(columns == 0, top, rest)], 1)
-
-
-def unpack(message, width):
-    size = message.shape[0]
-    parts = message[:, width:].astype(F32)
-    both = parts[:, :size] + parts[:, size : 2 * size]
-    diagonal = parts[:, 2 * size : 2 * size + 1] + parts[:, 2 * size + 1 : 2 * size + 2]
+    diagonal = jnp.sum(jnp.where(rows == columns, grams[:, size:], 0.0), axis=0, keepdims=True)
+    parts = jnp.concatenate(split16(both), 1)
+    last = jnp.concatenate(split16(jnp.broadcast_to(diagonal, (16, size))), 1)
+    return jnp.concatenate([compact(block), parts, last], 0)
+
+
+def unpack(message, size):
+    end = message.shape[0]
+    parts = message[end - 16 - size : end - 16].astype(F32)
+    last = message[end - 16 :].astype(F32)
+    both = parts[:, :size] + parts[:, size:]
+    diagonal = (last[:, :size] + last[:, size:])[:1]
     rows = lax.broadcasted_iota(jnp.int32, (size, size), 0)
     columns = lax.broadcasted_iota(jnp.int32, (size, size), 1)
     turned = both.T
     first = jnp.where(rows >= columns, both, turned)
     second = jnp.where(rows < columns, both, turned)
-    return jnp.concatenate([first, jnp.where(rows == columns, diagonal, second)], 1)
+    second = jnp.where(rows == columns, diagonal, second)
+    return spread(message[: end - 16 - size], size).astype(F32), jnp.concatenate([first, second], 1)
 
 
 def held_slots(count, slots, work):
@@ -107,17 +131,17 @@
 
 
 def round_kernel(value, out):
-    out[...] = value[...].astype(BF16)
-
-
-def forward_kernel(index, tiles, *rest, n_row):
+    out[...] = compact(value[...].astype(BF16))
+
+
+def forward_kernel(index, tiles, after, *rest, n_row):
     far_in = rest[:n_row]
     give_core, acc, far = rest[n_row:]
     n_chip = give_core.shape[0]
     slots = tiles.shape[0]
     place = places(index, slots, n_row, n_chip)
     for d, block in enumerate(far_in):
-        far[d] = block[...]
+        far[d] = spread(block[...], far.shape[1])
     acc[...] = jnp.zeros_like(acc)
 
     def work(slot, held):
@@ -129,18 +153,26 @@
         give_core[d] = acc[n_chip + d].astype(BF16)
 
 
-def gram_kernel(acc, came, diag, residual, *rest):
-    *near, keep, own_out, grams = rest
+def own_kernel(near, diag, residual, own_out, grams):
     size = residual.shape[0]
-    own = dot16(near[0][...], diag[...], NT)
+    block = spread(near[...], size)
+    own = dot16(block, diag[...], NT)
     own_out[...] = own
-    half = 0.5 * dot_exact16(near[0][...], own, NT)
+    half = 0.5 * dot_exact16(block, own, NT)
+    grams[:, :size] = half + half.T
+    grams[:, size:] = dot32(residual[...], residual[...], NT)
+
+
+def gram_kernel(acc, came, grams_own, *rest):
+    *near, keep, grams = rest
+    size = grams.shape[0]
+    half = jnp.zeros((size, size), F32)
     for d, block in enumerate(near):
         both = acc[d] + came[d].astype(F32)
         keep[d] = both
-        half += dot_exact16(block[...], both, NT)
-    grams[:, :size] = half + half.T
-    grams[:, size:] = dot32(residual[...], residual[...], NT)
+        half += dot_exact16(spread(block[...], size), both, NT)
+    grams[:, :size] = grams_own[:, :size] + half + half.T
+    grams[:, size:] = grams_own[:, size:]
 
 
 def mirrored_kernel(index, near_own, near_far, tiles, acc, near):
@@ -148,8 +180,8 @@
     slots = tiles.shape[0]
     place = places(index, slots, acc.shape[0], n_chip)
     for d in range(n_chip):
-        near[d] = near_own[d]
-        near[n_chip + d] = near_far[d]
+        near[d] = spread(near_own[d], near.shape[1])
+        near[n_chip + d] = spread(near_far[d], near.shape[1])
     acc[...] = jnp.zeros_like(acc)
 
     def work(slot, held):
@@ -176,10 +208,10 @@
 
 def gather_sums(mine, grams, rest, n_in):
     image, total = mine, grams
-    width = image.shape[1]
     for message in rest[:n_in]:
-        image += message[:, :width].astype(F32)
-        total += unpack(message[...], width)
+        block, matrices = unpack(message[...], image.shape[0])
+        image += block
+        total += matrices
     return image, total, rest[n_in:]
 
 
@@ -189,7 +221,7 @@
     )
     (alpha,) = eliminate([total])
     residual = probes[...] - dot32(alpha, image, TN)
-    rounded[...] = residual.astype(BF16)
+    rounded[...] = compact(residual.astype(BF16))
     residual_out[...] = residual
     image_out[...] = image
     totals[...] = total
@@ -240,7 +272,7 @@
     p_size, width = probes.shape[1:]
     shape = jax.ShapeDtypeStruct
     block32 = shape((p_size, width), F32)
-    block16 = shape((p_size, width), BF16)
+    block16 = shape((p_size * width // 128, 128), BF16)
 
     def over(value, axis, delta):
         size = n_row if axis == "row" else n_col
@@ -260,16 +292,17 @@
     slots = tiles.shape[2]
     passes = 2 * slots * p_size * width * width
 
-    message = shape((p_size, width + 3 * p_size), BF16)
+    message = shape((block16.shape[0] + p_size + 16, 128), BF16)
 
     def apply_operator(rounded, residual):
         from_rows = over_rows(rounded)
         near = over_chips(rounded)
+        own, grams = call(own_kernel, [block32, square], [rounded, diag, residual], name="own")
         give_core, acc_row = call(
             functools.partial(forward_kernel, n_row=n_row),
             [shape((n_chip, p_size, width), BF16), shape((n_col, p_size, width), F32)],
-            [index, held, rounded, *from_rows],
-            [SMEM] + [VMEM] * (1 + n_row),
+            [index, held, grams, rounded, *from_rows],
+            [SMEM, VMEM, ANY] + [VMEM] * n_row,
             [pltpu.VMEM((n_row, p_size, width), BF16)],
             name="forward",
             work=1,
@@ -278,10 +311,10 @@
         came = over(give_core, "col", 1)
         near_own = jnp.stack([rounded, *near])
         near_far = over(near_own, "col", 1)
-        keep, own, grams = call(
+        keep, grams = call(
             gram_kernel,
-            [shape((n_chip, p_size, width), F32), block32, square],
-            [acc_row, came, diag, residual, rounded, *near],
+            [shape((n_chip, p_size, width), F32), square],
+            [acc_row, came, grams, rounded, *near],
             name="gram",
         )
         grams_came = over(grams, "col", 1)

time: 86.8 us -> 82.3 us (0.948)
  waiting for transfers between devices: 26.1 us -> 23.9 us
  starting transfers between devices: 37.9 us -> 36.6 us
  Pallas kernels: 19.8 us -> 18.9 us
    ppermute x30, waiting for transfers between devices: 26.1 us -> 23.9 us  [over(): return lax.ppermute(value, axis, [(i, i ^ delta) for i in range(size)])]
    ppermute x30, starting transfers between devices: 37.9 us -> 36.6 us  [over(): return lax.ppermute(value, axis, [(i, i ^ delta) for i in range(size)])]
    pallas_call x14 -> x16, Pallas kernels: 19.8 us -> 18.9 us  [call(): pl.pallas_call(kernel, out_shape=outs, in_specs=[VMEM] * len(args) if spe...]
  transfers between devices with their start and end apart: 30 -> 30, of which waited for: 18 -> 15; matrix products, arithmetic and copies ran while one was open for 0% -> 0% of each run, Pallas kernels for 14% -> 15%
where the time goes in v5:
time: 82.3 us; the launch traced here: 82.1 us
  starting transfers between devices  36.6 us (44%)
  waiting for transfers between devices  23.9 us (29%)
  Pallas kernels  18.9 us (23%)
  between operations  1.51 us (2%)
  local copies, waits for them, and re-layouts  1.09 us (1%)
    ppermute x30, starting transfers between devices, over(): return lax.ppermute(value, axis, [(i, i ^ delta) for i in range(size)])  36.6 us
    ppermute x30, waiting for transfers between devices, over(): return lax.ppermute(value, axis, [(i, i ^ delta) for i in range(size)])  23.9 us
    pallas_call x16, Pallas kernels, call(): pl.pallas_call(kernel, out_shape=outs, in_specs=[VMEM] * len(args) if spe...  18.9 us
  transfers between devices with their start and end apart: 30, of which 15 were waited for; matrix products, arithmetic and copies ran while one was open for 0% of the time, Pallas kernels for 15%

profile of v5, /device:TPU:0, one launch (start us, length us, event | category | flops | bytes accessed | tf_op | source)
XLA Modules:
  0.0 82.1 jit_solution(5284761290397530404)
XLA Ops:
  0.6 0.0 copy-start.1
  0.7 1.1 %copy-done.1 = f32[1,64,576]{2,1,0:T(8,128)S(1)} copy-done((f32[1,64,576]{2,1,0:T(8,128)S(1)}, f32[1,64,576]{2,1,0:T(8,128)}, u32[]{:S(2)}) %copy-start.1) | copy-done | bytes 147480
  1.7 0.0 slice-start.2
  1.7 0.1 round.1.near.rest_0_
  1.8 3.0 %collective-permute-start = (bf16[288,128]{1,0:T(8,128)(2,1)S(1)}, bf16[288,128]{1,0:T(8,128)(2,1)S(1)}, u32[]{:S(2)}, u32[]{:S(2)}) collective-permute-start(bf16[288,128]{1,0:T(8,128)(2,1)S(1)} %round.1.near.rest_0_), channel_id=1, source_target_pairs={{0,8},{8,0},{16,24},{24,16},{1,9},{9,1},{17,25},{25,17},{2,10},{10... | collective-permute-start | bytes 221192 | tf_op jit(solution)/shard_map/ppermute | solution.py:279
  4.8 2.6 %collective-permute-start.1 = (bf16[288,128]{1,0:T(8,128)(2,1)S(1)}, bf16[288,128]{1,0:T(8,128)(2,1)S(1)}, u32[]{:S(2)}, u32[]{:S(2)}) collective-permute-start(bf16[288,128]{1,0:T(8,128)(2,1)S(1)} %round.1.near.rest_0_), channel_id=1, source_target_pairs={{0,16},{8,24},{16,0},{24,8},{1,17},{9,25},{17,1},{25,9},{2,18},{10... | collective-permute-start | bytes 221192 | tf_op jit(solution)/shard_map/ppermute | solution.py:279
  7.4 0.0 collective-permute-start.2
  7.4 1.7 %collective-permute-start.3 = (bf16[288,128]{1,0:T(8,128)(2,1)S(1)}, bf16[288,128]{1,0:T(8,128)(2,1)S(1)}, u32[]{:S(2)}, u32[]{:S(2)}) collective-permute-start(bf16[288,128]{1,0:T(8,128)(2,1)S(1)} %round.1.near.rest_0_), channel_id=1, source_target_pairs={{0,2},{1,3},{2,0},{3,1},{4,6},{5,7},{6,4},{7,5},{8,10},{9,11},{10,... | collective-permute-start | bytes 221192 | tf_op jit(solution)/shard_map/ppermute | solution.py:279
  9.1 1.5 %collective-permute-start.4 = (bf16[288,128]{1,0:T(8,128)(2,1)S(1)}, bf16[288,128]{1,0:T(8,128)(2,1)S(1)}, u32[]{:S(2)}, u32[]{:S(2)}) collective-permute-start(bf16[288,128]{1,0:T(8,128)(2,1)S(1)} %round.1.near.rest_0_), channel_id=1, source_target_pairs={{0,4},{1,5},{2,6},{3,7},{4,0},{5,1},{6,2},{7,3},{8,12},{9,13},{10,... | collective-permute-start | bytes 221192 | tf_op jit(solution)/shard_map/ppermute | solution.py:279
  11.3 0.9 %own.2 = (f32[64,576]{1,0:T(8,128)S(1)}, f32[64,128]{1,0:T(8,128)S(1)}) custom-call(bf16[288,128]{1,0:T(8,128)(2,1)S(1)} %round.1.near.rest_0_, bf16[576,576]{1,0:T(8,128)(2,1)S(1)} %bitcast.23, f32[64,576]{1,0:T(8,128)S(1)} %bitcast.26), custom_call_target="tpu_custom_call" | custom-call | tf_op jit(solution)/shard_map/own/pallas_call | solution.py:258
  12.3 0.0 collective-permute-done.rest_1_
  12.3 0.3 collective-permute-start.5
  12.6 0.1 pad_add_fusion.index
  12.7 1.0 %collective-permute-done.2.rest_3_ = bf16[288,128]{1,0:T(8,128)(2,1)S(1)} collective-permute-done((bf16[288,128]{1,0:T(8,128)(2,1)S(1)}, bf16[288,128]{1,0:T(8,128)(2,1)S(1)}, u32[]{:S(2)}, u32[]{:S(2)}) %collective-permute-start.2) | collective-permute-done | bytes 73760 | tf_op jit(solution)/shard_map/ppermute | solution.py:279
  13.7 1.7 %forward.2 = (bf16[4,64,576]{2,1,0:T(8,128)(2,1)S(1)}, f32[8,64,576]{2,1,0:T(8,128)S(1)}) custom-call(s32[33]{0:T(128)S(1)} %pad_add_fusion.index, bf16[16,576,576]{2,1,0:T(8,128)(2,1)S(1)} %bitcast.19, f32[64,128]{1,0:T(8,128)S(1)} %get-tuple-element.50.after.grams_own, bf16[288,128]{1,0:T(8,128)(2,1)S(1)} %round.1.near.rest_0_, ...), custom_call_target="tpu_custom_call" | custom-call | flops 1 | tf_op jit(solution)/shard_map/forward/pallas_call | solution.py:258
  15.4 0.0 collective-permute-done.3.rest_1_
  15.4 2.1 %collective-permute-done.5.rest_3_ = bf16[288,128]{1,0:T(8,128)(2,1)S(1)} collective-permute-done((bf16[288,128]{1,0:T(8,128)(2,1)S(1)}, bf16[288,128]{1,0:T(8,128)(2,1)S(1)}, u32[]{:S(2)}, u32[]{:S(2)}) %collective-permute-start.5) | collective-permute-done | bytes 73760 | tf_op jit(solution)/shard_map/ppermute | solution.py:279
  17.6 0.6 collective-permute-start.8
  18.2 1.0 %collective-permute-done.6.came = bf16[4,64,576]{2,1,0:T(8,128)(2,1)S(1)} collective-permute-done((bf16[4,64,576]{2,1,0:T(8,128)(2,1)S(1)}, bf16[4,64,576]{2,1,0:T(8,128)(2,1)S(1)}, u32[]{:S(2)}, u32[]{:S(2)}) %collective-permute-start.6) | collective-permute-done | bytes 294944 | tf_op jit(solution)/shard_map/ppermute | solution.py:279
  19.2 0.6 gram.2
  19.8 0.2 collective-permute-start.7
  20.0 1.1 %collective-permute-done.7.grams_came = f32[64,128]{1,0:T(8,128)S(1)} collective-permute-done((f32[64,128]{1,0:T(8,128)S(1)}, f32[64,128]{1,0:T(8,128)S(1)}, u32[]{:S(2)}, u32[]{:S(2)}) %collective-permute-start.7) | collective-permute-done | bytes 32800 | tf_op jit(solution)/shard_map/ppermute | solution.py:279
  21.1 0.2 join.2
  21.2 0.6 collective-permute-start.9
  21.9 0.4 collective-permute-start.10
  22.2 2.6 %collective-permute-start.11 = (bf16[368,128]{1,0:T(8,128)(2,1)S(1)}, bf16[368,128]{1,0:T(8,128)(2,1)S(1)}, u32[]{:S(2)}, u32[]{:S(2)}) collective-permute-start(bf16[368,128]{1,0:T(8,128)(2,1)S(1)} %get-tuple-element.63), channel_id=1, source_target_pairs={{0,6},{1,7},{2,4},{3,5},{4,2},{5,3},{6,0},{7,1},{8,14},{9,15},{10,... | collective-permute-start | bytes 282632 | tf_op jit(solution)/shard_map/ppermute | solution.py:279
  24.8 1.3 %mirrored.2.acc = f32[4,64,576]{2,1,0:T(8,128)S(1)} custom-call(s32[33]{0:T(128)S(1)} %pad_add_fusion.index, bf16[4,288,128]{2,1,0:T(8,128)(2,1)S(1)} %pad_maximum_fusion.near_own, bf16[4,288,128]{2,1,0:T(8,128)(2,1)S(1)} %collective-permute-done.8.near_far, bf16[16,576,576]{2,1,0:T(8,128)(2,1)S(1)} %bitcast.20), custom_call_target="tpu_custom_call" | custom-call | flops 679477248 | tf_op jit(solution)/shard_map/mirrored/pallas_call | solution.py:258
  26.1 0.0 copy-start.2
  26.1 0.6 collective-permute-done.9.rest_0_
  26.7 1.7 %collective-permute-done.10.rest_1_ = bf16[368,128]{1,0:T(8,128)(2,1)S(1)} collective-permute-done((bf16[368,128]{1,0:T(8,128)(2,1)S(1)}, bf16[368,128]{1,0:T(8,128)(2,1)S(1)}, u32[]{:S(2)}, u32[]{:S(2)}) %collective-permute-start.10) | collective-permute-done | bytes 94240 | tf_op jit(solution)/shard_map/ppermute | solution.py:279
  28.4 0.4 rows.2
  28.8 1.5 %collective-permute-start.12 = (bf16[368,128]{1,0:T(8,128)(2,1)S(1)}, bf16[368,128]{1,0:T(8,128)(2,1)S(1)}, u32[]{:S(2)}, u32[]{:S(2)}) collective-permute-start(bf16[368,128]{1,0:T(8,128)(2,1)S(1)} %get-tuple-element.66), channel_id=1, source_target_pairs={{0,8},{8,0},{16,24},{24,16},{1,9},{9,1},{17,25},{25,17},{2,10},{10... | collective-permute-start | bytes 282632 | tf_op jit(solution)/shard_map/ppermute | solution.py:279
  30.3 4.3 %collective-permute-start.13 = (bf16[368,128]{1,0:T(8,128)(2,1)S(1)}, bf16[368,128]{1,0:T(8,128)(2,1)S(1)}, u32[]{:S(2)}, u32[]{:S(2)}) collective-permute-start(bf16[368,128]{1,0:T(8,128)(2,1)S(1)} %get-tuple-element.67), channel_id=1, source_target_pairs={{0,16},{8,24},{16,0},{24,8},{1,17},{9,25},{17,1},{25,9},{2,18},{10... | collective-permute-start | bytes 282632 | tf_op jit(solution)/shard_map/ppermute | solution.py:279
  34.6 5.1 %collective-permute-done.13.rest_1_ = bf16[368,128]{1,0:T(8,128)(2,1)S(1)} collective-permute-done((bf16[368,128]{1,0:T(8,128)(2,1)S(1)}, bf16[368,128]{1,0:T(8,128)(2,1)S(1)}, u32[]{:S(2)}, u32[]{:S(2)}) %collective-permute-start.13) | collective-permute-done | bytes 94240 | tf_op jit(solution)/shard_map/ppermute | solution.py:279
  39.7 1.4 %collective-permute-done.14.rest_2_ = bf16[368,128]{1,0:T(8,128)(2,1)S(1)} collective-permute-done((bf16[368,128]{1,0:T(8,128)(2,1)S(1)}, bf16[368,128]{1,0:T(8,128)(2,1)S(1)}, u32[]{:S(2)}, u32[]{:S(2)}) %collective-permute-start.14) | collective-permute-done | bytes 94240 | tf_op jit(solution)/shard_map/ppermute | solution.py:279
  41.1 2.3 %first_step.1 = (f32[64,576]{1,0:T(8,128)S(1)}, f32[64,576]{1,0:T(8,128)S(1)}, bf16[288,128]{1,0:T(8,128)(2,1)S(1)}, f32[64,128]{1,0:T(8,128)S(1)}, f32[64,64]{1,0:T(8,128)S(1)}) custom-call(f32[64,576]{1,0:T(8,128)S(1)} %get-tuple-element.64.mine, f32[64,128]{1,0:T(8,128)S(1)} %get-tuple-element.65.grams, f32[64,576]{1,0:T(8,128)S(1)} %bitcast.27, ...), custom_call_target="tpu_custom_call" | custom-call | tf_op jit(solution)/shard_map/first_step/pallas_call | solution.py:258
  43.4 1.2 %collective-permute-start.15 = (bf16[288,128]{1,0:T(8,128)(2,1)S(1)}, bf16[288,128]{1,0:T(8,128)(2,1)S(1)}, u32[]{:S(2)}, u32[]{:S(2)}) collective-permute-start(bf16[288,128]{1,0:T(8,128)(2,1)S(1)} %get-tuple-element.69.near.rest_0_), channel_id=1, source_target_pairs={{0,8},{8,0},{16,24},{24,16},{1,9},{9,1},{17,25},{25,17},{2,10},{10... | collective-permute-start | bytes 221192 | tf_op jit(solution)/shard_map/ppermute | solution.py:279
  44.6 1.4 %collective-permute-start.16 = (bf16[288,128]{1,0:T(8,128)(2,1)S(1)}, bf16[288,128]{1,0:T(8,128)(2,1)S(1)}, u32[]{:S(2)}, u32[]{:S(2)}) collective-permute-start(bf16[288,128]{1,0:T(8,128)(2,1)S(1)} %get-tuple-element.69.near.rest_0_), channel_id=1, source_target_pairs={{0,16},{8,24},{16,0},{24,8},{1,17},{9,25},{17,1},{25,9},{2,18},{10... | collective-permute-start | bytes 221192 | tf_op jit(solution)/shard_map/ppermute | solution.py:279
  46.0 1.8 %collective-permute-start.17 = (bf16[288,128]{1,0:T(8,128)(2,1)S(1)}, bf16[288,128]{1,0:T(8,128)(2,1)S(1)}, u32[]{:S(2)}, u32[]{:S(2)}) collective-permute-start(bf16[288,128]{1,0:T(8,128)(2,1)S(1)} %get-tuple-element.69.near.rest_0_), channel_id=1, source_target_pairs={{0,24},{8,16},{16,8},{24,0},{1,25},{9,17},{17,9},{25,1},{2,26},{10... | collective-permute-start | bytes 221192 | tf_op jit(solution)/shard_map/ppermute | solution.py:279
  47.8 1.2 %collective-permute-start.18 = (bf16[288,128]{1,0:T(8,128)(2,1)S(1)}, bf16[288,128]{1,0:T(8,128)(2,1)S(1)}, u32[]{:S(2)}, u32[]{:S(2)}) collective-permute-start(bf16[288,128]{1,0:T(8,128)(2,1)S(1)} %get-tuple-element.69.near.rest_0_), channel_id=1, source_target_pairs={{0,2},{1,3},{2,0},{3,1},{4,6},{5,7},{6,4},{7,5},{8,10},{9,11},{10,... | collective-permute-start | bytes 221192 | tf_op jit(solution)/shard_map/ppermute | solution.py:279
  49.0 0.7 collective-permute-start.19
  49.6 1.6 %collective-permute-start.20 = (bf16[288,128]{1,0:T(8,128)(2,1)S(1)}, bf16[288,128]{1,0:T(8,128)(2,1)S(1)}, u32[]{:S(2)}, u32[]{:S(2)}) collective-permute-start(bf16[288,128]{1,0:T(8,128)(2,1)S(1)} %get-tuple-element.69.near.rest_0_), channel_id=1, source_target_pairs={{0,6},{1,7},{2,4},{3,5},{4,2},{5,3},{6,0},{7,1},{8,14},{9,15},{10,... | collective-permute-start | bytes 221192 | tf_op jit(solution)/shard_map/ppermute | solution.py:279
  51.3 0.9 %own.3 = (f32[64,576]{1,0:T(8,128)S(1)}, f32[64,128]{1,0:T(8,128)S(1)}) custom-call(bf16[288,128]{1,0:T(8,128)(2,1)S(1)} %get-tuple-element.69.near.rest_0_, bf16[576,576]{1,0:T(8,128)(2,1)S(1)} %bitcast.24, f32[64,576]{1,0:T(8,128)S(1)} %get-tuple-element.70.residual.residual_in), custom_call_target="tpu_custom_call" | custom-call | tf_op jit(solution)/shard_map/own/pallas_call | solution.py:258
  52.2 0.1 collective-permute-done.17.rest_3_
  52.3 1.7 %forward.3 = (bf16[4,64,576]{2,1,0:T(8,128)(2,1)S(1)}, f32[8,64,576]{2,1,0:T(8,128)S(1)}) custom-call(s32[33]{0:T(128)S(1)} %pad_add_fusion.index, bf16[16,576,576]{2,1,0:T(8,128)(2,1)S(1)} %bitcast.21, f32[64,128]{1,0:T(8,128)S(1)} %get-tuple-element.71.after.grams_own, bf16[288,128]{1,0:T(8,128)(2,1)S(1)} %get-tuple-element.69.near.rest_0_, ...), custom_call_target="tpu_custom_call" | custom-call | flops 1 | tf_op jit(solution)/shard_map/forward/pallas_call | solution.py:258
  54.0 0.9 %collective-permute-done.20.rest_3_ = bf16[288,128]{1,0:T(8,128)(2,1)S(1)} collective-permute-done((bf16[288,128]{1,0:T(8,128)(2,1)S(1)}, bf16[288,128]{1,0:T(8,128)(2,1)S(1)}, u32[]{:S(2)}, u32[]{:S(2)}) %collective-permute-start.20) | collective-permute-done | bytes 73760 | tf_op jit(solution)/shard_map/ppermute | solution.py:279
  54.9 0.6 collective-permute-start.23
  55.5 1.0 %collective-permute-done.21.came = bf16[4,64,576]{2,1,0:T(8,128)(2,1)S(1)} collective-permute-done((bf16[4,64,576]{2,1,0:T(8,128)(2,1)S(1)}, bf16[4,64,576]{2,1,0:T(8,128)(2,1)S(1)}, u32[]{:S(2)}, u32[]{:S(2)}) %collective-permute-start.21) | collective-permute-done | bytes 294944 | tf_op jit(solution)/shard_map/ppermute | solution.py:279
  56.5 0.6 gram.3
  57.1 0.2 collective-permute-start.22
  57.3 1.1 %collective-permute-done.22.grams_came = f32[64,128]{1,0:T(8,128)S(1)} collective-permute-done((f32[64,128]{1,0:T(8,128)S(1)}, f32[64,128]{1,0:T(8,128)S(1)}, u32[]{:S(2)}, u32[]{:S(2)}) %collective-permute-start.22) | collective-permute-done | bytes 32800 | tf_op jit(solution)/shard_map/ppermute | solution.py:279
  58.4 0.2 join.3
  58.6 1.4 %collective-permute-start.24 = (bf16[368,128]{1,0:T(8,128)(2,1)S(1)}, bf16[368,128]{1,0:T(8,128)(2,1)S(1)}, u32[]{:S(2)}, u32[]{:S(2)}) collective-permute-start(bf16[368,128]{1,0:T(8,128)(2,1)S(1)} %get-tuple-element.82), channel_id=1, source_target_pairs={{0,2},{1,3},{2,0},{3,1},{4,6},{5,7},{6,4},{7,5},{8,10},{9,11},{10,... | collective-permute-start | bytes 282632 | tf_op jit(solution)/shard_map/ppermute | solution.py:279
  59.9 0.9 %collective-permute-start.25 = (bf16[368,128]{1,0:T(8,128)(2,1)S(1)}, bf16[368,128]{1,0:T(8,128)(2,1)S(1)}, u32[]{:S(2)}, u32[]{:S(2)}) collective-permute-start(bf16[368,128]{1,0:T(8,128)(2,1)S(1)} %get-tuple-element.83), channel_id=1, source_target_pairs={{0,4},{1,5},{2,6},{3,7},{4,0},{5,1},{6,2},{7,3},{8,12},{9,13},{10,... | collective-permute-start | bytes 282632 | tf_op jit(solution)/shard_map/ppermute | solution.py:279
  60.8 1.3 %collective-permute-start.26 = (bf16[368,128]{1,0:T(8,128)(2,1)S(1)}, bf16[368,128]{1,0:T(8,128)(2,1)S(1)}, u32[]{:S(2)}, u32[]{:S(2)}) collective-permute-start(bf16[368,128]{1,0:T(8,128)(2,1)S(1)} %get-tuple-element.84), channel_id=1, source_target_pairs={{0,6},{1,7},{2,4},{3,5},{4,2},{5,3},{6,0},{7,1},{8,14},{9,15},{10,... | collective-permute-start | bytes 282632 | tf_op jit(solution)/shard_map/ppermute | solution.py:279
  62.1 1.5 %mirrored.3.acc = f32[4,64,576]{2,1,0:T(8,128)S(1)} custom-call(s32[33]{0:T(128)S(1)} %pad_add_fusion.index, bf16[4,288,128]{2,1,0:T(8,128)(2,1)S(1)} %pad_maximum_fusion.1.near_own, bf16[4,288,128]{2,1,0:T(8,128)(2,1)S(1)} %collective-permute-done.23.near_far, bf16[16,576,576]{2,1,0:T(8,128)(2,1)S(1)} %bitcast.22), custom_call_target="tpu_custom_call" | custom-call | flops 679477248 | tf_op jit(solution)/shard_map/mirrored/pallas_call | solution.py:258
  63.6 2.9 %collective-permute-done.25.rest_1_ = bf16[368,128]{1,0:T(8,128)(2,1)S(1)} collective-permute-done((bf16[368,128]{1,0:T(8,128)(2,1)S(1)}, bf16[368,128]{1,0:T(8,128)(2,1)S(1)}, u32[]{:S(2)}, u32[]{:S(2)}) %collective-permute-start.25) | collective-permute-done | bytes 94240 | tf_op jit(solution)/shard_map/ppermute | solution.py:279
  66.5 0.4 rows.3
  66.9 1.7 %collective-permute-start.27 = (bf16[368,128]{1,0:T(8,128)(2,1)S(1)}, bf16[368,128]{1,0:T(8,128)(2,1)S(1)}, u32[]{:S(2)}, u32[]{:S(2)}) collective-permute-start(bf16[368,128]{1,0:T(8,128)(2,1)S(1)} %get-tuple-element.93), channel_id=1, source_target_pairs={{0,8},{8,0},{16,24},{24,16},{1,9},{9,1},{17,25},{25,17},{2,10},{10... | collective-permute-start | bytes 282632 | tf_op jit(solution)/shard_map/ppermute | solution.py:279
  68.6 3.4 %collective-permute-start.28 = (bf16[368,128]{1,0:T(8,128)(2,1)S(1)}, bf16[368,128]{1,0:T(8,128)(2,1)S(1)}, u32[]{:S(2)}, u32[]{:S(2)}) collective-permute-start(bf16[368,128]{1,0:T(8,128)(2,1)S(1)} %get-tuple-element.94), channel_id=1, source_target_pairs={{0,16},{8,24},{16,0},{24,8},{1,17},{9,25},{17,1},{25,9},{2,18},{10... | collective-permute-start | bytes 282632 | tf_op jit(solution)/shard_map/ppermute | solution.py:279
  72.0 2.5 %between.1 = (f32[64,64]{1,0:T(8,128)S(1)}, f32[64,64]{1,0:T(8,128)S(1)}, f32[64,576]{1,0:T(8,128)S(1)}) custom-call(f32[64,128]{1,0:T(8,128)S(1)} %get-tuple-element.88.totals, f32[64,64]{1,0:T(8,128)S(1)} %get-tuple-element.89.alpha, f32[64,576]{1,0:T(8,128)S(1)} %bitcast.28), custom_call_target="tpu_custom_call" | custom-call | tf_op jit(solution)/shard_map/between/pallas_call | solution.py:258
  74.6 2.3 %collective-permute-done.28.rest_1_ = bf16[368,128]{1,0:T(8,128)(2,1)S(1)} collective-permute-done((bf16[368,128]{1,0:T(8,128)(2,1)S(1)}, bf16[368,128]{1,0:T(8,128)(2,1)S(1)}, u32[]{:S(2)}, u32[]{:S(2)}) %collective-permute-start.28) | collective-permute-done | bytes 94240 | tf_op jit(solution)/shard_map/ppermute | solution.py:279
  76.8 1.7 %collective-permute-done.29.rest_2_ = bf16[368,128]{1,0:T(8,128)(2,1)S(1)} collective-permute-done((bf16[368,128]{1,0:T(8,128)(2,1)S(1)}, bf16[368,128]{1,0:T(8,128)(2,1)S(1)}, u32[]{:S(2)}, u32[]{:S(2)}) %collective-permute-start.29) | collective-permute-done | bytes 94240 | tf_op jit(solution)/shard_map/ppermute | solution.py:279
  78.5 3.6 %last_step.1 = (f32[64,576]{1,0:T(8,128)}, f32[64,576]{1,0:T(8,128)}) custom-call(f32[64,576]{1,0:T(8,128)S(1)} %get-tuple-element.85.mine, f32[64,128]{1,0:T(8,128)S(1)} %get-tuple-element.86.grams, f32[64,576]{1,0:T(8,128)S(1)} %bitcast.29, f32[64,576]{1,0:T(8,128)S(1)} %get-tuple-element.87.image_in, ...), custom_call_target="tpu_custom_call" | custom-call | tf_op jit(solution)/shard_map/last_step/pallas_call | solution.py:258
  (32 shorter events, 0.1 us)
Async XLA Ops:
  0.6 13.1 %slice-start = ((s8[11796480]{0:T(1024)(128)(4,1)}), s8[4194304]{0:T(1024)(128)(4,1)S(1)}, s32[]{:S(2)}) async-start(s8[11796480]{0:T(1024)(128)(4,1)} %bitcast.17), calls=%async_computation | async-start | bytes 8388608
  0.6 1.1 %copy-start.1 = (f32[1,64,576]{2,1,0:T(8,128)S(1)}, f32[1,64,576]{2,1,0:T(8,128)}, u32[]{:S(2)}) copy-start(f32[1,64,576]{2,1,0:T(8,128)} %param.8) | copy-start | bytes 442372
  1.7 9.6 %copy-start = (bf16[1,576,576]{2,1,0:T(8,128)(2,1)S(1)}, bf16[1,576,576]{2,1,0:T(8,128)(2,1)}, u32[]{:S(2)}) copy-start(bf16[1,576,576]{2,1,0:T(8,128)(2,1)} %param.7) | copy-start | bytes 1990660
  1.7 10.9 %copy-start.3 = (s32[1,1,16]{2,1,0:T(1,128)S(1)}, s32[1,1,16]{2,1,0:T(1,128)}, u32[]{:S(2)}) copy-start(s32[1,1,16]{2,1,0:T(1,128)} %param.10) | copy-start | bytes 196
  1.7 10.9 %copy-start.4 = (s32[1,1,16]{2,1,0:T(1,128)S(1)}, s32[1,1,16]{2,1,0:T(1,128)}, u32[]{:S(2)}) copy-start(s32[1,1,16]{2,1,0:T(1,128)} %param.9) | copy-start | bytes 196
  1.7 12.0 %slice-start.1 = ((s8[11796480]{0:T(1024)(128)(4,1)}), s8[4194304]{0:T(1024)(128)(4,1)S(1)}, s32[]{:S(2)}) async-start(s8[11796480]{0:T(1024)(128)(4,1)} %bitcast.17), calls=%async_computation.1 | async-start | bytes 8388608
  1.7 12.0 %slice-start.2 = ((s8[11796480]{0:T(1024)(128)(4,1)}), s8[3407872]{0:T(1024)(128)(4,1)S(1)}, s32[]{:S(2)}) async-start(s8[11796480]{0:T(1024)(128)(4,1)} %bitcast.17), calls=%async_computation.2 | async-start | bytes 6815744
  1.8 10.5 %collective-permute-start = (bf16[288,128]{1,0:T(8,128)(2,1)S(1)}, bf16[288,128]{1,0:T(8,128)(2,1)S(1)}, u32[]{:S(2)}, u32[]{:S(2)}) collective-permute-start(bf16[288,128]{1,0:T(8,128)(2,1)S(1)} %round.1.near.rest_0_), channel_id=1, source_target_pairs={{0,8},{8,0},{16,24},{24,16},{1,9},{9,1},{17,25},{25,17},{2,10},{10... | collective-permute-start | bytes 221192 | tf_op jit(solution)/shard_map/ppermute | solution.py:279
  4.8 7.8 %collective-permute-start.1 = (bf16[288,128]{1,0:T(8,128)(2,1)S(1)}, bf16[288,128]{1,0:T(8,128)(2,1)S(1)}, u32[]{:S(2)}, u32[]{:S(2)}) collective-permute-start(bf16[288,128]{1,0:T(8,128)(2,1)S(1)} %round.1.near.rest_0_), channel_id=1, source_target_pairs={{0,16},{8,24},{16,0},{24,8},{1,17},{9,25},{17,1},{25,9},{2,18},{10... | collective-permute-start | bytes 221192 | tf_op jit(solution)/shard_map/ppermute | solution.py:279
  7.4 6.3 %collective-permute-start.2 = (bf16[288,128]{1,0:T(8,128)(2,1)S(1)}, bf16[288,128]{1,0:T(8,128)(2,1)S(1)}, u32[]{:S(2)}, u32[]{:S(2)}) collective-permute-start(bf16[288,128]{1,0:T(8,128)(2,1)S(1)} %round.1.near.rest_0_), channel_id=1, source_target_pairs={{0,24},{8,16},{16,8},{24,0},{1,25},{9,17},{17,9},{25,1},{2,26},{10... | collective-permute-start | bytes 221192 | tf_op jit(solution)/shard_map/ppermute | solution.py:279
  7.4 8.0 %collective-permute-start.3 = (bf16[288,128]{1,0:T(8,128)(2,1)S(1)}, bf16[288,128]{1,0:T(8,128)(2,1)S(1)}, u32[]{:S(2)}, u32[]{:S(2)}) collective-permute-start(bf16[288,128]{1,0:T(8,128)(2,1)S(1)} %round.1.near.rest_0_), channel_id=1, source_target_pairs={{0,2},{1,3},{2,0},{3,1},{4,6},{5,7},{6,4},{7,5},{8,10},{9,11},{10,... | collective-permute-start | bytes 221192 | tf_op jit(solution)/shard_map/ppermute | solution.py:279
  9.1 6.3 %collective-permute-start.4 = (bf16[288,128]{1,0:T(8,128)(2,1)S(1)}, bf16[288,128]{1,0:T(8,128)(2,1)S(1)}, u32[]{:S(2)}, u32[]{:S(2)}) collective-permute-start(bf16[288,128]{1,0:T(8,128)(2,1)S(1)} %round.1.near.rest_0_), channel_id=1, source_target_pairs={{0,4},{1,5},{2,6},{3,7},{4,0},{5,1},{6,2},{7,3},{8,12},{9,13},{10,... | collective-permute-start | bytes 221192 | tf_op jit(solution)/shard_map/ppermute | solution.py:279
  12.3 5.3 %collective-permute-start.5 = (bf16[288,128]{1,0:T(8,128)(2,1)S(1)}, bf16[288,128]{1,0:T(8,128)(2,1)S(1)}, u32[]{:S(2)}, u32[]{:S(2)}) collective-permute-start(bf16[288,128]{1,0:T(8,128)(2,1)S(1)} %round.1.near.rest_0_), channel_id=1, source_target_pairs={{0,6},{1,7},{2,4},{3,5},{4,2},{5,3},{6,0},{7,1},{8,14},{9,15},{10,... | collective-permute-start | bytes 221192 | tf_op jit(solution)/shard_map/ppermute | solution.py:279
  17.6 1.6 %collective-permute-start.6 = (bf16[4,64,576]{2,1,0:T(8,128)(2,1)S(1)}, bf16[4,64,576]{2,1,0:T(8,128)(2,1)S(1)}, u32[]{:S(2)}, u32[]{:S(2)}) collective-permute-start(bf16[4,64,576]{2,1,0:T(8,128)(2,1)S(1)} %get-tuple-element.53), channel_id=1, source_target_pairs={{0,1},{1,0},{2,3},{3,2},{4,5},{5,4},{6,7},{7,6},{8,9},{9,8},{10,11... | collective-permute-start | bytes 884744 | tf_op jit(solution)/shard_map/ppermute | solution.py:279
  17.6 7.2 %collective-permute-start.8 = (bf16[4,288,128]{2,1,0:T(8,128)(2,1)S(1)}, bf16[4,288,128]{2,1,0:T(8,128)(2,1)S(1)}, u32[]{:S(2)}, u32[]{:S(2)}) collective-permute-start(bf16[4,288,128]{2,1,0:T(8,128)(2,1)S(1)} %pad_maximum_fusion.near_own), channel_id=1, source_target_pairs={{0,1},{1,0},{2,3},{3,2},{4,5},{5,4},{6,7},{7,6},{8,9},{9,8},{10,11... | collective-permute-start | bytes 884744 | tf_op jit(solution)/shard_map/ppermute | solution.py:279
  19.8 1.3 %collective-permute-start.7 = (f32[64,128]{1,0:T(8,128)S(1)}, f32[64,128]{1,0:T(8,128)S(1)}, u32[]{:S(2)}, u32[]{:S(2)}) collective-permute-start(f32[64,128]{1,0:T(8,128)S(1)} %get-tuple-element.58.grams), channel_id=1, source_target_pairs={{0,1},{1,0},{2,3},{3,2},{4,5},{5,4},{6,7},{7,6},{8,9},{9,8},{10,11... | collective-permute-start | bytes 98312 | tf_op jit(solution)/shard_map/ppermute | solution.py:279
  21.2 5.5 %collective-permute-start.9 = (bf16[368,128]{1,0:T(8,128)(2,1)S(1)}, bf16[368,128]{1,0:T(8,128)(2,1)S(1)}, u32[]{:S(2)}, u32[]{:S(2)}) collective-permute-start(bf16[368,128]{1,0:T(8,128)(2,1)S(1)} %get-tuple-element.61), channel_id=1, source_target_pairs={{0,2},{1,3},{2,0},{3,1},{4,6},{5,7},{6,4},{7,5},{8,10},{9,11},{10,... | collective-permute-start | bytes 282632 | tf_op jit(solution)/shard_map/ppermute | solution.py:279
  21.9 6.6 %collective-permute-start.10 = (bf16[368,128]{1,0:T(8,128)(2,1)S(1)}, bf16[368,128]{1,0:T(8,128)(2,1)S(1)}, u32[]{:S(2)}, u32[]{:S(2)}) collective-permute-start(bf16[368,128]{1,0:T(8,128)(2,1)S(1)} %get-tuple-element.62), channel_id=1, source_target_pairs={{0,4},{1,5},{2,6},{3,7},{4,0},{5,1},{6,2},{7,3},{8,12},{9,13},{10,... | collective-permute-start | bytes 282632 | tf_op jit(solution)/shard_map/ppermute | solution.py:279
  22.2 6.2 %collective-permute-start.11 = (bf16[368,128]{1,0:T(8,128)(2,1)S(1)}, bf16[368,128]{1,0:T(8,128)(2,1)S(1)}, u32[]{:S(2)}, u32[]{:S(2)}) collective-permute-start(bf16[368,128]{1,0:T(8,128)(2,1)S(1)} %get-tuple-element.63), channel_id=1, source_target_pairs={{0,6},{1,7},{2,4},{3,5},{4,2},{5,3},{6,0},{7,1},{8,14},{9,15},{10,... | collective-permute-start | bytes 282632 | tf_op jit(solution)/shard_map/ppermute | solution.py:279
  26.1 15.0 %copy-start.2 = (f32[1,64,576]{2,1,0:T(8,128)S(1)}, f32[1,64,576]{2,1,0:T(8,128)}, u32[]{:S(2)}) copy-start(f32[1,64,576]{2,1,0:T(8,128)} %param.8) | copy-start | bytes 442372
  28.8 5.8 %collective-permute-start.12 = (bf16[368,128]{1,0:T(8,128)(2,1)S(1)}, bf16[368,128]{1,0:T(8,128)(2,1)S(1)}, u32[]{:S(2)}, u32[]{:S(2)}) collective-permute-start(bf16[368,128]{1,0:T(8,128)(2,1)S(1)} %get-tuple-element.66), channel_id=1, source_target_pairs={{0,8},{8,0},{16,24},{24,16},{1,9},{9,1},{17,25},{25,17},{2,10},{10... | collective-permute-start | bytes 282632 | tf_op jit(solution)/shard_map/ppermute | solution.py:279
  30.3 9.4 %collective-permute-start.13 = (bf16[368,128]{1,0:T(8,128)(2,1)S(1)}, bf16[368,128]{1,0:T(8,128)(2,1)S(1)}, u32[]{:S(2)}, u32[]{:S(2)}) collective-permute-start(bf16[368,128]{1,0:T(8,128)(2,1)S(1)} %get-tuple-element.67), channel_id=1, source_target_pairs={{0,16},{8,24},{16,0},{24,8},{1,17},{9,25},{17,1},{25,9},{2,18},{10... | collective-permute-start | bytes 282632 | tf_op jit(solution)/shard_map/ppermute | solution.py:279
  34.6 6.5 %collective-permute-start.14 = (bf16[368,128]{1,0:T(8,128)(2,1)S(1)}, bf16[368,128]{1,0:T(8,128)(2,1)S(1)}, u32[]{:S(2)}, u32[]{:S(2)}) collective-permute-start(bf16[368,128]{1,0:T(8,128)(2,1)S(1)} %get-tuple-element.68), channel_id=1, source_target_pairs={{0,24},{8,16},{16,8},{24,0},{1,25},{9,17},{17,9},{25,1},{2,26},{10... | collective-permute-start | bytes 282632 | tf_op jit(solution)/shard_map/ppermute | solution.py:279
  43.4 6.3 %collective-permute-start.15 = (bf16[288,128]{1,0:T(8,128)(2,1)S(1)}, bf16[288,128]{1,0:T(8,128)(2,1)S(1)}, u32[]{:S(2)}, u32[]{:S(2)}) collective-permute-start(bf16[288,128]{1,0:T(8,128)(2,1)S(1)} %get-tuple-element.69.near.rest_0_), channel_id=1, source_target_pairs={{0,8},{8,0},{16,24},{24,16},{1,9},{9,1},{17,25},{25,17},{2,10},{10... | collective-permute-start | bytes 221192 | tf_op jit(solution)/shard_map/ppermute | solution.py:279
  44.6 7.6 %collective-permute-start.16 = (bf16[288,128]{1,0:T(8,128)(2,1)S(1)}, bf16[288,128]{1,0:T(8,128)(2,1)S(1)}, u32[]{:S(2)}, u32[]{:S(2)}) collective-permute-start(bf16[288,128]{1,0:T(8,128)(2,1)S(1)} %get-tuple-element.69.near.rest_0_), channel_id=1, source_target_pairs={{0,16},{8,24},{16,0},{24,8},{1,17},{9,25},{17,1},{25,9},{2,18},{10... | collective-permute-start | bytes 221192 | tf_op jit(solution)/shard_map/ppermute | solution.py:279
  46.0 6.3 %collective-permute-start.17 = (bf16[288,128]{1,0:T(8,128)(2,1)S(1)}, bf16[288,128]{1,0:T(8,128)(2,1)S(1)}, u32[]{:S(2)}, u32[]{:S(2)}) collective-permute-start(bf16[288,128]{1,0:T(8,128)(2,1)S(1)} %get-tuple-element.69.near.rest_0_), channel_id=1, source_target_pairs={{0,24},{8,16},{16,8},{24,0},{1,25},{9,17},{17,9},{25,1},{2,26},{10... | collective-permute-start | bytes 221192 | tf_op jit(solution)/shard_map/ppermute | solution.py:279
  47.8 6.2 %collective-permute-start.18 = (bf16[288,128]{1,0:T(8,128)(2,1)S(1)}, bf16[288,128]{1,0:T(8,128)(2,1)S(1)}, u32[]{:S(2)}, u32[]{:S(2)}) collective-permute-start(bf16[288,128]{1,0:T(8,128)(2,1)S(1)} %get-tuple-element.69.near.rest_0_), channel_id=1, source_target_pairs={{0,2},{1,3},{2,0},{3,1},{4,6},{5,7},{6,4},{7,5},{8,10},{9,11},{10,... | collective-permute-start | bytes 221192 | tf_op jit(solution)/shard_map/ppermute | solution.py:279
  49.0 5.0 %collective-permute-start.19 = (bf16[288,128]{1,0:T(8,128)(2,1)S(1)}, bf16[288,128]{1,0:T(8,128)(2,1)S(1)}, u32[]{:S(2)}, u32[]{:S(2)}) collective-permute-start(bf16[288,128]{1,0:T(8,128)(2,1)S(1)} %get-tuple-element.69.near.rest_0_), channel_id=1, source_target_pairs={{0,4},{1,5},{2,6},{3,7},{4,0},{5,1},{6,2},{7,3},{8,12},{9,13},{10,... | collective-permute-start | bytes 221192 | tf_op jit(solution)/shard_map/ppermute | solution.py:279
  49.6 5.3 %collective-permute-start.20 = (bf16[288,128]{1,0:T(8,128)(2,1)S(1)}, bf16[288,128]{1,0:T(8,128)(2,1)S(1)}, u32[]{:S(2)}, u32[]{:S(2)}) collective-permute-start(bf16[288,128]{1,0:T(8,128)(2,1)S(1)} %get-tuple-element.69.near.rest_0_), channel_id=1, source_target_pairs={{0,6},{1,7},{2,4},{3,5},{4,2},{5,3},{6,0},{7,1},{8,14},{9,15},{10,... | collective-permute-start | bytes 221192 | tf_op jit(solution)/shard_map/ppermute | solution.py:279
  54.9 1.6 %collective-permute-start.21 = (bf16[4,64,576]{2,1,0:T(8,128)(2,1)S(1)}, bf16[4,64,576]{2,1,0:T(8,128)(2,1)S(1)}, u32[]{:S(2)}, u32[]{:S(2)}) collective-permute-start(bf16[4,64,576]{2,1,0:T(8,128)(2,1)S(1)} %get-tuple-element.74), channel_id=1, source_target_pairs={{0,1},{1,0},{2,3},{3,2},{4,5},{5,4},{6,7},{7,6},{8,9},{9,8},{10,11... | collective-permute-start | bytes 884744 | tf_op jit(solution)/shard_map/ppermute | solution.py:279
  54.9 7.2 %collective-permute-start.23 = (bf16[4,288,128]{2,1,0:T(8,128)(2,1)S(1)}, bf16[4,288,128]{2,1,0:T(8,128)(2,1)S(1)}, u32[]{:S(2)}, u32[]{:S(2)}) collective-permute-start(bf16[4,288,128]{2,1,0:T(8,128)(2,1)S(1)} %pad_maximum_fusion.1.near_own), channel_id=1, source_target_pairs={{0,1},{1,0},{2,3},{3,2},{4,5},{5,4},{6,7},{7,6},{8,9},{9,8},{10,11... | collective-permute-start | bytes 884744 | tf_op jit(solution)/shard_map/ppermute | solution.py:279
  57.1 1.3 %collective-permute-start.22 = (f32[64,128]{1,0:T(8,128)S(1)}, f32[64,128]{1,0:T(8,128)S(1)}, u32[]{:S(2)}, u32[]{:S(2)}) collective-permute-start(f32[64,128]{1,0:T(8,128)S(1)} %get-tuple-element.79.grams), channel_id=1, source_target_pairs={{0,1},{1,0},{2,3},{3,2},{4,5},{5,4},{6,7},{7,6},{8,9},{9,8},{10,11... | collective-permute-start | bytes 98312 | tf_op jit(solution)/shard_map/ppermute | solution.py:279
  58.6 5.1 %collective-permute-start.24 = (bf16[368,128]{1,0:T(8,128)(2,1)S(1)}, bf16[368,128]{1,0:T(8,128)(2,1)S(1)}, u32[]{:S(2)}, u32[]{:S(2)}) collective-permute-start(bf16[368,128]{1,0:T(8,128)(2,1)S(1)} %get-tuple-element.82), channel_id=1, source_target_pairs={{0,2},{1,3},{2,0},{3,1},{4,6},{5,7},{6,4},{7,5},{8,10},{9,11},{10,... | collective-permute-start | bytes 282632 | tf_op jit(solution)/shard_map/ppermute | solution.py:279
  59.9 6.6 %collective-permute-start.25 = (bf16[368,128]{1,0:T(8,128)(2,1)S(1)}, bf16[368,128]{1,0:T(8,128)(2,1)S(1)}, u32[]{:S(2)}, u32[]{:S(2)}) collective-permute-start(bf16[368,128]{1,0:T(8,128)(2,1)S(1)} %get-tuple-element.83), channel_id=1, source_target_pairs={{0,4},{1,5},{2,6},{3,7},{4,0},{5,1},{6,2},{7,3},{8,12},{9,13},{10,... | collective-permute-start | bytes 282632 | tf_op jit(solution)/shard_map/ppermute | solution.py:279
  60.8 5.7 %collective-permute-start.26 = (bf16[368,128]{1,0:T(8,128)(2,1)S(1)}, bf16[368,128]{1,0:T(8,128)(2,1)S(1)}, u32[]{:S(2)}, u32[]{:S(2)}) collective-permute-start(bf16[368,128]{1,0:T(8,128)(2,1)S(1)} %get-tuple-element.84), channel_id=1, source_target_pairs={{0,6},{1,7},{2,4},{3,5},{4,2},{5,3},{6,0},{7,1},{8,14},{9,15},{10,... | collective-permute-start | bytes 282632 | tf_op jit(solution)/shard_map/ppermute | solution.py:279
  66.9 7.6 %collective-permute-start.27 = (bf16[368,128]{1,0:T(8,128)(2,1)S(1)}, bf16[368,128]{1,0:T(8,128)(2,1)S(1)}, u32[]{:S(2)}, u32[]{:S(2)}) collective-permute-start(bf16[368,128]{1,0:T(8,128)(2,1)S(1)} %get-tuple-element.93), channel_id=1, source_target_pairs={{0,8},{8,0},{16,24},{24,16},{1,9},{9,1},{17,25},{25,17},{2,10},{10... | collective-permute-start | bytes 282632 | tf_op jit(solution)/shard_map/ppermute | solution.py:279
  68.6 8.2 %collective-permute-start.28 = (bf16[368,128]{1,0:T(8,128)(2,1)S(1)}, bf16[368,128]{1,0:T(8,128)(2,1)S(1)}, u32[]{:S(2)}, u32[]{:S(2)}) collective-permute-start(bf16[368,128]{1,0:T(8,128)(2,1)S(1)} %get-tuple-element.94), channel_id=1, source_target_pairs={{0,16},{8,24},{16,0},{24,8},{1,17},{9,25},{17,1},{25,9},{2,18},{10... | collective-permute-start | bytes 282632 | tf_op jit(solution)/shard_map/ppermute | solution.py:279
  72.0 6.5 %collective-permute-start.29 = (bf16[368,128]{1,0:T(8,128)(2,1)S(1)}, bf16[368,128]{1,0:T(8,128)(2,1)S(1)}, u32[]{:S(2)}, u32[]{:S(2)}) collective-permute-start(bf16[368,128]{1,0:T(8,128)(2,1)S(1)} %get-tuple-element.95), channel_id=1, source_target_pairs={{0,24},{8,16},{16,8},{24,0},{1,25},{9,17},{17,9},{25,1},{2,26},{10... | collective-permute-start | bytes 282632 | tf_op jit(solution)/shard_map/ppermute | solution.py:279

commit v6 on v5

--- a/solution.py
+++ b/solution.py
@@ -27,39 +27,41 @@
     return lax.dot_general(left, right, dims, preferred_element_type=F32)
 
 
+def split16(value):
+    first = value.astype(BF16)
+    return first, (value - first.astype(F32)).astype(BF16)
+
+
 def dot_exact16(left, right, dims):
-    first = right.astype(BF16)
-    rest = right - first.astype(F32)
-    second = rest.astype(BF16)
-    third = (rest - second.astype(F32)).astype(BF16)
-    return dot16(left, first, dims) + (dot16(left, second, dims) + dot16(left, third, dims))
+    first, second = split16(right)
+    return dot16(left, first, dims) + dot16(left, second, dims)
+
+
+def dot_two(left, right, dims):
+    first, second = split16(left)
+    top, rest = split16(right)
+    return dot16(first, top, dims) + (dot16(first, rest, dims) + dot16(second, top, dims))
 
 
 def eliminate(systems, group=16):
     size, width = systems[0].shape
     rows = lax.broadcasted_iota(jnp.int32, (size, width), 0)
+    scales = [jnp.zeros((size, width), F32) for system in systems]
     for start in range(0, size, group):
-        after = []
-        for system in systems:
+        for at, system in enumerate(systems):
             columns = [
                 jnp.broadcast_to(system[:, k : k + 1], (size, width)) for k in range(start, start + group)
             ]
             for place, k in enumerate(range(start, start + group)):
                 inverse = 1.0 / columns[place][k : k + 1, :]
                 here = rows == k
-                scaled = system[k : k + 1, :] * inverse
+                factors = jnp.where(here, 0.0, columns[place])
+                scales[at] = jnp.where(here, inverse, scales[at])
                 for later in range(place + 1, group):
-                    factor = columns[later][k : k + 1, :] * inverse
-                    columns[later] = jnp.where(here, factor, columns[later] - columns[place] * factor)
-                system = jnp.where(here, scaled, system - columns[place] * scaled)
-            after.append(system)
-        systems = after
-    return [system[:, size:] for system in systems]
-
-
-def split16(value):
-    first = value.astype(BF16)
-    return first, (value - first.astype(F32)).astype(BF16)
+                    columns[later] = columns[later] - factors * (columns[later][k : k + 1, :] * inverse)
+                system = system - factors * (system[k : k + 1, :] * inverse)
+            systems[at] = system
+    return [(system * scale)[:, size:] for system, scale in zip(systems, scales)]
 
 
 def compact(block):
@@ -94,10 +96,12 @@
     return jnp.concatenate([compact(block), parts, last], 0)
 
 
-def unpack(message, size):
-    end = message.shape[0]
-    parts = message[end - 16 - size : end - 16].astype(F32)
-    last = message[end - 16 :].astype(F32)
+def unpack(messages, size):
+    end = messages[0].shape[0]
+    blocks, parts, last = (
+        sum(message[rows].astype(F32) for message in messages)
+        for rows in (slice(0, end - 16 - size), slice(end - 16 - size, end - 16), slice(end - 16, end))
+    )
     both = parts[:, :size] + parts[:, size:]
     diagonal = (last[:, :size] + last[:, size:])[:1]
     rows = lax.broadcasted_iota(jnp.int32, (size, size), 0)
@@ -106,7 +110,7 @@
     first = jnp.where(rows >= columns, both, turned)
     second = jnp.where(rows < columns, both, turned)
     second = jnp.where(rows == columns, diagonal, second)
-    return spread(message[: end - 16 - size], size).astype(F32), jnp.concatenate([first, second], 1)
+    return spread(blocks, size), jnp.concatenate([first, second], 1)
 
 
 def held_slots(count, slots, work):
@@ -120,12 +124,12 @@
     lax.fori_loop(0, (count + group - 1) // group, turn, 0)
 
 
-def places(index, slots, n_row, n_chip):
+def places(rows_list, cols_list, n_chip):
     row, column = lax.axis_index("row"), lax.axis_index("col")
 
     def place(slot):
-        apart = index[1 + slot] ^ column
-        return (apart % 2) * n_chip + apart // 2, index[1 + slots + slot] ^ row
+        apart = rows_list[slot] ^ column
+        return (apart % 2) * n_chip + apart // 2, cols_list[slot] ^ row
 
     return place
 
@@ -134,12 +138,12 @@
     out[...] = compact(value[...].astype(BF16))
 
 
-def forward_kernel(index, tiles, after, *rest, n_row):
+def forward_kernel(counts, rows_list, cols_list, tiles, *rest, n_row):
     far_in = rest[:n_row]
     give_core, acc, far = rest[n_row:]
     n_chip = give_core.shape[0]
     slots = tiles.shape[0]
-    place = places(index, slots, n_row, n_chip)
+    place = places(rows_list, cols_list, n_chip)
     for d, block in enumerate(far_in):
         far[d] = spread(block[...], far.shape[1])
     acc[...] = jnp.zeros_like(acc)
@@ -148,19 +152,19 @@
         i, j = place(slot)
         acc[i] += jnp.where(held, dot16(far[j], tiles[slot], NT), 0.0)
 
-    held_slots(index[0], slots, work)
+    held_slots(counts[0], slots, work)
     for d in range(n_chip):
         give_core[d] = acc[n_chip + d].astype(BF16)
 
 
-def own_kernel(near, diag, residual, own_out, grams):
+def own_kernel(near, diag, residual, after, own_out, grams):
     size = residual.shape[0]
     block = spread(near[...], size)
     own = dot16(block, diag[...], NT)
     own_out[...] = own
     half = 0.5 * dot_exact16(block, own, NT)
     grams[:, :size] = half + half.T
-    grams[:, size:] = dot32(residual[...], residual[...], NT)
+    grams[:, size:] = dot_two(residual[...], residual[...], NT)
 
 
 def gram_kernel(acc, came, grams_own, *rest):
@@ -175,10 +179,10 @@
     grams[:, size:] = grams_own[:, size:]
 
 
-def mirrored_kernel(index, near_own, near_far, tiles, acc, near):
+def mirrored_kernel(counts, rows_list, cols_list, near_own, near_far, tiles, acc, near):
     n_chip = near_own.shape[0]
     slots = tiles.shape[0]
-    place = places(index, slots, acc.shape[0], n_chip)
+    place = places(rows_list, cols_list, n_chip)
     for d in range(n_chip):
         near[d] = spread(near_own[d], near.shape[1])
         near[n_chip + d] = spread(near_far[d], near.shape[1])
@@ -188,7 +192,7 @@
         i, j = place(slot)
         acc[j] += jnp.where(held, dot16(near[i], tiles[slot], NN), 0.0)
 
-    held_slots(index[0], slots, work)
+    held_slots(counts[0], slots, work)
 
 
 def join_kernel(keep, grams, grams_came, grams_out, *give):
@@ -207,12 +211,8 @@
 
 
 def gather_sums(mine, grams, rest, n_in):
-    image, total = mine, grams
-    for message in rest[:n_in]:
-        block, matrices = unpack(message[...], image.shape[0])
-        image += block
-        total += matrices
-    return image, total, rest[n_in:]
+    block, matrices = unpack([message[...] for message in rest[:n_in]], mine.shape[0])
+    return mine + block, grams + matrices, rest[n_in:]
 
 
 def first_kernel(mine, grams, probes, *rest, n_in):
@@ -220,7 +220,7 @@
         mine[...], grams[...], rest, n_in
     )
     (alpha,) = eliminate([total])
-    residual = probes[...] - dot32(alpha, image, TN)
+    residual = probes[...] - dot_two(alpha, image, TN)
     rounded[...] = compact(residual.astype(BF16))
     residual_out[...] = residual
     image_out[...] = image
@@ -237,7 +237,7 @@
     (inverse,) = eliminate([jnp.concatenate([totals[:, size:], eye], 1)])
     inverse_out[...] = inverse
     middle_out[...] = dot32(inverse, dot32(totals[:, :size], inverse, NN), TN)
-    solved_out[...] = dot32(alpha[...], probes[...], TN)
+    solved_out[...] = dot_two(alpha[...], probes[...], TN)
 
 
 def last_kernel(mine, grams, probes, image_in, residual_in, inverse, middle, solved, *rest, n_in):
@@ -247,11 +247,11 @@
     curv = total[:, :size] - dot32(norm, dot32(middle[...], norm, NN), TN)
     beta = dot32(inverse[...], norm, NN)
     residual = residual_in[...]
-    direction = residual + dot32(beta, probes[...], TN)
-    image = forward + dot32(beta, image_in[...], TN)
+    direction = residual + dot_two(beta, probes[...], TN)
+    image = forward + dot_two(beta, image_in[...], TN)
     (step,) = eliminate([jnp.concatenate([curv, norm], 1)])
-    solution_out[...] = solved[...] + dot32(step, direction, TN)
-    residual_out[...] = residual - dot32(step, image, TN)
+    solution_out[...] = solved[...] + dot_two(step, direction, TN)
+    residual_out[...] = residual - dot_two(step, image, TN)
 
 
 def call(kernel, outs, args, specs=None, scratch=(), limit=32, name=None, work=None):
@@ -284,7 +284,7 @@
     def over_rows(value):
         return [over(value, "row", d) for d in range(1, n_row)]
 
-    index = jnp.concatenate([counts[0], rows_list[0, 0], cols_list[0, 0]])
+    index = [counts[0], rows_list[0, 0], cols_list[0, 0]]
     probes = probes[0]
     diag = diag_tiles[0]
     held = tiles[0, 0]
@@ -297,18 +297,20 @@
     def apply_operator(rounded, residual):
         from_rows = over_rows(rounded)
         near = over_chips(rounded)
-        own, grams = call(own_kernel, [block32, square], [rounded, diag, residual], name="own")
         give_core, acc_row = call(
             functools.partial(forward_kernel, n_row=n_row),
             [shape((n_chip, p_size, width), BF16), shape((n_col, p_size, width), F32)],
-            [index, held, grams, rounded, *from_rows],
-            [SMEM, VMEM, ANY] + [VMEM] * n_row,
+            [*index, held, rounded, *from_rows],
+            [SMEM] * 3 + [VMEM] * (1 + n_row),
             [pltpu.VMEM((n_row, p_size, width), BF16)],
             name="forward",
             work=1,
         )
         give_core, *near = lax.optimization_barrier((give_core, *near))
         came = over(give_core, "col", 1)
+        own, grams = call(
+            own_kernel, [block32, square], [rounded, diag, residual, acc_row], [VMEM] * 3 + [ANY], name="own"
+        )
         near_own = jnp.stack([rounded, *near])
         near_far = over(near_own, "col", 1)
         keep, grams = call(
@@ -325,8 +327,8 @@
         (acc_col,) = call(
             mirrored_kernel,
             [shape((n_row, p_size, width), F32)],
-            [index, near_own, near_far, held],
-            [SMEM] + [VMEM] * 3,
+            [*index, near_own, near_far, held],
+            [SMEM] * 3 + [VMEM] * 3,
             [pltpu.VMEM((n_col, p_size, width), BF16)],
             name="mirrored",
             work=passes,

time: 82.3 us -> 81 us (0.984)
  Pallas kernels: 18.9 us -> 17.4 us
    pallas_call x16, Pallas kernels: 18.9 us -> 17.4 us  [call(): pl.pallas_call(kernel, out_shape=outs, in_specs=[VMEM] * len(args) if spe...]
  transfers between devices with their start and end apart: 30 -> 30, of which waited for: 15 -> 16; matrix products, arithmetic and copies ran while one was open for 0% -> 0% of each run, Pallas kernels for 15% -> 14%
where the time goes in v6:
time: 81 us; the launch traced here: 80.9 us
  starting transfers between devices  36.6 us (45%)
  waiting for transfers between devices  24.2 us (30%)
  Pallas kernels  17.4 us (21%)
  between operations  1.51 us (2%)
  local copies, waits for them, and re-layouts  1.09 us (1%)
    ppermute x30, starting transfers between devices, over(): return lax.ppermute(value, axis, [(i, i ^ delta) for i in range(size)])  36.6 us
    ppermute x30, waiting for transfers between devices, over(): return lax.ppermute(value, axis, [(i, i ^ delta) for i in range(size)])  24.2 us
    pallas_call x16, Pallas kernels, call(): pl.pallas_call(kernel, out_shape=outs, in_specs=[VMEM] * len(args) if spe...  17.4 us
  transfers between devices with their start and end apart: 30, of which 16 were waited for; matrix products, arithmetic and copies ran while one was open for 0% of the time, Pallas kernels for 14%

profile of v6, /device:TPU:0, one launch (start us, length us, event | category | flops | bytes accessed | tf_op | source)
XLA Modules:
  0.0 80.9 jit_solution(2506114337020136336)
XLA Ops:
  0.6 0.0 slice-start
  0.6 0.0 copy-start.1
  0.7 1.1 %copy-done.1 = f32[1,64,576]{2,1,0:T(8,128)S(1)} copy-done((f32[1,64,576]{2,1,0:T(8,128)S(1)}, f32[1,64,576]{2,1,0:T(8,128)}, u32[]{:S(2)}) %copy-start.1) | copy-done | bytes 147480
  1.7 0.1 round.1.rest_0_.near
  1.8 3.0 %collective-permute-start = (bf16[288,128]{1,0:T(8,128)(2,1)S(1)}, bf16[288,128]{1,0:T(8,128)(2,1)S(1)}, u32[]{:S(2)}, u32[]{:S(2)}) collective-permute-start(bf16[288,128]{1,0:T(8,128)(2,1)S(1)} %round.1.rest_0_.near), channel_id=1, source_target_pairs={{0,8},{8,0},{16,24},{24,16},{1,9},{9,1},{17,25},{25,17},{2,10},{10... | collective-permute-start | bytes 221192 | tf_op jit(solution)/shard_map/ppermute | solution.py:279
  4.8 2.6 %collective-permute-start.1 = (bf16[288,128]{1,0:T(8,128)(2,1)S(1)}, bf16[288,128]{1,0:T(8,128)(2,1)S(1)}, u32[]{:S(2)}, u32[]{:S(2)}) collective-permute-start(bf16[288,128]{1,0:T(8,128)(2,1)S(1)} %round.1.rest_0_.near), channel_id=1, source_target_pairs={{0,16},{8,24},{16,0},{24,8},{1,17},{9,25},{17,1},{25,9},{2,18},{10... | collective-permute-start | bytes 221192 | tf_op jit(solution)/shard_map/ppermute | solution.py:279
  7.4 1.7 %collective-permute-start.3 = (bf16[288,128]{1,0:T(8,128)(2,1)S(1)}, bf16[288,128]{1,0:T(8,128)(2,1)S(1)}, u32[]{:S(2)}, u32[]{:S(2)}) collective-permute-start(bf16[288,128]{1,0:T(8,128)(2,1)S(1)} %round.1.rest_0_.near), channel_id=1, source_target_pairs={{0,2},{1,3},{2,0},{3,1},{4,6},{5,7},{6,4},{7,5},{8,10},{9,11},{10,... | collective-permute-start | bytes 221192 | tf_op jit(solution)/shard_map/ppermute | solution.py:279
  9.1 1.5 %collective-permute-start.4 = (bf16[288,128]{1,0:T(8,128)(2,1)S(1)}, bf16[288,128]{1,0:T(8,128)(2,1)S(1)}, u32[]{:S(2)}, u32[]{:S(2)}) collective-permute-start(bf16[288,128]{1,0:T(8,128)(2,1)S(1)} %round.1.rest_0_.near), channel_id=1, source_target_pairs={{0,4},{1,5},{2,6},{3,7},{4,0},{5,1},{6,2},{7,3},{8,12},{9,13},{10,... | collective-permute-start | bytes 221192 | tf_op jit(solution)/shard_map/ppermute | solution.py:279
  10.7 0.3 collective-permute-start.5
  11.6 1.0 %collective-permute-done.1.rest_2_ = bf16[288,128]{1,0:T(8,128)(2,1)S(1)} collective-permute-done((bf16[288,128]{1,0:T(8,128)(2,1)S(1)}, bf16[288,128]{1,0:T(8,128)(2,1)S(1)}, u32[]{:S(2)}, u32[]{:S(2)}) %collective-permute-start.1) | collective-permute-done | bytes 73760 | tf_op jit(solution)/shard_map/ppermute | solution.py:279
  12.6 1.1 %collective-permute-done.2.rest_3_ = bf16[288,128]{1,0:T(8,128)(2,1)S(1)} collective-permute-done((bf16[288,128]{1,0:T(8,128)(2,1)S(1)}, bf16[288,128]{1,0:T(8,128)(2,1)S(1)}, u32[]{:S(2)}, u32[]{:S(2)}) %collective-permute-start.2) | collective-permute-done | bytes 73760 | tf_op jit(solution)/shard_map/ppermute | solution.py:279
  13.7 0.0 copy-start
  13.7 0.0 copy-start.2
  13.7 1.7 %forward.2 = (bf16[4,64,576]{2,1,0:T(8,128)(2,1)S(1)}, f32[8,64,576]{2,1,0:T(8,128)S(1)}) custom-call(s32[1]{0:T(128)} %bitcast.16.counts, s32[16]{0:T(128)S(1)} %bitcast.41, s32[16]{0:T(128)S(1)} %bitcast.45, bf16[16,576,576]{2,1,0:T(8,128)(2,1)S(1)} %bitcast.22, bf16[288,128]{1,0:T(8,128)(2,1)S(1)} %round.1.rest_0_.near, ...), custom_call_target="tpu_custom_call" | custom-call | flops 1 | tf_op jit(solution)/shard_map/forward/pallas_call | solution.py:258
  15.4 0.0 collective-permute-done.3.rest_1_
  15.5 0.4 collective-permute-done.5.rest_3_
  16.0 0.6 collective-permute-start.8
  16.5 0.7 own.2
  17.3 0.3 collective-permute-done.6.came
  17.5 0.5 gram.2
  18.0 0.2 collective-permute-start.7
  18.2 1.1 %collective-permute-done.7.grams_came = f32[64,128]{1,0:T(8,128)S(1)} collective-permute-done((f32[64,128]{1,0:T(8,128)S(1)}, f32[64,128]{1,0:T(8,128)S(1)}, u32[]{:S(2)}, u32[]{:S(2)}) %collective-permute-start.7) | collective-permute-done | bytes 32800 | tf_op jit(solution)/shard_map/ppermute | solution.py:279
  19.3 0.2 join.2
  19.5 1.2 %collective-permute-start.9 = (bf16[368,128]{1,0:T(8,128)(2,1)S(1)}, bf16[368,128]{1,0:T(8,128)(2,1)S(1)}, u32[]{:S(2)}, u32[]{:S(2)}) collective-permute-start(bf16[368,128]{1,0:T(8,128)(2,1)S(1)} %get-tuple-element.61), channel_id=1, source_target_pairs={{0,2},{1,3},{2,0},{3,1},{4,6},{5,7},{6,4},{7,5},{8,10},{9,11},{10,... | collective-permute-start | bytes 282632 | tf_op jit(solution)/shard_map/ppermute | solution.py:279
  20.7 1.5 %collective-permute-start.10 = (bf16[368,128]{1,0:T(8,128)(2,1)S(1)}, bf16[368,128]{1,0:T(8,128)(2,1)S(1)}, u32[]{:S(2)}, u32[]{:S(2)}) collective-permute-start(bf16[368,128]{1,0:T(8,128)(2,1)S(1)} %get-tuple-element.62), channel_id=1, source_target_pairs={{0,4},{1,5},{2,6},{3,7},{4,0},{5,1},{6,2},{7,3},{8,12},{9,13},{10,... | collective-permute-start | bytes 282632 | tf_op jit(solution)/shard_map/ppermute | solution.py:279
  22.2 0.8 %collective-permute-start.11 = (bf16[368,128]{1,0:T(8,128)(2,1)S(1)}, bf16[368,128]{1,0:T(8,128)(2,1)S(1)}, u32[]{:S(2)}, u32[]{:S(2)}) collective-permute-start(bf16[368,128]{1,0:T(8,128)(2,1)S(1)} %get-tuple-element.63), channel_id=1, source_target_pairs={{0,6},{1,7},{2,4},{3,5},{4,2},{5,3},{6,0},{7,1},{8,14},{9,15},{10,... | collective-permute-start | bytes 282632 | tf_op jit(solution)/shard_map/ppermute | solution.py:279
  23.0 1.3 %mirrored.2.acc = f32[4,64,576]{2,1,0:T(8,128)S(1)} custom-call(s32[1]{0:T(128)} %bitcast.17.counts, s32[16]{0:T(128)S(1)} %bitcast.42, s32[16]{0:T(128)S(1)} %bitcast.46, bf16[4,288,128]{2,1,0:T(8,128)(2,1)S(1)} %pad_maximum_fusion.near_own, bf16[4,288,128]{2,1,0:T(8,128)(2,1)S(1)} %collective-permute-done.8.near_far, bf16[16,576,576]{2,1,0:T(8,128)(2,1)S(1)} %bitcast.23), custom_call_target="tpu_custom_call" | custom-call | flops 679477248 | tf_op jit(solution)/shard_map/mirrored/pallas_call | solution.py:258
  24.3 0.0 collective-permute-done.9.rest_0_
  24.4 2.0 %collective-permute-done.10.rest_1_ = bf16[368,128]{1,0:T(8,128)(2,1)S(1)} collective-permute-done((bf16[368,128]{1,0:T(8,128)(2,1)S(1)}, bf16[368,128]{1,0:T(8,128)(2,1)S(1)}, u32[]{:S(2)}, u32[]{:S(2)}) %collective-permute-start.10) | collective-permute-done | bytes 94240 | tf_op jit(solution)/shard_map/ppermute | solution.py:279
  26.3 1.3 %collective-permute-done.11.rest_2_ = bf16[368,128]{1,0:T(8,128)(2,1)S(1)} collective-permute-done((bf16[368,128]{1,0:T(8,128)(2,1)S(1)}, bf16[368,128]{1,0:T(8,128)(2,1)S(1)}, u32[]{:S(2)}, u32[]{:S(2)}) %collective-permute-start.11) | collective-permute-done | bytes 94240 | tf_op jit(solution)/shard_map/ppermute | solution.py:279
  27.6 0.4 rows.2
  28.1 2.1 %collective-permute-start.12 = (bf16[368,128]{1,0:T(8,128)(2,1)S(1)}, bf16[368,128]{1,0:T(8,128)(2,1)S(1)}, u32[]{:S(2)}, u32[]{:S(2)}) collective-permute-start(bf16[368,128]{1,0:T(8,128)(2,1)S(1)} %get-tuple-element.66), channel_id=1, source_target_pairs={{0,8},{8,0},{16,24},{24,16},{1,9},{9,1},{17,25},{25,17},{2,10},{10... | collective-permute-start | bytes 282632 | tf_op jit(solution)/shard_map/ppermute | solution.py:279
  30.2 3.7 %collective-permute-start.13 = (bf16[368,128]{1,0:T(8,128)(2,1)S(1)}, bf16[368,128]{1,0:T(8,128)(2,1)S(1)}, u32[]{:S(2)}, u32[]{:S(2)}) collective-permute-start(bf16[368,128]{1,0:T(8,128)(2,1)S(1)} %get-tuple-element.67), channel_id=1, source_target_pairs={{0,16},{8,24},{16,0},{24,8},{1,17},{9,25},{17,1},{25,9},{2,18},{10... | collective-permute-start | bytes 282632 | tf_op jit(solution)/shard_map/ppermute | solution.py:279
  33.9 5.1 %collective-permute-done.13.rest_1_ = bf16[368,128]{1,0:T(8,128)(2,1)S(1)} collective-permute-done((bf16[368,128]{1,0:T(8,128)(2,1)S(1)}, bf16[368,128]{1,0:T(8,128)(2,1)S(1)}, u32[]{:S(2)}, u32[]{:S(2)}) %collective-permute-start.13) | collective-permute-done | bytes 94240 | tf_op jit(solution)/shard_map/ppermute | solution.py:279
  39.0 1.4 %collective-permute-done.14.rest_2_ = bf16[368,128]{1,0:T(8,128)(2,1)S(1)} collective-permute-done((bf16[368,128]{1,0:T(8,128)(2,1)S(1)}, bf16[368,128]{1,0:T(8,128)(2,1)S(1)}, u32[]{:S(2)}, u32[]{:S(2)}) %collective-permute-start.14) | collective-permute-done | bytes 94240 | tf_op jit(solution)/shard_map/ppermute | solution.py:279
  40.4 2.1 %first_step.1 = (f32[64,576]{1,0:T(8,128)S(1)}, f32[64,576]{1,0:T(8,128)S(1)}, bf16[288,128]{1,0:T(8,128)(2,1)S(1)}, f32[64,128]{1,0:T(8,128)S(1)}, f32[64,64]{1,0:T(8,128)S(1)}) custom-call(f32[64,576]{1,0:T(8,128)S(1)} %get-tuple-element.64.mine, f32[64,128]{1,0:T(8,128)S(1)} %get-tuple-element.65.grams, f32[64,576]{1,0:T(8,128)S(1)} %bitcast.30, ...), custom_call_target="tpu_custom_call" | custom-call | tf_op jit(solution)/shard_map/first_step/pallas_call | solution.py:258
  42.5 1.2 %collective-permute-start.15 = (bf16[288,128]{1,0:T(8,128)(2,1)S(1)}, bf16[288,128]{1,0:T(8,128)(2,1)S(1)}, u32[]{:S(2)}, u32[]{:S(2)}) collective-permute-start(bf16[288,128]{1,0:T(8,128)(2,1)S(1)} %get-tuple-element.69.rest_0_.near), channel_id=1, source_target_pairs={{0,8},{8,0},{16,24},{24,16},{1,9},{9,1},{17,25},{25,17},{2,10},{10... | collective-permute-start | bytes 221192 | tf_op jit(solution)/shard_map/ppermute | solution.py:279
  43.7 1.4 %collective-permute-start.16 = (bf16[288,128]{1,0:T(8,128)(2,1)S(1)}, bf16[288,128]{1,0:T(8,128)(2,1)S(1)}, u32[]{:S(2)}, u32[]{:S(2)}) collective-permute-start(bf16[288,128]{1,0:T(8,128)(2,1)S(1)} %get-tuple-element.69.rest_0_.near), channel_id=1, source_target_pairs={{0,16},{8,24},{16,0},{24,8},{1,17},{9,25},{17,1},{25,9},{2,18},{10... | collective-permute-start | bytes 221192 | tf_op jit(solution)/shard_map/ppermute | solution.py:279
  45.2 1.8 %collective-permute-start.17 = (bf16[288,128]{1,0:T(8,128)(2,1)S(1)}, bf16[288,128]{1,0:T(8,128)(2,1)S(1)}, u32[]{:S(2)}, u32[]{:S(2)}) collective-permute-start(bf16[288,128]{1,0:T(8,128)(2,1)S(1)} %get-tuple-element.69.rest_0_.near), channel_id=1, source_target_pairs={{0,24},{8,16},{16,8},{24,0},{1,25},{9,17},{17,9},{25,1},{2,26},{10... | collective-permute-start | bytes 221192 | tf_op jit(solution)/shard_map/ppermute | solution.py:279
  46.9 1.1 %collective-permute-start.18 = (bf16[288,128]{1,0:T(8,128)(2,1)S(1)}, bf16[288,128]{1,0:T(8,128)(2,1)S(1)}, u32[]{:S(2)}, u32[]{:S(2)}) collective-permute-start(bf16[288,128]{1,0:T(8,128)(2,1)S(1)} %get-tuple-element.69.rest_0_.near), channel_id=1, source_target_pairs={{0,2},{1,3},{2,0},{3,1},{4,6},{5,7},{6,4},{7,5},{8,10},{9,11},{10,... | collective-permute-start | bytes 221192 | tf_op jit(solution)/shard_map/ppermute | solution.py:279
  48.1 0.7 collective-permute-start.19
  48.8 1.7 %collective-permute-start.20 = (bf16[288,128]{1,0:T(8,128)(2,1)S(1)}, bf16[288,128]{1,0:T(8,128)(2,1)S(1)}, u32[]{:S(2)}, u32[]{:S(2)}) collective-permute-start(bf16[288,128]{1,0:T(8,128)(2,1)S(1)} %get-tuple-element.69.rest_0_.near), channel_id=1, source_target_pairs={{0,6},{1,7},{2,4},{3,5},{4,2},{5,3},{6,0},{7,1},{8,14},{9,15},{10,... | collective-permute-start | bytes 221192 | tf_op jit(solution)/shard_map/ppermute | solution.py:279
  50.4 1.0 %collective-permute-done.17.rest_3_ = bf16[288,128]{1,0:T(8,128)(2,1)S(1)} collective-permute-done((bf16[288,128]{1,0:T(8,128)(2,1)S(1)}, bf16[288,128]{1,0:T(8,128)(2,1)S(1)}, u32[]{:S(2)}, u32[]{:S(2)}) %collective-permute-start.17) | collective-permute-done | bytes 73760 | tf_op jit(solution)/shard_map/ppermute | solution.py:279
  51.4 1.7 %forward.3 = (bf16[4,64,576]{2,1,0:T(8,128)(2,1)S(1)}, f32[8,64,576]{2,1,0:T(8,128)S(1)}) custom-call(s32[1]{0:T(128)} %bitcast.18.counts, s32[16]{0:T(128)S(1)} %bitcast.43, s32[16]{0:T(128)S(1)} %bitcast.47, bf16[16,576,576]{2,1,0:T(8,128)(2,1)S(1)} %bitcast.24, bf16[288,128]{1,0:T(8,128)(2,1)S(1)} %get-tuple-element.69.rest_0_.near, ...), custom_call_target="tpu_custom_call" | custom-call | flops 1 | tf_op jit(solution)/shard_map/forward/pallas_call | solution.py:258
  53.1 0.9 %collective-permute-done.20.rest_3_ = bf16[288,128]{1,0:T(8,128)(2,1)S(1)} collective-permute-done((bf16[288,128]{1,0:T(8,128)(2,1)S(1)}, bf16[288,128]{1,0:T(8,128)(2,1)S(1)}, u32[]{:S(2)}, u32[]{:S(2)}) %collective-permute-start.20) | collective-permute-done | bytes 73760 | tf_op jit(solution)/shard_map/ppermute | solution.py:279
  54.1 0.6 collective-permute-start.23
  54.6 0.7 own.3
  55.4 0.3 collective-permute-done.21.came
  55.6 0.5 gram.3
  56.1 0.2 collective-permute-start.22
  56.3 1.1 %collective-permute-done.22.grams_came = f32[64,128]{1,0:T(8,128)S(1)} collective-permute-done((f32[64,128]{1,0:T(8,128)S(1)}, f32[64,128]{1,0:T(8,128)S(1)}, u32[]{:S(2)}, u32[]{:S(2)}) %collective-permute-start.22) | collective-permute-done | bytes 32800 | tf_op jit(solution)/shard_map/ppermute | solution.py:279
  57.4 0.2 join.3
  57.6 1.4 %collective-permute-start.24 = (bf16[368,128]{1,0:T(8,128)(2,1)S(1)}, bf16[368,128]{1,0:T(8,128)(2,1)S(1)}, u32[]{:S(2)}, u32[]{:S(2)}) collective-permute-start(bf16[368,128]{1,0:T(8,128)(2,1)S(1)} %get-tuple-element.82), channel_id=1, source_target_pairs={{0,2},{1,3},{2,0},{3,1},{4,6},{5,7},{6,4},{7,5},{8,10},{9,11},{10,... | collective-permute-start | bytes 282632 | tf_op jit(solution)/shard_map/ppermute | solution.py:279
  59.0 0.9 %collective-permute-start.25 = (bf16[368,128]{1,0:T(8,128)(2,1)S(1)}, bf16[368,128]{1,0:T(8,128)(2,1)S(1)}, u32[]{:S(2)}, u32[]{:S(2)}) collective-permute-start(bf16[368,128]{1,0:T(8,128)(2,1)S(1)} %get-tuple-element.83), channel_id=1, source_target_pairs={{0,4},{1,5},{2,6},{3,7},{4,0},{5,1},{6,2},{7,3},{8,12},{9,13},{10,... | collective-permute-start | bytes 282632 | tf_op jit(solution)/shard_map/ppermute | solution.py:279
  59.9 1.3 %collective-permute-start.26 = (bf16[368,128]{1,0:T(8,128)(2,1)S(1)}, bf16[368,128]{1,0:T(8,128)(2,1)S(1)}, u32[]{:S(2)}, u32[]{:S(2)}) collective-permute-start(bf16[368,128]{1,0:T(8,128)(2,1)S(1)} %get-tuple-element.84), channel_id=1, source_target_pairs={{0,6},{1,7},{2,4},{3,5},{4,2},{5,3},{6,0},{7,1},{8,14},{9,15},{10,... | collective-permute-start | bytes 282632 | tf_op jit(solution)/shard_map/ppermute | solution.py:279
  61.1 1.5 %mirrored.3.acc = f32[4,64,576]{2,1,0:T(8,128)S(1)} custom-call(s32[1]{0:T(128)} %bitcast.19.counts, s32[16]{0:T(128)S(1)} %bitcast.44, s32[16]{0:T(128)S(1)} %bitcast.48, bf16[4,288,128]{2,1,0:T(8,128)(2,1)S(1)} %pad_maximum_fusion.1.near_own, bf16[4,288,128]{2,1,0:T(8,128)(2,1)S(1)} %collective-permute-done.23.near_far, bf16[16,576,576]{2,1,0:T(8,128)(2,1)S(1)} %bitcast.25), custom_call_target="tpu_custom_call" | custom-call | flops 679477248 | tf_op jit(solution)/shard_map/mirrored/pallas_call | solution.py:258
  62.6 2.9 %collective-permute-done.25.rest_1_ = bf16[368,128]{1,0:T(8,128)(2,1)S(1)} collective-permute-done((bf16[368,128]{1,0:T(8,128)(2,1)S(1)}, bf16[368,128]{1,0:T(8,128)(2,1)S(1)}, u32[]{:S(2)}, u32[]{:S(2)}) %collective-permute-start.25) | collective-permute-done | bytes 94240 | tf_op jit(solution)/shard_map/ppermute | solution.py:279
  65.6 0.4 rows.3
  66.0 2.0 %collective-permute-start.27 = (bf16[368,128]{1,0:T(8,128)(2,1)S(1)}, bf16[368,128]{1,0:T(8,128)(2,1)S(1)}, u32[]{:S(2)}, u32[]{:S(2)}) collective-permute-start(bf16[368,128]{1,0:T(8,128)(2,1)S(1)} %get-tuple-element.93), channel_id=1, source_target_pairs={{0,8},{8,0},{16,24},{24,16},{1,9},{9,1},{17,25},{25,17},{2,10},{10... | collective-permute-start | bytes 282632 | tf_op jit(solution)/shard_map/ppermute | solution.py:279
  68.0 3.1 %collective-permute-start.28 = (bf16[368,128]{1,0:T(8,128)(2,1)S(1)}, bf16[368,128]{1,0:T(8,128)(2,1)S(1)}, u32[]{:S(2)}, u32[]{:S(2)}) collective-permute-start(bf16[368,128]{1,0:T(8,128)(2,1)S(1)} %get-tuple-element.94), channel_id=1, source_target_pairs={{0,16},{8,24},{16,0},{24,8},{1,17},{9,25},{17,1},{25,9},{2,18},{10... | collective-permute-start | bytes 282632 | tf_op jit(solution)/shard_map/ppermute | solution.py:279
  71.1 2.1 %between.1 = (f32[64,64]{1,0:T(8,128)S(1)}, f32[64,64]{1,0:T(8,128)S(1)}, f32[64,576]{1,0:T(8,128)S(1)}) custom-call(f32[64,128]{1,0:T(8,128)S(1)} %get-tuple-element.88.totals, f32[64,64]{1,0:T(8,128)S(1)} %get-tuple-element.89.alpha, f32[64,576]{1,0:T(8,128)S(1)} %bitcast.31), custom_call_target="tpu_custom_call" | custom-call | tf_op jit(solution)/shard_map/between/pallas_call | solution.py:258
  73.2 2.6 %collective-permute-done.28.rest_1_ = bf16[368,128]{1,0:T(8,128)(2,1)S(1)} collective-permute-done((bf16[368,128]{1,0:T(8,128)(2,1)S(1)}, bf16[368,128]{1,0:T(8,128)(2,1)S(1)}, u32[]{:S(2)}, u32[]{:S(2)}) %collective-permute-start.28) | collective-permute-done | bytes 94240 | tf_op jit(solution)/shard_map/ppermute | solution.py:279
  75.8 1.8 %collective-permute-done.29.rest_2_ = bf16[368,128]{1,0:T(8,128)(2,1)S(1)} collective-permute-done((bf16[368,128]{1,0:T(8,128)(2,1)S(1)}, bf16[368,128]{1,0:T(8,128)(2,1)S(1)}, u32[]{:S(2)}, u32[]{:S(2)}) %collective-permute-start.29) | collective-permute-done | bytes 94240 | tf_op jit(solution)/shard_map/ppermute | solution.py:279
  77.5 3.3 %last_step.1 = (f32[64,576]{1,0:T(8,128)}, f32[64,576]{1,0:T(8,128)}) custom-call(f32[64,576]{1,0:T(8,128)S(1)} %get-tuple-element.85.mine, f32[64,128]{1,0:T(8,128)S(1)} %get-tuple-element.86.grams, f32[64,576]{1,0:T(8,128)S(1)} %bitcast.32, f32[64,576]{1,0:T(8,128)S(1)} %get-tuple-element.87.image_in, ...), custom_call_target="tpu_custom_call" | custom-call | tf_op jit(solution)/shard_map/last_step/pallas_call | solution.py:258
  (31 shorter events, 0.1 us)
Async XLA Ops:
  0.6 13.1 %slice-start = ((s8[11796480]{0:T(1024)(128)(4,1)}), s8[4194304]{0:T(1024)(128)(4,1)S(1)}, s32[]{:S(2)}) async-start(s8[11796480]{0:T(1024)(128)(4,1)} %bitcast.20), calls=%async_computation | async-start | bytes 8388608
  0.6 1.1 %copy-start.1 = (f32[1,64,576]{2,1,0:T(8,128)S(1)}, f32[1,64,576]{2,1,0:T(8,128)}, u32[]{:S(2)}) copy-start(f32[1,64,576]{2,1,0:T(8,128)} %param.8) | copy-start | bytes 442372
  1.7 12.0 %slice-start.1 = ((s8[11796480]{0:T(1024)(128)(4,1)}), s8[4194304]{0:T(1024)(128)(4,1)S(1)}, s32[]{:S(2)}) async-start(s8[11796480]{0:T(1024)(128)(4,1)} %bitcast.20), calls=%async_computation.1 | async-start | bytes 8388608
  1.7 12.0 %slice-start.2 = ((s8[11796480]{0:T(1024)(128)(4,1)}), s8[3407872]{0:T(1024)(128)(4,1)S(1)}, s32[]{:S(2)}) async-start(s8[11796480]{0:T(1024)(128)(4,1)} %bitcast.20), calls=%async_computation.2 | async-start | bytes 6815744
  1.7 12.0 %copy-start.3 = (s32[1,1,16]{2,1,0:T(1,128)S(1)}, s32[1,1,16]{2,1,0:T(1,128)}, u32[]{:S(2)}) copy-start(s32[1,1,16]{2,1,0:T(1,128)} %param.9) | copy-start | bytes 196
  1.7 12.0 %copy-start.4 = (s32[1,1,16]{2,1,0:T(1,128)S(1)}, s32[1,1,16]{2,1,0:T(1,128)}, u32[]{:S(2)}) copy-start(s32[1,1,16]{2,1,0:T(1,128)} %param.10) | copy-start | bytes 196
  1.8 8.9 %collective-permute-start = (bf16[288,128]{1,0:T(8,128)(2,1)S(1)}, bf16[288,128]{1,0:T(8,128)(2,1)S(1)}, u32[]{:S(2)}, u32[]{:S(2)}) collective-permute-start(bf16[288,128]{1,0:T(8,128)(2,1)S(1)} %round.1.rest_0_.near), channel_id=1, source_target_pairs={{0,8},{8,0},{16,24},{24,16},{1,9},{9,1},{17,25},{25,17},{2,10},{10... | collective-permute-start | bytes 221192 | tf_op jit(solution)/shard_map/ppermute | solution.py:279
  4.8 7.8 %collective-permute-start.1 = (bf16[288,128]{1,0:T(8,128)(2,1)S(1)}, bf16[288,128]{1,0:T(8,128)(2,1)S(1)}, u32[]{:S(2)}, u32[]{:S(2)}) collective-permute-start(bf16[288,128]{1,0:T(8,128)(2,1)S(1)} %round.1.rest_0_.near), channel_id=1, source_target_pairs={{0,16},{8,24},{16,0},{24,8},{1,17},{9,25},{17,1},{25,9},{2,18},{10... | collective-permute-start | bytes 221192 | tf_op jit(solution)/shard_map/ppermute | solution.py:279
  7.4 6.3 %collective-permute-start.2 = (bf16[288,128]{1,0:T(8,128)(2,1)S(1)}, bf16[288,128]{1,0:T(8,128)(2,1)S(1)}, u32[]{:S(2)}, u32[]{:S(2)}) collective-permute-start(bf16[288,128]{1,0:T(8,128)(2,1)S(1)} %round.1.rest_0_.near), channel_id=1, source_target_pairs={{0,24},{8,16},{16,8},{24,0},{1,25},{9,17},{17,9},{25,1},{2,26},{10... | collective-permute-start | bytes 221192 | tf_op jit(solution)/shard_map/ppermute | solution.py:279
  7.4 8.0 %collective-permute-start.3 = (bf16[288,128]{1,0:T(8,128)(2,1)S(1)}, bf16[288,128]{1,0:T(8,128)(2,1)S(1)}, u32[]{:S(2)}, u32[]{:S(2)}) collective-permute-start(bf16[288,128]{1,0:T(8,128)(2,1)S(1)} %round.1.rest_0_.near), channel_id=1, source_target_pairs={{0,2},{1,3},{2,0},{3,1},{4,6},{5,7},{6,4},{7,5},{8,10},{9,11},{10,... | collective-permute-start | bytes 221192 | tf_op jit(solution)/shard_map/ppermute | solution.py:279
  9.1 6.3 %collective-permute-start.4 = (bf16[288,128]{1,0:T(8,128)(2,1)S(1)}, bf16[288,128]{1,0:T(8,128)(2,1)S(1)}, u32[]{:S(2)}, u32[]{:S(2)}) collective-permute-start(bf16[288,128]{1,0:T(8,128)(2,1)S(1)} %round.1.rest_0_.near), channel_id=1, source_target_pairs={{0,4},{1,5},{2,6},{3,7},{4,0},{5,1},{6,2},{7,3},{8,12},{9,13},{10,... | collective-permute-start | bytes 221192 | tf_op jit(solution)/shard_map/ppermute | solution.py:279
  10.7 5.3 %collective-permute-start.5 = (bf16[288,128]{1,0:T(8,128)(2,1)S(1)}, bf16[288,128]{1,0:T(8,128)(2,1)S(1)}, u32[]{:S(2)}, u32[]{:S(2)}) collective-permute-start(bf16[288,128]{1,0:T(8,128)(2,1)S(1)} %round.1.rest_0_.near), channel_id=1, source_target_pairs={{0,6},{1,7},{2,4},{3,5},{4,2},{5,3},{6,0},{7,1},{8,14},{9,15},{10,... | collective-permute-start | bytes 221192 | tf_op jit(solution)/shard_map/ppermute | solution.py:279
  13.7 2.8 %copy-start = (bf16[1,576,576]{2,1,0:T(8,128)(2,1)S(1)}, bf16[1,576,576]{2,1,0:T(8,128)(2,1)}, u32[]{:S(2)}) copy-start(bf16[1,576,576]{2,1,0:T(8,128)(2,1)} %param.7) | copy-start | bytes 1990660
  13.7 2.8 %copy-start.2 = (f32[1,64,576]{2,1,0:T(8,128)S(1)}, f32[1,64,576]{2,1,0:T(8,128)}, u32[]{:S(2)}) copy-start(f32[1,64,576]{2,1,0:T(8,128)} %param.8) | copy-start | bytes 442372
  15.9 1.6 %collective-permute-start.6 = (bf16[4,64,576]{2,1,0:T(8,128)(2,1)S(1)}, bf16[4,64,576]{2,1,0:T(8,128)(2,1)S(1)}, u32[]{:S(2)}, u32[]{:S(2)}) collective-permute-start(bf16[4,64,576]{2,1,0:T(8,128)(2,1)S(1)} %get-tuple-element.52), channel_id=1, source_target_pairs={{0,1},{1,0},{2,3},{3,2},{4,5},{5,4},{6,7},{7,6},{8,9},{9,8},{10,11... | collective-permute-start | bytes 884744 | tf_op jit(solution)/shard_map/ppermute | solution.py:279
  16.0 7.1 %collective-permute-start.8 = (bf16[4,288,128]{2,1,0:T(8,128)(2,1)S(1)}, bf16[4,288,128]{2,1,0:T(8,128)(2,1)S(1)}, u32[]{:S(2)}, u32[]{:S(2)}) collective-permute-start(bf16[4,288,128]{2,1,0:T(8,128)(2,1)S(1)} %pad_maximum_fusion.near_own), channel_id=1, source_target_pairs={{0,1},{1,0},{2,3},{3,2},{4,5},{5,4},{6,7},{7,6},{8,9},{9,8},{10,11... | collective-permute-start | bytes 884744 | tf_op jit(solution)/shard_map/ppermute | solution.py:279
  18.0 1.3 %collective-permute-start.7 = (f32[64,128]{1,0:T(8,128)S(1)}, f32[64,128]{1,0:T(8,128)S(1)}, u32[]{:S(2)}, u32[]{:S(2)}) collective-permute-start(f32[64,128]{1,0:T(8,128)S(1)} %get-tuple-element.58.grams), channel_id=1, source_target_pairs={{0,1},{1,0},{2,3},{3,2},{4,5},{5,4},{6,7},{7,6},{8,9},{9,8},{10,11... | collective-permute-start | bytes 98312 | tf_op jit(solution)/shard_map/ppermute | solution.py:279
  19.5 4.9 %collective-permute-start.9 = (bf16[368,128]{1,0:T(8,128)(2,1)S(1)}, bf16[368,128]{1,0:T(8,128)(2,1)S(1)}, u32[]{:S(2)}, u32[]{:S(2)}) collective-permute-start(bf16[368,128]{1,0:T(8,128)(2,1)S(1)} %get-tuple-element.61), channel_id=1, source_target_pairs={{0,2},{1,3},{2,0},{3,1},{4,6},{5,7},{6,4},{7,5},{8,10},{9,11},{10,... | collective-permute-start | bytes 282632 | tf_op jit(solution)/shard_map/ppermute | solution.py:279
  20.7 5.7 %collective-permute-start.10 = (bf16[368,128]{1,0:T(8,128)(2,1)S(1)}, bf16[368,128]{1,0:T(8,128)(2,1)S(1)}, u32[]{:S(2)}, u32[]{:S(2)}) collective-permute-start(bf16[368,128]{1,0:T(8,128)(2,1)S(1)} %get-tuple-element.62), channel_id=1, source_target_pairs={{0,4},{1,5},{2,6},{3,7},{4,0},{5,1},{6,2},{7,3},{8,12},{9,13},{10,... | collective-permute-start | bytes 282632 | tf_op jit(solution)/shard_map/ppermute | solution.py:279
  22.2 5.5 %collective-permute-start.11 = (bf16[368,128]{1,0:T(8,128)(2,1)S(1)}, bf16[368,128]{1,0:T(8,128)(2,1)S(1)}, u32[]{:S(2)}, u32[]{:S(2)}) collective-permute-start(bf16[368,128]{1,0:T(8,128)(2,1)S(1)} %get-tuple-element.63), channel_id=1, source_target_pairs={{0,6},{1,7},{2,4},{3,5},{4,2},{5,3},{6,0},{7,1},{8,14},{9,15},{10,... | collective-permute-start | bytes 282632 | tf_op jit(solution)/shard_map/ppermute | solution.py:279
  28.1 5.9 %collective-permute-start.12 = (bf16[368,128]{1,0:T(8,128)(2,1)S(1)}, bf16[368,128]{1,0:T(8,128)(2,1)S(1)}, u32[]{:S(2)}, u32[]{:S(2)}) collective-permute-start(bf16[368,128]{1,0:T(8,128)(2,1)S(1)} %get-tuple-element.66), channel_id=1, source_target_pairs={{0,8},{8,0},{16,24},{24,16},{1,9},{9,1},{17,25},{25,17},{2,10},{10... | collective-permute-start | bytes 282632 | tf_op jit(solution)/shard_map/ppermute | solution.py:279
  30.2 8.8 %collective-permute-start.13 = (bf16[368,128]{1,0:T(8,128)(2,1)S(1)}, bf16[368,128]{1,0:T(8,128)(2,1)S(1)}, u32[]{:S(2)}, u32[]{:S(2)}) collective-permute-start(bf16[368,128]{1,0:T(8,128)(2,1)S(1)} %get-tuple-element.67), channel_id=1, source_target_pairs={{0,16},{8,24},{16,0},{24,8},{1,17},{9,25},{17,1},{25,9},{2,18},{10... | collective-permute-start | bytes 282632 | tf_op jit(solution)/shard_map/ppermute | solution.py:279
  33.9 6.5 %collective-permute-start.14 = (bf16[368,128]{1,0:T(8,128)(2,1)S(1)}, bf16[368,128]{1,0:T(8,128)(2,1)S(1)}, u32[]{:S(2)}, u32[]{:S(2)}) collective-permute-start(bf16[368,128]{1,0:T(8,128)(2,1)S(1)} %get-tuple-element.68), channel_id=1, source_target_pairs={{0,24},{8,16},{16,8},{24,0},{1,25},{9,17},{17,9},{25,1},{2,26},{10... | collective-permute-start | bytes 282632 | tf_op jit(solution)/shard_map/ppermute | solution.py:279
  42.5 6.2 %collective-permute-start.15 = (bf16[288,128]{1,0:T(8,128)(2,1)S(1)}, bf16[288,128]{1,0:T(8,128)(2,1)S(1)}, u32[]{:S(2)}, u32[]{:S(2)}) collective-permute-start(bf16[288,128]{1,0:T(8,128)(2,1)S(1)} %get-tuple-element.69.rest_0_.near), channel_id=1, source_target_pairs={{0,8},{8,0},{16,24},{24,16},{1,9},{9,1},{17,25},{25,17},{2,10},{10... | collective-permute-start | bytes 221192 | tf_op jit(solution)/shard_map/ppermute | solution.py:279
  43.7 6.7 %collective-permute-start.16 = (bf16[288,128]{1,0:T(8,128)(2,1)S(1)}, bf16[288,128]{1,0:T(8,128)(2,1)S(1)}, u32[]{:S(2)}, u32[]{:S(2)}) collective-permute-start(bf16[288,128]{1,0:T(8,128)(2,1)S(1)} %get-tuple-element.69.rest_0_.near), channel_id=1, source_target_pairs={{0,16},{8,24},{16,0},{24,8},{1,17},{9,25},{17,1},{25,9},{2,18},{10... | collective-permute-start | bytes 221192 | tf_op jit(solution)/shard_map/ppermute | solution.py:279
  45.2 6.3 %collective-permute-start.17 = (bf16[288,128]{1,0:T(8,128)(2,1)S(1)}, bf16[288,128]{1,0:T(8,128)(2,1)S(1)}, u32[]{:S(2)}, u32[]{:S(2)}) collective-permute-start(bf16[288,128]{1,0:T(8,128)(2,1)S(1)} %get-tuple-element.69.rest_0_.near), channel_id=1, source_target_pairs={{0,24},{8,16},{16,8},{24,0},{1,25},{9,17},{17,9},{25,1},{2,26},{10... | collective-permute-start | bytes 221192 | tf_op jit(solution)/shard_map/ppermute | solution.py:279
  46.9 6.2 %collective-permute-start.18 = (bf16[288,128]{1,0:T(8,128)(2,1)S(1)}, bf16[288,128]{1,0:T(8,128)(2,1)S(1)}, u32[]{:S(2)}, u32[]{:S(2)}) collective-permute-start(bf16[288,128]{1,0:T(8,128)(2,1)S(1)} %get-tuple-element.69.rest_0_.near), channel_id=1, source_target_pairs={{0,2},{1,3},{2,0},{3,1},{4,6},{5,7},{6,4},{7,5},{8,10},{9,11},{10,... | collective-permute-start | bytes 221192 | tf_op jit(solution)/shard_map/ppermute | solution.py:279
  48.1 5.1 %collective-permute-start.19 = (bf16[288,128]{1,0:T(8,128)(2,1)S(1)}, bf16[288,128]{1,0:T(8,128)(2,1)S(1)}, u32[]{:S(2)}, u32[]{:S(2)}) collective-permute-start(bf16[288,128]{1,0:T(8,128)(2,1)S(1)} %get-tuple-element.69.rest_0_.near), channel_id=1, source_target_pairs={{0,4},{1,5},{2,6},{3,7},{4,0},{5,1},{6,2},{7,3},{8,12},{9,13},{10,... | collective-permute-start | bytes 221192 | tf_op jit(solution)/shard_map/ppermute | solution.py:279
  48.8 5.3 %collective-permute-start.20 = (bf16[288,128]{1,0:T(8,128)(2,1)S(1)}, bf16[288,128]{1,0:T(8,128)(2,1)S(1)}, u32[]{:S(2)}, u32[]{:S(2)}) collective-permute-start(bf16[288,128]{1,0:T(8,128)(2,1)S(1)} %get-tuple-element.69.rest_0_.near), channel_id=1, source_target_pairs={{0,6},{1,7},{2,4},{3,5},{4,2},{5,3},{6,0},{7,1},{8,14},{9,15},{10,... | collective-permute-start | bytes 221192 | tf_op jit(solution)/shard_map/ppermute | solution.py:279
  54.0 1.6 %collective-permute-start.21 = (bf16[4,64,576]{2,1,0:T(8,128)(2,1)S(1)}, bf16[4,64,576]{2,1,0:T(8,128)(2,1)S(1)}, u32[]{:S(2)}, u32[]{:S(2)}) collective-permute-start(bf16[4,64,576]{2,1,0:T(8,128)(2,1)S(1)} %get-tuple-element.72), channel_id=1, source_target_pairs={{0,1},{1,0},{2,3},{3,2},{4,5},{5,4},{6,7},{7,6},{8,9},{9,8},{10,11... | collective-permute-start | bytes 884744 | tf_op jit(solution)/shard_map/ppermute | solution.py:279
  54.1 7.1 %collective-permute-start.23 = (bf16[4,288,128]{2,1,0:T(8,128)(2,1)S(1)}, bf16[4,288,128]{2,1,0:T(8,128)(2,1)S(1)}, u32[]{:S(2)}, u32[]{:S(2)}) collective-permute-start(bf16[4,288,128]{2,1,0:T(8,128)(2,1)S(1)} %pad_maximum_fusion.1.near_own), channel_id=1, source_target_pairs={{0,1},{1,0},{2,3},{3,2},{4,5},{5,4},{6,7},{7,6},{8,9},{9,8},{10,11... | collective-permute-start | bytes 884744 | tf_op jit(solution)/shard_map/ppermute | solution.py:279
  56.1 1.3 %collective-permute-start.22 = (f32[64,128]{1,0:T(8,128)S(1)}, f32[64,128]{1,0:T(8,128)S(1)}, u32[]{:S(2)}, u32[]{:S(2)}) collective-permute-start(f32[64,128]{1,0:T(8,128)S(1)} %get-tuple-element.79.grams), channel_id=1, source_target_pairs={{0,1},{1,0},{2,3},{3,2},{4,5},{5,4},{6,7},{7,6},{8,9},{9,8},{10,11... | collective-permute-start | bytes 98312 | tf_op jit(solution)/shard_map/ppermute | solution.py:279
  57.6 5.1 %collective-permute-start.24 = (bf16[368,128]{1,0:T(8,128)(2,1)S(1)}, bf16[368,128]{1,0:T(8,128)(2,1)S(1)}, u32[]{:S(2)}, u32[]{:S(2)}) collective-permute-start(bf16[368,128]{1,0:T(8,128)(2,1)S(1)} %get-tuple-element.82), channel_id=1, source_target_pairs={{0,2},{1,3},{2,0},{3,1},{4,6},{5,7},{6,4},{7,5},{8,10},{9,11},{10,... | collective-permute-start | bytes 282632 | tf_op jit(solution)/shard_map/ppermute | solution.py:279
  59.0 6.6 %collective-permute-start.25 = (bf16[368,128]{1,0:T(8,128)(2,1)S(1)}, bf16[368,128]{1,0:T(8,128)(2,1)S(1)}, u32[]{:S(2)}, u32[]{:S(2)}) collective-permute-start(bf16[368,128]{1,0:T(8,128)(2,1)S(1)} %get-tuple-element.83), channel_id=1, source_target_pairs={{0,4},{1,5},{2,6},{3,7},{4,0},{5,1},{6,2},{7,3},{8,12},{9,13},{10,... | collective-permute-start | bytes 282632 | tf_op jit(solution)/shard_map/ppermute | solution.py:279
  59.9 5.7 %collective-permute-start.26 = (bf16[368,128]{1,0:T(8,128)(2,1)S(1)}, bf16[368,128]{1,0:T(8,128)(2,1)S(1)}, u32[]{:S(2)}, u32[]{:S(2)}) collective-permute-start(bf16[368,128]{1,0:T(8,128)(2,1)S(1)} %get-tuple-element.84), channel_id=1, source_target_pairs={{0,6},{1,7},{2,4},{3,5},{4,2},{5,3},{6,0},{7,1},{8,14},{9,15},{10,... | collective-permute-start | bytes 282632 | tf_op jit(solution)/shard_map/ppermute | solution.py:279
  66.0 7.2 %collective-permute-start.27 = (bf16[368,128]{1,0:T(8,128)(2,1)S(1)}, bf16[368,128]{1,0:T(8,128)(2,1)S(1)}, u32[]{:S(2)}, u32[]{:S(2)}) collective-permute-start(bf16[368,128]{1,0:T(8,128)(2,1)S(1)} %get-tuple-element.93), channel_id=1, source_target_pairs={{0,8},{8,0},{16,24},{24,16},{1,9},{9,1},{17,25},{25,17},{2,10},{10... | collective-permute-start | bytes 282632 | tf_op jit(solution)/shard_map/ppermute | solution.py:279
  68.0 7.8 %collective-permute-start.28 = (bf16[368,128]{1,0:T(8,128)(2,1)S(1)}, bf16[368,128]{1,0:T(8,128)(2,1)S(1)}, u32[]{:S(2)}, u32[]{:S(2)}) collective-permute-start(bf16[368,128]{1,0:T(8,128)(2,1)S(1)} %get-tuple-element.94), channel_id=1, source_target_pairs={{0,16},{8,24},{16,0},{24,8},{1,17},{9,25},{17,1},{25,9},{2,18},{10... | collective-permute-start | bytes 282632 | tf_op jit(solution)/shard_map/ppermute | solution.py:279
  71.1 6.5 %collective-permute-start.29 = (bf16[368,128]{1,0:T(8,128)(2,1)S(1)}, bf16[368,128]{1,0:T(8,128)(2,1)S(1)}, u32[]{:S(2)}, u32[]{:S(2)}) collective-permute-start(bf16[368,128]{1,0:T(8,128)(2,1)S(1)} %get-tuple-element.95), channel_id=1, source_target_pairs={{0,24},{8,16},{16,8},{24,0},{1,25},{9,17},{17,9},{25,1},{2,26},{10... | collective-permute-start | bytes 282632 | tf_op jit(solution)/shard_map/ppermute | solution.py:279

commit v7 on v6

--- a/solution.py
+++ b/solution.py
@@ -138,7 +138,14 @@
     out[...] = compact(value[...].astype(BF16))
 
 
-def forward_kernel(counts, rows_list, cols_list, tiles, *rest, n_row):
+def turn_kernel(counts, tiles, after, out):
+    def work(slot, held):
+        out[slot] = tiles[slot].T
+
+    held_slots(counts[0], tiles.shape[0], work)
+
+
+def forward_kernel(counts, rows_list, cols_list, tiles, *rest, n_row, dims):
     far_in = rest[:n_row]
     give_core, acc, far = rest[n_row:]
     n_chip = give_core.shape[0]
@@ -150,7 +157,7 @@
 
     def work(slot, held):
         i, j = place(slot)
-        acc[i] += jnp.where(held, dot16(far[j], tiles[slot], NT), 0.0)
+        acc[i] += jnp.where(held, dot16(far[j], tiles[slot], dims), 0.0)
 
     held_slots(counts[0], slots, work)
     for d in range(n_chip):
@@ -254,7 +261,7 @@
     residual_out[...] = residual - dot_two(step, image, TN)
 
 
-def call(kernel, outs, args, specs=None, scratch=(), limit=32, name=None, work=None):
+def call(kernel, outs, args, specs=None, scratch=(), limit=24, name=None, work=None):
     return pl.pallas_call(
         kernel,
         out_shape=outs,
@@ -294,13 +301,13 @@
 
     message = shape((block16.shape[0] + p_size + 16, 128), BF16)
 
-    def apply_operator(rounded, residual):
+    def apply_operator(rounded, residual, turned=None):
         from_rows = over_rows(rounded)
         near = over_chips(rounded)
         give_core, acc_row = call(
-            functools.partial(forward_kernel, n_row=n_row),
+            functools.partial(forward_kernel, n_row=n_row, dims=NT if turned is None else NN),
             [shape((n_chip, p_size, width), BF16), shape((n_col, p_size, width), F32)],
-            [*index, held, rounded, *from_rows],
+            [*index, held if turned is None else turned, rounded, *from_rows],
             [SMEM] * 3 + [VMEM] * (1 + n_row),
             [pltpu.VMEM((n_row, p_size, width), BF16)],
             name="forward",
@@ -339,11 +346,22 @@
             [keep, grams, own, acc_col, *parts],
             name="rows",
         )
-        return mine, grams, [over(block, "row", d + 1) for d, block in enumerate(give)]
+        parts = [over(block, "row", d + 1) for d, block in enumerate(give)]
+        if turned is None:
+            (turned,) = call(
+                turn_kernel,
+                [shape(held.shape, BF16)],
+                [index[0], held, grams],
+                [SMEM, VMEM, ANY],
+                name="turn",
+                limit=28,
+            )
+            turned, *parts = lax.optimization_barrier((turned, *parts))
+        return mine, grams, parts, turned
 
     small = shape((p_size, p_size), F32)
     (rounded,) = call(round_kernel, [block16], [probes], name="round", work=START)
-    mine, grams, parts = apply_operator(rounded, probes)
+    mine, grams, parts, turned = apply_operator(rounded, probes)
     image, residual, rounded, totals, alpha = call(
         functools.partial(first_kernel, n_in=n_row - 1),
         [block32, block32, block16, square, small],
@@ -353,7 +371,7 @@
     inverse, middle, solved = call(
         between_kernel, [small, small, block32], [totals, alpha, probes], name="between"
     )
-    mine, grams, parts = apply_operator(rounded, residual)
+    mine, grams, parts, turned = apply_operator(rounded, residual, turned)
     solved, residual = call(
         functools.partial(last_kernel, n_in=n_row - 1),
         [block32, block32],

time: 81 us -> 79.4 us (0.980)
  waiting for transfers between devices: 24.2 us -> 22.9 us
    ppermute x30, waiting for transfers between devices: 24.2 us -> 22.9 us  [over(): return lax.ppermute(value, axis, [(i, i ^ delta) for i in range(size)])]
    pallas_call x16 -> x17, Pallas kernels: 17.4 us -> 17.9 us  [call(): pl.pallas_call(kernel, out_shape=outs, in_specs=[VMEM] * len(args) if spe...]
  transfers between devices with their start and end apart: 30 -> 30, of which waited for: 16 -> 16; matrix products, arithmetic and copies ran while one was open for 0% -> 0% of each run, Pallas kernels for 14% -> 15%
where the time goes in v7:
time: 79.4 us; the launch traced here: 79.2 us
  starting transfers between devices  36 us (45%)
  waiting for transfers between devices  22.9 us (29%)
  Pallas kernels  17.9 us (23%)
  between operations  1.47 us (2%)
  local copies, waits for them, and re-layouts  0.93 us (1%)
    ppermute x30, starting transfers between devices, over(): return lax.ppermute(value, axis, [(i, i ^ delta) for i in range(size)])  36 us
    ppermute x30, waiting for transfers between devices, over(): return lax.ppermute(value, axis, [(i, i ^ delta) for i in range(size)])  22.9 us
    pallas_call x17, Pallas kernels, call(): pl.pallas_call(kernel, out_shape=outs, in_specs=[VMEM] * len(args) if spe...  17.9 us
  transfers between devices with their start and end apart: 30, of which 16 were waited for; matrix products, arithmetic and copies ran while one was open for 0% of the time, Pallas kernels for 15%

profile of v7, /device:TPU:0, one launch (start us, length us, event | category | flops | bytes accessed | tf_op | source)
XLA Modules:
  0.0 79.2 jit_solution(9244273086573380131)
XLA Ops:
  0.6 0.0 copy-start.2
  0.6 0.9 %copy-done.2 = f32[1,64,576]{2,1,0:T(8,128)S(1)} copy-done((f32[1,64,576]{2,1,0:T(8,128)S(1)}, f32[1,64,576]{2,1,0:T(8,128)}, u32[]{:S(2)}) %copy-start.2) | copy-done | bytes 147480
  1.6 0.1 round.1.rest_0_.near
  1.6 3.1 %collective-permute-start = (bf16[288,128]{1,0:T(8,128)(2,1)S(1)}, bf16[288,128]{1,0:T(8,128)(2,1)S(1)}, u32[]{:S(2)}, u32[]{:S(2)}) collective-permute-start(bf16[288,128]{1,0:T(8,128)(2,1)S(1)} %round.1.rest_0_.near), channel_id=1, source_target_pairs={{0,8},{8,0},{16,24},{24,16},{1,9},{9,1},{17,25},{25,17},{2,10},{10... | collective-permute-start | bytes 221192 | tf_op jit(solution)/shard_map/ppermute | solution.py:286
  4.7 2.6 %collective-permute-start.1 = (bf16[288,128]{1,0:T(8,128)(2,1)S(1)}, bf16[288,128]{1,0:T(8,128)(2,1)S(1)}, u32[]{:S(2)}, u32[]{:S(2)}) collective-permute-start(bf16[288,128]{1,0:T(8,128)(2,1)S(1)} %round.1.rest_0_.near), channel_id=1, source_target_pairs={{0,16},{8,24},{16,0},{24,8},{1,17},{9,25},{17,1},{25,9},{2,18},{10... | collective-permute-start | bytes 221192 | tf_op jit(solution)/shard_map/ppermute | solution.py:286
  7.3 0.0 collective-permute-start.2
  7.3 1.7 %collective-permute-start.3 = (bf16[288,128]{1,0:T(8,128)(2,1)S(1)}, bf16[288,128]{1,0:T(8,128)(2,1)S(1)}, u32[]{:S(2)}, u32[]{:S(2)}) collective-permute-start(bf16[288,128]{1,0:T(8,128)(2,1)S(1)} %round.1.rest_0_.near), channel_id=1, source_target_pairs={{0,2},{1,3},{2,0},{3,1},{4,6},{5,7},{6,4},{7,5},{8,10},{9,11},{10,... | collective-permute-start | bytes 221192 | tf_op jit(solution)/shard_map/ppermute | solution.py:286
  9.0 1.5 %collective-permute-start.4 = (bf16[288,128]{1,0:T(8,128)(2,1)S(1)}, bf16[288,128]{1,0:T(8,128)(2,1)S(1)}, u32[]{:S(2)}, u32[]{:S(2)}) collective-permute-start(bf16[288,128]{1,0:T(8,128)(2,1)S(1)} %round.1.rest_0_.near), channel_id=1, source_target_pairs={{0,4},{1,5},{2,6},{3,7},{4,0},{5,1},{6,2},{7,3},{8,12},{9,13},{10,... | collective-permute-start | bytes 221192 | tf_op jit(solution)/shard_map/ppermute | solution.py:286
  10.5 0.3 collective-permute-start.5
  11.4 1.0 %collective-permute-done.1.rest_2_ = bf16[288,128]{1,0:T(8,128)(2,1)S(1)} collective-permute-done((bf16[288,128]{1,0:T(8,128)(2,1)S(1)}, bf16[288,128]{1,0:T(8,128)(2,1)S(1)}, u32[]{:S(2)}, u32[]{:S(2)}) %collective-permute-start.1) | collective-permute-done | bytes 73760 | tf_op jit(solution)/shard_map/ppermute | solution.py:286
  12.5 1.1 %collective-permute-done.2.rest_3_ = bf16[288,128]{1,0:T(8,128)(2,1)S(1)} collective-permute-done((bf16[288,128]{1,0:T(8,128)(2,1)S(1)}, bf16[288,128]{1,0:T(8,128)(2,1)S(1)}, u32[]{:S(2)}, u32[]{:S(2)}) %collective-permute-start.2) | collective-permute-done | bytes 73760 | tf_op jit(solution)/shard_map/ppermute | solution.py:286
  13.6 1.7 %forward.2 = (bf16[4,64,576]{2,1,0:T(8,128)(2,1)S(1)}, f32[8,64,576]{2,1,0:T(8,128)S(1)}) custom-call(s32[1]{0:T(128)} %bitcast.16.counts, s32[16]{0:T(128)S(1)} %bitcast.40, s32[16]{0:T(128)S(1)} %bitcast.44, bf16[16,576,576]{2,1,0:T(8,128)(2,1)S(1)} %bitcast.21, bf16[288,128]{1,0:T(8,128)(2,1)S(1)} %round.1.rest_0_.near, ...), custom_call_target="tpu_custom_call" | custom-call | flops 1 | tf_op jit(solution)/shard_map/forward/pallas_call | solution.py:265
  15.3 0.0 collective-permute-done.4.rest_2_
  15.3 0.5 collective-permute-done.5.rest_3_
  15.8 0.6 collective-permute-start.8
  16.4 0.7 own.2
  17.1 0.3 collective-permute-done.6.came
  17.4 0.5 gram.2
  17.9 0.2 collective-permute-start.7
  18.1 1.1 %collective-permute-done.7.grams_came = f32[64,128]{1,0:T(8,128)S(1)} collective-permute-done((f32[64,128]{1,0:T(8,128)S(1)}, f32[64,128]{1,0:T(8,128)S(1)}, u32[]{:S(2)}, u32[]{:S(2)}) %collective-permute-start.7) | collective-permute-done | bytes 32800 | tf_op jit(solution)/shard_map/ppermute | solution.py:286
  19.2 0.2 join.2
  19.3 1.1 %collective-permute-start.9 = (bf16[368,128]{1,0:T(8,128)(2,1)S(1)}, bf16[368,128]{1,0:T(8,128)(2,1)S(1)}, u32[]{:S(2)}, u32[]{:S(2)}) collective-permute-start(bf16[368,128]{1,0:T(8,128)(2,1)S(1)} %get-tuple-element.65), channel_id=1, source_target_pairs={{0,2},{1,3},{2,0},{3,1},{4,6},{5,7},{6,4},{7,5},{8,10},{9,11},{10,... | collective-permute-start | bytes 282632 | tf_op jit(solution)/shard_map/ppermute | solution.py:286
  20.4 1.5 %collective-permute-start.10 = (bf16[368,128]{1,0:T(8,128)(2,1)S(1)}, bf16[368,128]{1,0:T(8,128)(2,1)S(1)}, u32[]{:S(2)}, u32[]{:S(2)}) collective-permute-start(bf16[368,128]{1,0:T(8,128)(2,1)S(1)} %get-tuple-element.66), channel_id=1, source_target_pairs={{0,4},{1,5},{2,6},{3,7},{4,0},{5,1},{6,2},{7,3},{8,12},{9,13},{10,... | collective-permute-start | bytes 282632 | tf_op jit(solution)/shard_map/ppermute | solution.py:286
  22.0 0.9 %collective-permute-start.11 = (bf16[368,128]{1,0:T(8,128)(2,1)S(1)}, bf16[368,128]{1,0:T(8,128)(2,1)S(1)}, u32[]{:S(2)}, u32[]{:S(2)}) collective-permute-start(bf16[368,128]{1,0:T(8,128)(2,1)S(1)} %get-tuple-element.67), channel_id=1, source_target_pairs={{0,6},{1,7},{2,4},{3,5},{4,2},{5,3},{6,0},{7,1},{8,14},{9,15},{10,... | collective-permute-start | bytes 282632 | tf_op jit(solution)/shard_map/ppermute | solution.py:286
  22.9 1.3 %mirrored.2.acc = f32[4,64,576]{2,1,0:T(8,128)S(1)} custom-call(s32[1]{0:T(128)} %bitcast.17.counts, s32[16]{0:T(128)S(1)} %bitcast.41, s32[16]{0:T(128)S(1)} %bitcast.45, bf16[4,288,128]{2,1,0:T(8,128)(2,1)S(1)} %pad_maximum_fusion.near_own, bf16[4,288,128]{2,1,0:T(8,128)(2,1)S(1)} %collective-permute-done.8.near_far, bf16[16,576,576]{2,1,0:T(8,128)(2,1)S(1)} %bitcast.22), custom_call_target="tpu_custom_call" | custom-call | flops 679477248 | tf_op jit(solution)/shard_map/mirrored/pallas_call | solution.py:265
  24.2 0.0 collective-permute-done.9.rest_0_
  24.2 1.9 %collective-permute-done.10.rest_1_ = bf16[368,128]{1,0:T(8,128)(2,1)S(1)} collective-permute-done((bf16[368,128]{1,0:T(8,128)(2,1)S(1)}, bf16[368,128]{1,0:T(8,128)(2,1)S(1)}, u32[]{:S(2)}, u32[]{:S(2)}) %collective-permute-start.10) | collective-permute-done | bytes 94240 | tf_op jit(solution)/shard_map/ppermute | solution.py:286
  26.1 1.3 %collective-permute-done.11.rest_2_ = bf16[368,128]{1,0:T(8,128)(2,1)S(1)} collective-permute-done((bf16[368,128]{1,0:T(8,128)(2,1)S(1)}, bf16[368,128]{1,0:T(8,128)(2,1)S(1)}, u32[]{:S(2)}, u32[]{:S(2)}) %collective-permute-start.11) | collective-permute-done | bytes 94240 | tf_op jit(solution)/shard_map/ppermute | solution.py:286
  27.4 0.4 rows.2
  27.9 2.1 %collective-permute-start.12 = (bf16[368,128]{1,0:T(8,128)(2,1)S(1)}, bf16[368,128]{1,0:T(8,128)(2,1)S(1)}, u32[]{:S(2)}, u32[]{:S(2)}) collective-permute-start(bf16[368,128]{1,0:T(8,128)(2,1)S(1)} %get-tuple-element.69), channel_id=1, source_target_pairs={{0,8},{8,0},{16,24},{24,16},{1,9},{9,1},{17,25},{25,17},{2,10},{10... | collective-permute-start | bytes 282632 | tf_op jit(solution)/shard_map/ppermute | solution.py:286
  30.0 3.7 %collective-permute-start.13 = (bf16[368,128]{1,0:T(8,128)(2,1)S(1)}, bf16[368,128]{1,0:T(8,128)(2,1)S(1)}, u32[]{:S(2)}, u32[]{:S(2)}) collective-permute-start(bf16[368,128]{1,0:T(8,128)(2,1)S(1)} %get-tuple-element.70), channel_id=1, source_target_pairs={{0,16},{8,24},{16,0},{24,8},{1,17},{9,25},{17,1},{25,9},{2,18},{10... | collective-permute-start | bytes 282632 | tf_op jit(solution)/shard_map/ppermute | solution.py:286
  33.7 0.9 %turn.1.tiles = bf16[16,576,576]{2,1,0:T(8,128)(2,1)S(1)} custom-call(s32[1]{0:T(128)} %bitcast.18.counts, bf16[16,576,576]{2,1,0:T(8,128)(2,1)S(1)} %bitcast.23, f32[64,128]{1,0:T(8,128)S(1)} %get-tuple-element.68.after.grams), custom_call_target="tpu_custom_call" | custom-call | tf_op jit(solution)/shard_map/turn/pallas_call | solution.py:265
  34.6 4.2 %collective-permute-done.13.rest_1_ = bf16[368,128]{1,0:T(8,128)(2,1)S(1)} collective-permute-done((bf16[368,128]{1,0:T(8,128)(2,1)S(1)}, bf16[368,128]{1,0:T(8,128)(2,1)S(1)}, u32[]{:S(2)}, u32[]{:S(2)}) %collective-permute-start.13) | collective-permute-done | bytes 94240 | tf_op jit(solution)/shard_map/ppermute | solution.py:286
  38.8 1.4 %collective-permute-done.14.rest_2_ = bf16[368,128]{1,0:T(8,128)(2,1)S(1)} collective-permute-done((bf16[368,128]{1,0:T(8,128)(2,1)S(1)}, bf16[368,128]{1,0:T(8,128)(2,1)S(1)}, u32[]{:S(2)}, u32[]{:S(2)}) %collective-permute-start.14) | collective-permute-done | bytes 94240 | tf_op jit(solution)/shard_map/ppermute | solution.py:286
  40.2 2.1 %first_step.1 = (f32[64,576]{1,0:T(8,128)S(1)}, f32[64,576]{1,0:T(8,128)S(1)}, bf16[288,128]{1,0:T(8,128)(2,1)S(1)}, f32[64,128]{1,0:T(8,128)S(1)}, f32[64,64]{1,0:T(8,128)S(1)}) custom-call(f32[64,576]{1,0:T(8,128)S(1)} %get-tuple-element.73.mine, f32[64,128]{1,0:T(8,128)S(1)} %get-tuple-element.68.after.grams, f32[64,576]{1,0:T(8,128)S(1)} %bitcast.29, ...), custom_call_target="tpu_custom_call" | custom-call | tf_op jit(solution)/shard_map/first_step/pallas_call | solution.py:265
  42.3 1.2 %collective-permute-start.15 = (bf16[288,128]{1,0:T(8,128)(2,1)S(1)}, bf16[288,128]{1,0:T(8,128)(2,1)S(1)}, u32[]{:S(2)}, u32[]{:S(2)}) collective-permute-start(bf16[288,128]{1,0:T(8,128)(2,1)S(1)} %get-tuple-element.77.rest_0_.near), channel_id=1, source_target_pairs={{0,8},{8,0},{16,24},{24,16},{1,9},{9,1},{17,25},{25,17},{2,10},{10... | collective-permute-start | bytes 221192 | tf_op jit(solution)/shard_map/ppermute | solution.py:286
  43.5 1.4 %collective-permute-start.16 = (bf16[288,128]{1,0:T(8,128)(2,1)S(1)}, bf16[288,128]{1,0:T(8,128)(2,1)S(1)}, u32[]{:S(2)}, u32[]{:S(2)}) collective-permute-start(bf16[288,128]{1,0:T(8,128)(2,1)S(1)} %get-tuple-element.77.rest_0_.near), channel_id=1, source_target_pairs={{0,16},{8,24},{16,0},{24,8},{1,17},{9,25},{17,1},{25,9},{2,18},{10... | collective-permute-start | bytes 221192 | tf_op jit(solution)/shard_map/ppermute | solution.py:286
  44.9 1.8 %collective-permute-start.17 = (bf16[288,128]{1,0:T(8,128)(2,1)S(1)}, bf16[288,128]{1,0:T(8,128)(2,1)S(1)}, u32[]{:S(2)}, u32[]{:S(2)}) collective-permute-start(bf16[288,128]{1,0:T(8,128)(2,1)S(1)} %get-tuple-element.77.rest_0_.near), channel_id=1, source_target_pairs={{0,24},{8,16},{16,8},{24,0},{1,25},{9,17},{17,9},{25,1},{2,26},{10... | collective-permute-start | bytes 221192 | tf_op jit(solution)/shard_map/ppermute | solution.py:286
  46.7 1.1 %collective-permute-start.18 = (bf16[288,128]{1,0:T(8,128)(2,1)S(1)}, bf16[288,128]{1,0:T(8,128)(2,1)S(1)}, u32[]{:S(2)}, u32[]{:S(2)}) collective-permute-start(bf16[288,128]{1,0:T(8,128)(2,1)S(1)} %get-tuple-element.77.rest_0_.near), channel_id=1, source_target_pairs={{0,2},{1,3},{2,0},{3,1},{4,6},{5,7},{6,4},{7,5},{8,10},{9,11},{10,... | collective-permute-start | bytes 221192 | tf_op jit(solution)/shard_map/ppermute | solution.py:286
  47.8 0.6 collective-permute-start.19
  48.5 1.7 %collective-permute-start.20 = (bf16[288,128]{1,0:T(8,128)(2,1)S(1)}, bf16[288,128]{1,0:T(8,128)(2,1)S(1)}, u32[]{:S(2)}, u32[]{:S(2)}) collective-permute-start(bf16[288,128]{1,0:T(8,128)(2,1)S(1)} %get-tuple-element.77.rest_0_.near), channel_id=1, source_target_pairs={{0,6},{1,7},{2,4},{3,5},{4,2},{5,3},{6,0},{7,1},{8,14},{9,15},{10,... | collective-permute-start | bytes 221192 | tf_op jit(solution)/shard_map/ppermute | solution.py:286
  50.2 1.0 %collective-permute-done.17.rest_3_ = bf16[288,128]{1,0:T(8,128)(2,1)S(1)} collective-permute-done((bf16[288,128]{1,0:T(8,128)(2,1)S(1)}, bf16[288,128]{1,0:T(8,128)(2,1)S(1)}, u32[]{:S(2)}, u32[]{:S(2)}) %collective-permute-start.17) | collective-permute-done | bytes 73760 | tf_op jit(solution)/shard_map/ppermute | solution.py:286
  51.2 1.3 %forward.3 = (bf16[4,64,576]{2,1,0:T(8,128)(2,1)S(1)}, f32[8,64,576]{2,1,0:T(8,128)S(1)}) custom-call(s32[1]{0:T(128)} %bitcast.19.counts, s32[16]{0:T(128)S(1)} %bitcast.42, s32[16]{0:T(128)S(1)} %bitcast.46, bf16[16,576,576]{2,1,0:T(8,128)(2,1)S(1)} %turn.1.tiles, bf16[288,128]{1,0:T(8,128)(2,1)S(1)} %get-tuple-element.77.rest_0_.near, ...), custom_call_target="tpu_custom_call" | custom-call | flops 1 | tf_op jit(solution)/shard_map/forward/pallas_call | solution.py:265
  52.6 1.2 %collective-permute-done.20.rest_3_ = bf16[288,128]{1,0:T(8,128)(2,1)S(1)} collective-permute-done((bf16[288,128]{1,0:T(8,128)(2,1)S(1)}, bf16[288,128]{1,0:T(8,128)(2,1)S(1)}, u32[]{:S(2)}, u32[]{:S(2)}) %collective-permute-start.20) | collective-permute-done | bytes 73760 | tf_op jit(solution)/shard_map/ppermute | solution.py:286
  53.8 0.6 collective-permute-start.23
  54.3 0.7 own.3
  55.1 0.3 collective-permute-done.21.came
  55.4 0.5 gram.3
  55.8 0.2 collective-permute-start.22
  56.0 1.1 %collective-permute-done.22.grams_came = f32[64,128]{1,0:T(8,128)S(1)} collective-permute-done((f32[64,128]{1,0:T(8,128)S(1)}, f32[64,128]{1,0:T(8,128)S(1)}, u32[]{:S(2)}, u32[]{:S(2)}) %collective-permute-start.22) | collective-permute-done | bytes 32800 | tf_op jit(solution)/shard_map/ppermute | solution.py:286
  57.1 0.2 join.3
  57.3 1.4 %collective-permute-start.24 = (bf16[368,128]{1,0:T(8,128)(2,1)S(1)}, bf16[368,128]{1,0:T(8,128)(2,1)S(1)}, u32[]{:S(2)}, u32[]{:S(2)}) collective-permute-start(bf16[368,128]{1,0:T(8,128)(2,1)S(1)} %get-tuple-element.90), channel_id=1, source_target_pairs={{0,2},{1,3},{2,0},{3,1},{4,6},{5,7},{6,4},{7,5},{8,10},{9,11},{10,... | collective-permute-start | bytes 282632 | tf_op jit(solution)/shard_map/ppermute | solution.py:286
  58.7 0.9 %collective-permute-start.25 = (bf16[368,128]{1,0:T(8,128)(2,1)S(1)}, bf16[368,128]{1,0:T(8,128)(2,1)S(1)}, u32[]{:S(2)}, u32[]{:S(2)}) collective-permute-start(bf16[368,128]{1,0:T(8,128)(2,1)S(1)} %get-tuple-element.91), channel_id=1, source_target_pairs={{0,4},{1,5},{2,6},{3,7},{4,0},{5,1},{6,2},{7,3},{8,12},{9,13},{10,... | collective-permute-start | bytes 282632 | tf_op jit(solution)/shard_map/ppermute | solution.py:286
  59.6 1.2 %collective-permute-start.26 = (bf16[368,128]{1,0:T(8,128)(2,1)S(1)}, bf16[368,128]{1,0:T(8,128)(2,1)S(1)}, u32[]{:S(2)}, u32[]{:S(2)}) collective-permute-start(bf16[368,128]{1,0:T(8,128)(2,1)S(1)} %get-tuple-element.92), channel_id=1, source_target_pairs={{0,6},{1,7},{2,4},{3,5},{4,2},{5,3},{6,0},{7,1},{8,14},{9,15},{10,... | collective-permute-start | bytes 282632 | tf_op jit(solution)/shard_map/ppermute | solution.py:286
  60.8 1.5 %mirrored.3.acc = f32[4,64,576]{2,1,0:T(8,128)S(1)} custom-call(s32[1]{0:T(128)} %bitcast.20.counts, s32[16]{0:T(128)S(1)} %bitcast.43, s32[16]{0:T(128)S(1)} %bitcast.47, bf16[4,288,128]{2,1,0:T(8,128)(2,1)S(1)} %pad_maximum_fusion.1.near_own, bf16[4,288,128]{2,1,0:T(8,128)(2,1)S(1)} %collective-permute-done.23.near_far, bf16[16,576,576]{2,1,0:T(8,128)(2,1)S(1)} %bitcast.24), custom_call_target="tpu_custom_call" | custom-call | flops 679477248 | tf_op jit(solution)/shard_map/mirrored/pallas_call | solution.py:265
  62.3 3.0 %collective-permute-done.25.rest_1_ = bf16[368,128]{1,0:T(8,128)(2,1)S(1)} collective-permute-done((bf16[368,128]{1,0:T(8,128)(2,1)S(1)}, bf16[368,128]{1,0:T(8,128)(2,1)S(1)}, u32[]{:S(2)}, u32[]{:S(2)}) %collective-permute-start.25) | collective-permute-done | bytes 94240 | tf_op jit(solution)/shard_map/ppermute | solution.py:286
  65.3 0.4 rows.3
  65.7 1.3 %collective-permute-start.27 = (bf16[368,128]{1,0:T(8,128)(2,1)S(1)}, bf16[368,128]{1,0:T(8,128)(2,1)S(1)}, u32[]{:S(2)}, u32[]{:S(2)}) collective-permute-start(bf16[368,128]{1,0:T(8,128)(2,1)S(1)} %get-tuple-element.101), channel_id=1, source_target_pairs={{0,8},{8,0},{16,24},{24,16},{1,9},{9,1},{17,25},{25,17},{2,10},{10... | collective-permute-start | bytes 282632 | tf_op jit(solution)/shard_map/ppermute | solution.py:286
  67.0 2.4 %collective-permute-start.28 = (bf16[368,128]{1,0:T(8,128)(2,1)S(1)}, bf16[368,128]{1,0:T(8,128)(2,1)S(1)}, u32[]{:S(2)}, u32[]{:S(2)}) collective-permute-start(bf16[368,128]{1,0:T(8,128)(2,1)S(1)} %get-tuple-element.102), channel_id=1, source_target_pairs={{0,16},{8,24},{16,0},{24,8},{1,17},{9,25},{17,1},{25,9},{2,18},{10... | collective-permute-start | bytes 282632 | tf_op jit(solution)/shard_map/ppermute | solution.py:286
  69.4 0.8 collective-permute-start.29
  70.2 2.1 %between.1 = (f32[64,64]{1,0:T(8,128)S(1)}, f32[64,64]{1,0:T(8,128)S(1)}, f32[64,576]{1,0:T(8,128)S(1)}) custom-call(f32[64,128]{1,0:T(8,128)S(1)} %get-tuple-element.96.totals, f32[64,64]{1,0:T(8,128)S(1)} %get-tuple-element.97.alpha, f32[64,576]{1,0:T(8,128)S(1)} %bitcast.30), custom_call_target="tpu_custom_call" | custom-call | tf_op jit(solution)/shard_map/between/pallas_call | solution.py:265
  72.3 2.2 %collective-permute-done.28.rest_1_ = bf16[368,128]{1,0:T(8,128)(2,1)S(1)} collective-permute-done((bf16[368,128]{1,0:T(8,128)(2,1)S(1)}, bf16[368,128]{1,0:T(8,128)(2,1)S(1)}, u32[]{:S(2)}, u32[]{:S(2)}) %collective-permute-start.28) | collective-permute-done | bytes 94240 | tf_op jit(solution)/shard_map/ppermute | solution.py:286
  74.6 1.3 %collective-permute-done.29.rest_2_ = bf16[368,128]{1,0:T(8,128)(2,1)S(1)} collective-permute-done((bf16[368,128]{1,0:T(8,128)(2,1)S(1)}, bf16[368,128]{1,0:T(8,128)(2,1)S(1)}, u32[]{:S(2)}, u32[]{:S(2)}) %collective-permute-start.29) | collective-permute-done | bytes 94240 | tf_op jit(solution)/shard_map/ppermute | solution.py:286
  75.9 3.3 %last_step.1 = (f32[64,576]{1,0:T(8,128)}, f32[64,576]{1,0:T(8,128)}) custom-call(f32[64,576]{1,0:T(8,128)S(1)} %get-tuple-element.93.mine, f32[64,128]{1,0:T(8,128)S(1)} %get-tuple-element.94.grams, f32[64,576]{1,0:T(8,128)S(1)} %bitcast.31, f32[64,576]{1,0:T(8,128)S(1)} %get-tuple-element.95.image_in, ...), custom_call_target="tpu_custom_call" | custom-call | tf_op jit(solution)/shard_map/last_step/pallas_call | solution.py:265
  (27 shorter events, 0.1 us)
Async XLA Ops:
  0.6 0.9 %copy-start.2 = (f32[1,64,576]{2,1,0:T(8,128)S(1)}, f32[1,64,576]{2,1,0:T(8,128)}, u32[]{:S(2)}) copy-start(f32[1,64,576]{2,1,0:T(8,128)} %param.8) | copy-start | bytes 442372
  1.5 12.0 %copy-start = (bf16[1,1,16,576,576]{4,3,2,1,0:T(8,128)(2,1)S(1)}, bf16[1,1,16,576,576]{4,3,2,1,0:T(8,128)(2,1)}, u32[]{:S(2)}) copy-start(bf16[1,1,16,576,576]{4,3,2,1,0:T(8,128)(2,1)} %param.6) | copy-start | bytes 31850500
  1.6 12.0 %copy-start.4 = (s32[1,1,16]{2,1,0:T(1,128)S(1)}, s32[1,1,16]{2,1,0:T(1,128)}, u32[]{:S(2)}) copy-start(s32[1,1,16]{2,1,0:T(1,128)} %param.9) | copy-start | bytes 196
  1.6 12.0 %copy-start.5 = (s32[1,1,16]{2,1,0:T(1,128)S(1)}, s32[1,1,16]{2,1,0:T(1,128)}, u32[]{:S(2)}) copy-start(s32[1,1,16]{2,1,0:T(1,128)} %param.10) | copy-start | bytes 196
  1.6 14.8 %copy-start.1 = (bf16[1,576,576]{2,1,0:T(8,128)(2,1)S(1)}, bf16[1,576,576]{2,1,0:T(8,128)(2,1)}, u32[]{:S(2)}) copy-start(bf16[1,576,576]{2,1,0:T(8,128)(2,1)} %param.7) | copy-start | bytes 1990660
  1.6 14.8 %copy-start.3 = (f32[1,64,576]{2,1,0:T(8,128)S(1)}, f32[1,64,576]{2,1,0:T(8,128)}, u32[]{:S(2)}) copy-start(f32[1,64,576]{2,1,0:T(8,128)} %param.8) | copy-start | bytes 442372
  1.6 8.9 %collective-permute-start = (bf16[288,128]{1,0:T(8,128)(2,1)S(1)}, bf16[288,128]{1,0:T(8,128)(2,1)S(1)}, u32[]{:S(2)}, u32[]{:S(2)}) collective-permute-start(bf16[288,128]{1,0:T(8,128)(2,1)S(1)} %round.1.rest_0_.near), channel_id=1, source_target_pairs={{0,8},{8,0},{16,24},{24,16},{1,9},{9,1},{17,25},{25,17},{2,10},{10... | collective-permute-start | bytes 221192 | tf_op jit(solution)/shard_map/ppermute | solution.py:286
  4.7 7.8 %collective-permute-start.1 = (bf16[288,128]{1,0:T(8,128)(2,1)S(1)}, bf16[288,128]{1,0:T(8,128)(2,1)S(1)}, u32[]{:S(2)}, u32[]{:S(2)}) collective-permute-start(bf16[288,128]{1,0:T(8,128)(2,1)S(1)} %round.1.rest_0_.near), channel_id=1, source_target_pairs={{0,16},{8,24},{16,0},{24,8},{1,17},{9,25},{17,1},{25,9},{2,18},{10... | collective-permute-start | bytes 221192 | tf_op jit(solution)/shard_map/ppermute | solution.py:286
  7.3 6.3 %collective-permute-start.2 = (bf16[288,128]{1,0:T(8,128)(2,1)S(1)}, bf16[288,128]{1,0:T(8,128)(2,1)S(1)}, u32[]{:S(2)}, u32[]{:S(2)}) collective-permute-start(bf16[288,128]{1,0:T(8,128)(2,1)S(1)} %round.1.rest_0_.near), channel_id=1, source_target_pairs={{0,24},{8,16},{16,8},{24,0},{1,25},{9,17},{17,9},{25,1},{2,26},{10... | collective-permute-start | bytes 221192 | tf_op jit(solution)/shard_map/ppermute | solution.py:286
  7.3 8.0 %collective-permute-start.3 = (bf16[288,128]{1,0:T(8,128)(2,1)S(1)}, bf16[288,128]{1,0:T(8,128)(2,1)S(1)}, u32[]{:S(2)}, u32[]{:S(2)}) collective-permute-start(bf16[288,128]{1,0:T(8,128)(2,1)S(1)} %round.1.rest_0_.near), channel_id=1, source_target_pairs={{0,2},{1,3},{2,0},{3,1},{4,6},{5,7},{6,4},{7,5},{8,10},{9,11},{10,... | collective-permute-start | bytes 221192 | tf_op jit(solution)/shard_map/ppermute | solution.py:286
  9.0 6.3 %collective-permute-start.4 = (bf16[288,128]{1,0:T(8,128)(2,1)S(1)}, bf16[288,128]{1,0:T(8,128)(2,1)S(1)}, u32[]{:S(2)}, u32[]{:S(2)}) collective-permute-start(bf16[288,128]{1,0:T(8,128)(2,1)S(1)} %round.1.rest_0_.near), channel_id=1, source_target_pairs={{0,4},{1,5},{2,6},{3,7},{4,0},{5,1},{6,2},{7,3},{8,12},{9,13},{10,... | collective-permute-start | bytes 221192 | tf_op jit(solution)/shard_map/ppermute | solution.py:286
  10.5 5.3 %collective-permute-start.5 = (bf16[288,128]{1,0:T(8,128)(2,1)S(1)}, bf16[288,128]{1,0:T(8,128)(2,1)S(1)}, u32[]{:S(2)}, u32[]{:S(2)}) collective-permute-start(bf16[288,128]{1,0:T(8,128)(2,1)S(1)} %round.1.rest_0_.near), channel_id=1, source_target_pairs={{0,6},{1,7},{2,4},{3,5},{4,2},{5,3},{6,0},{7,1},{8,14},{9,15},{10,... | collective-permute-start | bytes 221192 | tf_op jit(solution)/shard_map/ppermute | solution.py:286
  15.8 1.6 %collective-permute-start.6 = (bf16[4,64,576]{2,1,0:T(8,128)(2,1)S(1)}, bf16[4,64,576]{2,1,0:T(8,128)(2,1)S(1)}, u32[]{:S(2)}, u32[]{:S(2)}) collective-permute-start(bf16[4,64,576]{2,1,0:T(8,128)(2,1)S(1)} %get-tuple-element.56), channel_id=1, source_target_pairs={{0,1},{1,0},{2,3},{3,2},{4,5},{5,4},{6,7},{7,6},{8,9},{9,8},{10,11... | collective-permute-start | bytes 884744 | tf_op jit(solution)/shard_map/ppermute | solution.py:286
  15.8 7.1 %collective-permute-start.8 = (bf16[4,288,128]{2,1,0:T(8,128)(2,1)S(1)}, bf16[4,288,128]{2,1,0:T(8,128)(2,1)S(1)}, u32[]{:S(2)}, u32[]{:S(2)}) collective-permute-start(bf16[4,288,128]{2,1,0:T(8,128)(2,1)S(1)} %pad_maximum_fusion.near_own), channel_id=1, source_target_pairs={{0,1},{1,0},{2,3},{3,2},{4,5},{5,4},{6,7},{7,6},{8,9},{9,8},{10,11... | collective-permute-start | bytes 884744 | tf_op jit(solution)/shard_map/ppermute | solution.py:286
  17.9 1.3 %collective-permute-start.7 = (f32[64,128]{1,0:T(8,128)S(1)}, f32[64,128]{1,0:T(8,128)S(1)}, u32[]{:S(2)}, u32[]{:S(2)}) collective-permute-start(f32[64,128]{1,0:T(8,128)S(1)} %get-tuple-element.62.grams), channel_id=1, source_target_pairs={{0,1},{1,0},{2,3},{3,2},{4,5},{5,4},{6,7},{7,6},{8,9},{9,8},{10,11... | collective-permute-start | bytes 98312 | tf_op jit(solution)/shard_map/ppermute | solution.py:286
  19.3 4.9 %collective-permute-start.9 = (bf16[368,128]{1,0:T(8,128)(2,1)S(1)}, bf16[368,128]{1,0:T(8,128)(2,1)S(1)}, u32[]{:S(2)}, u32[]{:S(2)}) collective-permute-start(bf16[368,128]{1,0:T(8,128)(2,1)S(1)} %get-tuple-element.65), channel_id=1, source_target_pairs={{0,2},{1,3},{2,0},{3,1},{4,6},{5,7},{6,4},{7,5},{8,10},{9,11},{10,... | collective-permute-start | bytes 282632 | tf_op jit(solution)/shard_map/ppermute | solution.py:286
  20.4 5.7 %collective-permute-start.10 = (bf16[368,128]{1,0:T(8,128)(2,1)S(1)}, bf16[368,128]{1,0:T(8,128)(2,1)S(1)}, u32[]{:S(2)}, u32[]{:S(2)}) collective-permute-start(bf16[368,128]{1,0:T(8,128)(2,1)S(1)} %get-tuple-element.66), channel_id=1, source_target_pairs={{0,4},{1,5},{2,6},{3,7},{4,0},{5,1},{6,2},{7,3},{8,12},{9,13},{10,... | collective-permute-start | bytes 282632 | tf_op jit(solution)/shard_map/ppermute | solution.py:286
  22.0 5.5 %collective-permute-start.11 = (bf16[368,128]{1,0:T(8,128)(2,1)S(1)}, bf16[368,128]{1,0:T(8,128)(2,1)S(1)}, u32[]{:S(2)}, u32[]{:S(2)}) collective-permute-start(bf16[368,128]{1,0:T(8,128)(2,1)S(1)} %get-tuple-element.67), channel_id=1, source_target_pairs={{0,6},{1,7},{2,4},{3,5},{4,2},{5,3},{6,0},{7,1},{8,14},{9,15},{10,... | collective-permute-start | bytes 282632 | tf_op jit(solution)/shard_map/ppermute | solution.py:286
  27.9 6.7 %collective-permute-start.12 = (bf16[368,128]{1,0:T(8,128)(2,1)S(1)}, bf16[368,128]{1,0:T(8,128)(2,1)S(1)}, u32[]{:S(2)}, u32[]{:S(2)}) collective-permute-start(bf16[368,128]{1,0:T(8,128)(2,1)S(1)} %get-tuple-element.69), channel_id=1, source_target_pairs={{0,8},{8,0},{16,24},{24,16},{1,9},{9,1},{17,25},{25,17},{2,10},{10... | collective-permute-start | bytes 282632 | tf_op jit(solution)/shard_map/ppermute | solution.py:286
  30.0 8.8 %collective-permute-start.13 = (bf16[368,128]{1,0:T(8,128)(2,1)S(1)}, bf16[368,128]{1,0:T(8,128)(2,1)S(1)}, u32[]{:S(2)}, u32[]{:S(2)}) collective-permute-start(bf16[368,128]{1,0:T(8,128)(2,1)S(1)} %get-tuple-element.70), channel_id=1, source_target_pairs={{0,16},{8,24},{16,0},{24,8},{1,17},{9,25},{17,1},{25,9},{2,18},{10... | collective-permute-start | bytes 282632 | tf_op jit(solution)/shard_map/ppermute | solution.py:286
  33.7 6.5 %collective-permute-start.14 = (bf16[368,128]{1,0:T(8,128)(2,1)S(1)}, bf16[368,128]{1,0:T(8,128)(2,1)S(1)}, u32[]{:S(2)}, u32[]{:S(2)}) collective-permute-start(bf16[368,128]{1,0:T(8,128)(2,1)S(1)} %get-tuple-element.71), channel_id=1, source_target_pairs={{0,24},{8,16},{16,8},{24,0},{1,25},{9,17},{17,9},{25,1},{2,26},{10... | collective-permute-start | bytes 282632 | tf_op jit(solution)/shard_map/ppermute | solution.py:286
  42.3 6.2 %collective-permute-start.15 = (bf16[288,128]{1,0:T(8,128)(2,1)S(1)}, bf16[288,128]{1,0:T(8,128)(2,1)S(1)}, u32[]{:S(2)}, u32[]{:S(2)}) collective-permute-start(bf16[288,128]{1,0:T(8,128)(2,1)S(1)} %get-tuple-element.77.rest_0_.near), channel_id=1, source_target_pairs={{0,8},{8,0},{16,24},{24,16},{1,9},{9,1},{17,25},{25,17},{2,10},{10... | collective-permute-start | bytes 221192 | tf_op jit(solution)/shard_map/ppermute | solution.py:286
  43.5 6.7 %collective-permute-start.16 = (bf16[288,128]{1,0:T(8,128)(2,1)S(1)}, bf16[288,128]{1,0:T(8,128)(2,1)S(1)}, u32[]{:S(2)}, u32[]{:S(2)}) collective-permute-start(bf16[288,128]{1,0:T(8,128)(2,1)S(1)} %get-tuple-element.77.rest_0_.near), channel_id=1, source_target_pairs={{0,16},{8,24},{16,0},{24,8},{1,17},{9,25},{17,1},{25,9},{2,18},{10... | collective-permute-start | bytes 221192 | tf_op jit(solution)/shard_map/ppermute | solution.py:286
  44.9 6.3 %collective-permute-start.17 = (bf16[288,128]{1,0:T(8,128)(2,1)S(1)}, bf16[288,128]{1,0:T(8,128)(2,1)S(1)}, u32[]{:S(2)}, u32[]{:S(2)}) collective-permute-start(bf16[288,128]{1,0:T(8,128)(2,1)S(1)} %get-tuple-element.77.rest_0_.near), channel_id=1, source_target_pairs={{0,24},{8,16},{16,8},{24,0},{1,25},{9,17},{17,9},{25,1},{2,26},{10... | collective-permute-start | bytes 221192 | tf_op jit(solution)/shard_map/ppermute | solution.py:286
  46.7 5.8 %collective-permute-start.18 = (bf16[288,128]{1,0:T(8,128)(2,1)S(1)}, bf16[288,128]{1,0:T(8,128)(2,1)S(1)}, u32[]{:S(2)}, u32[]{:S(2)}) collective-permute-start(bf16[288,128]{1,0:T(8,128)(2,1)S(1)} %get-tuple-element.77.rest_0_.near), channel_id=1, source_target_pairs={{0,2},{1,3},{2,0},{3,1},{4,6},{5,7},{6,4},{7,5},{8,10},{9,11},{10,... | collective-permute-start | bytes 221192 | tf_op jit(solution)/shard_map/ppermute | solution.py:286
  47.8 4.7 %collective-permute-start.19 = (bf16[288,128]{1,0:T(8,128)(2,1)S(1)}, bf16[288,128]{1,0:T(8,128)(2,1)S(1)}, u32[]{:S(2)}, u32[]{:S(2)}) collective-permute-start(bf16[288,128]{1,0:T(8,128)(2,1)S(1)} %get-tuple-element.77.rest_0_.near), channel_id=1, source_target_pairs={{0,4},{1,5},{2,6},{3,7},{4,0},{5,1},{6,2},{7,3},{8,12},{9,13},{10,... | collective-permute-start | bytes 221192 | tf_op jit(solution)/shard_map/ppermute | solution.py:286
  48.5 5.3 %collective-permute-start.20 = (bf16[288,128]{1,0:T(8,128)(2,1)S(1)}, bf16[288,128]{1,0:T(8,128)(2,1)S(1)}, u32[]{:S(2)}, u32[]{:S(2)}) collective-permute-start(bf16[288,128]{1,0:T(8,128)(2,1)S(1)} %get-tuple-element.77.rest_0_.near), channel_id=1, source_target_pairs={{0,6},{1,7},{2,4},{3,5},{4,2},{5,3},{6,0},{7,1},{8,14},{9,15},{10,... | collective-permute-start | bytes 221192 | tf_op jit(solution)/shard_map/ppermute | solution.py:286
  53.7 1.6 %collective-permute-start.21 = (bf16[4,64,576]{2,1,0:T(8,128)(2,1)S(1)}, bf16[4,64,576]{2,1,0:T(8,128)(2,1)S(1)}, u32[]{:S(2)}, u32[]{:S(2)}) collective-permute-start(bf16[4,64,576]{2,1,0:T(8,128)(2,1)S(1)} %get-tuple-element.80), channel_id=1, source_target_pairs={{0,1},{1,0},{2,3},{3,2},{4,5},{5,4},{6,7},{7,6},{8,9},{9,8},{10,11... | collective-permute-start | bytes 884744 | tf_op jit(solution)/shard_map/ppermute | solution.py:286
  53.8 7.1 %collective-permute-start.23 = (bf16[4,288,128]{2,1,0:T(8,128)(2,1)S(1)}, bf16[4,288,128]{2,1,0:T(8,128)(2,1)S(1)}, u32[]{:S(2)}, u32[]{:S(2)}) collective-permute-start(bf16[4,288,128]{2,1,0:T(8,128)(2,1)S(1)} %pad_maximum_fusion.1.near_own), channel_id=1, source_target_pairs={{0,1},{1,0},{2,3},{3,2},{4,5},{5,4},{6,7},{7,6},{8,9},{9,8},{10,11... | collective-permute-start | bytes 884744 | tf_op jit(solution)/shard_map/ppermute | solution.py:286
  55.8 1.3 %collective-permute-start.22 = (f32[64,128]{1,0:T(8,128)S(1)}, f32[64,128]{1,0:T(8,128)S(1)}, u32[]{:S(2)}, u32[]{:S(2)}) collective-permute-start(f32[64,128]{1,0:T(8,128)S(1)} %get-tuple-element.87.grams), channel_id=1, source_target_pairs={{0,1},{1,0},{2,3},{3,2},{4,5},{5,4},{6,7},{7,6},{8,9},{9,8},{10,11... | collective-permute-start | bytes 98312 | tf_op jit(solution)/shard_map/ppermute | solution.py:286
  57.3 5.0 %collective-permute-start.24 = (bf16[368,128]{1,0:T(8,128)(2,1)S(1)}, bf16[368,128]{1,0:T(8,128)(2,1)S(1)}, u32[]{:S(2)}, u32[]{:S(2)}) collective-permute-start(bf16[368,128]{1,0:T(8,128)(2,1)S(1)} %get-tuple-element.90), channel_id=1, source_target_pairs={{0,2},{1,3},{2,0},{3,1},{4,6},{5,7},{6,4},{7,5},{8,10},{9,11},{10,... | collective-permute-start | bytes 282632 | tf_op jit(solution)/shard_map/ppermute | solution.py:286
  58.7 6.6 %collective-permute-start.25 = (bf16[368,128]{1,0:T(8,128)(2,1)S(1)}, bf16[368,128]{1,0:T(8,128)(2,1)S(1)}, u32[]{:S(2)}, u32[]{:S(2)}) collective-permute-start(bf16[368,128]{1,0:T(8,128)(2,1)S(1)} %get-tuple-element.91), channel_id=1, source_target_pairs={{0,4},{1,5},{2,6},{3,7},{4,0},{5,1},{6,2},{7,3},{8,12},{9,13},{10,... | collective-permute-start | bytes 282632 | tf_op jit(solution)/shard_map/ppermute | solution.py:286
  59.6 5.7 %collective-permute-start.26 = (bf16[368,128]{1,0:T(8,128)(2,1)S(1)}, bf16[368,128]{1,0:T(8,128)(2,1)S(1)}, u32[]{:S(2)}, u32[]{:S(2)}) collective-permute-start(bf16[368,128]{1,0:T(8,128)(2,1)S(1)} %get-tuple-element.92), channel_id=1, source_target_pairs={{0,6},{1,7},{2,4},{3,5},{4,2},{5,3},{6,0},{7,1},{8,14},{9,15},{10,... | collective-permute-start | bytes 282632 | tf_op jit(solution)/shard_map/ppermute | solution.py:286
  65.7 6.6 %collective-permute-start.27 = (bf16[368,128]{1,0:T(8,128)(2,1)S(1)}, bf16[368,128]{1,0:T(8,128)(2,1)S(1)}, u32[]{:S(2)}, u32[]{:S(2)}) collective-permute-start(bf16[368,128]{1,0:T(8,128)(2,1)S(1)} %get-tuple-element.101), channel_id=1, source_target_pairs={{0,8},{8,0},{16,24},{24,16},{1,9},{9,1},{17,25},{25,17},{2,10},{10... | collective-permute-start | bytes 282632 | tf_op jit(solution)/shard_map/ppermute | solution.py:286
  67.0 7.6 %collective-permute-start.28 = (bf16[368,128]{1,0:T(8,128)(2,1)S(1)}, bf16[368,128]{1,0:T(8,128)(2,1)S(1)}, u32[]{:S(2)}, u32[]{:S(2)}) collective-permute-start(bf16[368,128]{1,0:T(8,128)(2,1)S(1)} %get-tuple-element.102), channel_id=1, source_target_pairs={{0,16},{8,24},{16,0},{24,8},{1,17},{9,25},{17,1},{25,9},{2,18},{10... | collective-permute-start | bytes 282632 | tf_op jit(solution)/shard_map/ppermute | solution.py:286
  69.4 6.5 %collective-permute-start.29 = (bf16[368,128]{1,0:T(8,128)(2,1)S(1)}, bf16[368,128]{1,0:T(8,128)(2,1)S(1)}, u32[]{:S(2)}, u32[]{:S(2)}) collective-permute-start(bf16[368,128]{1,0:T(8,128)(2,1)S(1)} %get-tuple-element.103), channel_id=1, source_target_pairs={{0,24},{8,16},{16,8},{24,0},{1,25},{9,17},{17,9},{25,1},{2,26},{10... | collective-permute-start | bytes 282632 | tf_op jit(solution)/shard_map/ppermute | solution.py:286

commit v8 on v7

--- a/solution.py
+++ b/solution.py
@@ -145,7 +145,7 @@
     held_slots(counts[0], tiles.shape[0], work)
 
 
-def forward_kernel(counts, rows_list, cols_list, tiles, *rest, n_row, dims):
+def forward_kernel(counts, rows_list, cols_list, tiles, after, *rest, n_row, dims):
     far_in = rest[:n_row]
     give_core, acc, far = rest[n_row:]
     n_chip = give_core.shape[0]
@@ -164,7 +164,7 @@
         give_core[d] = acc[n_chip + d].astype(BF16)
 
 
-def own_kernel(near, diag, residual, after, own_out, grams):
+def own_kernel(near, diag, residual, own_out, grams):
     size = residual.shape[0]
     block = spread(near[...], size)
     own = dot16(block, diag[...], NT)
@@ -174,16 +174,24 @@
     grams[:, size:] = dot_two(residual[...], residual[...], NT)
 
 
-def gram_kernel(acc, came, grams_own, *rest):
-    *near, keep, grams = rest
+def near_kernel(acc, grams_own, *rest):
+    *near, grams = rest
     size = grams.shape[0]
     half = jnp.zeros((size, size), F32)
     for d, block in enumerate(near):
-        both = acc[d] + came[d].astype(F32)
-        keep[d] = both
-        half += dot_exact16(spread(block[...], size), both, NT)
+        half += dot_exact16(spread(block[...], size), acc[d], NT)
     grams[:, :size] = grams_own[:, :size] + half + half.T
     grams[:, size:] = grams_own[:, size:]
+
+
+def gram_kernel(came, grams_in, *rest):
+    *near, grams = rest
+    size = grams.shape[0]
+    half = jnp.zeros((size, size), F32)
+    for d, block in enumerate(near):
+        half += dot16(spread(block[...], size), came[d], NT)
+    grams[:, :size] = grams_in[:, :size] + half + half.T
+    grams[:, size:] = grams_in[:, size:]
 
 
 def mirrored_kernel(counts, rows_list, cols_list, near_own, near_far, tiles, acc, near):
@@ -202,15 +210,16 @@
     held_slots(counts[0], slots, work)
 
 
-def join_kernel(keep, grams, grams_came, grams_out, *give):
+def join_kernel(acc, came, grams, grams_came, mine, grams_out, *give):
+    mine[...] = acc[0] + came[0].astype(F32)
     total = grams[...] + grams_came[...]
     grams_out[...] = total
-    for d in range(1, keep.shape[0]):
-        give[d - 1][...] = pack(keep[d].astype(BF16), total)
-
-
-def rows_kernel(keep, grams, own, acc, *rest, n_in):
-    image, total, (mine_out, grams_out, *give) = gather_sums(keep[0], grams[...], rest, n_in)
+    for d in range(1, came.shape[0]):
+        give[d - 1][...] = pack((acc[d] + came[d].astype(F32)).astype(BF16), total)
+
+
+def rows_kernel(mine, grams, own, acc, *rest, n_in):
+    image, total, (mine_out, grams_out, *give) = gather_sums(mine[...], grams[...], rest, n_in)
     mine_out[...] = image + own[...] + acc[0]
     grams_out[...] = total
     for d in range(1, acc.shape[0]):
@@ -251,8 +260,8 @@
     forward, total, (solution_out, residual_out) = gather_sums(mine[...], grams[...], rest, n_in)
     size = forward.shape[0]
     norm = total[:, size:]
-    curv = total[:, :size] - dot32(norm, dot32(middle[...], norm, NN), TN)
-    beta = dot32(inverse[...], norm, NN)
+    curv = total[:, :size] - dot_two(norm, dot_two(middle[...], norm, NN), TN)
+    beta = dot_two(inverse[...], norm, NN)
     residual = residual_in[...]
     direction = residual + dot_two(beta, probes[...], TN)
     image = forward + dot_two(beta, image_in[...], TN)
@@ -304,31 +313,25 @@
     def apply_operator(rounded, residual, turned=None):
         from_rows = over_rows(rounded)
         near = over_chips(rounded)
+        own, grams = call(own_kernel, [block32, square], [rounded, diag, residual], name="own")
         give_core, acc_row = call(
             functools.partial(forward_kernel, n_row=n_row, dims=NT if turned is None else NN),
             [shape((n_chip, p_size, width), BF16), shape((n_col, p_size, width), F32)],
-            [*index, held if turned is None else turned, rounded, *from_rows],
-            [SMEM] * 3 + [VMEM] * (1 + n_row),
+            [*index, held if turned is None else turned, grams, rounded, *from_rows],
+            [SMEM] * 3 + [VMEM, ANY] + [VMEM] * n_row,
             [pltpu.VMEM((n_row, p_size, width), BF16)],
             name="forward",
             work=1,
         )
         give_core, *near = lax.optimization_barrier((give_core, *near))
         came = over(give_core, "col", 1)
-        own, grams = call(
-            own_kernel, [block32, square], [rounded, diag, residual, acc_row], [VMEM] * 3 + [ANY], name="own"
-        )
         near_own = jnp.stack([rounded, *near])
         near_far = over(near_own, "col", 1)
-        keep, grams = call(
-            gram_kernel,
-            [shape((n_chip, p_size, width), F32), square],
-            [acc_row, came, grams, rounded, *near],
-            name="gram",
-        )
+        (grams,) = call(near_kernel, [square], [acc_row, grams, rounded, *near], name="near")
+        (grams,) = call(gram_kernel, [square], [came, grams, rounded, *near], name="gram")
         grams_came = over(grams, "col", 1)
-        grams, *give = call(
-            join_kernel, [square] + [message] * (n_chip - 1), [keep, grams, grams_came], name="join"
+        mine, grams, *give = call(
+            join_kernel, [block32, square] + [message] * (n_chip - 1), [acc_row, came, grams, grams_came], name="join"
         )
         parts = [over(block, "col", 2 * d + 2) for d, block in enumerate(give)]
         (acc_col,) = call(
@@ -343,7 +346,7 @@
         mine, grams, *give = call(
             functools.partial(rows_kernel, n_in=n_chip - 1),
             [block32, square] + [message] * (n_row - 1),
-            [keep, grams, own, acc_col, *parts],
+            [mine, grams, own, acc_col, *parts],
             name="rows",
         )
         parts = [over(block, "row", d + 1) for d, block in enumerate(give)]

time: 79.4 us -> 79.2 us (level)
  waiting for transfers between devices: 22.9 us -> 21.8 us
    ppermute x30, waiting for transfers between devices: 22.9 us -> 21.8 us  [over(): return lax.ppermute(value, axis, [(i, i ^ delta) for i in range(size)])]
    pallas_call x17 -> x19, Pallas kernels: 17.9 us -> 18.5 us  [call(): pl.pallas_call(kernel, out_shape=outs, in_specs=[VMEM] * len(args) if spe...]
where the time goes in v8:
time: 79.2 us; the launch traced here: 79.1 us
  starting transfers between devices  36.2 us (46%)
  waiting for transfers between devices  21.8 us (28%)
  Pallas kernels  18.5 us (23%)
  between operations  1.51 us (2%)
  local copies, waits for them, and re-layouts  0.93 us (1%)
    ppermute x30, starting transfers between devices, over(): return lax.ppermute(value, axis, [(i, i ^ delta) for i in range(size)])  36.2 us
    ppermute x30, waiting for transfers between devices, over(): return lax.ppermute(value, axis, [(i, i ^ delta) for i in range(size)])  21.8 us
    pallas_call x19, Pallas kernels, call(): pl.pallas_call(kernel, out_shape=outs, in_specs=[VMEM] * len(args) if spe...  18.5 us
  transfers between devices with their start and end apart: 30, of which 16 were waited for; matrix products, arithmetic and copies ran while one was open for 0% of the time, Pallas kernels for 15%

profile of v8, /device:TPU:0, one launch (start us, length us, event | category | flops | bytes accessed | tf_op | source)
XLA Modules:
  0.0 79.1 jit_solution(7712028895652934384)
XLA Ops:
  0.6 0.0 copy-start.2
  0.6 0.9 %copy-done.2 = f32[1,64,576]{2,1,0:T(8,128)S(1)} copy-done((f32[1,64,576]{2,1,0:T(8,128)S(1)}, f32[1,64,576]{2,1,0:T(8,128)}, u32[]{:S(2)}) %copy-start.2) | copy-done | bytes 147480
  1.6 0.1 round.1.near.rest_0_
  1.6 3.0 %collective-permute-start = (bf16[288,128]{1,0:T(8,128)(2,1)S(1)}, bf16[288,128]{1,0:T(8,128)(2,1)S(1)}, u32[]{:S(2)}, u32[]{:S(2)}) collective-permute-start(bf16[288,128]{1,0:T(8,128)(2,1)S(1)} %round.1.near.rest_0_), channel_id=1, source_target_pairs={{0,8},{8,0},{16,24},{24,16},{1,9},{9,1},{17,25},{25,17},{2,10},{10... | collective-permute-start | bytes 221192 | tf_op jit(solution)/shard_map/ppermute | solution.py:295
  4.7 2.6 %collective-permute-start.1 = (bf16[288,128]{1,0:T(8,128)(2,1)S(1)}, bf16[288,128]{1,0:T(8,128)(2,1)S(1)}, u32[]{:S(2)}, u32[]{:S(2)}) collective-permute-start(bf16[288,128]{1,0:T(8,128)(2,1)S(1)} %round.1.near.rest_0_), channel_id=1, source_target_pairs={{0,16},{8,24},{16,0},{24,8},{1,17},{9,25},{17,1},{25,9},{2,18},{10... | collective-permute-start | bytes 221192 | tf_op jit(solution)/shard_map/ppermute | solution.py:295
  7.3 1.7 %collective-permute-start.3 = (bf16[288,128]{1,0:T(8,128)(2,1)S(1)}, bf16[288,128]{1,0:T(8,128)(2,1)S(1)}, u32[]{:S(2)}, u32[]{:S(2)}) collective-permute-start(bf16[288,128]{1,0:T(8,128)(2,1)S(1)} %round.1.near.rest_0_), channel_id=1, source_target_pairs={{0,2},{1,3},{2,0},{3,1},{4,6},{5,7},{6,4},{7,5},{8,10},{9,11},{10,... | collective-permute-start | bytes 221192 | tf_op jit(solution)/shard_map/ppermute | solution.py:295
  9.0 1.5 %collective-permute-start.4 = (bf16[288,128]{1,0:T(8,128)(2,1)S(1)}, bf16[288,128]{1,0:T(8,128)(2,1)S(1)}, u32[]{:S(2)}, u32[]{:S(2)}) collective-permute-start(bf16[288,128]{1,0:T(8,128)(2,1)S(1)} %round.1.near.rest_0_), channel_id=1, source_target_pairs={{0,4},{1,5},{2,6},{3,7},{4,0},{5,1},{6,2},{7,3},{8,12},{9,13},{10,... | collective-permute-start | bytes 221192 | tf_op jit(solution)/shard_map/ppermute | solution.py:295
  10.5 0.3 collective-permute-start.5
  11.4 0.7 own.2
  12.1 0.3 collective-permute-done.1.rest_2_
  12.5 1.1 %collective-permute-done.2.rest_3_ = bf16[288,128]{1,0:T(8,128)(2,1)S(1)} collective-permute-done((bf16[288,128]{1,0:T(8,128)(2,1)S(1)}, bf16[288,128]{1,0:T(8,128)(2,1)S(1)}, u32[]{:S(2)}, u32[]{:S(2)}) %collective-permute-start.2) | collective-permute-done | bytes 73760 | tf_op jit(solution)/shard_map/ppermute | solution.py:295
  13.5 1.7 %forward.2 = (bf16[4,64,576]{2,1,0:T(8,128)(2,1)S(1)}, f32[8,64,576]{2,1,0:T(8,128)S(1)}) custom-call(s32[1]{0:T(128)} %bitcast.16.counts, s32[16]{0:T(128)S(1)} %bitcast.40, s32[16]{0:T(128)S(1)} %bitcast.44, bf16[16,576,576]{2,1,0:T(8,128)(2,1)S(1)} %bitcast.21, f32[64,128]{1,0:T(8,128)S(1)} %get-tuple-element.52.after.grams_own, ...), custom_call_target="tpu_custom_call" | custom-call | flops 1 | tf_op jit(solution)/shard_map/forward/pallas_call | solution.py:274
  15.3 0.5 collective-permute-done.5.rest_3_
  15.8 0.6 collective-permute-start.8
  16.4 0.5 near.2.grams_in
  16.9 0.5 collective-permute-done.6.came
  17.4 0.4 gram.2.grams
  17.7 0.2 collective-permute-start.7
  17.9 1.1 %collective-permute-done.7.grams_came = f32[64,128]{1,0:T(8,128)S(1)} collective-permute-done((f32[64,128]{1,0:T(8,128)S(1)}, f32[64,128]{1,0:T(8,128)S(1)}, u32[]{:S(2)}, u32[]{:S(2)}) %collective-permute-start.7) | collective-permute-done | bytes 32800 | tf_op jit(solution)/shard_map/ppermute | solution.py:295
  19.0 0.2 join.2
  19.2 1.1 %collective-permute-start.9 = (bf16[368,128]{1,0:T(8,128)(2,1)S(1)}, bf16[368,128]{1,0:T(8,128)(2,1)S(1)}, u32[]{:S(2)}, u32[]{:S(2)}) collective-permute-start(bf16[368,128]{1,0:T(8,128)(2,1)S(1)} %get-tuple-element.62), channel_id=1, source_target_pairs={{0,2},{1,3},{2,0},{3,1},{4,6},{5,7},{6,4},{7,5},{8,10},{9,11},{10,... | collective-permute-start | bytes 282632 | tf_op jit(solution)/shard_map/ppermute | solution.py:295
  20.3 1.5 %collective-permute-start.10 = (bf16[368,128]{1,0:T(8,128)(2,1)S(1)}, bf16[368,128]{1,0:T(8,128)(2,1)S(1)}, u32[]{:S(2)}, u32[]{:S(2)}) collective-permute-start(bf16[368,128]{1,0:T(8,128)(2,1)S(1)} %get-tuple-element.63), channel_id=1, source_target_pairs={{0,4},{1,5},{2,6},{3,7},{4,0},{5,1},{6,2},{7,3},{8,12},{9,13},{10,... | collective-permute-start | bytes 282632 | tf_op jit(solution)/shard_map/ppermute | solution.py:295
  21.8 0.9 %collective-permute-start.11 = (bf16[368,128]{1,0:T(8,128)(2,1)S(1)}, bf16[368,128]{1,0:T(8,128)(2,1)S(1)}, u32[]{:S(2)}, u32[]{:S(2)}) collective-permute-start(bf16[368,128]{1,0:T(8,128)(2,1)S(1)} %get-tuple-element.64), channel_id=1, source_target_pairs={{0,6},{1,7},{2,4},{3,5},{4,2},{5,3},{6,0},{7,1},{8,14},{9,15},{10,... | collective-permute-start | bytes 282632 | tf_op jit(solution)/shard_map/ppermute | solution.py:295
  22.7 1.3 %mirrored.2.acc = f32[4,64,576]{2,1,0:T(8,128)S(1)} custom-call(s32[1]{0:T(128)} %bitcast.17.counts, s32[16]{0:T(128)S(1)} %bitcast.41, s32[16]{0:T(128)S(1)} %bitcast.45, bf16[4,288,128]{2,1,0:T(8,128)(2,1)S(1)} %pad_maximum_fusion.near_own, bf16[4,288,128]{2,1,0:T(8,128)(2,1)S(1)} %collective-permute-done.8.near_far, bf16[16,576,576]{2,1,0:T(8,128)(2,1)S(1)} %bitcast.22), custom_call_target="tpu_custom_call" | custom-call | flops 679477248 | tf_op jit(solution)/shard_map/mirrored/pallas_call | solution.py:274
  24.0 0.0 collective-permute-done.9.rest_0_
  24.1 1.9 %collective-permute-done.10.rest_1_ = bf16[368,128]{1,0:T(8,128)(2,1)S(1)} collective-permute-done((bf16[368,128]{1,0:T(8,128)(2,1)S(1)}, bf16[368,128]{1,0:T(8,128)(2,1)S(1)}, u32[]{:S(2)}, u32[]{:S(2)}) %collective-permute-start.10) | collective-permute-done | bytes 94240 | tf_op jit(solution)/shard_map/ppermute | solution.py:295
  26.0 1.3 %collective-permute-done.11.rest_2_ = bf16[368,128]{1,0:T(8,128)(2,1)S(1)} collective-permute-done((bf16[368,128]{1,0:T(8,128)(2,1)S(1)}, bf16[368,128]{1,0:T(8,128)(2,1)S(1)}, u32[]{:S(2)}, u32[]{:S(2)}) %collective-permute-start.11) | collective-permute-done | bytes 94240 | tf_op jit(solution)/shard_map/ppermute | solution.py:295
  27.3 0.4 rows.2
  27.7 2.2 %collective-permute-start.12 = (bf16[368,128]{1,0:T(8,128)(2,1)S(1)}, bf16[368,128]{1,0:T(8,128)(2,1)S(1)}, u32[]{:S(2)}, u32[]{:S(2)}) collective-permute-start(bf16[368,128]{1,0:T(8,128)(2,1)S(1)} %get-tuple-element.66), channel_id=1, source_target_pairs={{0,8},{8,0},{16,24},{24,16},{1,9},{9,1},{17,25},{25,17},{2,10},{10... | collective-permute-start | bytes 282632 | tf_op jit(solution)/shard_map/ppermute | solution.py:295
  29.9 4.0 %collective-permute-start.13 = (bf16[368,128]{1,0:T(8,128)(2,1)S(1)}, bf16[368,128]{1,0:T(8,128)(2,1)S(1)}, u32[]{:S(2)}, u32[]{:S(2)}) collective-permute-start(bf16[368,128]{1,0:T(8,128)(2,1)S(1)} %get-tuple-element.67), channel_id=1, source_target_pairs={{0,16},{8,24},{16,0},{24,8},{1,17},{9,25},{17,1},{25,9},{2,18},{10... | collective-permute-start | bytes 282632 | tf_op jit(solution)/shard_map/ppermute | solution.py:295
  33.8 0.9 %turn.1.tiles = bf16[16,576,576]{2,1,0:T(8,128)(2,1)S(1)} custom-call(s32[1]{0:T(128)} %bitcast.18.counts, bf16[16,576,576]{2,1,0:T(8,128)(2,1)S(1)} %bitcast.23, f32[64,128]{1,0:T(8,128)S(1)} %get-tuple-element.65.after.grams), custom_call_target="tpu_custom_call" | custom-call | tf_op jit(solution)/shard_map/turn/pallas_call | solution.py:274
  34.7 4.2 %collective-permute-done.13.rest_1_ = bf16[368,128]{1,0:T(8,128)(2,1)S(1)} collective-permute-done((bf16[368,128]{1,0:T(8,128)(2,1)S(1)}, bf16[368,128]{1,0:T(8,128)(2,1)S(1)}, u32[]{:S(2)}, u32[]{:S(2)}) %collective-permute-start.13) | collective-permute-done | bytes 94240 | tf_op jit(solution)/shard_map/ppermute | solution.py:295
  38.9 1.4 %collective-permute-done.14.rest_2_ = bf16[368,128]{1,0:T(8,128)(2,1)S(1)} collective-permute-done((bf16[368,128]{1,0:T(8,128)(2,1)S(1)}, bf16[368,128]{1,0:T(8,128)(2,1)S(1)}, u32[]{:S(2)}, u32[]{:S(2)}) %collective-permute-start.14) | collective-permute-done | bytes 94240 | tf_op jit(solution)/shard_map/ppermute | solution.py:295
  40.3 2.1 %first_step.1 = (f32[64,576]{1,0:T(8,128)S(1)}, f32[64,576]{1,0:T(8,128)S(1)}, bf16[288,128]{1,0:T(8,128)(2,1)S(1)}, f32[64,128]{1,0:T(8,128)S(1)}, f32[64,64]{1,0:T(8,128)S(1)}) custom-call(f32[64,576]{1,0:T(8,128)S(1)} %get-tuple-element.70.mine, f32[64,128]{1,0:T(8,128)S(1)} %get-tuple-element.65.after.grams, f32[64,576]{1,0:T(8,128)S(1)} %bitcast.29, ...), custom_call_target="tpu_custom_call" | custom-call | tf_op jit(solution)/shard_map/first_step/pallas_call | solution.py:274
  42.5 1.2 %collective-permute-start.15 = (bf16[288,128]{1,0:T(8,128)(2,1)S(1)}, bf16[288,128]{1,0:T(8,128)(2,1)S(1)}, u32[]{:S(2)}, u32[]{:S(2)}) collective-permute-start(bf16[288,128]{1,0:T(8,128)(2,1)S(1)} %get-tuple-element.74.near.rest_0_), channel_id=1, source_target_pairs={{0,8},{8,0},{16,24},{24,16},{1,9},{9,1},{17,25},{25,17},{2,10},{10... | collective-permute-start | bytes 221192 | tf_op jit(solution)/shard_map/ppermute | solution.py:295
  43.7 1.4 %collective-permute-start.16 = (bf16[288,128]{1,0:T(8,128)(2,1)S(1)}, bf16[288,128]{1,0:T(8,128)(2,1)S(1)}, u32[]{:S(2)}, u32[]{:S(2)}) collective-permute-start(bf16[288,128]{1,0:T(8,128)(2,1)S(1)} %get-tuple-element.74.near.rest_0_), channel_id=1, source_target_pairs={{0,16},{8,24},{16,0},{24,8},{1,17},{9,25},{17,1},{25,9},{2,18},{10... | collective-permute-start | bytes 221192 | tf_op jit(solution)/shard_map/ppermute | solution.py:295
  45.1 1.8 %collective-permute-start.17 = (bf16[288,128]{1,0:T(8,128)(2,1)S(1)}, bf16[288,128]{1,0:T(8,128)(2,1)S(1)}, u32[]{:S(2)}, u32[]{:S(2)}) collective-permute-start(bf16[288,128]{1,0:T(8,128)(2,1)S(1)} %get-tuple-element.74.near.rest_0_), channel_id=1, source_target_pairs={{0,24},{8,16},{16,8},{24,0},{1,25},{9,17},{17,9},{25,1},{2,26},{10... | collective-permute-start | bytes 221192 | tf_op jit(solution)/shard_map/ppermute | solution.py:295
  46.9 1.2 %collective-permute-start.18 = (bf16[288,128]{1,0:T(8,128)(2,1)S(1)}, bf16[288,128]{1,0:T(8,128)(2,1)S(1)}, u32[]{:S(2)}, u32[]{:S(2)}) collective-permute-start(bf16[288,128]{1,0:T(8,128)(2,1)S(1)} %get-tuple-element.74.near.rest_0_), channel_id=1, source_target_pairs={{0,2},{1,3},{2,0},{3,1},{4,6},{5,7},{6,4},{7,5},{8,10},{9,11},{10,... | collective-permute-start | bytes 221192 | tf_op jit(solution)/shard_map/ppermute | solution.py:295
  48.1 0.6 collective-permute-start.19
  48.6 1.7 %collective-permute-start.20 = (bf16[288,128]{1,0:T(8,128)(2,1)S(1)}, bf16[288,128]{1,0:T(8,128)(2,1)S(1)}, u32[]{:S(2)}, u32[]{:S(2)}) collective-permute-start(bf16[288,128]{1,0:T(8,128)(2,1)S(1)} %get-tuple-element.74.near.rest_0_), channel_id=1, source_target_pairs={{0,6},{1,7},{2,4},{3,5},{4,2},{5,3},{6,0},{7,1},{8,14},{9,15},{10,... | collective-permute-start | bytes 221192 | tf_op jit(solution)/shard_map/ppermute | solution.py:295
  50.4 0.7 own.3
  51.1 0.3 collective-permute-done.17.rest_3_
  51.4 1.3 %forward.3 = (bf16[4,64,576]{2,1,0:T(8,128)(2,1)S(1)}, f32[8,64,576]{2,1,0:T(8,128)S(1)}) custom-call(s32[1]{0:T(128)} %bitcast.19.counts, s32[16]{0:T(128)S(1)} %bitcast.42, s32[16]{0:T(128)S(1)} %bitcast.46, bf16[16,576,576]{2,1,0:T(8,128)(2,1)S(1)} %turn.1.tiles, f32[64,128]{1,0:T(8,128)S(1)} %get-tuple-element.76.after.grams_own, ...), custom_call_target="tpu_custom_call" | custom-call | flops 1 | tf_op jit(solution)/shard_map/forward/pallas_call | solution.py:274
  52.7 1.2 %collective-permute-done.20.rest_3_ = bf16[288,128]{1,0:T(8,128)(2,1)S(1)} collective-permute-done((bf16[288,128]{1,0:T(8,128)(2,1)S(1)}, bf16[288,128]{1,0:T(8,128)(2,1)S(1)}, u32[]{:S(2)}, u32[]{:S(2)}) %collective-permute-start.20) | collective-permute-done | bytes 73760 | tf_op jit(solution)/shard_map/ppermute | solution.py:295
  53.9 0.6 collective-permute-start.23
  54.5 0.5 near.3.grams_in
  55.0 0.5 collective-permute-done.21.came
  55.5 0.4 gram.3.grams
  55.9 0.2 collective-permute-start.22
  56.1 1.1 %collective-permute-done.22.grams_came = f32[64,128]{1,0:T(8,128)S(1)} collective-permute-done((f32[64,128]{1,0:T(8,128)S(1)}, f32[64,128]{1,0:T(8,128)S(1)}, u32[]{:S(2)}, u32[]{:S(2)}) %collective-permute-start.22) | collective-permute-done | bytes 32800 | tf_op jit(solution)/shard_map/ppermute | solution.py:295
  57.2 0.2 join.3
  57.3 1.4 %collective-permute-start.24 = (bf16[368,128]{1,0:T(8,128)(2,1)S(1)}, bf16[368,128]{1,0:T(8,128)(2,1)S(1)}, u32[]{:S(2)}, u32[]{:S(2)}) collective-permute-start(bf16[368,128]{1,0:T(8,128)(2,1)S(1)} %get-tuple-element.86), channel_id=1, source_target_pairs={{0,2},{1,3},{2,0},{3,1},{4,6},{5,7},{6,4},{7,5},{8,10},{9,11},{10,... | collective-permute-start | bytes 282632 | tf_op jit(solution)/shard_map/ppermute | solution.py:295
  58.8 0.9 %collective-permute-start.25 = (bf16[368,128]{1,0:T(8,128)(2,1)S(1)}, bf16[368,128]{1,0:T(8,128)(2,1)S(1)}, u32[]{:S(2)}, u32[]{:S(2)}) collective-permute-start(bf16[368,128]{1,0:T(8,128)(2,1)S(1)} %get-tuple-element.87), channel_id=1, source_target_pairs={{0,4},{1,5},{2,6},{3,7},{4,0},{5,1},{6,2},{7,3},{8,12},{9,13},{10,... | collective-permute-start | bytes 282632 | tf_op jit(solution)/shard_map/ppermute | solution.py:295
  59.7 1.2 %collective-permute-start.26 = (bf16[368,128]{1,0:T(8,128)(2,1)S(1)}, bf16[368,128]{1,0:T(8,128)(2,1)S(1)}, u32[]{:S(2)}, u32[]{:S(2)}) collective-permute-start(bf16[368,128]{1,0:T(8,128)(2,1)S(1)} %get-tuple-element.88), channel_id=1, source_target_pairs={{0,6},{1,7},{2,4},{3,5},{4,2},{5,3},{6,0},{7,1},{8,14},{9,15},{10,... | collective-permute-start | bytes 282632 | tf_op jit(solution)/shard_map/ppermute | solution.py:295
  60.9 1.5 %mirrored.3.acc = f32[4,64,576]{2,1,0:T(8,128)S(1)} custom-call(s32[1]{0:T(128)} %bitcast.20.counts, s32[16]{0:T(128)S(1)} %bitcast.43, s32[16]{0:T(128)S(1)} %bitcast.47, bf16[4,288,128]{2,1,0:T(8,128)(2,1)S(1)} %pad_maximum_fusion.1.near_own, bf16[4,288,128]{2,1,0:T(8,128)(2,1)S(1)} %collective-permute-done.23.near_far, bf16[16,576,576]{2,1,0:T(8,128)(2,1)S(1)} %bitcast.24), custom_call_target="tpu_custom_call" | custom-call | flops 679477248 | tf_op jit(solution)/shard_map/mirrored/pallas_call | solution.py:274
  62.4 3.0 %collective-permute-done.25.rest_1_ = bf16[368,128]{1,0:T(8,128)(2,1)S(1)} collective-permute-done((bf16[368,128]{1,0:T(8,128)(2,1)S(1)}, bf16[368,128]{1,0:T(8,128)(2,1)S(1)}, u32[]{:S(2)}, u32[]{:S(2)}) %collective-permute-start.25) | collective-permute-done | bytes 94240 | tf_op jit(solution)/shard_map/ppermute | solution.py:295
  65.4 0.4 rows.3
  65.8 1.0 %collective-permute-start.27 = (bf16[368,128]{1,0:T(8,128)(2,1)S(1)}, bf16[368,128]{1,0:T(8,128)(2,1)S(1)}, u32[]{:S(2)}, u32[]{:S(2)}) collective-permute-start(bf16[368,128]{1,0:T(8,128)(2,1)S(1)} %get-tuple-element.97), channel_id=1, source_target_pairs={{0,8},{8,0},{16,24},{24,16},{1,9},{9,1},{17,25},{25,17},{2,10},{10... | collective-permute-start | bytes 282632 | tf_op jit(solution)/shard_map/ppermute | solution.py:295
  66.8 2.5 %collective-permute-start.28 = (bf16[368,128]{1,0:T(8,128)(2,1)S(1)}, bf16[368,128]{1,0:T(8,128)(2,1)S(1)}, u32[]{:S(2)}, u32[]{:S(2)}) collective-permute-start(bf16[368,128]{1,0:T(8,128)(2,1)S(1)} %get-tuple-element.98), channel_id=1, source_target_pairs={{0,16},{8,24},{16,0},{24,8},{1,17},{9,25},{17,1},{25,9},{2,18},{10... | collective-permute-start | bytes 282632 | tf_op jit(solution)/shard_map/ppermute | solution.py:295
  69.3 1.0 %collective-permute-start.29 = (bf16[368,128]{1,0:T(8,128)(2,1)S(1)}, bf16[368,128]{1,0:T(8,128)(2,1)S(1)}, u32[]{:S(2)}, u32[]{:S(2)}) collective-permute-start(bf16[368,128]{1,0:T(8,128)(2,1)S(1)} %get-tuple-element.99), channel_id=1, source_target_pairs={{0,24},{8,16},{16,8},{24,0},{1,25},{9,17},{17,9},{25,1},{2,26},{10... | collective-permute-start | bytes 282632 | tf_op jit(solution)/shard_map/ppermute | solution.py:295
  70.2 2.1 %between.1 = (f32[64,64]{1,0:T(8,128)S(1)}, f32[64,64]{1,0:T(8,128)S(1)}, f32[64,576]{1,0:T(8,128)S(1)}) custom-call(f32[64,128]{1,0:T(8,128)S(1)} %get-tuple-element.92.totals, f32[64,64]{1,0:T(8,128)S(1)} %get-tuple-element.93.alpha, f32[64,576]{1,0:T(8,128)S(1)} %bitcast.30), custom_call_target="tpu_custom_call" | custom-call | tf_op jit(solution)/shard_map/between/pallas_call | solution.py:274
  72.4 2.0 %collective-permute-done.28.rest_1_ = bf16[368,128]{1,0:T(8,128)(2,1)S(1)} collective-permute-done((bf16[368,128]{1,0:T(8,128)(2,1)S(1)}, bf16[368,128]{1,0:T(8,128)(2,1)S(1)}, u32[]{:S(2)}, u32[]{:S(2)}) %collective-permute-start.28) | collective-permute-done | bytes 94240 | tf_op jit(solution)/shard_map/ppermute | solution.py:295
  74.4 1.4 %collective-permute-done.29.rest_2_ = bf16[368,128]{1,0:T(8,128)(2,1)S(1)} collective-permute-done((bf16[368,128]{1,0:T(8,128)(2,1)S(1)}, bf16[368,128]{1,0:T(8,128)(2,1)S(1)}, u32[]{:S(2)}, u32[]{:S(2)}) %collective-permute-start.29) | collective-permute-done | bytes 94240 | tf_op jit(solution)/shard_map/ppermute | solution.py:295
  75.8 3.3 %last_step.1 = (f32[64,576]{1,0:T(8,128)}, f32[64,576]{1,0:T(8,128)}) custom-call(f32[64,576]{1,0:T(8,128)S(1)} %get-tuple-element.89.mine, f32[64,128]{1,0:T(8,128)S(1)} %get-tuple-element.90.grams, f32[64,576]{1,0:T(8,128)S(1)} %bitcast.31, f32[64,576]{1,0:T(8,128)S(1)} %get-tuple-element.91.image_in, ...), custom_call_target="tpu_custom_call" | custom-call | tf_op jit(solution)/shard_map/last_step/pallas_call | solution.py:274
  (29 shorter events, 0.1 us)
Async XLA Ops:
  0.6 0.9 %copy-start.2 = (f32[1,64,576]{2,1,0:T(8,128)S(1)}, f32[1,64,576]{2,1,0:T(8,128)}, u32[]{:S(2)}) copy-start(f32[1,64,576]{2,1,0:T(8,128)} %param.8) | copy-start | bytes 442372
  1.5 9.9 %copy-start.1 = (bf16[1,576,576]{2,1,0:T(8,128)(2,1)S(1)}, bf16[1,576,576]{2,1,0:T(8,128)(2,1)}, u32[]{:S(2)}) copy-start(bf16[1,576,576]{2,1,0:T(8,128)(2,1)} %param.7) | copy-start | bytes 1990660
  1.6 12.0 %copy-start = (bf16[1,1,16,576,576]{4,3,2,1,0:T(8,128)(2,1)S(1)}, bf16[1,1,16,576,576]{4,3,2,1,0:T(8,128)(2,1)}, u32[]{:S(2)}) copy-start(bf16[1,1,16,576,576]{4,3,2,1,0:T(8,128)(2,1)} %param.6) | copy-start | bytes 31850500
  1.6 12.0 %copy-start.4 = (s32[1,1,16]{2,1,0:T(1,128)S(1)}, s32[1,1,16]{2,1,0:T(1,128)}, u32[]{:S(2)}) copy-start(s32[1,1,16]{2,1,0:T(1,128)} %param.9) | copy-start | bytes 196
  1.6 12.0 %copy-start.5 = (s32[1,1,16]{2,1,0:T(1,128)S(1)}, s32[1,1,16]{2,1,0:T(1,128)}, u32[]{:S(2)}) copy-start(s32[1,1,16]{2,1,0:T(1,128)} %param.10) | copy-start | bytes 196
  1.6 8.9 %collective-permute-start = (bf16[288,128]{1,0:T(8,128)(2,1)S(1)}, bf16[288,128]{1,0:T(8,128)(2,1)S(1)}, u32[]{:S(2)}, u32[]{:S(2)}) collective-permute-start(bf16[288,128]{1,0:T(8,128)(2,1)S(1)} %round.1.near.rest_0_), channel_id=1, source_target_pairs={{0,8},{8,0},{16,24},{24,16},{1,9},{9,1},{17,25},{25,17},{2,10},{10... | collective-permute-start | bytes 221192 | tf_op jit(solution)/shard_map/ppermute | solution.py:295
  4.7 7.8 %collective-permute-start.1 = (bf16[288,128]{1,0:T(8,128)(2,1)S(1)}, bf16[288,128]{1,0:T(8,128)(2,1)S(1)}, u32[]{:S(2)}, u32[]{:S(2)}) collective-permute-start(bf16[288,128]{1,0:T(8,128)(2,1)S(1)} %round.1.near.rest_0_), channel_id=1, source_target_pairs={{0,16},{8,24},{16,0},{24,8},{1,17},{9,25},{17,1},{25,9},{2,18},{10... | collective-permute-start | bytes 221192 | tf_op jit(solution)/shard_map/ppermute | solution.py:295
  7.3 6.3 %collective-permute-start.2 = (bf16[288,128]{1,0:T(8,128)(2,1)S(1)}, bf16[288,128]{1,0:T(8,128)(2,1)S(1)}, u32[]{:S(2)}, u32[]{:S(2)}) collective-permute-start(bf16[288,128]{1,0:T(8,128)(2,1)S(1)} %round.1.near.rest_0_), channel_id=1, source_target_pairs={{0,24},{8,16},{16,8},{24,0},{1,25},{9,17},{17,9},{25,1},{2,26},{10... | collective-permute-start | bytes 221192 | tf_op jit(solution)/shard_map/ppermute | solution.py:295
  7.3 8.0 %collective-permute-start.3 = (bf16[288,128]{1,0:T(8,128)(2,1)S(1)}, bf16[288,128]{1,0:T(8,128)(2,1)S(1)}, u32[]{:S(2)}, u32[]{:S(2)}) collective-permute-start(bf16[288,128]{1,0:T(8,128)(2,1)S(1)} %round.1.near.rest_0_), channel_id=1, source_target_pairs={{0,2},{1,3},{2,0},{3,1},{4,6},{5,7},{6,4},{7,5},{8,10},{9,11},{10,... | collective-permute-start | bytes 221192 | tf_op jit(solution)/shard_map/ppermute | solution.py:295
  9.0 6.3 %collective-permute-start.4 = (bf16[288,128]{1,0:T(8,128)(2,1)S(1)}, bf16[288,128]{1,0:T(8,128)(2,1)S(1)}, u32[]{:S(2)}, u32[]{:S(2)}) collective-permute-start(bf16[288,128]{1,0:T(8,128)(2,1)S(1)} %round.1.near.rest_0_), channel_id=1, source_target_pairs={{0,4},{1,5},{2,6},{3,7},{4,0},{5,1},{6,2},{7,3},{8,12},{9,13},{10,... | collective-permute-start | bytes 221192 | tf_op jit(solution)/shard_map/ppermute | solution.py:295
  10.5 5.3 %collective-permute-start.5 = (bf16[288,128]{1,0:T(8,128)(2,1)S(1)}, bf16[288,128]{1,0:T(8,128)(2,1)S(1)}, u32[]{:S(2)}, u32[]{:S(2)}) collective-permute-start(bf16[288,128]{1,0:T(8,128)(2,1)S(1)} %round.1.near.rest_0_), channel_id=1, source_target_pairs={{0,6},{1,7},{2,4},{3,5},{4,2},{5,3},{6,0},{7,1},{8,14},{9,15},{10,... | collective-permute-start | bytes 221192 | tf_op jit(solution)/shard_map/ppermute | solution.py:295
  15.8 1.6 %collective-permute-start.6 = (bf16[4,64,576]{2,1,0:T(8,128)(2,1)S(1)}, bf16[4,64,576]{2,1,0:T(8,128)(2,1)S(1)}, u32[]{:S(2)}, u32[]{:S(2)}) collective-permute-start(bf16[4,64,576]{2,1,0:T(8,128)(2,1)S(1)} %get-tuple-element.55), channel_id=1, source_target_pairs={{0,1},{1,0},{2,3},{3,2},{4,5},{5,4},{6,7},{7,6},{8,9},{9,8},{10,11... | collective-permute-start | bytes 884744 | tf_op jit(solution)/shard_map/ppermute | solution.py:295
  15.8 6.9 %collective-permute-start.8 = (bf16[4,288,128]{2,1,0:T(8,128)(2,1)S(1)}, bf16[4,288,128]{2,1,0:T(8,128)(2,1)S(1)}, u32[]{:S(2)}, u32[]{:S(2)}) collective-permute-start(bf16[4,288,128]{2,1,0:T(8,128)(2,1)S(1)} %pad_maximum_fusion.near_own), channel_id=1, source_target_pairs={{0,1},{1,0},{2,3},{3,2},{4,5},{5,4},{6,7},{7,6},{8,9},{9,8},{10,11... | collective-permute-start | bytes 884744 | tf_op jit(solution)/shard_map/ppermute | solution.py:295
  17.7 1.3 %collective-permute-start.7 = (f32[64,128]{1,0:T(8,128)S(1)}, f32[64,128]{1,0:T(8,128)S(1)}, u32[]{:S(2)}, u32[]{:S(2)}) collective-permute-start(f32[64,128]{1,0:T(8,128)S(1)} %gram.2.grams), channel_id=1, source_target_pairs={{0,1},{1,0},{2,3},{3,2},{4,5},{5,4},{6,7},{7,6},{8,9},{9,8},{10,11... | collective-permute-start | bytes 98312 | tf_op jit(solution)/shard_map/ppermute | solution.py:295
  19.2 4.9 %collective-permute-start.9 = (bf16[368,128]{1,0:T(8,128)(2,1)S(1)}, bf16[368,128]{1,0:T(8,128)(2,1)S(1)}, u32[]{:S(2)}, u32[]{:S(2)}) collective-permute-start(bf16[368,128]{1,0:T(8,128)(2,1)S(1)} %get-tuple-element.62), channel_id=1, source_target_pairs={{0,2},{1,3},{2,0},{3,1},{4,6},{5,7},{6,4},{7,5},{8,10},{9,11},{10,... | collective-permute-start | bytes 282632 | tf_op jit(solution)/shard_map/ppermute | solution.py:295
  20.3 5.7 %collective-permute-start.10 = (bf16[368,128]{1,0:T(8,128)(2,1)S(1)}, bf16[368,128]{1,0:T(8,128)(2,1)S(1)}, u32[]{:S(2)}, u32[]{:S(2)}) collective-permute-start(bf16[368,128]{1,0:T(8,128)(2,1)S(1)} %get-tuple-element.63), channel_id=1, source_target_pairs={{0,4},{1,5},{2,6},{3,7},{4,0},{5,1},{6,2},{7,3},{8,12},{9,13},{10,... | collective-permute-start | bytes 282632 | tf_op jit(solution)/shard_map/ppermute | solution.py:295
  21.8 5.5 %collective-permute-start.11 = (bf16[368,128]{1,0:T(8,128)(2,1)S(1)}, bf16[368,128]{1,0:T(8,128)(2,1)S(1)}, u32[]{:S(2)}, u32[]{:S(2)}) collective-permute-start(bf16[368,128]{1,0:T(8,128)(2,1)S(1)} %get-tuple-element.64), channel_id=1, source_target_pairs={{0,6},{1,7},{2,4},{3,5},{4,2},{5,3},{6,0},{7,1},{8,14},{9,15},{10,... | collective-permute-start | bytes 282632 | tf_op jit(solution)/shard_map/ppermute | solution.py:295
  27.7 7.0 %collective-permute-start.12 = (bf16[368,128]{1,0:T(8,128)(2,1)S(1)}, bf16[368,128]{1,0:T(8,128)(2,1)S(1)}, u32[]{:S(2)}, u32[]{:S(2)}) collective-permute-start(bf16[368,128]{1,0:T(8,128)(2,1)S(1)} %get-tuple-element.66), channel_id=1, source_target_pairs={{0,8},{8,0},{16,24},{24,16},{1,9},{9,1},{17,25},{25,17},{2,10},{10... | collective-permute-start | bytes 282632 | tf_op jit(solution)/shard_map/ppermute | solution.py:295
  29.9 9.0 %collective-permute-start.13 = (bf16[368,128]{1,0:T(8,128)(2,1)S(1)}, bf16[368,128]{1,0:T(8,128)(2,1)S(1)}, u32[]{:S(2)}, u32[]{:S(2)}) collective-permute-start(bf16[368,128]{1,0:T(8,128)(2,1)S(1)} %get-tuple-element.67), channel_id=1, source_target_pairs={{0,16},{8,24},{16,0},{24,8},{1,17},{9,25},{17,1},{25,9},{2,18},{10... | collective-permute-start | bytes 282632 | tf_op jit(solution)/shard_map/ppermute | solution.py:295
  33.8 6.5 %collective-permute-start.14 = (bf16[368,128]{1,0:T(8,128)(2,1)S(1)}, bf16[368,128]{1,0:T(8,128)(2,1)S(1)}, u32[]{:S(2)}, u32[]{:S(2)}) collective-permute-start(bf16[368,128]{1,0:T(8,128)(2,1)S(1)} %get-tuple-element.68), channel_id=1, source_target_pairs={{0,24},{8,16},{16,8},{24,0},{1,25},{9,17},{17,9},{25,1},{2,26},{10... | collective-permute-start | bytes 282632 | tf_op jit(solution)/shard_map/ppermute | solution.py:295
  33.8 6.5 %copy-start.3 = (f32[1,64,576]{2,1,0:T(8,128)S(1)}, f32[1,64,576]{2,1,0:T(8,128)}, u32[]{:S(2)}) copy-start(f32[1,64,576]{2,1,0:T(8,128)} %param.8) | copy-start | bytes 442372
  42.5 6.2 %collective-permute-start.15 = (bf16[288,128]{1,0:T(8,128)(2,1)S(1)}, bf16[288,128]{1,0:T(8,128)(2,1)S(1)}, u32[]{:S(2)}, u32[]{:S(2)}) collective-permute-start(bf16[288,128]{1,0:T(8,128)(2,1)S(1)} %get-tuple-element.74.near.rest_0_), channel_id=1, source_target_pairs={{0,8},{8,0},{16,24},{24,16},{1,9},{9,1},{17,25},{25,17},{2,10},{10... | collective-permute-start | bytes 221192 | tf_op jit(solution)/shard_map/ppermute | solution.py:295
  43.7 7.4 %collective-permute-start.16 = (bf16[288,128]{1,0:T(8,128)(2,1)S(1)}, bf16[288,128]{1,0:T(8,128)(2,1)S(1)}, u32[]{:S(2)}, u32[]{:S(2)}) collective-permute-start(bf16[288,128]{1,0:T(8,128)(2,1)S(1)} %get-tuple-element.74.near.rest_0_), channel_id=1, source_target_pairs={{0,16},{8,24},{16,0},{24,8},{1,17},{9,25},{17,1},{25,9},{2,18},{10... | collective-permute-start | bytes 221192 | tf_op jit(solution)/shard_map/ppermute | solution.py:295
  45.1 6.3 %collective-permute-start.17 = (bf16[288,128]{1,0:T(8,128)(2,1)S(1)}, bf16[288,128]{1,0:T(8,128)(2,1)S(1)}, u32[]{:S(2)}, u32[]{:S(2)}) collective-permute-start(bf16[288,128]{1,0:T(8,128)(2,1)S(1)} %get-tuple-element.74.near.rest_0_), channel_id=1, source_target_pairs={{0,24},{8,16},{16,8},{24,0},{1,25},{9,17},{17,9},{25,1},{2,26},{10... | collective-permute-start | bytes 221192 | tf_op jit(solution)/shard_map/ppermute | solution.py:295
  46.9 5.8 %collective-permute-start.18 = (bf16[288,128]{1,0:T(8,128)(2,1)S(1)}, bf16[288,128]{1,0:T(8,128)(2,1)S(1)}, u32[]{:S(2)}, u32[]{:S(2)}) collective-permute-start(bf16[288,128]{1,0:T(8,128)(2,1)S(1)} %get-tuple-element.74.near.rest_0_), channel_id=1, source_target_pairs={{0,2},{1,3},{2,0},{3,1},{4,6},{5,7},{6,4},{7,5},{8,10},{9,11},{10,... | collective-permute-start | bytes 221192 | tf_op jit(solution)/shard_map/ppermute | solution.py:295
  48.1 4.7 %collective-permute-start.19 = (bf16[288,128]{1,0:T(8,128)(2,1)S(1)}, bf16[288,128]{1,0:T(8,128)(2,1)S(1)}, u32[]{:S(2)}, u32[]{:S(2)}) collective-permute-start(bf16[288,128]{1,0:T(8,128)(2,1)S(1)} %get-tuple-element.74.near.rest_0_), channel_id=1, source_target_pairs={{0,4},{1,5},{2,6},{3,7},{4,0},{5,1},{6,2},{7,3},{8,12},{9,13},{10,... | collective-permute-start | bytes 221192 | tf_op jit(solution)/shard_map/ppermute | solution.py:295
  48.6 5.3 %collective-permute-start.20 = (bf16[288,128]{1,0:T(8,128)(2,1)S(1)}, bf16[288,128]{1,0:T(8,128)(2,1)S(1)}, u32[]{:S(2)}, u32[]{:S(2)}) collective-permute-start(bf16[288,128]{1,0:T(8,128)(2,1)S(1)} %get-tuple-element.74.near.rest_0_), channel_id=1, source_target_pairs={{0,6},{1,7},{2,4},{3,5},{4,2},{5,3},{6,0},{7,1},{8,14},{9,15},{10,... | collective-permute-start | bytes 221192 | tf_op jit(solution)/shard_map/ppermute | solution.py:295
  53.9 1.6 %collective-permute-start.21 = (bf16[4,64,576]{2,1,0:T(8,128)(2,1)S(1)}, bf16[4,64,576]{2,1,0:T(8,128)(2,1)S(1)}, u32[]{:S(2)}, u32[]{:S(2)}) collective-permute-start(bf16[4,64,576]{2,1,0:T(8,128)(2,1)S(1)} %get-tuple-element.79), channel_id=1, source_target_pairs={{0,1},{1,0},{2,3},{3,2},{4,5},{5,4},{6,7},{7,6},{8,9},{9,8},{10,11... | collective-permute-start | bytes 884744 | tf_op jit(solution)/shard_map/ppermute | solution.py:295
  53.9 6.9 %collective-permute-start.23 = (bf16[4,288,128]{2,1,0:T(8,128)(2,1)S(1)}, bf16[4,288,128]{2,1,0:T(8,128)(2,1)S(1)}, u32[]{:S(2)}, u32[]{:S(2)}) collective-permute-start(bf16[4,288,128]{2,1,0:T(8,128)(2,1)S(1)} %pad_maximum_fusion.1.near_own), channel_id=1, source_target_pairs={{0,1},{1,0},{2,3},{3,2},{4,5},{5,4},{6,7},{7,6},{8,9},{9,8},{10,11... | collective-permute-start | bytes 884744 | tf_op jit(solution)/shard_map/ppermute | solution.py:295
  55.9 1.3 %collective-permute-start.22 = (f32[64,128]{1,0:T(8,128)S(1)}, f32[64,128]{1,0:T(8,128)S(1)}, u32[]{:S(2)}, u32[]{:S(2)}) collective-permute-start(f32[64,128]{1,0:T(8,128)S(1)} %gram.3.grams), channel_id=1, source_target_pairs={{0,1},{1,0},{2,3},{3,2},{4,5},{5,4},{6,7},{7,6},{8,9},{9,8},{10,11... | collective-permute-start | bytes 98312 | tf_op jit(solution)/shard_map/ppermute | solution.py:295
  57.3 5.0 %collective-permute-start.24 = (bf16[368,128]{1,0:T(8,128)(2,1)S(1)}, bf16[368,128]{1,0:T(8,128)(2,1)S(1)}, u32[]{:S(2)}, u32[]{:S(2)}) collective-permute-start(bf16[368,128]{1,0:T(8,128)(2,1)S(1)} %get-tuple-element.86), channel_id=1, source_target_pairs={{0,2},{1,3},{2,0},{3,1},{4,6},{5,7},{6,4},{7,5},{8,10},{9,11},{10,... | collective-permute-start | bytes 282632 | tf_op jit(solution)/shard_map/ppermute | solution.py:295
  58.8 6.6 %collective-permute-start.25 = (bf16[368,128]{1,0:T(8,128)(2,1)S(1)}, bf16[368,128]{1,0:T(8,128)(2,1)S(1)}, u32[]{:S(2)}, u32[]{:S(2)}) collective-permute-start(bf16[368,128]{1,0:T(8,128)(2,1)S(1)} %get-tuple-element.87), channel_id=1, source_target_pairs={{0,4},{1,5},{2,6},{3,7},{4,0},{5,1},{6,2},{7,3},{8,12},{9,13},{10,... | collective-permute-start | bytes 282632 | tf_op jit(solution)/shard_map/ppermute | solution.py:295
  59.7 5.7 %collective-permute-start.26 = (bf16[368,128]{1,0:T(8,128)(2,1)S(1)}, bf16[368,128]{1,0:T(8,128)(2,1)S(1)}, u32[]{:S(2)}, u32[]{:S(2)}) collective-permute-start(bf16[368,128]{1,0:T(8,128)(2,1)S(1)} %get-tuple-element.88), channel_id=1, source_target_pairs={{0,6},{1,7},{2,4},{3,5},{4,2},{5,3},{6,0},{7,1},{8,14},{9,15},{10,... | collective-permute-start | bytes 282632 | tf_op jit(solution)/shard_map/ppermute | solution.py:295
  65.8 6.6 %collective-permute-start.27 = (bf16[368,128]{1,0:T(8,128)(2,1)S(1)}, bf16[368,128]{1,0:T(8,128)(2,1)S(1)}, u32[]{:S(2)}, u32[]{:S(2)}) collective-permute-start(bf16[368,128]{1,0:T(8,128)(2,1)S(1)} %get-tuple-element.97), channel_id=1, source_target_pairs={{0,8},{8,0},{16,24},{24,16},{1,9},{9,1},{17,25},{25,17},{2,10},{10... | collective-permute-start | bytes 282632 | tf_op jit(solution)/shard_map/ppermute | solution.py:295
  66.8 7.5 %collective-permute-start.28 = (bf16[368,128]{1,0:T(8,128)(2,1)S(1)}, bf16[368,128]{1,0:T(8,128)(2,1)S(1)}, u32[]{:S(2)}, u32[]{:S(2)}) collective-permute-start(bf16[368,128]{1,0:T(8,128)(2,1)S(1)} %get-tuple-element.98), channel_id=1, source_target_pairs={{0,16},{8,24},{16,0},{24,8},{1,17},{9,25},{17,1},{25,9},{2,18},{10... | collective-permute-start | bytes 282632 | tf_op jit(solution)/shard_map/ppermute | solution.py:295
  69.3 6.5 %collective-permute-start.29 = (bf16[368,128]{1,0:T(8,128)(2,1)S(1)}, bf16[368,128]{1,0:T(8,128)(2,1)S(1)}, u32[]{:S(2)}, u32[]{:S(2)}) collective-permute-start(bf16[368,128]{1,0:T(8,128)(2,1)S(1)} %get-tuple-element.99), channel_id=1, source_target_pairs={{0,24},{8,16},{16,8},{24,0},{1,25},{9,17},{17,9},{25,1},{2,26},{10... | collective-permute-start | bytes 282632 | tf_op jit(solution)/shard_map/ppermute | solution.py:295

commit v9 on v7

--- a/solution.py
+++ b/solution.py
@@ -288,8 +288,12 @@
     def over_chips(value):
         return [over(value, "col", 2 * d) for d in range(1, n_chip)]
 
+    def to_rows(values):
+        far = [over(value, "row", d) for d, value in enumerate(values[1:], 2)]
+        return [over(values[0], "row", 1), *far]
+
     def over_rows(value):
-        return [over(value, "row", d) for d in range(1, n_row)]
+        return to_rows([value] * (n_row - 1))
 
     index = [counts[0], rows_list[0, 0], cols_list[0, 0]]
     probes = probes[0]
@@ -346,7 +350,7 @@
             [keep, grams, own, acc_col, *parts],
             name="rows",
         )
-        parts = [over(block, "row", d + 1) for d, block in enumerate(give)]
+        parts = to_rows(give)
         if turned is None:
             (turned,) = call(
                 turn_kernel,

time: 79.4 us -> 79.4 us (level)
  no operation moved by 1% of the time
where the time goes in v9:
time: 79.4 us; the launch traced here: 79.2 us
  starting transfers between devices  36 us (45%)
  waiting for transfers between devices  22.9 us (29%)
  Pallas kernels  17.9 us (23%)
  between operations  1.47 us (2%)
  local copies, waits for them, and re-layouts  0.93 us (1%)
    ppermute x30, starting transfers between devices, over(): return lax.ppermute(value, axis, [(i, i ^ delta) for i in range(size)])  36 us
    ppermute x30, waiting for transfers between devices, over(): return lax.ppermute(value, axis, [(i, i ^ delta) for i in range(size)])  22.9 us
    pallas_call x17, Pallas kernels, call(): pl.pallas_call(kernel, out_shape=outs, in_specs=[VMEM] * len(args) if spe...  17.9 us
  transfers between devices with their start and end apart: 30, of which 16 were waited for; matrix products, arithmetic and copies ran while one was open for 0% of the time, Pallas kernels for 15%

profile of v9, /device:TPU:0, one launch (start us, length us, event | category | flops | bytes accessed | tf_op | source)
XLA Modules:
  0.0 79.2 jit_solution(9244273086573380131)
XLA Ops:
  0.6 0.0 copy-start.2
  0.6 0.9 %copy-done.2 = f32[1,64,576]{2,1,0:T(8,128)S(1)} copy-done((f32[1,64,576]{2,1,0:T(8,128)S(1)}, f32[1,64,576]{2,1,0:T(8,128)}, u32[]{:S(2)}) %copy-start.2) | copy-done | bytes 147480
  1.6 0.1 round.1.rest_0_.near
  1.6 3.1 %collective-permute-start = (bf16[288,128]{1,0:T(8,128)(2,1)S(1)}, bf16[288,128]{1,0:T(8,128)(2,1)S(1)}, u32[]{:S(2)}, u32[]{:S(2)}) collective-permute-start(bf16[288,128]{1,0:T(8,128)(2,1)S(1)} %round.1.rest_0_.near), channel_id=1, source_target_pairs={{0,8},{8,0},{16,24},{24,16},{1,9},{9,1},{17,25},{25,17},{2,10},{10... | collective-permute-start | bytes 221192 | tf_op jit(solution)/shard_map/ppermute | solution.py:286
  4.7 2.6 %collective-permute-start.1 = (bf16[288,128]{1,0:T(8,128)(2,1)S(1)}, bf16[288,128]{1,0:T(8,128)(2,1)S(1)}, u32[]{:S(2)}, u32[]{:S(2)}) collective-permute-start(bf16[288,128]{1,0:T(8,128)(2,1)S(1)} %round.1.rest_0_.near), channel_id=1, source_target_pairs={{0,16},{8,24},{16,0},{24,8},{1,17},{9,25},{17,1},{25,9},{2,18},{10... | collective-permute-start | bytes 221192 | tf_op jit(solution)/shard_map/ppermute | solution.py:286
  7.3 0.0 collective-permute-start.2
  7.3 1.7 %collective-permute-start.3 = (bf16[288,128]{1,0:T(8,128)(2,1)S(1)}, bf16[288,128]{1,0:T(8,128)(2,1)S(1)}, u32[]{:S(2)}, u32[]{:S(2)}) collective-permute-start(bf16[288,128]{1,0:T(8,128)(2,1)S(1)} %round.1.rest_0_.near), channel_id=1, source_target_pairs={{0,2},{1,3},{2,0},{3,1},{4,6},{5,7},{6,4},{7,5},{8,10},{9,11},{10,... | collective-permute-start | bytes 221192 | tf_op jit(solution)/shard_map/ppermute | solution.py:286
  9.0 1.5 %collective-permute-start.4 = (bf16[288,128]{1,0:T(8,128)(2,1)S(1)}, bf16[288,128]{1,0:T(8,128)(2,1)S(1)}, u32[]{:S(2)}, u32[]{:S(2)}) collective-permute-start(bf16[288,128]{1,0:T(8,128)(2,1)S(1)} %round.1.rest_0_.near), channel_id=1, source_target_pairs={{0,4},{1,5},{2,6},{3,7},{4,0},{5,1},{6,2},{7,3},{8,12},{9,13},{10,... | collective-permute-start | bytes 221192 | tf_op jit(solution)/shard_map/ppermute | solution.py:286
  10.5 0.3 collective-permute-start.5
  11.4 1.0 %collective-permute-done.1.rest_2_ = bf16[288,128]{1,0:T(8,128)(2,1)S(1)} collective-permute-done((bf16[288,128]{1,0:T(8,128)(2,1)S(1)}, bf16[288,128]{1,0:T(8,128)(2,1)S(1)}, u32[]{:S(2)}, u32[]{:S(2)}) %collective-permute-start.1) | collective-permute-done | bytes 73760 | tf_op jit(solution)/shard_map/ppermute | solution.py:286
  12.5 1.1 %collective-permute-done.2.rest_3_ = bf16[288,128]{1,0:T(8,128)(2,1)S(1)} collective-permute-done((bf16[288,128]{1,0:T(8,128)(2,1)S(1)}, bf16[288,128]{1,0:T(8,128)(2,1)S(1)}, u32[]{:S(2)}, u32[]{:S(2)}) %collective-permute-start.2) | collective-permute-done | bytes 73760 | tf_op jit(solution)/shard_map/ppermute | solution.py:286
  13.6 1.7 %forward.2 = (bf16[4,64,576]{2,1,0:T(8,128)(2,1)S(1)}, f32[8,64,576]{2,1,0:T(8,128)S(1)}) custom-call(s32[1]{0:T(128)} %bitcast.16.counts, s32[16]{0:T(128)S(1)} %bitcast.40, s32[16]{0:T(128)S(1)} %bitcast.44, bf16[16,576,576]{2,1,0:T(8,128)(2,1)S(1)} %bitcast.21, bf16[288,128]{1,0:T(8,128)(2,1)S(1)} %round.1.rest_0_.near, ...), custom_call_target="tpu_custom_call" | custom-call | flops 1 | tf_op jit(solution)/shard_map/forward/pallas_call | solution.py:265
  15.3 0.0 collective-permute-done.4.rest_2_
  15.3 0.5 collective-permute-done.5.rest_3_
  15.8 0.6 collective-permute-start.8
  16.4 0.7 own.2
  17.1 0.3 collective-permute-done.6.came
  17.4 0.5 gram.2
  17.9 0.2 collective-permute-start.7
  18.1 1.1 %collective-permute-done.7.grams_came = f32[64,128]{1,0:T(8,128)S(1)} collective-permute-done((f32[64,128]{1,0:T(8,128)S(1)}, f32[64,128]{1,0:T(8,128)S(1)}, u32[]{:S(2)}, u32[]{:S(2)}) %collective-permute-start.7) | collective-permute-done | bytes 32800 | tf_op jit(solution)/shard_map/ppermute | solution.py:286
  19.2 0.2 join.2
  19.3 1.1 %collective-permute-start.9 = (bf16[368,128]{1,0:T(8,128)(2,1)S(1)}, bf16[368,128]{1,0:T(8,128)(2,1)S(1)}, u32[]{:S(2)}, u32[]{:S(2)}) collective-permute-start(bf16[368,128]{1,0:T(8,128)(2,1)S(1)} %get-tuple-element.65), channel_id=1, source_target_pairs={{0,2},{1,3},{2,0},{3,1},{4,6},{5,7},{6,4},{7,5},{8,10},{9,11},{10,... | collective-permute-start | bytes 282632 | tf_op jit(solution)/shard_map/ppermute | solution.py:286
  20.4 1.5 %collective-permute-start.10 = (bf16[368,128]{1,0:T(8,128)(2,1)S(1)}, bf16[368,128]{1,0:T(8,128)(2,1)S(1)}, u32[]{:S(2)}, u32[]{:S(2)}) collective-permute-start(bf16[368,128]{1,0:T(8,128)(2,1)S(1)} %get-tuple-element.66), channel_id=1, source_target_pairs={{0,4},{1,5},{2,6},{3,7},{4,0},{5,1},{6,2},{7,3},{8,12},{9,13},{10,... | collective-permute-start | bytes 282632 | tf_op jit(solution)/shard_map/ppermute | solution.py:286
  22.0 0.9 %collective-permute-start.11 = (bf16[368,128]{1,0:T(8,128)(2,1)S(1)}, bf16[368,128]{1,0:T(8,128)(2,1)S(1)}, u32[]{:S(2)}, u32[]{:S(2)}) collective-permute-start(bf16[368,128]{1,0:T(8,128)(2,1)S(1)} %get-tuple-element.67), channel_id=1, source_target_pairs={{0,6},{1,7},{2,4},{3,5},{4,2},{5,3},{6,0},{7,1},{8,14},{9,15},{10,... | collective-permute-start | bytes 282632 | tf_op jit(solution)/shard_map/ppermute | solution.py:286
  22.9 1.3 %mirrored.2.acc = f32[4,64,576]{2,1,0:T(8,128)S(1)} custom-call(s32[1]{0:T(128)} %bitcast.17.counts, s32[16]{0:T(128)S(1)} %bitcast.41, s32[16]{0:T(128)S(1)} %bitcast.45, bf16[4,288,128]{2,1,0:T(8,128)(2,1)S(1)} %pad_maximum_fusion.near_own, bf16[4,288,128]{2,1,0:T(8,128)(2,1)S(1)} %collective-permute-done.8.near_far, bf16[16,576,576]{2,1,0:T(8,128)(2,1)S(1)} %bitcast.22), custom_call_target="tpu_custom_call" | custom-call | flops 679477248 | tf_op jit(solution)/shard_map/mirrored/pallas_call | solution.py:265
  24.2 0.0 collective-permute-done.9.rest_0_
  24.2 1.9 %collective-permute-done.10.rest_1_ = bf16[368,128]{1,0:T(8,128)(2,1)S(1)} collective-permute-done((bf16[368,128]{1,0:T(8,128)(2,1)S(1)}, bf16[368,128]{1,0:T(8,128)(2,1)S(1)}, u32[]{:S(2)}, u32[]{:S(2)}) %collective-permute-start.10) | collective-permute-done | bytes 94240 | tf_op jit(solution)/shard_map/ppermute | solution.py:286
  26.1 1.3 %collective-permute-done.11.rest_2_ = bf16[368,128]{1,0:T(8,128)(2,1)S(1)} collective-permute-done((bf16[368,128]{1,0:T(8,128)(2,1)S(1)}, bf16[368,128]{1,0:T(8,128)(2,1)S(1)}, u32[]{:S(2)}, u32[]{:S(2)}) %collective-permute-start.11) | collective-permute-done | bytes 94240 | tf_op jit(solution)/shard_map/ppermute | solution.py:286
  27.4 0.4 rows.2
  27.9 2.1 %collective-permute-start.12 = (bf16[368,128]{1,0:T(8,128)(2,1)S(1)}, bf16[368,128]{1,0:T(8,128)(2,1)S(1)}, u32[]{:S(2)}, u32[]{:S(2)}) collective-permute-start(bf16[368,128]{1,0:T(8,128)(2,1)S(1)} %get-tuple-element.69), channel_id=1, source_target_pairs={{0,8},{8,0},{16,24},{24,16},{1,9},{9,1},{17,25},{25,17},{2,10},{10... | collective-permute-start | bytes 282632 | tf_op jit(solution)/shard_map/ppermute | solution.py:286
  30.0 3.7 %collective-permute-start.13 = (bf16[368,128]{1,0:T(8,128)(2,1)S(1)}, bf16[368,128]{1,0:T(8,128)(2,1)S(1)}, u32[]{:S(2)}, u32[]{:S(2)}) collective-permute-start(bf16[368,128]{1,0:T(8,128)(2,1)S(1)} %get-tuple-element.70), channel_id=1, source_target_pairs={{0,16},{8,24},{16,0},{24,8},{1,17},{9,25},{17,1},{25,9},{2,18},{10... | collective-permute-start | bytes 282632 | tf_op jit(solution)/shard_map/ppermute | solution.py:286
  33.7 0.9 %turn.1.tiles = bf16[16,576,576]{2,1,0:T(8,128)(2,1)S(1)} custom-call(s32[1]{0:T(128)} %bitcast.18.counts, bf16[16,576,576]{2,1,0:T(8,128)(2,1)S(1)} %bitcast.23, f32[64,128]{1,0:T(8,128)S(1)} %get-tuple-element.68.after.grams), custom_call_target="tpu_custom_call" | custom-call | tf_op jit(solution)/shard_map/turn/pallas_call | solution.py:265
  34.6 4.2 %collective-permute-done.13.rest_1_ = bf16[368,128]{1,0:T(8,128)(2,1)S(1)} collective-permute-done((bf16[368,128]{1,0:T(8,128)(2,1)S(1)}, bf16[368,128]{1,0:T(8,128)(2,1)S(1)}, u32[]{:S(2)}, u32[]{:S(2)}) %collective-permute-start.13) | collective-permute-done | bytes 94240 | tf_op jit(solution)/shard_map/ppermute | solution.py:286
  38.8 1.4 %collective-permute-done.14.rest_2_ = bf16[368,128]{1,0:T(8,128)(2,1)S(1)} collective-permute-done((bf16[368,128]{1,0:T(8,128)(2,1)S(1)}, bf16[368,128]{1,0:T(8,128)(2,1)S(1)}, u32[]{:S(2)}, u32[]{:S(2)}) %collective-permute-start.14) | collective-permute-done | bytes 94240 | tf_op jit(solution)/shard_map/ppermute | solution.py:286
  40.2 2.1 %first_step.1 = (f32[64,576]{1,0:T(8,128)S(1)}, f32[64,576]{1,0:T(8,128)S(1)}, bf16[288,128]{1,0:T(8,128)(2,1)S(1)}, f32[64,128]{1,0:T(8,128)S(1)}, f32[64,64]{1,0:T(8,128)S(1)}) custom-call(f32[64,576]{1,0:T(8,128)S(1)} %get-tuple-element.73.mine, f32[64,128]{1,0:T(8,128)S(1)} %get-tuple-element.68.after.grams, f32[64,576]{1,0:T(8,128)S(1)} %bitcast.29, ...), custom_call_target="tpu_custom_call" | custom-call | tf_op jit(solution)/shard_map/first_step/pallas_call | solution.py:265
  42.3 1.2 %collective-permute-start.15 = (bf16[288,128]{1,0:T(8,128)(2,1)S(1)}, bf16[288,128]{1,0:T(8,128)(2,1)S(1)}, u32[]{:S(2)}, u32[]{:S(2)}) collective-permute-start(bf16[288,128]{1,0:T(8,128)(2,1)S(1)} %get-tuple-element.77.rest_0_.near), channel_id=1, source_target_pairs={{0,8},{8,0},{16,24},{24,16},{1,9},{9,1},{17,25},{25,17},{2,10},{10... | collective-permute-start | bytes 221192 | tf_op jit(solution)/shard_map/ppermute | solution.py:286
  43.5 1.4 %collective-permute-start.16 = (bf16[288,128]{1,0:T(8,128)(2,1)S(1)}, bf16[288,128]{1,0:T(8,128)(2,1)S(1)}, u32[]{:S(2)}, u32[]{:S(2)}) collective-permute-start(bf16[288,128]{1,0:T(8,128)(2,1)S(1)} %get-tuple-element.77.rest_0_.near), channel_id=1, source_target_pairs={{0,16},{8,24},{16,0},{24,8},{1,17},{9,25},{17,1},{25,9},{2,18},{10... | collective-permute-start | bytes 221192 | tf_op jit(solution)/shard_map/ppermute | solution.py:286
  44.9 1.8 %collective-permute-start.17 = (bf16[288,128]{1,0:T(8,128)(2,1)S(1)}, bf16[288,128]{1,0:T(8,128)(2,1)S(1)}, u32[]{:S(2)}, u32[]{:S(2)}) collective-permute-start(bf16[288,128]{1,0:T(8,128)(2,1)S(1)} %get-tuple-element.77.rest_0_.near), channel_id=1, source_target_pairs={{0,24},{8,16},{16,8},{24,0},{1,25},{9,17},{17,9},{25,1},{2,26},{10... | collective-permute-start | bytes 221192 | tf_op jit(solution)/shard_map/ppermute | solution.py:286
  46.7 1.1 %collective-permute-start.18 = (bf16[288,128]{1,0:T(8,128)(2,1)S(1)}, bf16[288,128]{1,0:T(8,128)(2,1)S(1)}, u32[]{:S(2)}, u32[]{:S(2)}) collective-permute-start(bf16[288,128]{1,0:T(8,128)(2,1)S(1)} %get-tuple-element.77.rest_0_.near), channel_id=1, source_target_pairs={{0,2},{1,3},{2,0},{3,1},{4,6},{5,7},{6,4},{7,5},{8,10},{9,11},{10,... | collective-permute-start | bytes 221192 | tf_op jit(solution)/shard_map/ppermute | solution.py:286
  47.8 0.6 collective-permute-start.19
  48.5 1.7 %collective-permute-start.20 = (bf16[288,128]{1,0:T(8,128)(2,1)S(1)}, bf16[288,128]{1,0:T(8,128)(2,1)S(1)}, u32[]{:S(2)}, u32[]{:S(2)}) collective-permute-start(bf16[288,128]{1,0:T(8,128)(2,1)S(1)} %get-tuple-element.77.rest_0_.near), channel_id=1, source_target_pairs={{0,6},{1,7},{2,4},{3,5},{4,2},{5,3},{6,0},{7,1},{8,14},{9,15},{10,... | collective-permute-start | bytes 221192 | tf_op jit(solution)/shard_map/ppermute | solution.py:286
  50.2 1.0 %collective-permute-done.17.rest_3_ = bf16[288,128]{1,0:T(8,128)(2,1)S(1)} collective-permute-done((bf16[288,128]{1,0:T(8,128)(2,1)S(1)}, bf16[288,128]{1,0:T(8,128)(2,1)S(1)}, u32[]{:S(2)}, u32[]{:S(2)}) %collective-permute-start.17) | collective-permute-done | bytes 73760 | tf_op jit(solution)/shard_map/ppermute | solution.py:286
  51.2 1.3 %forward.3 = (bf16[4,64,576]{2,1,0:T(8,128)(2,1)S(1)}, f32[8,64,576]{2,1,0:T(8,128)S(1)}) custom-call(s32[1]{0:T(128)} %bitcast.19.counts, s32[16]{0:T(128)S(1)} %bitcast.42, s32[16]{0:T(128)S(1)} %bitcast.46, bf16[16,576,576]{2,1,0:T(8,128)(2,1)S(1)} %turn.1.tiles, bf16[288,128]{1,0:T(8,128)(2,1)S(1)} %get-tuple-element.77.rest_0_.near, ...), custom_call_target="tpu_custom_call" | custom-call | flops 1 | tf_op jit(solution)/shard_map/forward/pallas_call | solution.py:265
  52.6 1.2 %collective-permute-done.20.rest_3_ = bf16[288,128]{1,0:T(8,128)(2,1)S(1)} collective-permute-done((bf16[288,128]{1,0:T(8,128)(2,1)S(1)}, bf16[288,128]{1,0:T(8,128)(2,1)S(1)}, u32[]{:S(2)}, u32[]{:S(2)}) %collective-permute-start.20) | collective-permute-done | bytes 73760 | tf_op jit(solution)/shard_map/ppermute | solution.py:286
  53.8 0.6 collective-permute-start.23
  54.3 0.7 own.3
  55.1 0.3 collective-permute-done.21.came
  55.4 0.5 gram.3
  55.8 0.2 collective-permute-start.22
  56.0 1.1 %collective-permute-done.22.grams_came = f32[64,128]{1,0:T(8,128)S(1)} collective-permute-done((f32[64,128]{1,0:T(8,128)S(1)}, f32[64,128]{1,0:T(8,128)S(1)}, u32[]{:S(2)}, u32[]{:S(2)}) %collective-permute-start.22) | collective-permute-done | bytes 32800 | tf_op jit(solution)/shard_map/ppermute | solution.py:286
  57.1 0.2 join.3
  57.3 1.4 %collective-permute-start.24 = (bf16[368,128]{1,0:T(8,128)(2,1)S(1)}, bf16[368,128]{1,0:T(8,128)(2,1)S(1)}, u32[]{:S(2)}, u32[]{:S(2)}) collective-permute-start(bf16[368,128]{1,0:T(8,128)(2,1)S(1)} %get-tuple-element.90), channel_id=1, source_target_pairs={{0,2},{1,3},{2,0},{3,1},{4,6},{5,7},{6,4},{7,5},{8,10},{9,11},{10,... | collective-permute-start | bytes 282632 | tf_op jit(solution)/shard_map/ppermute | solution.py:286
  58.7 0.9 %collective-permute-start.25 = (bf16[368,128]{1,0:T(8,128)(2,1)S(1)}, bf16[368,128]{1,0:T(8,128)(2,1)S(1)}, u32[]{:S(2)}, u32[]{:S(2)}) collective-permute-start(bf16[368,128]{1,0:T(8,128)(2,1)S(1)} %get-tuple-element.91), channel_id=1, source_target_pairs={{0,4},{1,5},{2,6},{3,7},{4,0},{5,1},{6,2},{7,3},{8,12},{9,13},{10,... | collective-permute-start | bytes 282632 | tf_op jit(solution)/shard_map/ppermute | solution.py:286
  59.6 1.2 %collective-permute-start.26 = (bf16[368,128]{1,0:T(8,128)(2,1)S(1)}, bf16[368,128]{1,0:T(8,128)(2,1)S(1)}, u32[]{:S(2)}, u32[]{:S(2)}) collective-permute-start(bf16[368,128]{1,0:T(8,128)(2,1)S(1)} %get-tuple-element.92), channel_id=1, source_target_pairs={{0,6},{1,7},{2,4},{3,5},{4,2},{5,3},{6,0},{7,1},{8,14},{9,15},{10,... | collective-permute-start | bytes 282632 | tf_op jit(solution)/shard_map/ppermute | solution.py:286
  60.8 1.5 %mirrored.3.acc = f32[4,64,576]{2,1,0:T(8,128)S(1)} custom-call(s32[1]{0:T(128)} %bitcast.20.counts, s32[16]{0:T(128)S(1)} %bitcast.43, s32[16]{0:T(128)S(1)} %bitcast.47, bf16[4,288,128]{2,1,0:T(8,128)(2,1)S(1)} %pad_maximum_fusion.1.near_own, bf16[4,288,128]{2,1,0:T(8,128)(2,1)S(1)} %collective-permute-done.23.near_far, bf16[16,576,576]{2,1,0:T(8,128)(2,1)S(1)} %bitcast.24), custom_call_target="tpu_custom_call" | custom-call | flops 679477248 | tf_op jit(solution)/shard_map/mirrored/pallas_call | solution.py:265
  62.3 3.0 %collective-permute-done.25.rest_1_ = bf16[368,128]{1,0:T(8,128)(2,1)S(1)} collective-permute-done((bf16[368,128]{1,0:T(8,128)(2,1)S(1)}, bf16[368,128]{1,0:T(8,128)(2,1)S(1)}, u32[]{:S(2)}, u32[]{:S(2)}) %collective-permute-start.25) | collective-permute-done | bytes 94240 | tf_op jit(solution)/shard_map/ppermute | solution.py:286
  65.3 0.4 rows.3
  65.7 1.3 %collective-permute-start.27 = (bf16[368,128]{1,0:T(8,128)(2,1)S(1)}, bf16[368,128]{1,0:T(8,128)(2,1)S(1)}, u32[]{:S(2)}, u32[]{:S(2)}) collective-permute-start(bf16[368,128]{1,0:T(8,128)(2,1)S(1)} %get-tuple-element.101), channel_id=1, source_target_pairs={{0,8},{8,0},{16,24},{24,16},{1,9},{9,1},{17,25},{25,17},{2,10},{10... | collective-permute-start | bytes 282632 | tf_op jit(solution)/shard_map/ppermute | solution.py:286
  67.0 2.4 %collective-permute-start.28 = (bf16[368,128]{1,0:T(8,128)(2,1)S(1)}, bf16[368,128]{1,0:T(8,128)(2,1)S(1)}, u32[]{:S(2)}, u32[]{:S(2)}) collective-permute-start(bf16[368,128]{1,0:T(8,128)(2,1)S(1)} %get-tuple-element.102), channel_id=1, source_target_pairs={{0,16},{8,24},{16,0},{24,8},{1,17},{9,25},{17,1},{25,9},{2,18},{10... | collective-permute-start | bytes 282632 | tf_op jit(solution)/shard_map/ppermute | solution.py:286
  69.4 0.8 collective-permute-start.29
  70.2 2.1 %between.1 = (f32[64,64]{1,0:T(8,128)S(1)}, f32[64,64]{1,0:T(8,128)S(1)}, f32[64,576]{1,0:T(8,128)S(1)}) custom-call(f32[64,128]{1,0:T(8,128)S(1)} %get-tuple-element.96.totals, f32[64,64]{1,0:T(8,128)S(1)} %get-tuple-element.97.alpha, f32[64,576]{1,0:T(8,128)S(1)} %bitcast.30), custom_call_target="tpu_custom_call" | custom-call | tf_op jit(solution)/shard_map/between/pallas_call | solution.py:265
  72.3 2.2 %collective-permute-done.28.rest_1_ = bf16[368,128]{1,0:T(8,128)(2,1)S(1)} collective-permute-done((bf16[368,128]{1,0:T(8,128)(2,1)S(1)}, bf16[368,128]{1,0:T(8,128)(2,1)S(1)}, u32[]{:S(2)}, u32[]{:S(2)}) %collective-permute-start.28) | collective-permute-done | bytes 94240 | tf_op jit(solution)/shard_map/ppermute | solution.py:286
  74.6 1.3 %collective-permute-done.29.rest_2_ = bf16[368,128]{1,0:T(8,128)(2,1)S(1)} collective-permute-done((bf16[368,128]{1,0:T(8,128)(2,1)S(1)}, bf16[368,128]{1,0:T(8,128)(2,1)S(1)}, u32[]{:S(2)}, u32[]{:S(2)}) %collective-permute-start.29) | collective-permute-done | bytes 94240 | tf_op jit(solution)/shard_map/ppermute | solution.py:286
  75.9 3.3 %last_step.1 = (f32[64,576]{1,0:T(8,128)}, f32[64,576]{1,0:T(8,128)}) custom-call(f32[64,576]{1,0:T(8,128)S(1)} %get-tuple-element.93.mine, f32[64,128]{1,0:T(8,128)S(1)} %get-tuple-element.94.grams, f32[64,576]{1,0:T(8,128)S(1)} %bitcast.31, f32[64,576]{1,0:T(8,128)S(1)} %get-tuple-element.95.image_in, ...), custom_call_target="tpu_custom_call" | custom-call | tf_op jit(solution)/shard_map/last_step/pallas_call | solution.py:265
  (27 shorter events, 0.1 us)
Async XLA Ops:
  0.6 0.9 %copy-start.2 = (f32[1,64,576]{2,1,0:T(8,128)S(1)}, f32[1,64,576]{2,1,0:T(8,128)}, u32[]{:S(2)}) copy-start(f32[1,64,576]{2,1,0:T(8,128)} %param.8) | copy-start | bytes 442372
  1.5 12.0 %copy-start = (bf16[1,1,16,576,576]{4,3,2,1,0:T(8,128)(2,1)S(1)}, bf16[1,1,16,576,576]{4,3,2,1,0:T(8,128)(2,1)}, u32[]{:S(2)}) copy-start(bf16[1,1,16,576,576]{4,3,2,1,0:T(8,128)(2,1)} %param.6) | copy-start | bytes 31850500
  1.6 12.0 %copy-start.4 = (s32[1,1,16]{2,1,0:T(1,128)S(1)}, s32[1,1,16]{2,1,0:T(1,128)}, u32[]{:S(2)}) copy-start(s32[1,1,16]{2,1,0:T(1,128)} %param.9) | copy-start | bytes 196
  1.6 12.0 %copy-start.5 = (s32[1,1,16]{2,1,0:T(1,128)S(1)}, s32[1,1,16]{2,1,0:T(1,128)}, u32[]{:S(2)}) copy-start(s32[1,1,16]{2,1,0:T(1,128)} %param.10) | copy-start | bytes 196
  1.6 14.8 %copy-start.1 = (bf16[1,576,576]{2,1,0:T(8,128)(2,1)S(1)}, bf16[1,576,576]{2,1,0:T(8,128)(2,1)}, u32[]{:S(2)}) copy-start(bf16[1,576,576]{2,1,0:T(8,128)(2,1)} %param.7) | copy-start | bytes 1990660
  1.6 14.8 %copy-start.3 = (f32[1,64,576]{2,1,0:T(8,128)S(1)}, f32[1,64,576]{2,1,0:T(8,128)}, u32[]{:S(2)}) copy-start(f32[1,64,576]{2,1,0:T(8,128)} %param.8) | copy-start | bytes 442372
  1.6 8.9 %collective-permute-start = (bf16[288,128]{1,0:T(8,128)(2,1)S(1)}, bf16[288,128]{1,0:T(8,128)(2,1)S(1)}, u32[]{:S(2)}, u32[]{:S(2)}) collective-permute-start(bf16[288,128]{1,0:T(8,128)(2,1)S(1)} %round.1.rest_0_.near), channel_id=1, source_target_pairs={{0,8},{8,0},{16,24},{24,16},{1,9},{9,1},{17,25},{25,17},{2,10},{10... | collective-permute-start | bytes 221192 | tf_op jit(solution)/shard_map/ppermute | solution.py:286
  4.7 7.8 %collective-permute-start.1 = (bf16[288,128]{1,0:T(8,128)(2,1)S(1)}, bf16[288,128]{1,0:T(8,128)(2,1)S(1)}, u32[]{:S(2)}, u32[]{:S(2)}) collective-permute-start(bf16[288,128]{1,0:T(8,128)(2,1)S(1)} %round.1.rest_0_.near), channel_id=1, source_target_pairs={{0,16},{8,24},{16,0},{24,8},{1,17},{9,25},{17,1},{25,9},{2,18},{10... | collective-permute-start | bytes 221192 | tf_op jit(solution)/shard_map/ppermute | solution.py:286
  7.3 6.3 %collective-permute-start.2 = (bf16[288,128]{1,0:T(8,128)(2,1)S(1)}, bf16[288,128]{1,0:T(8,128)(2,1)S(1)}, u32[]{:S(2)}, u32[]{:S(2)}) collective-permute-start(bf16[288,128]{1,0:T(8,128)(2,1)S(1)} %round.1.rest_0_.near), channel_id=1, source_target_pairs={{0,24},{8,16},{16,8},{24,0},{1,25},{9,17},{17,9},{25,1},{2,26},{10... | collective-permute-start | bytes 221192 | tf_op jit(solution)/shard_map/ppermute | solution.py:286
  7.3 8.0 %collective-permute-start.3 = (bf16[288,128]{1,0:T(8,128)(2,1)S(1)}, bf16[288,128]{1,0:T(8,128)(2,1)S(1)}, u32[]{:S(2)}, u32[]{:S(2)}) collective-permute-start(bf16[288,128]{1,0:T(8,128)(2,1)S(1)} %round.1.rest_0_.near), channel_id=1, source_target_pairs={{0,2},{1,3},{2,0},{3,1},{4,6},{5,7},{6,4},{7,5},{8,10},{9,11},{10,... | collective-permute-start | bytes 221192 | tf_op jit(solution)/shard_map/ppermute | solution.py:286
  9.0 6.3 %collective-permute-start.4 = (bf16[288,128]{1,0:T(8,128)(2,1)S(1)}, bf16[288,128]{1,0:T(8,128)(2,1)S(1)}, u32[]{:S(2)}, u32[]{:S(2)}) collective-permute-start(bf16[288,128]{1,0:T(8,128)(2,1)S(1)} %round.1.rest_0_.near), channel_id=1, source_target_pairs={{0,4},{1,5},{2,6},{3,7},{4,0},{5,1},{6,2},{7,3},{8,12},{9,13},{10,... | collective-permute-start | bytes 221192 | tf_op jit(solution)/shard_map/ppermute | solution.py:286
  10.5 5.3 %collective-permute-start.5 = (bf16[288,128]{1,0:T(8,128)(2,1)S(1)}, bf16[288,128]{1,0:T(8,128)(2,1)S(1)}, u32[]{:S(2)}, u32[]{:S(2)}) collective-permute-start(bf16[288,128]{1,0:T(8,128)(2,1)S(1)} %round.1.rest_0_.near), channel_id=1, source_target_pairs={{0,6},{1,7},{2,4},{3,5},{4,2},{5,3},{6,0},{7,1},{8,14},{9,15},{10,... | collective-permute-start | bytes 221192 | tf_op jit(solution)/shard_map/ppermute | solution.py:286
  15.8 1.6 %collective-permute-start.6 = (bf16[4,64,576]{2,1,0:T(8,128)(2,1)S(1)}, bf16[4,64,576]{2,1,0:T(8,128)(2,1)S(1)}, u32[]{:S(2)}, u32[]{:S(2)}) collective-permute-start(bf16[4,64,576]{2,1,0:T(8,128)(2,1)S(1)} %get-tuple-element.56), channel_id=1, source_target_pairs={{0,1},{1,0},{2,3},{3,2},{4,5},{5,4},{6,7},{7,6},{8,9},{9,8},{10,11... | collective-permute-start | bytes 884744 | tf_op jit(solution)/shard_map/ppermute | solution.py:286
  15.8 7.1 %collective-permute-start.8 = (bf16[4,288,128]{2,1,0:T(8,128)(2,1)S(1)}, bf16[4,288,128]{2,1,0:T(8,128)(2,1)S(1)}, u32[]{:S(2)}, u32[]{:S(2)}) collective-permute-start(bf16[4,288,128]{2,1,0:T(8,128)(2,1)S(1)} %pad_maximum_fusion.near_own), channel_id=1, source_target_pairs={{0,1},{1,0},{2,3},{3,2},{4,5},{5,4},{6,7},{7,6},{8,9},{9,8},{10,11... | collective-permute-start | bytes 884744 | tf_op jit(solution)/shard_map/ppermute | solution.py:286
  17.9 1.3 %collective-permute-start.7 = (f32[64,128]{1,0:T(8,128)S(1)}, f32[64,128]{1,0:T(8,128)S(1)}, u32[]{:S(2)}, u32[]{:S(2)}) collective-permute-start(f32[64,128]{1,0:T(8,128)S(1)} %get-tuple-element.62.grams), channel_id=1, source_target_pairs={{0,1},{1,0},{2,3},{3,2},{4,5},{5,4},{6,7},{7,6},{8,9},{9,8},{10,11... | collective-permute-start | bytes 98312 | tf_op jit(solution)/shard_map/ppermute | solution.py:286
  19.3 4.9 %collective-permute-start.9 = (bf16[368,128]{1,0:T(8,128)(2,1)S(1)}, bf16[368,128]{1,0:T(8,128)(2,1)S(1)}, u32[]{:S(2)}, u32[]{:S(2)}) collective-permute-start(bf16[368,128]{1,0:T(8,128)(2,1)S(1)} %get-tuple-element.65), channel_id=1, source_target_pairs={{0,2},{1,3},{2,0},{3,1},{4,6},{5,7},{6,4},{7,5},{8,10},{9,11},{10,... | collective-permute-start | bytes 282632 | tf_op jit(solution)/shard_map/ppermute | solution.py:286
  20.4 5.7 %collective-permute-start.10 = (bf16[368,128]{1,0:T(8,128)(2,1)S(1)}, bf16[368,128]{1,0:T(8,128)(2,1)S(1)}, u32[]{:S(2)}, u32[]{:S(2)}) collective-permute-start(bf16[368,128]{1,0:T(8,128)(2,1)S(1)} %get-tuple-element.66), channel_id=1, source_target_pairs={{0,4},{1,5},{2,6},{3,7},{4,0},{5,1},{6,2},{7,3},{8,12},{9,13},{10,... | collective-permute-start | bytes 282632 | tf_op jit(solution)/shard_map/ppermute | solution.py:286
  22.0 5.5 %collective-permute-start.11 = (bf16[368,128]{1,0:T(8,128)(2,1)S(1)}, bf16[368,128]{1,0:T(8,128)(2,1)S(1)}, u32[]{:S(2)}, u32[]{:S(2)}) collective-permute-start(bf16[368,128]{1,0:T(8,128)(2,1)S(1)} %get-tuple-element.67), channel_id=1, source_target_pairs={{0,6},{1,7},{2,4},{3,5},{4,2},{5,3},{6,0},{7,1},{8,14},{9,15},{10,... | collective-permute-start | bytes 282632 | tf_op jit(solution)/shard_map/ppermute | solution.py:286
  27.9 6.7 %collective-permute-start.12 = (bf16[368,128]{1,0:T(8,128)(2,1)S(1)}, bf16[368,128]{1,0:T(8,128)(2,1)S(1)}, u32[]{:S(2)}, u32[]{:S(2)}) collective-permute-start(bf16[368,128]{1,0:T(8,128)(2,1)S(1)} %get-tuple-element.69), channel_id=1, source_target_pairs={{0,8},{8,0},{16,24},{24,16},{1,9},{9,1},{17,25},{25,17},{2,10},{10... | collective-permute-start | bytes 282632 | tf_op jit(solution)/shard_map/ppermute | solution.py:286
  30.0 8.8 %collective-permute-start.13 = (bf16[368,128]{1,0:T(8,128)(2,1)S(1)}, bf16[368,128]{1,0:T(8,128)(2,1)S(1)}, u32[]{:S(2)}, u32[]{:S(2)}) collective-permute-start(bf16[368,128]{1,0:T(8,128)(2,1)S(1)} %get-tuple-element.70), channel_id=1, source_target_pairs={{0,16},{8,24},{16,0},{24,8},{1,17},{9,25},{17,1},{25,9},{2,18},{10... | collective-permute-start | bytes 282632 | tf_op jit(solution)/shard_map/ppermute | solution.py:286
  33.7 6.5 %collective-permute-start.14 = (bf16[368,128]{1,0:T(8,128)(2,1)S(1)}, bf16[368,128]{1,0:T(8,128)(2,1)S(1)}, u32[]{:S(2)}, u32[]{:S(2)}) collective-permute-start(bf16[368,128]{1,0:T(8,128)(2,1)S(1)} %get-tuple-element.71), channel_id=1, source_target_pairs={{0,24},{8,16},{16,8},{24,0},{1,25},{9,17},{17,9},{25,1},{2,26},{10... | collective-permute-start | bytes 282632 | tf_op jit(solution)/shard_map/ppermute | solution.py:286
  42.3 6.2 %collective-permute-start.15 = (bf16[288,128]{1,0:T(8,128)(2,1)S(1)}, bf16[288,128]{1,0:T(8,128)(2,1)S(1)}, u32[]{:S(2)}, u32[]{:S(2)}) collective-permute-start(bf16[288,128]{1,0:T(8,128)(2,1)S(1)} %get-tuple-element.77.rest_0_.near), channel_id=1, source_target_pairs={{0,8},{8,0},{16,24},{24,16},{1,9},{9,1},{17,25},{25,17},{2,10},{10... | collective-permute-start | bytes 221192 | tf_op jit(solution)/shard_map/ppermute | solution.py:286
  43.5 6.7 %collective-permute-start.16 = (bf16[288,128]{1,0:T(8,128)(2,1)S(1)}, bf16[288,128]{1,0:T(8,128)(2,1)S(1)}, u32[]{:S(2)}, u32[]{:S(2)}) collective-permute-start(bf16[288,128]{1,0:T(8,128)(2,1)S(1)} %get-tuple-element.77.rest_0_.near), channel_id=1, source_target_pairs={{0,16},{8,24},{16,0},{24,8},{1,17},{9,25},{17,1},{25,9},{2,18},{10... | collective-permute-start | bytes 221192 | tf_op jit(solution)/shard_map/ppermute | solution.py:286
  44.9 6.3 %collective-permute-start.17 = (bf16[288,128]{1,0:T(8,128)(2,1)S(1)}, bf16[288,128]{1,0:T(8,128)(2,1)S(1)}, u32[]{:S(2)}, u32[]{:S(2)}) collective-permute-start(bf16[288,128]{1,0:T(8,128)(2,1)S(1)} %get-tuple-element.77.rest_0_.near), channel_id=1, source_target_pairs={{0,24},{8,16},{16,8},{24,0},{1,25},{9,17},{17,9},{25,1},{2,26},{10... | collective-permute-start | bytes 221192 | tf_op jit(solution)/shard_map/ppermute | solution.py:286
  46.7 5.8 %collective-permute-start.18 = (bf16[288,128]{1,0:T(8,128)(2,1)S(1)}, bf16[288,128]{1,0:T(8,128)(2,1)S(1)}, u32[]{:S(2)}, u32[]{:S(2)}) collective-permute-start(bf16[288,128]{1,0:T(8,128)(2,1)S(1)} %get-tuple-element.77.rest_0_.near), channel_id=1, source_target_pairs={{0,2},{1,3},{2,0},{3,1},{4,6},{5,7},{6,4},{7,5},{8,10},{9,11},{10,... | collective-permute-start | bytes 221192 | tf_op jit(solution)/shard_map/ppermute | solution.py:286
  47.8 4.7 %collective-permute-start.19 = (bf16[288,128]{1,0:T(8,128)(2,1)S(1)}, bf16[288,128]{1,0:T(8,128)(2,1)S(1)}, u32[]{:S(2)}, u32[]{:S(2)}) collective-permute-start(bf16[288,128]{1,0:T(8,128)(2,1)S(1)} %get-tuple-element.77.rest_0_.near), channel_id=1, source_target_pairs={{0,4},{1,5},{2,6},{3,7},{4,0},{5,1},{6,2},{7,3},{8,12},{9,13},{10,... | collective-permute-start | bytes 221192 | tf_op jit(solution)/shard_map/ppermute | solution.py:286
  48.5 5.3 %collective-permute-start.20 = (bf16[288,128]{1,0:T(8,128)(2,1)S(1)}, bf16[288,128]{1,0:T(8,128)(2,1)S(1)}, u32[]{:S(2)}, u32[]{:S(2)}) collective-permute-start(bf16[288,128]{1,0:T(8,128)(2,1)S(1)} %get-tuple-element.77.rest_0_.near), channel_id=1, source_target_pairs={{0,6},{1,7},{2,4},{3,5},{4,2},{5,3},{6,0},{7,1},{8,14},{9,15},{10,... | collective-permute-start | bytes 221192 | tf_op jit(solution)/shard_map/ppermute | solution.py:286
  53.7 1.6 %collective-permute-start.21 = (bf16[4,64,576]{2,1,0:T(8,128)(2,1)S(1)}, bf16[4,64,576]{2,1,0:T(8,128)(2,1)S(1)}, u32[]{:S(2)}, u32[]{:S(2)}) collective-permute-start(bf16[4,64,576]{2,1,0:T(8,128)(2,1)S(1)} %get-tuple-element.80), channel_id=1, source_target_pairs={{0,1},{1,0},{2,3},{3,2},{4,5},{5,4},{6,7},{7,6},{8,9},{9,8},{10,11... | collective-permute-start | bytes 884744 | tf_op jit(solution)/shard_map/ppermute | solution.py:286
  53.8 7.1 %collective-permute-start.23 = (bf16[4,288,128]{2,1,0:T(8,128)(2,1)S(1)}, bf16[4,288,128]{2,1,0:T(8,128)(2,1)S(1)}, u32[]{:S(2)}, u32[]{:S(2)}) collective-permute-start(bf16[4,288,128]{2,1,0:T(8,128)(2,1)S(1)} %pad_maximum_fusion.1.near_own), channel_id=1, source_target_pairs={{0,1},{1,0},{2,3},{3,2},{4,5},{5,4},{6,7},{7,6},{8,9},{9,8},{10,11... | collective-permute-start | bytes 884744 | tf_op jit(solution)/shard_map/ppermute | solution.py:286
  55.8 1.3 %collective-permute-start.22 = (f32[64,128]{1,0:T(8,128)S(1)}, f32[64,128]{1,0:T(8,128)S(1)}, u32[]{:S(2)}, u32[]{:S(2)}) collective-permute-start(f32[64,128]{1,0:T(8,128)S(1)} %get-tuple-element.87.grams), channel_id=1, source_target_pairs={{0,1},{1,0},{2,3},{3,2},{4,5},{5,4},{6,7},{7,6},{8,9},{9,8},{10,11... | collective-permute-start | bytes 98312 | tf_op jit(solution)/shard_map/ppermute | solution.py:286
  57.3 5.0 %collective-permute-start.24 = (bf16[368,128]{1,0:T(8,128)(2,1)S(1)}, bf16[368,128]{1,0:T(8,128)(2,1)S(1)}, u32[]{:S(2)}, u32[]{:S(2)}) collective-permute-start(bf16[368,128]{1,0:T(8,128)(2,1)S(1)} %get-tuple-element.90), channel_id=1, source_target_pairs={{0,2},{1,3},{2,0},{3,1},{4,6},{5,7},{6,4},{7,5},{8,10},{9,11},{10,... | collective-permute-start | bytes 282632 | tf_op jit(solution)/shard_map/ppermute | solution.py:286
  58.7 6.6 %collective-permute-start.25 = (bf16[368,128]{1,0:T(8,128)(2,1)S(1)}, bf16[368,128]{1,0:T(8,128)(2,1)S(1)}, u32[]{:S(2)}, u32[]{:S(2)}) collective-permute-start(bf16[368,128]{1,0:T(8,128)(2,1)S(1)} %get-tuple-element.91), channel_id=1, source_target_pairs={{0,4},{1,5},{2,6},{3,7},{4,0},{5,1},{6,2},{7,3},{8,12},{9,13},{10,... | collective-permute-start | bytes 282632 | tf_op jit(solution)/shard_map/ppermute | solution.py:286
  59.6 5.7 %collective-permute-start.26 = (bf16[368,128]{1,0:T(8,128)(2,1)S(1)}, bf16[368,128]{1,0:T(8,128)(2,1)S(1)}, u32[]{:S(2)}, u32[]{:S(2)}) collective-permute-start(bf16[368,128]{1,0:T(8,128)(2,1)S(1)} %get-tuple-element.92), channel_id=1, source_target_pairs={{0,6},{1,7},{2,4},{3,5},{4,2},{5,3},{6,0},{7,1},{8,14},{9,15},{10,... | collective-permute-start | bytes 282632 | tf_op jit(solution)/shard_map/ppermute | solution.py:286
  65.7 6.6 %collective-permute-start.27 = (bf16[368,128]{1,0:T(8,128)(2,1)S(1)}, bf16[368,128]{1,0:T(8,128)(2,1)S(1)}, u32[]{:S(2)}, u32[]{:S(2)}) collective-permute-start(bf16[368,128]{1,0:T(8,128)(2,1)S(1)} %get-tuple-element.101), channel_id=1, source_target_pairs={{0,8},{8,0},{16,24},{24,16},{1,9},{9,1},{17,25},{25,17},{2,10},{10... | collective-permute-start | bytes 282632 | tf_op jit(solution)/shard_map/ppermute | solution.py:286
  67.0 7.6 %collective-permute-start.28 = (bf16[368,128]{1,0:T(8,128)(2,1)S(1)}, bf16[368,128]{1,0:T(8,128)(2,1)S(1)}, u32[]{:S(2)}, u32[]{:S(2)}) collective-permute-start(bf16[368,128]{1,0:T(8,128)(2,1)S(1)} %get-tuple-element.102), channel_id=1, source_target_pairs={{0,16},{8,24},{16,0},{24,8},{1,17},{9,25},{17,1},{25,9},{2,18},{10... | collective-permute-start | bytes 282632 | tf_op jit(solution)/shard_map/ppermute | solution.py:286
  69.4 6.5 %collective-permute-start.29 = (bf16[368,128]{1,0:T(8,128)(2,1)S(1)}, bf16[368,128]{1,0:T(8,128)(2,1)S(1)}, u32[]{:S(2)}, u32[]{:S(2)}) collective-permute-start(bf16[368,128]{1,0:T(8,128)(2,1)S(1)} %get-tuple-element.103), channel_id=1, source_target_pairs={{0,24},{8,16},{16,8},{24,0},{1,25},{9,17},{17,9},{25,1},{2,26},{10... | collective-permute-start | bytes 282632 | tf_op jit(solution)/shard_map/ppermute | solution.py:286
